TPU v7x, 32 devices: a whole 2x2x4 slice. The times are simulated.
32 devices in a mesh: gz: 4 (over z), gx: 8 (over y, x, core).
Axes of the slice: x: 2, y: 2, z: 4, core: 2. Of those that a mesh axis runs over, the one named last changes fastest.
Arguments:
- strain: float32 [6, 2, 1024, 1024], P(None, None, 'gx', 'gz'), may hold values from -6 to 6
- labels: int32 [2, 1024, 1024], P(None, 'gx', 'gz'), may hold values 0 or 1
- normals: int32 [2, 64, 64], P(None, 'gx', 'gz'), may hold values from 0 to 7
- moduli: float32 [5], replicated, may hold values from 0.5 to 4
- mean_strain: float32 [6], replicated, may hold values from -4 to 4
Outputs:
- strain_next: float32 [6, 2, 1024, 1024], P(None, None, 'gx', 'gz')
- stress_next: float32 [6, 2, 1024, 1024], P(None, None, 'gx', 'gz')
All inputs are finite; a program needn't handle non-finite values. No bound on the sum of `labels` on one device may be relied on, other than what follows from the above.
Results may differ from a plain program's by a relative error of at most 0.000082.
Values sent between devices are 32-bit elements; how exact they have to be, the bound alone decides.
No kernel may reach another device: no remote copies, remote signals or barrier semaphores. Data moves between devices by JAX's collectives and lax.ppermute only.
A program may use at most 128 MiB of HBM per device.

v0:
```python
import math

import jax
import jax.numpy as jnp
from jax import lax
from jax.sharding import PartitionSpec as P

ANGLES = 8
BLK = 16


def orientation(normals):
    tilt_angle = math.pi / ANGLES * normals.astype(jnp.float32)
    tilt_angle = jnp.repeat(jnp.repeat(tilt_angle, BLK, axis=1), BLK, axis=2)
    return (jnp.cos(tilt_angle), jnp.sin(tilt_angle))


def stress_law(strain_field, labels, cosine_tilt, sine_tilt, moduli):
    laminate = labels == 1
    lame_local = jnp.where(laminate, moduli[2], moduli[0])
    shear_local = jnp.where(laminate, moduli[3], moduli[1])
    trace_sum = strain_field[0] + strain_field[1] + strain_field[2]
    normal_part = (
        cosine_tilt * cosine_tilt * strain_field[0]
        + sine_tilt * sine_tilt * strain_field[2]
        + 2.0 * cosine_tilt * sine_tilt * strain_field[4]
    )
    laminate_term = moduli[4] * labels.astype(jnp.float32) * normal_part
    dyad = [
        cosine_tilt * cosine_tilt,
        None,
        sine_tilt * sine_tilt,
        None,
        cosine_tilt * sine_tilt,
        None,
    ]
    result = []
    for slot in range(6):
        value = 2.0 * shear_local * strain_field[slot]
        if slot < 3:
            value = value + lame_local * trace_sum
        if dyad[slot] is not None:
            value = value + laminate_term * dyad[slot]
        result.append(value)
    return jnp.stack(result)


def polarize(stresses, strain_field, lame_ref, shear_ref):
    trace_sum = strain_field[0] + strain_field[1] + strain_field[2]
    result = []
    for slot in range(6):
        value = stresses[slot] - 2.0 * shear_ref * strain_field[slot]
        if slot < 3:
            value = value - lame_ref * trace_sum
        result.append(value)
    return jnp.stack(result)


def green_apply(spectrum, unit_x, unit_z, lame_ref, shear_ref):
    coupling = (lame_ref + shear_ref) / (shear_ref * (lame_ref + 2.0 * shear_ref))
    traction_x = spectrum[0] * unit_x + spectrum[4] * unit_z
    traction_y = spectrum[5] * unit_x + spectrum[3] * unit_z
    traction_z = spectrum[4] * unit_x + spectrum[2] * unit_z
    normal_load = unit_x * traction_x + unit_z * traction_z
    half_inverse = 0.5 / shear_ref
    result = [
        2.0 * half_inverse * unit_x * traction_x - coupling * normal_load * unit_x * unit_x,
        jnp.zeros_like(traction_x),
        2.0 * half_inverse * unit_z * traction_z - coupling * normal_load * unit_z * unit_z,
        half_inverse * unit_z * traction_y,
        half_inverse * (unit_z * traction_x + unit_x * traction_z)
        - coupling * normal_load * unit_x * unit_z,
        half_inverse * unit_x * traction_y,
    ]
    return -jnp.stack(result)


def twiddle(left_ids, right_ids, length):
    product = left_ids[:, None] * right_ids[None, :] % length
    phase_angle = 2.0 * math.pi / length * product.astype(jnp.float32)
    return (jnp.cos(phase_angle), jnp.sin(phase_angle))


def contract(form, left_side, right_side):
    return jnp.einsum(
        form,
        left_side,
        right_side,
        precision=lax.Precision.HIGHEST,
        preferred_element_type=jnp.float32,
    )


def signed_value(counter, length):
    return jnp.where(counter < length // 2, counter, counter - length).astype(jnp.float32)


def shards(strain, labels, normals, moduli, mean_strain):
    z_devices = lax.axis_size("gz")
    x_devices = lax.axis_size("gx")
    z_index = lax.axis_index("gz")
    x_index = lax.axis_index("gx")
    sections = strain.shape[1]
    cells_x = strain.shape[2]
    cells_z = strain.shape[3]
    x_total = cells_x * x_devices
    z_total = cells_z * z_devices
    line_count = sections * cells_x
    kz_share = cells_z // x_devices
    cosine_tilt, sine_tilt = orientation(normals)
    lame_ref = 0.5 * (moduli[0] + moduli[2])
    shear_ref = 0.5 * (moduli[1] + moduli[3])
    stresses = stress_law(strain, labels, cosine_tilt, sine_tilt, moduli)
    polarized = polarize(stresses, strain, lame_ref, shear_ref)
    flattened = polarized.reshape(6, line_count, cells_z)
    own_block = z_index * cells_z + jnp.arange(cells_z, dtype=jnp.int32)
    empty_sum = jnp.zeros((6, cells_z, line_count), jnp.float32)
    pieces = lax.all_gather(flattened, "gz", axis=2, tiled=True)
    z_ids = jnp.arange(pieces.shape[2], dtype=jnp.int32)
    cos_table, sin_table = twiddle(z_ids, own_block, z_total)
    real_part = contract("cmz,zk->ckm", pieces, cos_table)
    imag_part = (empty_sum, empty_sum)[1] - contract("cmz,zk->ckm", pieces, sin_table)
    real_rows, imag_rows = (
        lax.all_to_all(real_part, "gx", split_axis=1, concat_axis=2, tiled=True),
        lax.all_to_all(imag_part, "gx", split_axis=1, concat_axis=2, tiled=True),
    )
    grid_shape = (6, kz_share, x_devices, sections, cells_x)
    real_rows = real_rows.reshape(grid_shape)
    imag_rows = imag_rows.reshape(grid_shape)
    every_x = jnp.arange(x_total, dtype=jnp.int32)
    cos_x, sin_x = twiddle(every_x, every_x, x_total)
    cos_x = cos_x.reshape(x_devices, cells_x, x_total)
    sin_x = sin_x.reshape(x_devices, cells_x, x_total)
    spec_real = contract("ckgsx,gxq->cksq", real_rows, cos_x) + contract(
        "ckgsx,gxq->cksq", imag_rows, sin_x
    )
    spec_imag = contract("ckgsx,gxq->cksq", imag_rows, cos_x) - contract(
        "ckgsx,gxq->cksq", real_rows, sin_x
    )
    kz_ids = z_index * cells_z + x_index * kz_share + jnp.arange(kz_share, dtype=jnp.int32)
    freq_z = signed_value(kz_ids, z_total)[:, None, None]
    freq_x = signed_value(every_x, x_total)[None, None, :]
    radius_sq = freq_x * freq_x + freq_z * freq_z
    at_anchor = radius_sq == 0.0
    safe_radius = jnp.sqrt(jnp.where(at_anchor, 1.0, radius_sq))
    unit_x = freq_x / safe_radius
    unit_z = freq_z / safe_radius
    anchor_term = jnp.where(at_anchor, float(x_total * z_total), 0.0)
    new_real = green_apply(spec_real, unit_x, unit_z, lame_ref, shear_ref)
    new_real = new_real + mean_strain[:, None, None, None] * anchor_term[None]
    new_imag = green_apply(spec_imag, unit_x, unit_z, lame_ref, shear_ref)
    back_real = contract("cksq,gxq->ckgsx", new_real, cos_x) - contract(
        "cksq,gxq->ckgsx", new_imag, sin_x
    )
    back_imag = contract("cksq,gxq->ckgsx", new_real, sin_x) + contract(
        "cksq,gxq->ckgsx", new_imag, cos_x
    )
    back_real = back_real.reshape(6, kz_share, x_devices * line_count)
    back_imag = back_imag.reshape(6, kz_share, x_devices * line_count)
    real_part, imag_part = (
        lax.all_to_all(back_real, "gx", split_axis=2, concat_axis=1, tiled=True),
        lax.all_to_all(back_imag, "gx", split_axis=2, concat_axis=1, tiled=True),
    )
    z_ids = jnp.arange(lax.axis_size("gz") * cells_z, dtype=jnp.int32)
    cos_table, sin_table = twiddle(own_block, z_ids, z_total)
    summed = lax.psum_scatter(
        contract("ckm,kz->zcm", real_part, cos_table)
        - contract("ckm,kz->zcm", imag_part, sin_table),
        "gz",
        scatter_dimension=0,
        tiled=True,
    )
    field_lines = jnp.transpose(summed, (1, 2, 0))
    strain_next = (field_lines * (1.0 / (x_total * z_total))).reshape(6, sections, cells_x, cells_z)
    stress_next = stress_law(strain_next, labels, cosine_tilt, sine_tilt, moduli)
    return (strain_next, stress_next)


def solution(mesh):
    in_specs = (P(None, None, "gx", "gz"), P(None, "gx", "gz"), P(None, "gx", "gz"), P(), P())
    out_specs = (P(None, None, "gx", "gz"), P(None, None, "gx", "gz"))
    return jax.shard_map(shards, mesh=mesh, in_specs=in_specs, out_specs=out_specs, check_vma=False)
```

profile of v0, /device:TPU:11, one launch (start us, length us, event | category | flops | bytes accessed | tf_op | source)
XLA Modules:
  0.0 617.4 jit_solution(9719802264566288627)
XLA Ops:
  16.0 4.4 fusion.116
  23.5 113.9 %all-gather.2.cloned.1.call-done = f32[6,256,1024]{2,1,0:T(8,128)} async-done(((f32[6,256,256]{2,1,0:T(8,128)}), f32[6,256,1024]{2,1,0:T(8,128)}) %all-gather.2.cloned.1.call-update) | async-done | bytes 6291472 | tf_op jit(solution)/shard_map/all_gather | solution.py:118
  137.4 12.1 %subtract_bitcast_fusion.1 = f32[6,256,256]{2,1,0:T(8,128)S(1)} fusion(f32[6,256,1024]{2,1,0:T(8,128)} %all-gather.2.cloned.1.call-done, s32[256]{0:T(256)S(1)} %iota_add_fusion), kind=kOutput, calls=%fused_computation.51 | convolution fusion | flops 4835901440 | bytes 7865344 | tf_op jit(solution)/shard_map/cmz,zk->ckm/dot_general | solution.py:85
  152.0 4.5 all-to-all-start.1
  156.5 12.0 %convolution_bitcast_fusion = f32[6,256,256]{2,1,0:T(8,128)S(1)} fusion(f32[6,256,1024]{2,1,0:T(8,128)} %all-gather.2.cloned.1.call-done, s32[256]{0:T(256)S(1)} %iota_add_fusion), kind=kOutput, calls=%fused_computation.58 | convolution fusion | flops 4835508224 | bytes 7865344 | tf_op jit(solution)/shard_map/cmz,zk->ckm/dot_general | solution.py:85
  170.9 10.7 %all-to-all-done.1 = f32[6,256,256]{2,0,1:T(8,128)S(1)} async-done(((f32[6,256,256]{2,0,1:T(8,128)}), f32[6,256,256]{2,0,1:T(8,128)S(1)}, u32[]{:S(2)}, u32[]{:S(2)}) %all-to-all-start.1) | async-done | bytes 1572896 | tf_op jit(solution)/shard_map/all_to_all | solution.py:125
  181.6 6.2 %all-to-all-start = ((f32[6,256,256]{2,0,1:T(8,128)}), f32[6,256,256]{2,0,1:T(8,128)}, u32[]{:S(2)}, u32[]{:S(2)}) async-start(f32[6,256,256]{2,0,1:T(8,128)} %copy.120), calls=%async_computation | async-start | bytes 4194304 | tf_op jit(solution)/shard_map/all_to_all | solution.py:124
  191.1 21.5 %all-to-all-done = f32[6,256,256]{2,0,1:T(8,128)} async-done(((f32[6,256,256]{2,0,1:T(8,128)}), f32[6,256,256]{2,0,1:T(8,128)}, u32[]{:S(2)}, u32[]{:S(2)}) %all-to-all-start) | async-done | bytes 1572896 | tf_op jit(solution)/shard_map/all_to_all | solution.py:124
  215.2 21.0 %fusion.16 = f32[6,32,2,1024,1]{3,1,4,2,0:T(8,128)S(1)} fusion(s32[8,128]{1,0:T(8,128)S(1)} %multiply_add_fusion, f32[6,32,8,2,128]{4,2,3,1,0:T(8,128)S(1)} %bitcast.385), kind=kOutput, calls=%fused_computation.22 | convolution fusion | flops 4846518272 | bytes 3149824 | tf_op jit(solution)/shard_map/ckgsx,gxq->cksq/dot_general | solution.py:85
  236.2 21.4 %fusion.14 = f32[6,32,2,1024,1]{3,1,4,2,0:T(8,128)S(1)} fusion(s32[8,128]{1,0:T(8,128)S(1)} %multiply_add_fusion, f32[6,32,8,2,128]{4,2,3,1,0:T(8,128)S(1)} %bitcast.387), kind=kOutput, calls=%fused_computation.20 | convolution fusion | flops 4846518272 | bytes 3149824 | tf_op jit(solution)/shard_map/ckgsx,gxq->cksq/dot_general | solution.py:85
  257.7 21.1 %bitcast_add_fusion = f32[6,32,2,1024]{3,1,2,0:T(8,128)S(1)} fusion(f32[6,32,2,1024,1]{3,1,4,2,0:T(8,128)S(1)} %fusion.16, s32[8,128]{1,0:T(8,128)S(1)} %multiply_add_fusion, f32[6,32,8,2,128]{4,2,3,1,0:T(8,128)S(1)} %bitcast.388), kind=kOutput, calls=%fused_computation.44 | convolution fusion | flops 4846911488 | bytes 4722688 | tf_op jit(solution)/shard_map/ckgsx,gxq->cksq/dot_general | solution.py:85
  278.8 21.3 %bitcast_subtract_fusion = f32[6,32,2,1024]{3,1,2,0:T(8,128)S(1)} fusion(f32[6,32,2,1024,1]{3,1,4,2,0:T(8,128)S(1)} %fusion.14, s32[8,128]{1,0:T(8,128)S(1)} %multiply_add_fusion, f32[6,32,8,2,128]{4,2,3,1,0:T(8,128)S(1)} %bitcast.386), kind=kOutput, calls=%fused_computation.41 | convolution fusion | flops 4846911488 | bytes 4722688 | tf_op jit(solution)/shard_map/ckgsx,gxq->cksq/dot_general | solution.py:85
  302.4 21.4 %fusion.6 = f32[8,128,6,32,2]{1,3,4,2,0:T(8,128)S(1)} fusion(s32[8,128]{1,0:T(8,128)S(1)} %multiply_add_fusion, f32[6,32,2,1024]{3,1,2,0:T(8,128)S(1)} %get-tuple-element.32), kind=kOutput, calls=%fused_computation.12 | convolution fusion | flops 4846911488 | bytes 3149824 | tf_op jit(solution)/shard_map/cksq,gxq->ckgsx/dot_general | solution.py:85
  323.8 21.1 %add_bitcast_fusion = f32[6,32,8,2,128]{4,1,3,0,2:T(8,128)S(1)} fusion(f32[8,128,6,32,2]{1,3,4,2,0:T(8,128)S(1)} %fusion.6, s32[8,128]{1,0:T(8,128)S(1)} %multiply_add_fusion, f32[6,32,2,1024]{3,1,2,0:T(8,128)S(1)} %get-tuple-element.33, f32[6,32,1024]{2,1,0:T(8,128)S(1)} %broadcast_multiply_fusion), kind=kOutput, calls=%fused_computation.48 | convolution fusion | flops 4847697920 | bytes 5509120 | tf_op jit(solution)/shard_map/cksq,gxq->ckgsx/dot_general | solution.py:85
  344.9 4.7 copy.165
  349.6 8.3 %reshape.484 = f32[8,1,49152]{2,1,0:T(1,128)} reshape(f32[2048,6,32]{2,1,0:T(8,128)} %bitcast.378) | data formatting | bytes 3145728
  357.9 5.6 all-to-all-start.3
  363.6 22.4 %fusion.8 = f32[8,128,6,32,2]{1,3,4,2,0:T(8,128)S(1)} fusion(s32[8,128]{1,0:T(8,128)S(1)} %multiply_add_fusion, f32[6,32,2,1024]{3,1,2,0:T(8,128)} %copy-done.12, f32[6,32,1024]{2,1,0:T(8,128)S(1)} %copy-done.4), kind=kOutput, calls=%fused_computation.14 | convolution fusion | flops 4847304704 | bytes 3936256 | tf_op jit(solution)/shard_map/cksq,gxq->ckgsx/dot_general | solution.py:85
  386.0 21.5 %subtract_bitcast_fusion = f32[6,32,8,2,128]{4,1,3,0,2:T(8,128)S(1)} fusion(f32[8,128,6,32,2]{1,3,4,2,0:T(8,128)S(1)} %fusion.8, f32[6,32,2,1024]{3,1,2,0:T(8,128)S(1)} %copy-done.11, s32[8,128]{1,0:T(8,128)S(1)} %multiply_add_fusion), kind=kOutput, calls=%fused_computation.49 | convolution fusion | flops 4847304704 | bytes 4722688 | tf_op jit(solution)/shard_map/cksq,gxq->ckgsx/dot_general | solution.py:85
  407.5 4.7 copy.162
  412.2 8.3 %reshape.482 = f32[8,1,49152]{2,1,0:T(1,128)} reshape(f32[2048,6,32]{2,1,0:T(8,128)} %bitcast.379) | data formatting | bytes 3145728
  420.5 4.3 all-to-all-start.2
  425.5 4.4 reduce.1
  429.9 6.3 %reshape.485 = f32[2048,6,32]{2,1,0:T(8,128)} reshape(f32[8,49152]{1,0:T(8,128)S(1)} %reduce.1) | data formatting | bytes 3145728
  436.2 5.0 copy.137
  441.2 3.2 all-to-all-done.2
  444.4 5.8 reduce
  450.2 6.3 %reshape.483 = f32[2048,6,32]{2,1,0:T(8,128)} reshape(f32[8,49152]{1,0:T(8,128)S(1)} %reduce) | data formatting | bytes 3145728
  456.4 5.1 copy.133
  461.5 9.3 %fusion.71 = f32[1024,6,256]{2,0,1:T(8,128)S(1)} fusion(f32[6,256,256]{2,1,0:T(8,128)S(1)} %bitcast.384, s32[256]{0:T(256)S(1)} %iota_add_fusion), kind=kOutput, calls=%fused_computation.74 | convolution fusion | flops 4835508224 | bytes 7865344 | tf_op jit(solution)/shard_map/ckm,kz->zcm/dot_general | solution.py:85
  470.8 11.3 %convolution_subtract_fusion = f32[1024,6,256]{2,0,1:T(8,128)} fusion(f32[1024,6,256]{2,0,1:T(8,128)S(1)} %fusion.71, f32[6,256,256]{2,1,0:T(8,128)S(1)} %bitcast.383, s32[256]{0:T(256)S(1)} %iota_add_fusion), kind=kOutput, calls=%fused_computation.34 | convolution fusion | flops 4837081088 | bytes 14156800 | tf_op jit(solution)/shard_map/ckm,kz->zcm/dot_general | solution.py:85
  482.2 110.8 %reduce-scatter.2.cloned.1.call-done = f32[256,6,256]{2,0,1:T(8,128)} async-done(((f32[1024,6,256]{2,0,1:T(8,128)}), f32[256,6,256]{2,0,1:T(8,128)}) %reduce-scatter.2.cloned.1.call-update) | async-done | bytes 1572880 | tf_op jit(solution)/shard_map/reduce_scatter | solution.py:166
  (101 shorter events, 39.4 us)
Async XLA Ops:
  7.2 130.2 %all-gather.2.cloned.1.call-start = ((), (), s32[]{:S(2)}) async-start(), calls=%async_computation.5 | async-start | bytes 7864320 | tf_op jit(solution)/shard_map/all_gather | solution.py:118
  8.7 1.7 copy-start.9
  10.4 0.8 copy-start.13
  22.3 1.1 copy-start
  152.0 29.6 %all-to-all-start.1 = ((f32[6,256,256]{2,0,1:T(8,128)}), f32[6,256,256]{2,0,1:T(8,128)S(1)}, u32[]{:S(2)}, u32[]{:S(2)}) async-start(f32[6,256,256]{2,0,1:T(8,128)} %copy.124), calls=%async_computation.1 | async-start | bytes 4194304 | tf_op jit(solution)/shard_map/all_to_all | solution.py:125
  170.9 18.0 %copy-start.14 = (f32[6]{0:T(128)S(1)}, f32[6]{0:T(128)}, u32[]{:S(2)}) copy-start(f32[6]{0:T(128)} %param.9) | copy-start | bytes 76
  181.6 31.0 %all-to-all-start = ((f32[6,256,256]{2,0,1:T(8,128)}), f32[6,256,256]{2,0,1:T(8,128)}, u32[]{:S(2)}, u32[]{:S(2)}) async-start(f32[6,256,256]{2,0,1:T(8,128)} %copy.120), calls=%async_computation | async-start | bytes 4194304 | tf_op jit(solution)/shard_map/all_to_all | solution.py:124
  189.0 134.8 %copy-start.3 = (f32[6,32,1024]{2,1,0:T(8,128)}, f32[6,32,1024]{2,1,0:T(8,128)S(1)}, u32[]{:S(2)}) copy-start(f32[6,32,1024]{2,1,0:T(8,128)S(1)} %broadcast_multiply_fusion) | copy-start | bytes 2359300
  212.6 2.6 copy-start.1
  278.7 21.3 %copy-start.8 = (f32[32,1024]{1,0:T(8,128)S(1)}, f32[32,1024]{1,0:T(8,128)}, u32[]{:S(2)}) copy-start(f32[32,1024]{1,0:T(8,128)} %get-tuple-element.44) | copy-start | bytes 393220
  300.1 0.9 copy-start.7
  300.3 0.9 copy-start.6
  301.4 0.9 copy-start.5
  302.4 21.4 %copy-start.10 = (f32[6,32,2,1024]{3,1,2,0:T(8,128)}, f32[6,32,2,1024]{3,1,2,0:T(8,128)S(1)}, u32[]{:S(2)}) copy-start(f32[6,32,2,1024]{3,1,2,0:T(8,128)S(1)} %get-tuple-element.32) | copy-start | bytes 4718596
  302.4 21.4 %copy-start.12 = (f32[6,32,2,1024]{3,1,2,0:T(8,128)}, f32[6,32,2,1024]{3,1,2,0:T(8,128)S(1)}, u32[]{:S(2)}) copy-start(f32[6,32,2,1024]{3,1,2,0:T(8,128)S(1)} %get-tuple-element.33) | copy-start | bytes 4718596
  357.9 5.6 copy-start.4
  357.9 62.6 %all-to-all-start.3 = ((f32[8,1,49152]{2,1,0:T(1,128)}), f32[8,1,49152]{2,1,0:T(1,128)S(1)}, u32[]{:S(2)}, u32[]{:S(2)}) async-start(f32[8,1,49152]{2,1,0:T(1,128)} %reshape.484), calls=%async_computation.3 | async-start | bytes 3145728 | tf_op jit(solution)/shard_map/all_to_all | solution.py:162
  363.6 22.4 %copy-start.11 = (f32[6,32,2,1024]{3,1,2,0:T(8,128)S(1)}, f32[6,32,2,1024]{3,1,2,0:T(8,128)}, u32[]{:S(2)}) copy-start(f32[6,32,2,1024]{3,1,2,0:T(8,128)} %copy-done.10) | copy-start | bytes 4718596
  420.5 23.9 %all-to-all-start.2 = ((f32[8,1,49152]{2,1,0:T(1,128)}), f32[8,1,49152]{2,1,0:T(1,128)}, u32[]{:S(2)}, u32[]{:S(2)}) async-start(f32[8,1,49152]{2,1,0:T(1,128)} %reshape.482), calls=%async_computation.2 | async-start | bytes 3145728 | tf_op jit(solution)/shard_map/all_to_all | solution.py:161
  424.8 168.2 %reduce-scatter.2.cloned.1.call-start = ((), (), s32[]{:S(2)}) async-start(), calls=%async_computation.6 | async-start | bytes 7864320 | tf_op jit(solution)/shard_map/reduce_scatter | solution.py:166
  605.4 1.7 copy-start.2
Sparse Core Ops, SparseCore 0:
  23.6 113.7 all-gather.1
  482.3 110.6 reduce-scatter.1
where the time goes:
time: 629 us; the launch traced here: 617 us
  waiting for transfers between devices  260 us (41%)
  matrix products  216 us (34%)
  local copies, waits for them, and re-layouts  71.8 us (11%)
  other arithmetic  30.7 us (5%)
  starting transfers between devices  20.8 us (3%)
  between operations  18 us (3%)
    dot_general x12, matrix products, contract(): jnp.einsum(form, left_side, right_side, precision=lax.Precision.HIGHEST,...  216 us
    all_gather x1, waiting for transfers between devices, shards(): pieces = lax.all_gather(flattened, 'gz', axis=2, tiled=True)  114 us
    reduce_scatter x1, waiting for transfers between devices, shards(): lax.psum_scatter(contract('ckm,kz->zcm', real_part, cos_table) - contract...  111 us
    unnamed x52, local copies, waits for them, and re-layouts  35.9 us
    all_to_all x1, waiting for transfers between devices, shards(): lax.all_to_all(real_part, 'gx', split_axis=1, concat_axis=2, tiled=True)  21.5 us
  transfers between devices with their start and end apart: 6, of which 5 were waited for; matrix products, arithmetic and copies ran while one was open for 15% of the time, Pallas kernels for 0%

commit v1 on v0

--- a/solution.py
+++ b/solution.py
@@ -1,17 +1,442 @@
+import functools
 import math
 
 import jax
 import jax.numpy as jnp
+import numpy as np
 from jax import lax
+from jax.experimental import pallas as pl
+from jax.experimental.pallas import tpu as pltpu
 from jax.sharding import PartitionSpec as P
 
 ANGLES = 8
-BLK = 16
-
-
-def orientation(normals):
+XX, YY, ZZ, YZ, XZ, XY = range(6)
+GROUPS = (
+    ((XY, 0), (YZ, 0)),
+    ((XX, 0), (ZZ, 0), (XZ, 0)),
+    ((XX, 1), (ZZ, 1), (XZ, 1)),
+    ((XY, 1), (YZ, 1)),
+)
+INPLANE = (1, 2)
+F32, BF16 = jnp.float32, jnp.bfloat16
+MIB = 1 << 20
+
+
+def split_table(table):
+    table = np.asarray(table, np.float32)
+    high = table.astype(jnp.bfloat16)
+    low = (table - high.astype(np.float32)).astype(jnp.bfloat16)
+    return jnp.asarray(high), jnp.asarray(low)
+
+
+def half_frequencies(length):
+    quarter = length // 4
+    return (
+        4 * np.arange(quarter) + 1,
+        4 * np.arange(quarter // 2),
+        4 * np.arange(quarter // 2) + 2,
+    )
+
+
+def interleave(real, imag, slots):
+    rows, count = real.shape
+    both = np.stack([real.reshape(rows, -1, slots), imag.reshape(rows, -1, slots)], 2)
+    return both.reshape(rows, 2 * count)
+
+
+def z_tables(length, slots, scale):
+    quarter = length // 4
+    z = np.arange(quarter, dtype=np.int64)[:, None]
+    ones, zeros, twos = half_frequencies(length)
+
+    def angles(freqs):
+        return 2.0 * math.pi / length * ((z * freqs[None, :]) % length)
+
+    one, zero, two = angles(ones), angles(zeros), angles(twos)
+    top = interleave(np.cos(one), -np.sin(one), slots)
+    bottom = interleave(-np.sin(one), -np.cos(one), slots)
+    forward_one = np.concatenate([top, bottom], 0)
+    real, imag = np.cos(zero), -np.sin(zero)
+    imag[:, 0] = np.where(np.arange(quarter) % 2 == 0, 1.0, -1.0)
+    forward_zero = interleave(real, imag, slots)
+    forward_two = interleave(np.cos(two), -np.sin(two), slots)
+    weight = 2.0 * scale
+    inverse_one = weight * np.concatenate(
+        [interleave(np.cos(one), -np.sin(one), slots), interleave(np.sin(one), np.cos(one), slots)], 0
+    ).T
+    half = np.full(quarter // 2, weight)
+    half[0] = scale
+    inverse_zero = interleave(real * half, imag * half, slots).T
+    inverse_two = weight * forward_two.T
+    return (
+        split_table(forward_one) + split_table(np.stack([forward_zero, forward_two])),
+        split_table(inverse_one) + split_table(np.stack([inverse_zero, inverse_two])),
+    )
+
+
+def x_tables(length):
+    quarter = length // 4
+    k = np.arange(quarter, dtype=np.int64)
+    forward, inverse = [], []
+    for residue in range(4):
+        angle = 2.0 * math.pi / length * (((4 * k[:, None] + residue) * k[None, :]) % length)
+        forward.append(np.concatenate([np.cos(angle), np.sin(angle)], 0))
+        inverse.append(np.concatenate([np.cos(angle.T), np.sin(angle.T)], 0))
+    return split_table(np.stack(forward)) + split_table(np.stack(inverse))
+
+
+def halves(value):
+    high = value.astype(BF16)
+    return high, (value - high.astype(F32)).astype(BF16)
+
+
+def dot(left, right):
+    return jnp.dot(left, right, preferred_element_type=F32)
+
+
+def dot_right(value, high_table, low_table):
+    high, low = halves(value)
+    return dot(high, high_table) + (dot(low, high_table) + dot(high, low_table))
+
+
+def dot_left(high_table, low_table, high, low):
+    return dot(high_table, high) + (dot(high_table, low) + dot(low_table, high))
+
+
+def tilt(normals, section, cells_z):
+    blocks = normals[section].astype(F32)
+    count = blocks.shape[1]
+    size = cells_z // count
+    owner = lax.broadcasted_iota(jnp.int32, (count, cells_z), 1) // size
+    own = lax.broadcasted_iota(jnp.int32, (count, cells_z), 0)
+    spread = jnp.where(owner == own, 1.0, 0.0).astype(F32)
+    angle = (math.pi / ANGLES) * dot(blocks, spread)
+    cosine, sine = jnp.cos(angle), jnp.sin(angle)
+    return cosine * cosine, sine * sine, cosine * sine
+
+
+def law(strain, label, squares, lame, shear, stiff):
+    cc, ss, cs = squares
+    laminate = label == 1
+    lame_local = jnp.where(laminate, lame[1], lame[0])
+    twice_shear = jnp.where(laminate, 2.0 * shear[1], 2.0 * shear[0])
+    spherical = lame_local * (strain[XX] + strain[YY] + strain[ZZ])
+    normal = cc * strain[XX] + ss * strain[ZZ] + 2.0 * cs * strain[XZ]
+    normal = jnp.where(laminate, stiff, 0.0) * normal
+    return {
+        XX: twice_shear * strain[XX] + spherical + normal * cc,
+        YY: twice_shear * strain[YY] + spherical,
+        ZZ: twice_shear * strain[ZZ] + spherical + normal * ss,
+        YZ: twice_shear * strain[YZ],
+        XZ: twice_shear * strain[XZ] + normal * cs,
+        XY: twice_shear * strain[XY],
+    }
+
+
+def row_of(squares, block, size):
+    return [jnp.broadcast_to(s[block : block + 1], (size, s.shape[1])) for s in squares]
+
+
+def polarize_kernel(moduli, strain, labels, normals, *rest):
+    outs, held = rest[:-1], rest[-1]
+    parts = len(GROUPS)
+    place = lax.axis_index("gz")
+    sections, cells_x, cells_z = labels.shape
+    size = cells_x // normals.shape[1]
+    lame_ref = 0.5 * (moduli[0] + moduli[2])
+    shear_ref = 0.5 * (moduli[1] + moduli[3])
+    lame = (moduli[0] - lame_ref, moduli[2] - lame_ref)
+    shear = (moduli[1] - shear_ref, moduli[3] - shear_ref)
+    for group, fields in enumerate(GROUPS):
+        if len(fields) < 3:
+            held[group, 2] = jnp.zeros((cells_x, cells_z), F32)
+    for section in range(sections):
+        squares = tilt(normals, section, cells_z)
+        for block in range(cells_x // size):
+            rows = pl.ds(block * size, size)
+            local = [strain[c, section, rows, :] for c in range(6)]
+            value = law(local, labels[section, rows, :], row_of(squares, block, size), lame, shear, moduli[4])
+            for group, fields in enumerate(GROUPS):
+                for slot, (component, of) in enumerate(fields):
+                    if of == section:
+                        held[group, slot, rows, :] = value[component]
+    for step in range(parts):
+        target = lax.rem(place + step, parts)
+        outs[step][...] = held[target, 0:2]
+        outs[parts + step][...] = held[target, 2:3]
+
+
+def z_forward_kernel(one_h, one_l, two_h, two_l, *rest):
+    parts = len(GROUPS)
+    pairs, thirds, out, held = rest[:parts], rest[parts : 2 * parts], rest[-2], rest[-1]
+    place = lax.axis_index("gz")
+    for step in range(parts):
+        source = lax.rem(place + parts - step, parts)
+        held[source, 0:2] = pairs[step][...]
+        held[source, 2:3] = thirds[step][...]
+    fields, rows, width = held.shape[1:]
+    lanes = out.shape[3]
+    z0, z1, z2, z3 = (held[k].reshape(fields * rows, width) for k in range(parts))
+    first = jnp.concatenate([z0 - z2, z1 - z3], 1)
+    even, odd = z0 + z2, z1 + z3
+    spectra = (
+        dot_right(first, one_h[...], one_l[...]),
+        dot_right(even + odd, two_h[0], two_l[0]),
+        dot_right(even - odd, two_h[1], two_l[1]),
+    )
+    target = 0
+    for spectrum in spectra:
+        for k in range(spectrum.shape[1] // lanes):
+            out[target] = spectrum[:, k * lanes : (k + 1) * lanes].reshape(fields, rows, lanes)
+            target += 1
+
+
+def quarter_turn(value, sign):
+    lanes = value.shape[1]
+    return jnp.concatenate(
+        [pltpu.roll(value[:, k : k + 128], 64, 1) for k in range(0, lanes, 128)], 1
+    ) * sign
+
+
+def green_kernel(x_cells, z_cells, moduli, mean, fwd_h, fwd_l, inv_h, inv_l, data, out, low_s, high_s, field_s):
+    sources, fields, rows, lanes = data.shape
+    quarter = x_cells // 4
+    per = quarter // rows
+    slots = lanes // 2
+    width = (fields + 1) * lanes
+    place, mine = lax.axis_index("gz"), lax.axis_index("gx")
+    inplane = functools.reduce(jnp.logical_or, [place == k for k in INPLANE])
+    lame_ref = 0.5 * (moduli[0] + moduli[2])
+    shear_ref = 0.5 * (moduli[1] + moduli[3])
+    half_inverse = 0.5 / shear_ref
+    coupling = (lame_ref + shear_ref) / (shear_ref * (lame_ref + 2.0 * shear_ref))
+    c1 = jnp.where(inplane, coupling, 0.0)
+    k1 = jnp.where(inplane, 2.0 * half_inverse, half_inverse)
+    k2 = jnp.where(inplane, half_inverse, 0.0)
+    ka = jnp.where(inplane, 0.0, half_inverse)
+    lane_all = lax.broadcasted_iota(jnp.int32, (1, width), 1) % lanes
+    sign_all = jnp.where(lane_all < slots, 1.0, -1.0)
+    sign = sign_all[:, : fields * lanes]
+    lane = lane_all[:, :lanes]
+
+    block = [
+        jnp.concatenate(
+            [data[a * per : (a + 1) * per, f].reshape(quarter, lanes) for f in range(fields)], 1
+        )
+        for a in range(4)
+    ]
+    even, odd = block[0] + block[2], block[1] + block[3]
+    diff, turned = block[0] - block[2], quarter_turn(block[1] - block[3], sign)
+    for residue, value in enumerate((even + odd, diff + turned, even - odd, diff - turned)):
+        high_s[residue, :, : fields * lanes], low_s[residue, :, : fields * lanes] = halves(value)
+
+    order = mine * slots + lane % slots
+    quarter_z = z_cells // 4
+    kz = jnp.where(
+        order < quarter_z,
+        4 * order + 1,
+        jnp.where(order < quarter_z + quarter_z // 2, 4 * (order - quarter_z), 4 * (order - quarter_z - quarter_z // 2) + 2),
+    )
+    special = jnp.logical_and(order == quarter_z, lane >= 0)
+    kz = jnp.where(kz < z_cells // 2, kz, kz - z_cells).astype(F32)
+
+    def coefficients(kx, kz, odd_mask):
+        radius = kx * kx + kz * kz
+        inverse = 1.0 / jnp.where(radius == 0.0, 1.0, radius)
+        a, b = kx * kx * inverse, kz * kz * inverse
+        d = kx * kz * inverse * odd_mask
+        ab = a * b
+        ca, cb = k2 - c1 * a, k2 - c1 * b
+        return (
+            a * (k1 - c1 * a),
+            b * (k1 - c1 * b),
+            ka * d - c1 * ab,
+            d * ca,
+            d * cb,
+            k2 - 2.0 * c1 * ab,
+        )
+
+    def apply(m, s):
+        m00, m11, m01, h02, h12, m22 = m
+        return (
+            -(m00 * s[0] + m01 * s[1] + 2.0 * (h02 * s[2])),
+            -(m01 * s[0] + m11 * s[1] + 2.0 * (h12 * s[2])),
+            -(h02 * s[0] + h12 * s[1] + m22 * s[2]),
+        )
+
+    for residue in range(4):
+        both = dot_left(
+            fwd_h[residue], fwd_l[residue], high_s[residue, :, : fields * lanes], low_s[residue, :, : fields * lanes]
+        )
+        spectrum = both[:quarter] + quarter_turn(both[quarter:], sign)
+        s = [spectrum[:, f * lanes : (f + 1) * lanes] for f in range(fields)]
+        kx = 4 * lax.broadcasted_iota(jnp.int32, (quarter, lanes), 0) + residue
+        kx_edge = kx == x_cells // 2
+        anchor = jnp.logical_and(kx == 0, special)
+        kx = jnp.where(kx < x_cells // 2, kx, kx - x_cells).astype(F32)
+        keep = jnp.where(kx_edge, 0.0, 1.0)
+        new = apply(coefficients(kx, jnp.broadcast_to(kz, kx.shape), keep), s)
+        real_lane = lane < slots
+        new = [
+            jnp.where(anchor, jnp.where(real_lane, float(x_cells * z_cells) * mean[f], 0.0), new[f])
+            for f in range(fields)
+        ]
+        keep = jnp.where(kx_edge, 1.0, 0.0)
+        edge = apply(coefficients(kx, jnp.full(kx.shape, -0.5 * z_cells, F32), keep), s)
+        extra = edge[0]
+        for f in range(1, fields):
+            extra = jnp.where(lane % slots == f, pltpu.roll(edge[f], f, 1), extra)
+        high_s[residue], low_s[residue] = halves(jnp.concatenate(list(new) + [extra], 1))
+
+    for residue in range(4):
+        both = dot_left(inv_h[residue], inv_l[residue], high_s[residue], low_s[residue])
+        field_s[residue] = both[:quarter] - quarter_turn(both[quarter:], sign_all)
+    h0, h1, h2, h3 = (field_s[k] for k in range(4))
+    even, odd = h0 + h2, h1 + h3
+    diff, turned = h0 - h2, quarter_turn(h1 - h3, sign_all)
+    swap = jnp.logical_and(special, lane >= slots)
+    for a, value in enumerate((even + odd, diff - turned, even - odd, diff + turned)):
+        extra = value[:, fields * lanes :]
+        for f in range(fields):
+            moved = extra if f == 0 else pltpu.roll(extra, lanes - f, 1)
+            final = jnp.where(swap, moved, value[:, f * lanes : (f + 1) * lanes])
+            out[a * per : (a + 1) * per, f] = final.reshape(per, rows, lanes)
+
+
+def z_inverse_kernel(one_h, one_l, two_h, two_l, data, *rest):
+    outs, held = rest[:-1], rest[-1]
+    parts = len(GROUPS)
+    place = lax.axis_index("gz")
+    sources, fields, rows, lanes = data.shape
+    half = sources // 2
+    fourth = sources // 4
+
+    def columns(begin, end):
+        return jnp.concatenate([data[k].reshape(fields * rows, lanes) for k in range(begin, end)], 1)
+
+    first = dot_right(columns(0, half), one_h[...], one_l[...])
+    zero = dot_right(columns(half, half + fourth), two_h[0], two_l[0])
+    two = dot_right(columns(half + fourth, sources), two_h[1], two_l[1])
+    width = zero.shape[1]
+    real, imag = first[:, :width], first[:, width:]
+    plus, minus = zero + two, zero - two
+    for k, value in enumerate((plus + real, minus - imag, plus - real, minus + imag)):
+        held[k] = value.reshape(fields, rows, width)
+    for step in range(parts):
+        target = lax.rem(place + step, parts)
+        outs[step][...] = held[target, 0:2]
+        outs[parts + step][...] = held[target, 2:3]
+
+
+def stress_kernel(moduli, mean, labels, normals, *rest):
+    parts = len(GROUPS)
+    pairs, thirds = rest[:parts], rest[parts : 2 * parts]
+    strain_out, stress_out, held = rest[2 * parts :]
+    place = lax.axis_index("gz")
+    sections, cells_x, cells_z = labels.shape
+    size = cells_x // normals.shape[1]
+    for step in range(parts):
+        source = lax.rem(place + parts - step, parts)
+        held[source, 0:2] = pairs[step][...]
+        held[source, 2:3] = thirds[step][...]
+    for section in range(sections):
+        squares = tilt(normals, section, cells_z)
+        for block in range(cells_x // size):
+            rows = pl.ds(block * size, size)
+            local = {YY: jnp.full((size, cells_z), mean[YY], F32)}
+            for group, fields in enumerate(GROUPS):
+                for slot, (component, of) in enumerate(fields):
+                    if of == section:
+                        local[component] = held[group, slot, rows, :]
+            value = law(
+                local,
+                labels[section, rows, :],
+                row_of(squares, block, size),
+                (moduli[0], moduli[2]),
+                (moduli[1], moduli[3]),
+                moduli[4],
+            )
+            for component in range(6):
+                strain_out[component, section, rows, :] = local[component]
+                stress_out[component, section, rows, :] = value[component]
+
+
+def call(kernel, outs, scratch, smem, args, limit, flops=0):
+    vmem = pl.BlockSpec(memory_space=pltpu.VMEM)
+    scalar = pl.BlockSpec(memory_space=pltpu.SMEM)
+    moved = sum(a.size * a.dtype.itemsize for a in args) + sum(math.prod(o) * 4 for o in outs)
+    return pl.pallas_call(
+        kernel,
+        out_shape=[jax.ShapeDtypeStruct(o, F32) for o in outs],
+        in_specs=[scalar] * smem + [vmem] * (len(args) - smem),
+        out_specs=[vmem] * len(outs),
+        scratch_shapes=scratch,
+        compiler_params=pltpu.CompilerParams(vmem_limit_bytes=limit * MIB),
+        cost_estimate=pl.CostEstimate(flops=flops, bytes_accessed=moved, transcendentals=0),
+    )(*args)
+
+
+def shards(strain, labels, normals, moduli, mean_strain):
+    parts = lax.axis_size("gz")
+    x_devices = lax.axis_size("gx")
+    _, sections, cells_x, cells_z = strain.shape
+    x_total, z_total = cells_x * x_devices, cells_z * parts
+    slots = z_total // 2 // x_devices
+    lanes = 2 * slots
+    z_fwd, z_inv = z_tables(z_total, slots, 1.0 / (x_total * z_total))
+    x_tab = x_tables(x_total)
+    pair, third = (2, cells_x, cells_z), (1, cells_x, cells_z)
+
+    def travel(outs, sources, targets):
+        pairs, thirds = list(outs[:parts]), list(outs[parts:])
+        for step in range(1, parts):
+            way = [(k, (k + step) % parts) for k in range(parts)]
+            some = [(a, b) for a, b in way if a in sources and b in targets]
+            pairs[step] = lax.ppermute(pairs[step], "gz", way)
+            thirds[step] = lax.ppermute(thirds[step], "gz", some)
+        return pairs + thirds
+
+    everyone = range(parts)
+    held = pltpu.VMEM((parts, 3, cells_x, cells_z), F32)
+    sent = call(
+        polarize_kernel, [pair] * parts + [third] * parts, [held], 1, (moduli, strain, labels, normals), 16
+    )
+    arrived = travel(sent, everyone, INPLANE)
+    grid = (x_devices, 3, cells_x, lanes)
+    (rows,) = call(z_forward_kernel, [grid], [held], 0, (*z_fwd, *arrived), 24)
+    rows = lax.all_to_all(rows, "gx", 0, 0, tiled=True)
+    index = lax.axis_index("gz")
+    inplane = functools.reduce(jnp.logical_or, [index == k for k in INPLANE])
+    mean = jnp.where(
+        inplane,
+        jnp.stack([mean_strain[XX], mean_strain[ZZ], mean_strain[XZ]]),
+        jnp.stack([mean_strain[XY], mean_strain[YZ], mean_strain[XZ]]),
+    )
+    quarter = x_total // 4
+    (rows,) = call(
+        functools.partial(green_kernel, x_total, z_total),
+        [grid],
+        [
+            pltpu.VMEM((4, quarter, 4 * lanes), BF16),
+            pltpu.VMEM((4, quarter, 4 * lanes), BF16),
+            pltpu.VMEM((4, quarter, 4 * lanes), F32),
+        ],
+        2,
+        (moduli, mean, *x_tab, rows),
+        32,
+    )
+    rows = lax.all_to_all(rows, "gx", 0, 0, tiled=True)
+    sent = call(z_inverse_kernel, [pair] * parts + [third] * parts, [held], 0, (*z_inv, rows), 24)
+    arrived = travel(sent, INPLANE, everyone)
+    full = (6, sections, cells_x, cells_z)
+    return tuple(
+        call(stress_kernel, [full, full], [held], 2, (moduli, mean_strain, labels, normals, *arrived), 16)
+    )
+
+
+def orientation(normals, blk):
     tilt_angle = math.pi / ANGLES * normals.astype(jnp.float32)
-    tilt_angle = jnp.repeat(jnp.repeat(tilt_angle, BLK, axis=1), BLK, axis=2)
+    tilt_angle = jnp.repeat(jnp.repeat(tilt_angle, blk, axis=1), blk, axis=2)
     return (jnp.cos(tilt_angle), jnp.sin(tilt_angle))
 
 
@@ -95,7 +520,7 @@
     return jnp.where(counter < length // 2, counter, counter - length).astype(jnp.float32)
 
 
-def shards(strain, labels, normals, moduli, mean_strain):
+def shards_general(strain, labels, normals, moduli, mean_strain):
     z_devices = lax.axis_size("gz")
     x_devices = lax.axis_size("gx")
     z_index = lax.axis_index("gz")
@@ -107,7 +532,7 @@
     z_total = cells_z * z_devices
     line_count = sections * cells_x
     kz_share = cells_z // x_devices
-    cosine_tilt, sine_tilt = orientation(normals)
+    cosine_tilt, sine_tilt = orientation(normals, strain.shape[2] // normals.shape[1])
     lame_ref = 0.5 * (moduli[0] + moduli[2])
     shear_ref = 0.5 * (moduli[1] + moduli[3])
     stresses = stress_law(strain, labels, cosine_tilt, sine_tilt, moduli)
@@ -179,4 +604,19 @@
 def solution(mesh):
     in_specs = (P(None, None, "gx", "gz"), P(None, "gx", "gz"), P(None, "gx", "gz"), P(), P())
     out_specs = (P(None, None, "gx", "gz"), P(None, None, "gx", "gz"))
-    return jax.shard_map(shards, mesh=mesh, in_specs=in_specs, out_specs=out_specs, check_vma=False)
+
+    def run(strain, labels, normals, moduli, mean_strain):
+        _, sections, x_total, z_total = strain.shape
+        parts, x_devices = mesh.shape["gz"], mesh.shape["gx"]
+        grouped = (
+            sections == 2
+            and parts == len(GROUPS)
+            and x_devices % 8 == 0
+            and z_total == 128 * x_devices
+            and x_total % (128 * x_devices) == 0
+        )
+        body = shards if grouped else shards_general
+        mapped = jax.shard_map(body, mesh=mesh, in_specs=in_specs, out_specs=out_specs, check_vma=False)
+        return mapped(strain, labels, normals, moduli, mean_strain)
+
+    return run

time: 629 us -> 135 us (0.21); the launches traced: 617 us -> 135 us
  matrix products: 216 us -> 0 us
  waiting for transfers between devices: 260 us -> 64.4 us
  local copies, waits for them, and re-layouts: 71.8 us -> 8.17 us
  other arithmetic: 30.7 us -> 2.64 us
  blocking collectives: 0 us -> 23.4 us
  between operations: 18 us -> 0.87 us
  Pallas kernels: 0 us -> 13.4 us
    dot_general x12 -> x0, matrix products: 216 us -> none  [contract(): jnp.einsum(form, left_side, right_side, precision=lax.Precision.HIGHEST,...]
    all_gather x1 -> x0, waiting for transfers between devices: 114 us -> none  [shards(): pieces = lax.all_gather(flattened, 'gz', axis=2, tiled=True)]
    reduce_scatter x1 -> x0, waiting for transfers between devices: 111 us -> none  [shards(): lax.psum_scatter(contract('ckm,kz->zcm', real_part, cos_table) - contract...]
    ppermute x0 -> x12, waiting for transfers between devices: none -> 48.3 us  [the longest x6 48.3 us: travel(): thirds[step] = lax.ppermute(thirds[step], 'gz', some)]
    unnamed x52 -> x40, local copies, waits for them, and re-layouts: 35.9 us -> 7.44 us
    all_to_all x0 -> x1, blocking collectives: none -> 23.4 us  [shards(): rows = lax.all_to_all(rows, 'gx', 0, 0, tiled=True)]
    all_to_all x4 -> x1, waiting for transfers between devices: 35.4 us -> 16.1 us  [shards(): rows = lax.all_to_all(rows, 'gx', 0, 0, tiled=True)]
    ppermute x0 -> x12, starting transfers between devices: none -> 17.1 us  [the longest x6 12.6 us: travel(): thirds[step] = lax.ppermute(thirds[step], 'gz', some)]
  transfers between devices with their start and end apart: 6 -> 13, of which waited for: 5 -> 5; matrix products, arithmetic and copies ran while one was open for 15% -> 2% of each run, Pallas kernels for 0% -> 0%
where the time goes in v1:
time: 135 us
  waiting for transfers between devices  64.4 us (48%)
  blocking collectives  23.4 us (17%)
  starting transfers between devices  21.6 us (16%)
  Pallas kernels  13.4 us (10%)
  local copies, waits for them, and re-layouts  8.17 us (6%)
  other arithmetic  2.64 us (2%)
    ppermute x6, waiting for transfers between devices, travel(): thirds[step] = lax.ppermute(thirds[step], 'gz', some)  48.3 us
    all_to_all x1, blocking collectives, shards(): rows = lax.all_to_all(rows, 'gx', 0, 0, tiled=True)  23.4 us
    all_to_all x1, waiting for transfers between devices, shards(): rows = lax.all_to_all(rows, 'gx', 0, 0, tiled=True)  16.1 us
    pallas_call x5, Pallas kernels, call(): pl.pallas_call(kernel, out_shape=[jax.ShapeDtypeStruct(o, F32) for o in o...  13.4 us
    ppermute x6, starting transfers between devices, travel(): thirds[step] = lax.ppermute(thirds[step], 'gz', some)  12.6 us
    unnamed x40, local copies, waits for them, and re-layouts  7.44 us
    all_to_all x1, starting transfers between devices, shards(): rows = lax.all_to_all(rows, 'gx', 0, 0, tiled=True)  4.52 us
    ppermute x6, starting transfers between devices, travel(): pairs[step] = lax.ppermute(pairs[step], 'gz', way)  4.48 us
  transfers between devices with their start and end apart: 13, of which 5 were waited for; matrix products, arithmetic and copies ran while one was open for 2% of the time, Pallas kernels for 0%

profile of v1, /device:TPU:11, one launch (start us, length us, event | category | flops | bytes accessed | tf_op | source)
XLA Modules:
  0.0 134.5 jit_solution(6557953791670482109)
XLA Ops:
  0.6 1.4 %copy-done = f32[6,2,128,256]{3,2,1,0:T(8,128)S(1)} copy-done((f32[6,2,128,256]{3,2,1,0:T(8,128)S(1)}, f32[6,2,128,256]{3,2,1,0:T(8,128)}, u32[]{:S(2)}) %copy-start) | copy-done | bytes 1572888
  2.0 0.9 copy-done.1
  3.0 0.7 copy-done.15
  3.7 0.7 copy-done.18
  4.4 1.1 shard_map.176
  5.4 3.2 %collective-permute-start.3 = (f32[1,128,256]{2,1,0:T(8,128)S(1)}, f32[1,128,256]{2,1,0:T(8,128)S(1)}, u32[]{:S(2)}, u32[]{:S(2)}) collective-permute-start(f32[1,128,256]{2,1,0:T(8,128)S(1)} %get-tuple-element.23), channel_id=1, source_target_pairs={{0,8},{8,16},{1,9},{9,17},{2,10},{10,18},{3,11},{11,19},{4,12},{12... | collective-permute-start | bytes 393224 | tf_op jit(solution)/shard_map/ppermute | solution.py:396
  8.6 0.1 collective-permute-start
  8.7 2.2 %collective-permute-start.1 = (f32[2,128,256]{2,1,0:T(8,128)S(1)}, f32[2,128,256]{2,1,0:T(8,128)S(1)}, u32[]{:S(2)}, u32[]{:S(2)}) collective-permute-start(f32[2,128,256]{2,1,0:T(8,128)S(1)} %get-tuple-element.20), channel_id=1, source_target_pairs={{0,16},{8,24},{16,0},{24,8},{1,17},{9,25},{17,1},{25,9},{2,18},{10... | collective-permute-start | bytes 786440 | tf_op jit(solution)/shard_map/ppermute | solution.py:395
  10.9 1.3 collective-permute-start.4
  12.2 1.3 collective-permute-start.5
  13.5 16.6 %collective-permute-done.4.rest_6_ = f32[1,128,256]{2,1,0:T(8,128)S(1)} collective-permute-done((f32[1,128,256]{2,1,0:T(8,128)S(1)}, f32[1,128,256]{2,1,0:T(8,128)S(1)}, u32[]{:S(2)}, u32[]{:S(2)}) %collective-permute-start.4) | collective-permute-done | bytes 131104 | tf_op jit(solution)/shard_map/ppermute | solution.py:396
  30.2 10.0 %collective-permute-done.5.rest_7_ = f32[1,128,256]{2,1,0:T(8,128)S(1)} collective-permute-done((f32[1,128,256]{2,1,0:T(8,128)S(1)}, f32[1,128,256]{2,1,0:T(8,128)S(1)}, u32[]{:S(2)}, u32[]{:S(2)}) %collective-permute-start.5) | collective-permute-done | bytes 131104 | tf_op jit(solution)/shard_map/ppermute | solution.py:396
  40.3 2.5 %shard_map.177 = f32[8,3,128,128]{3,2,1,0:T(8,128)} custom-call(bf16[512,512]{1,0:T(8,128)(2,1)S(1)} %copy-done.8, bf16[512,512]{1,0:T(8,128)(2,1)S(1)} %copy-done.7, bf16[2,256,256]{2,1,0:T(8,128)(2,1)S(1)} %copy-done.14, bf16[2,256,256]{2,1,0:T(8,128)(2,1)S(1)} %copy-done.13, f32[2,128,256]{2,1,0:T(8,128)S(1)} %get-tuple-element.18.rest_0_, ...), custom_call_target="tpu_custom_call" | custom-call | bytes 4718592 | tf_op jit(solution)/shard_map/pallas_call | solution.py:368
  42.7 4.5 %all-to-all-start = ((f32[8,3,128,128]{3,2,1,0:T(8,128)}), f32[8,3,128,128]{3,2,1,0:T(8,128)S(1)}, u32[]{:S(2)}, u32[]{:S(2)}) async-start(f32[8,3,128,128]{3,2,1,0:T(8,128)} %shard_map.177), calls=%async_computation | async-start | bytes 3145728 | tf_op jit(solution)/shard_map/all_to_all | solution.py:407
  47.2 0.1 slice.21
  47.3 0.7 fusion
  48.0 2.6 %broadcast_select_fusion.mean = f32[3]{0:T(128)S(1)} fusion(pred[]{:T(512)S(6)} %or.3, f32[1]{0:T(128)} %get-tuple-element.35, f32[1]{0:T(128)} %get-tuple-element.36, f32[1]{0:T(128)} %get-tuple-element.37, f32[2]{0:T(128)S(1)} %slice.21, f32[1]{0:T(128)} %get-tuple-element.34), kind=kLoop, calls=%fused_computation | loop fusion | flops 12 | bytes 37 | tf_op jit(solution)/shard_map/jit(_where)/select_n | solution.py:410
  50.6 16.1 %all-to-all-done.data = f32[8,3,128,128]{3,2,1,0:T(8,128)S(1)} async-done(((f32[8,3,128,128]{3,2,1,0:T(8,128)}), f32[8,3,128,128]{3,2,1,0:T(8,128)S(1)}, u32[]{:S(2)}, u32[]{:S(2)}) %all-to-all-start) | async-done | bytes 1572896 | tf_op jit(solution)/shard_map/all_to_all | solution.py:407
  66.7 1.2 copy-done.4
  67.9 1.2 copy-done.5
  69.1 1.2 copy-done.6
  70.4 5.8 %shard_map.178 = f32[8,3,128,128]{3,2,1,0:T(8,128)S(1)} custom-call(f32[5]{0:T(128)S(1)} %copy-done.19, f32[3]{0:T(128)S(1)} %broadcast_select_fusion.mean, bf16[4,512,256]{2,1,0:T(8,128)(2,1)S(1)} %copy-done.6, bf16[4,512,256]{2,1,0:T(8,128)(2,1)S(1)} %copy-done.5, bf16[4,512,256]{2,1,0:T(8,128)(2,1)S(1)} %copy-done.4, bf16[4,512,256]{2,1,0:T(8,128)(2,1)S(1)} %copy-done.3, ...), custom_call_target="tpu_custom_call" | custom-call | bytes 7340064 | tf_op jit(solution)/shard_map/pallas_call | solution.py:368
  76.2 23.4 %all_to_all.10.data = f32[8,3,128,128]{3,2,1,0:T(8,128)S(1)} all-to-all(f32[8,3,128,128]{3,2,1,0:T(8,128)S(1)} %shard_map.178), channel_id=1, replica_groups=mesh['gz'=4,'gx'=8] {'gx'}, dimensions={0} | all-to-all | bytes 3145728 | tf_op jit(solution)/shard_map/all_to_all | solution.py:428
  99.7 1.3 shard_map.179
  101.1 1.3 collective-permute-start.9
  102.4 0.9 collective-permute-start.6
  103.3 1.3 collective-permute-start.8
  104.5 3.6 %collective-permute-start.10 = (f32[1,128,256]{2,1,0:T(8,128)S(1)}, f32[1,128,256]{2,1,0:T(8,128)S(1)}, u32[]{:S(2)}, u32[]{:S(2)}) collective-permute-start(f32[1,128,256]{2,1,0:T(8,128)S(1)} %get-tuple-element.32), channel_id=1, source_target_pairs={{8,24},{16,0},{9,25},{17,1},{10,26},{18,2},{11,27},{19,3},{12,28},... | collective-permute-start | bytes 393224 | tf_op jit(solution)/shard_map/ppermute | solution.py:396
  108.2 1.9 %collective-permute-start.11 = (f32[1,128,256]{2,1,0:T(8,128)S(1)}, f32[1,128,256]{2,1,0:T(8,128)S(1)}, u32[]{:S(2)}, u32[]{:S(2)}) collective-permute-start(f32[1,128,256]{2,1,0:T(8,128)S(1)} %get-tuple-element.33), channel_id=1, source_target_pairs={{8,0},{16,8},{9,1},{17,9},{10,2},{18,10},{11,3},{19,11},{12,4},{20... | collective-permute-start | bytes 393224 | tf_op jit(solution)/shard_map/ppermute | solution.py:396
  110.1 19.9 %collective-permute-done.10.rest_6_ = f32[1,128,256]{2,1,0:T(8,128)S(1)} collective-permute-done((f32[1,128,256]{2,1,0:T(8,128)S(1)}, f32[1,128,256]{2,1,0:T(8,128)S(1)}, u32[]{:S(2)}, u32[]{:S(2)}) %collective-permute-start.10) | collective-permute-done | bytes 131104 | tf_op jit(solution)/shard_map/ppermute | solution.py:396
  130.0 1.7 %collective-permute-done.11.rest_7_ = f32[1,128,256]{2,1,0:T(8,128)S(1)} collective-permute-done((f32[1,128,256]{2,1,0:T(8,128)S(1)}, f32[1,128,256]{2,1,0:T(8,128)S(1)}, u32[]{:S(2)}, u32[]{:S(2)}) %collective-permute-start.11) | collective-permute-done | bytes 131104 | tf_op jit(solution)/shard_map/ppermute | solution.py:396
  131.7 2.8 %shard_map.180 = (f32[6,2,128,256]{3,2,1,0:T(8,128)}, f32[6,2,128,256]{3,2,1,0:T(8,128)}) custom-call(f32[5]{0:T(128)S(1)} %copy-done.19, f32[6]{0:T(128)S(1)} %copy-done.17, s32[2,128,256]{2,1,0:T(8,128)S(1)} %copy-done.2, s32[2,8,16]{2,1,0:T(8,128)S(1)} %copy-done.16, f32[2,128,256]{2,1,0:T(8,128)S(1)} %get-tuple-element.26.rest_0_, ...), custom_call_target="tpu_custom_call" | custom-call | bytes 4981804 | tf_op jit(solution)/shard_map/pallas_call | solution.py:368
  (43 shorter events, 0.1 us)
Async XLA Ops:
  0.6 1.4 %copy-start = (f32[6,2,128,256]{3,2,1,0:T(8,128)S(1)}, f32[6,2,128,256]{3,2,1,0:T(8,128)}, u32[]{:S(2)}) copy-start(f32[6,2,128,256]{3,2,1,0:T(8,128)} %strain.1) | copy-start | bytes 4718596
  2.0 0.9 copy-start.1
  3.0 0.7 copy-start.15
  4.3 35.9 %copy-start.7 = (bf16[512,512]{1,0:T(8,128)(2,1)S(1)}, bf16[512,512]{1,0:T(8,128)(2,1)}, u32[]{:S(2)}) copy-start(bf16[512,512]{1,0:T(8,128)(2,1)} %constant.34.clone.one_l) | copy-start | bytes 1572868
  4.3 35.9 %copy-start.8 = (bf16[512,512]{1,0:T(8,128)(2,1)S(1)}, bf16[512,512]{1,0:T(8,128)(2,1)}, u32[]{:S(2)}) copy-start(bf16[512,512]{1,0:T(8,128)(2,1)} %constant.33.clone.one_h) | copy-start | bytes 1572868
  4.3 35.9 %copy-start.13 = (bf16[2,256,256]{2,1,0:T(8,128)(2,1)S(1)}, bf16[2,256,256]{2,1,0:T(8,128)(2,1)}, u32[]{:S(2)}) copy-start(bf16[2,256,256]{2,1,0:T(8,128)(2,1)} %constant.36.clone.two_l) | copy-start | bytes 786436
  4.3 35.9 %copy-start.14 = (bf16[2,256,256]{2,1,0:T(8,128)(2,1)S(1)}, bf16[2,256,256]{2,1,0:T(8,128)(2,1)}, u32[]{:S(2)}) copy-start(bf16[2,256,256]{2,1,0:T(8,128)(2,1)} %constant.35.clone.two_h) | copy-start | bytes 786436
  5.4 6.8 %collective-permute-start.3 = (f32[1,128,256]{2,1,0:T(8,128)S(1)}, f32[1,128,256]{2,1,0:T(8,128)S(1)}, u32[]{:S(2)}, u32[]{:S(2)}) collective-permute-start(f32[1,128,256]{2,1,0:T(8,128)S(1)} %get-tuple-element.23), channel_id=1, source_target_pairs={{0,8},{8,16},{1,9},{9,17},{2,10},{10,18},{3,11},{11,19},{4,12},{12... | collective-permute-start | bytes 393224 | tf_op jit(solution)/shard_map/ppermute | solution.py:396
  8.6 31.6 %collective-permute-start = (f32[2,128,256]{2,1,0:T(8,128)S(1)}, f32[2,128,256]{2,1,0:T(8,128)S(1)}, u32[]{:S(2)}, u32[]{:S(2)}) collective-permute-start(f32[2,128,256]{2,1,0:T(8,128)S(1)} %get-tuple-element.19), channel_id=1, source_target_pairs={{0,8},{8,16},{16,24},{24,0},{1,9},{9,17},{17,25},{25,1},{2,10},{10... | collective-permute-start | bytes 786440 | tf_op jit(solution)/shard_map/ppermute | solution.py:395
  8.7 31.5 %collective-permute-start.1 = (f32[2,128,256]{2,1,0:T(8,128)S(1)}, f32[2,128,256]{2,1,0:T(8,128)S(1)}, u32[]{:S(2)}, u32[]{:S(2)}) collective-permute-start(f32[2,128,256]{2,1,0:T(8,128)S(1)} %get-tuple-element.20), channel_id=1, source_target_pairs={{0,16},{8,24},{16,0},{24,8},{1,17},{9,25},{17,1},{25,9},{2,18},{10... | collective-permute-start | bytes 786440 | tf_op jit(solution)/shard_map/ppermute | solution.py:395
  10.9 29.3 %collective-permute-start.2 = (f32[2,128,256]{2,1,0:T(8,128)S(1)}, f32[2,128,256]{2,1,0:T(8,128)S(1)}, u32[]{:S(2)}, u32[]{:S(2)}) collective-permute-start(f32[2,128,256]{2,1,0:T(8,128)S(1)} %get-tuple-element.21), channel_id=1, source_target_pairs={{0,24},{8,0},{16,8},{24,16},{1,25},{9,1},{17,9},{25,17},{2,26},{10... | collective-permute-start | bytes 786440 | tf_op jit(solution)/shard_map/ppermute | solution.py:395
  10.9 19.2 %collective-permute-start.4 = (f32[1,128,256]{2,1,0:T(8,128)S(1)}, f32[1,128,256]{2,1,0:T(8,128)S(1)}, u32[]{:S(2)}, u32[]{:S(2)}) collective-permute-start(f32[1,128,256]{2,1,0:T(8,128)S(1)} %get-tuple-element.24), channel_id=1, source_target_pairs={{0,16},{24,8},{1,17},{25,9},{2,18},{26,10},{3,19},{27,11},{4,20},{... | collective-permute-start | bytes 393224 | tf_op jit(solution)/shard_map/ppermute | solution.py:396
  12.2 28.0 %collective-permute-start.5 = (f32[1,128,256]{2,1,0:T(8,128)S(1)}, f32[1,128,256]{2,1,0:T(8,128)S(1)}, u32[]{:S(2)}, u32[]{:S(2)}) collective-permute-start(f32[1,128,256]{2,1,0:T(8,128)S(1)} %get-tuple-element.25), channel_id=1, source_target_pairs={{16,8},{24,16},{17,9},{25,17},{18,10},{26,18},{19,11},{27,19},{20,... | collective-permute-start | bytes 393224 | tf_op jit(solution)/shard_map/ppermute | solution.py:396
  42.7 4.5 %copy-start.17 = (f32[6]{0:T(128)S(1)}, f32[6]{0:T(128)}, u32[]{:S(2)}) copy-start(f32[6]{0:T(128)} %mean.1) | copy-start | bytes 76
  42.7 24.0 %copy-start.3 = (bf16[4,512,256]{2,1,0:T(8,128)(2,1)S(1)}, bf16[4,512,256]{2,1,0:T(8,128)(2,1)}, u32[]{:S(2)}) copy-start(bf16[4,512,256]{2,1,0:T(8,128)(2,1)} %constant.44.clone.inv_l) | copy-start | bytes 3145732
  42.7 24.0 %copy-start.19 = (f32[5]{0:T(128)S(1)}, f32[5]{0:T(128)}, u32[]{:S(2)}) copy-start(f32[5]{0:T(128)} %moduli.5) | copy-start | bytes 64
  42.7 24.0 %all-to-all-start = ((f32[8,3,128,128]{3,2,1,0:T(8,128)}), f32[8,3,128,128]{3,2,1,0:T(8,128)S(1)}, u32[]{:S(2)}, u32[]{:S(2)}) async-start(f32[8,3,128,128]{3,2,1,0:T(8,128)} %shard_map.177), calls=%async_computation | async-start | bytes 3145728 | tf_op jit(solution)/shard_map/all_to_all | solution.py:407
  66.7 1.2 copy-start.4
  67.9 1.2 copy-start.5
  69.1 1.2 copy-start.6
  76.2 23.5 %copy-start.9 = (bf16[512,512]{1,0:T(8,128)(2,1)S(1)}, bf16[512,512]{1,0:T(8,128)(2,1)}, u32[]{:S(2)}) copy-start(bf16[512,512]{1,0:T(8,128)(2,1)} %constant.38.clone.one_l) | copy-start | bytes 1572868
  76.2 23.5 %copy-start.10 = (bf16[512,512]{1,0:T(8,128)(2,1)S(1)}, bf16[512,512]{1,0:T(8,128)(2,1)}, u32[]{:S(2)}) copy-start(bf16[512,512]{1,0:T(8,128)(2,1)} %constant.37.clone.one_h) | copy-start | bytes 1572868
  76.2 23.5 %copy-start.11 = (bf16[2,256,256]{2,1,0:T(8,128)(2,1)S(1)}, bf16[2,256,256]{2,1,0:T(8,128)(2,1)}, u32[]{:S(2)}) copy-start(bf16[2,256,256]{2,1,0:T(8,128)(2,1)} %constant.40.clone.two_l) | copy-start | bytes 786436
  76.2 23.5 %copy-start.12 = (bf16[2,256,256]{2,1,0:T(8,128)(2,1)S(1)}, bf16[2,256,256]{2,1,0:T(8,128)(2,1)}, u32[]{:S(2)}) copy-start(bf16[2,256,256]{2,1,0:T(8,128)(2,1)} %constant.39.clone.two_h) | copy-start | bytes 786436
  99.7 32.0 %copy-start.2 = (s32[2,128,256]{2,1,0:T(8,128)S(1)}, s32[2,128,256]{2,1,0:T(8,128)}, u32[]{:S(2)}) copy-start(s32[2,128,256]{2,1,0:T(8,128)} %labels.3) | copy-start | bytes 786436
  99.7 32.0 %copy-start.16 = (s32[2,8,16]{2,1,0:T(8,128)S(1)}, s32[2,8,16]{2,1,0:T(8,128)}, u32[]{:S(2)}) copy-start(s32[2,8,16]{2,1,0:T(8,128)} %normals.3) | copy-start | bytes 3076
  101.1 7.1 %collective-permute-start.9 = (f32[1,128,256]{2,1,0:T(8,128)S(1)}, f32[1,128,256]{2,1,0:T(8,128)S(1)}, u32[]{:S(2)}, u32[]{:S(2)}) collective-permute-start(f32[1,128,256]{2,1,0:T(8,128)S(1)} %get-tuple-element.31), channel_id=1, source_target_pairs={{8,16},{16,24},{9,17},{17,25},{10,18},{18,26},{11,19},{19,27},{12,... | collective-permute-start | bytes 393224 | tf_op jit(solution)/shard_map/ppermute | solution.py:396
  102.4 29.4 %collective-permute-start.6 = (f32[2,128,256]{2,1,0:T(8,128)S(1)}, f32[2,128,256]{2,1,0:T(8,128)S(1)}, u32[]{:S(2)}, u32[]{:S(2)}) collective-permute-start(f32[2,128,256]{2,1,0:T(8,128)S(1)} %get-tuple-element.27), channel_id=1, source_target_pairs={{0,8},{8,16},{16,24},{24,0},{1,9},{9,17},{17,25},{25,1},{2,10},{10... | collective-permute-start | bytes 786440 | tf_op jit(solution)/shard_map/ppermute | solution.py:395
  103.3 28.4 %collective-permute-start.7 = (f32[2,128,256]{2,1,0:T(8,128)S(1)}, f32[2,128,256]{2,1,0:T(8,128)S(1)}, u32[]{:S(2)}, u32[]{:S(2)}) collective-permute-start(f32[2,128,256]{2,1,0:T(8,128)S(1)} %get-tuple-element.28), channel_id=1, source_target_pairs={{0,16},{8,24},{16,0},{24,8},{1,17},{9,25},{17,1},{25,9},{2,18},{10... | collective-permute-start | bytes 786440 | tf_op jit(solution)/shard_map/ppermute | solution.py:395
  103.3 28.4 %collective-permute-start.8 = (f32[2,128,256]{2,1,0:T(8,128)S(1)}, f32[2,128,256]{2,1,0:T(8,128)S(1)}, u32[]{:S(2)}, u32[]{:S(2)}) collective-permute-start(f32[2,128,256]{2,1,0:T(8,128)S(1)} %get-tuple-element.29), channel_id=1, source_target_pairs={{0,24},{8,0},{16,8},{24,16},{1,25},{9,1},{17,9},{25,17},{2,26},{10... | collective-permute-start | bytes 786440 | tf_op jit(solution)/shard_map/ppermute | solution.py:395
  104.5 25.5 %collective-permute-start.10 = (f32[1,128,256]{2,1,0:T(8,128)S(1)}, f32[1,128,256]{2,1,0:T(8,128)S(1)}, u32[]{:S(2)}, u32[]{:S(2)}) collective-permute-start(f32[1,128,256]{2,1,0:T(8,128)S(1)} %get-tuple-element.32), channel_id=1, source_target_pairs={{8,24},{16,0},{9,25},{17,1},{10,26},{18,2},{11,27},{19,3},{12,28},... | collective-permute-start | bytes 393224 | tf_op jit(solution)/shard_map/ppermute | solution.py:396
  108.2 23.5 %collective-permute-start.11 = (f32[1,128,256]{2,1,0:T(8,128)S(1)}, f32[1,128,256]{2,1,0:T(8,128)S(1)}, u32[]{:S(2)}, u32[]{:S(2)}) collective-permute-start(f32[1,128,256]{2,1,0:T(8,128)S(1)} %get-tuple-element.33), channel_id=1, source_target_pairs={{8,0},{16,8},{9,1},{17,9},{10,2},{18,10},{11,3},{19,11},{12,4},{20... | collective-permute-start | bytes 393224 | tf_op jit(solution)/shard_map/ppermute | solution.py:396
  (1 other events, 0.7 us)

commit v2 on v1

--- a/solution.py
+++ b/solution.py
@@ -18,6 +18,8 @@
     ((XY, 1), (YZ, 1)),
 )
 INPLANE = (1, 2)
+FIELDS = 3
+CHUNKS = ((2, 0), (1,))
 F32, BF16 = jnp.float32, jnp.bfloat16
 MIB = 1 << 20
 
@@ -26,7 +28,7 @@
     table = np.asarray(table, np.float32)
     high = table.astype(jnp.bfloat16)
     low = (table - high.astype(np.float32)).astype(jnp.bfloat16)
-    return jnp.asarray(high), jnp.asarray(low)
+    return jnp.asarray(np.stack([high, low]))
 
 
 def half_frequencies(length):
@@ -68,21 +70,21 @@
     half[0] = scale
     inverse_zero = interleave(real * half, imag * half, slots).T
     inverse_two = weight * forward_two.T
-    return (
-        split_table(forward_one) + split_table(np.stack([forward_zero, forward_two])),
-        split_table(inverse_one) + split_table(np.stack([inverse_zero, inverse_two])),
-    )
+
+    def pack(first, second, third):
+        return split_table(np.concatenate([first, np.concatenate([second, third], 1)], 0))
+
+    return pack(forward_one, forward_zero, forward_two), pack(inverse_one, inverse_zero, inverse_two)
 
 
 def x_tables(length):
     quarter = length // 4
     k = np.arange(quarter, dtype=np.int64)
-    forward, inverse = [], []
-    for residue in range(4):
-        angle = 2.0 * math.pi / length * (((4 * k[:, None] + residue) * k[None, :]) % length)
-        forward.append(np.concatenate([np.cos(angle), np.sin(angle)], 0))
-        inverse.append(np.concatenate([np.cos(angle.T), np.sin(angle.T)], 0))
-    return split_table(np.stack(forward)) + split_table(np.stack(inverse))
+    angle = 2.0 * math.pi / quarter * ((k[:, None] * k[None, :]) % quarter)
+    turn = 2.0 * math.pi / length * k
+    columns = [f(residue * turn) for residue in (1, 2, 3) for f in (np.cos, np.sin)]
+    twiddles = jnp.asarray(np.stack(columns + columns[:2], 1).astype(np.float32))
+    return split_table(np.concatenate([np.cos(angle), np.sin(angle)], 0)), twiddles
 
 
 def halves(value):
@@ -94,13 +96,19 @@
     return jnp.dot(left, right, preferred_element_type=F32)
 
 
-def dot_right(value, high_table, low_table):
+def dot_right(value, table, part):
+    big = table.shape[2]
+    half = big // 2
+    rows = slice(0, big) if part == 0 else slice(big, big + half)
+    columns = slice(0, big) if part == 0 else slice((part - 1) * half, part * half)
+    high_table, low_table = table[0, rows, columns], table[1, rows, columns]
     high, low = halves(value)
     return dot(high, high_table) + (dot(low, high_table) + dot(high, low_table))
 
 
-def dot_left(high_table, low_table, high, low):
-    return dot(high_table, high) + (dot(high_table, low) + dot(low_table, high))
+def dot_left(table, value):
+    high, low = halves(value)
+    return dot(table[0], high) + (dot(table[0], low) + dot(table[1], high))
 
 
 def tilt(normals, section, cells_z):
@@ -137,11 +145,22 @@
     return [jnp.broadcast_to(s[block : block + 1], (size, s.shape[1])) for s in squares]
 
 
-def polarize_kernel(moduli, strain, labels, normals, *rest):
-    outs, held = rest[:-1], rest[-1]
+def polarize_kernel(moduli_h, strain_h, labels_h, normals_h, *rest):
+    outs, (held, strain, labels, normals, moduli, sems) = rest[:-6], rest[-6:]
+    sections, cells_x, cells_z = labels.shape
+    copies = [
+        pltpu.make_async_copy(moduli_h, moduli, sems.at[0]),
+        pltpu.make_async_copy(normals_h, normals, sems.at[1]),
+    ]
+    for k in range(sections):
+        copies.append(pltpu.make_async_copy(labels_h.at[k], labels.at[k], sems.at[2 + 2 * k]))
+        copies.append(pltpu.make_async_copy(strain_h.at[:, k], strain.at[:, k], sems.at[3 + 2 * k]))
+    for copy in copies:
+        copy.start()
+    for copy in copies[:2]:
+        copy.wait()
     parts = len(GROUPS)
     place = lax.axis_index("gz")
-    sections, cells_x, cells_z = labels.shape
     size = cells_x // normals.shape[1]
     lame_ref = 0.5 * (moduli[0] + moduli[2])
     shear_ref = 0.5 * (moduli[1] + moduli[3])
@@ -151,6 +170,8 @@
         if len(fields) < 3:
             held[group, 2] = jnp.zeros((cells_x, cells_z), F32)
     for section in range(sections):
+        copies[2 + 2 * section].wait()
+        copies[3 + 2 * section].wait()
         squares = tilt(normals, section, cells_z)
         for block in range(cells_x // size):
             rows = pl.ds(block * size, size)
@@ -162,27 +183,37 @@
                         held[group, slot, rows, :] = value[component]
     for step in range(parts):
         target = lax.rem(place + step, parts)
-        outs[step][...] = held[target, 0:2]
-        outs[parts + step][...] = held[target, 2:3]
-
-
-def z_forward_kernel(one_h, one_l, two_h, two_l, *rest):
+        for slot in range(FIELDS):
+            outs[slot * parts + step][...] = held[target, slot]
+
+
+def z_forward_kernel(table, *rest):
     parts = len(GROUPS)
-    pairs, thirds, out, held = rest[:parts], rest[parts : 2 * parts], rest[-2], rest[-1]
+    size = (len(rest) - 1) // parts
+    arrived, out, held, sems = rest[: size * parts], *rest[size * parts :][:2], rest[size * parts + 2 :]
     place = lax.axis_index("gz")
+    copies = []
     for step in range(parts):
         source = lax.rem(place + parts - step, parts)
-        held[source, 0:2] = pairs[step][...]
-        held[source, 2:3] = thirds[step][...]
+        for slot in range(size):
+            block = arrived[slot * parts + step]
+            if sems:
+                copies.append(pltpu.make_async_copy(block, held.at[source, slot], sems[0].at[len(copies)]))
+            else:
+                held[source, slot] = block[...]
+    for copy in copies:
+        copy.start()
+    for copy in copies:
+        copy.wait()
     fields, rows, width = held.shape[1:]
     lanes = out.shape[3]
     z0, z1, z2, z3 = (held[k].reshape(fields * rows, width) for k in range(parts))
     first = jnp.concatenate([z0 - z2, z1 - z3], 1)
     even, odd = z0 + z2, z1 + z3
     spectra = (
-        dot_right(first, one_h[...], one_l[...]),
-        dot_right(even + odd, two_h[0], two_l[0]),
-        dot_right(even - odd, two_h[1], two_l[1]),
+        dot_right(first, table, 0),
+        dot_right(even + odd, table, 1),
+        dot_right(even - odd, table, 2),
     )
     target = 0
     for spectrum in spectra:
@@ -191,19 +222,95 @@
             target += 1
 
 
-def quarter_turn(value, sign):
+def swap(value):
     lanes = value.shape[1]
-    return jnp.concatenate(
-        [pltpu.roll(value[:, k : k + 128], 64, 1) for k in range(0, lanes, 128)], 1
-    ) * sign
-
-
-def green_kernel(x_cells, z_cells, moduli, mean, fwd_h, fwd_l, inv_h, inv_l, data, out, low_s, high_s, field_s):
+    return jnp.concatenate([pltpu.roll(value[:, k : k + 128], 64, 1) for k in range(0, lanes, 128)], 1)
+
+
+def turn_sign(width):
+    lane = lax.broadcasted_iota(jnp.int32, (1, width), 1) % 128
+    return jnp.where(lane < 64, 1.0, -1.0).astype(F32)
+
+
+def twiddle(twiddles, residue, value, sign):
+    if residue == 0:
+        return value
+    pick = 2 * (residue - 1)
+    quarter = value.shape[0]
+    cosine = jnp.broadcast_to(twiddles[:, pick : pick + 1], (quarter, 128))
+    sine = jnp.broadcast_to(twiddles[:, pick + 1 : pick + 2], (quarter, 128)) * sign[:, :128]
+    pieces = []
+    for k in range(0, value.shape[1], 128):
+        piece = value[:, k : k + 128]
+        pieces.append(cosine * piece + sine * pltpu.roll(piece, 64, 1))
+    return jnp.concatenate(pieces, 1)
+
+
+def x_forward(data, table, twiddles):
     sources, fields, rows, lanes = data.shape
+    quarter = sources * rows // 4
+    per = sources // 4
+    sign = turn_sign(fields * lanes)
+    block = [
+        jnp.concatenate([data[a * per : (a + 1) * per, f].reshape(quarter, lanes) for f in range(fields)], 1)
+        for a in range(4)
+    ]
+    even, odd = block[0] + block[2], block[1] + block[3]
+    diff, turned = block[0] - block[2], sign * swap(block[1] - block[3])
+    for residue, value in enumerate((even + odd, diff + turned, even - odd, diff - turned)):
+        both = dot_left(table, twiddle(twiddles, residue, value, sign))
+        yield both[:quarter] + sign * swap(both[quarter:])
+
+
+def x_inverse(spectra, table, twiddles, is_special, out):
+    sources, fields, rows, lanes = out.shape
+    quarter = sources * rows // 4
+    per = sources // 4
+    sign = turn_sign((fields + 1) * lanes)
+    parts = []
+    for residue in range(4):
+        both = dot_left(table, spectra(residue))
+        parts.append(twiddle(twiddles, residue, both[:quarter] - sign * swap(both[quarter:]), -sign))
+    h0, h1, h2, h3 = parts
+    even, odd = h0 + h2, h1 + h3
+    diff, turned = h0 - h2, sign * swap(h1 - h3)
+    lane = lax.broadcasted_iota(jnp.int32, (1, lanes), 1)
+    edge = jnp.logical_and(is_special, lane == lanes // 2)
+    for a, value in enumerate((even + odd, diff - turned, even - odd, diff + turned)):
+        extra = value[:, fields * lanes :]
+        for f in range(fields):
+            moved = extra if f == 0 else pltpu.roll(extra, lanes - f, 1)
+            final = jnp.where(edge, moved, value[:, f * lanes : (f + 1) * lanes])
+            out[a * per : (a + 1) * per, f] = final.reshape(per, rows, lanes)
+
+
+def holds_edge(slots, z_cells):
+    return lax.axis_index("gx") * slots == z_cells // 4
+
+
+def x_forward_kernel(table, twiddles, data_h, out, data, sem):
+    copy = pltpu.make_async_copy(data_h, data, sem)
+    copy.start()
+    copy.wait()
+    fields, lanes = data.shape[1], data.shape[3]
+    for residue, spectrum in enumerate(x_forward(data, table, twiddles)):
+        for f in range(fields):
+            out[residue, f] = spectrum[:, f * lanes : (f + 1) * lanes]
+
+
+def x_inverse_kernel(z_cells, table, twiddles, data_h, out, data, sem):
+    copy = pltpu.make_async_copy(data_h, data, sem)
+    copy.start()
+    copy.wait()
+    special = holds_edge(out.shape[3] // 2, z_cells)
+    x_inverse(lambda residue: data[residue], table, twiddles, special, out)
+
+
+def green_kernel(x_cells, z_cells, chunks, moduli, mean, table, twiddles, done, data, out, rest_h, own, new, rest_out, sem):
+    rest_chunk, own_chunk = chunks
+    lanes = data.shape[3]
+    slots = lanes // 2
     quarter = x_cells // 4
-    per = quarter // rows
-    slots = lanes // 2
-    width = (fields + 1) * lanes
     place, mine = lax.axis_index("gz"), lax.axis_index("gx")
     inplane = functools.reduce(jnp.logical_or, [place == k for k in INPLANE])
     lame_ref = 0.5 * (moduli[0] + moduli[2])
@@ -214,96 +321,97 @@
     k1 = jnp.where(inplane, 2.0 * half_inverse, half_inverse)
     k2 = jnp.where(inplane, half_inverse, 0.0)
     ka = jnp.where(inplane, 0.0, half_inverse)
-    lane_all = lax.broadcasted_iota(jnp.int32, (1, width), 1) % lanes
-    sign_all = jnp.where(lane_all < slots, 1.0, -1.0)
-    sign = sign_all[:, : fields * lanes]
-    lane = lane_all[:, :lanes]
-
-    block = [
-        jnp.concatenate(
-            [data[a * per : (a + 1) * per, f].reshape(quarter, lanes) for f in range(fields)], 1
-        )
-        for a in range(4)
-    ]
-    even, odd = block[0] + block[2], block[1] + block[3]
-    diff, turned = block[0] - block[2], quarter_turn(block[1] - block[3], sign)
-    for residue, value in enumerate((even + odd, diff + turned, even - odd, diff - turned)):
-        high_s[residue, :, : fields * lanes], low_s[residue, :, : fields * lanes] = halves(value)
-
-    order = mine * slots + lane % slots
-    quarter_z = z_cells // 4
-    kz = jnp.where(
-        order < quarter_z,
-        4 * order + 1,
-        jnp.where(order < quarter_z + quarter_z // 2, 4 * (order - quarter_z), 4 * (order - quarter_z - quarter_z // 2) + 2),
-    )
-    special = jnp.logical_and(order == quarter_z, lane >= 0)
-    kz = jnp.where(kz < z_cells // 2, kz, kz - z_cells).astype(F32)
-
-    def coefficients(kx, kz, odd_mask):
+    total = float(x_cells * z_cells)
+    means = (
+        total * jnp.where(inplane, mean[XX], mean[XY]),
+        total * jnp.where(inplane, mean[ZZ], mean[YZ]),
+        total * mean[XZ],
+    )
+
+    for residue, spectrum in enumerate(x_forward(data, table, twiddles)):
+        for slot in range(len(own_chunk)):
+            own[residue, slot] = spectrum[:, slot * lanes : (slot + 1) * lanes]
+
+    def load(field, residue, rows):
+        if field in own_chunk:
+            return own[residue, own_chunk.index(field), rows, :]
+        return done[residue, rest_chunk.index(field), rows, :]
+
+    def store(chunk, residue, rows, block, value):
+        columns = slice(block * lanes, (block + 1) * lanes)
+        if chunk is own_chunk:
+            new[residue, rows, columns] = value
+        else:
+            rest_out[residue, rows, columns] = value
+
+    def green(kx, kz, odd_kx, s):
         radius = kx * kx + kz * kz
         inverse = 1.0 / jnp.where(radius == 0.0, 1.0, radius)
         a, b = kx * kx * inverse, kz * kz * inverse
-        d = kx * kz * inverse * odd_mask
-        ab = a * b
-        ca, cb = k2 - c1 * a, k2 - c1 * b
+        d = odd_kx * kz * inverse
+        ab = c1 * (a * b)
+        ca, cb = c1 * a, c1 * b
+        h02, h12 = d * (ca - k2), d * (cb - k2)
+        m01 = ab - ka * d
+        twice = 2.0 * s[2]
         return (
-            a * (k1 - c1 * a),
-            b * (k1 - c1 * b),
-            ka * d - c1 * ab,
-            d * ca,
-            d * cb,
-            k2 - 2.0 * c1 * ab,
+            a * (ca - k1) * s[0] + m01 * s[1] + h02 * twice,
+            m01 * s[0] + b * (cb - k1) * s[1] + h12 * twice,
+            h02 * s[0] + h12 * s[1] + (2.0 * ab - k2) * s[2],
         )
 
-    def apply(m, s):
-        m00, m11, m01, h02, h12, m22 = m
-        return (
-            -(m00 * s[0] + m01 * s[1] + 2.0 * (h02 * s[2])),
-            -(m01 * s[0] + m11 * s[1] + 2.0 * (h12 * s[2])),
-            -(h02 * s[0] + h12 * s[1] + m22 * s[2]),
-        )
-
-    for residue in range(4):
-        both = dot_left(
-            fwd_h[residue], fwd_l[residue], high_s[residue, :, : fields * lanes], low_s[residue, :, : fields * lanes]
-        )
-        spectrum = both[:quarter] + quarter_turn(both[quarter:], sign)
-        s = [spectrum[:, f * lanes : (f + 1) * lanes] for f in range(fields)]
-        kx = 4 * lax.broadcasted_iota(jnp.int32, (quarter, lanes), 0) + residue
-        kx_edge = kx == x_cells // 2
-        anchor = jnp.logical_and(kx == 0, special)
-        kx = jnp.where(kx < x_cells // 2, kx, kx - x_cells).astype(F32)
-        keep = jnp.where(kx_edge, 0.0, 1.0)
-        new = apply(coefficients(kx, jnp.broadcast_to(kz, kx.shape), keep), s)
-        real_lane = lane < slots
-        new = [
-            jnp.where(anchor, jnp.where(real_lane, float(x_cells * z_cells) * mean[f], 0.0), new[f])
-            for f in range(fields)
-        ]
-        keep = jnp.where(kx_edge, 1.0, 0.0)
-        edge = apply(coefficients(kx, jnp.full(kx.shape, -0.5 * z_cells, F32), keep), s)
-        extra = edge[0]
-        for f in range(1, fields):
-            extra = jnp.where(lane % slots == f, pltpu.roll(edge[f], f, 1), extra)
-        high_s[residue], low_s[residue] = halves(jnp.concatenate(list(new) + [extra], 1))
-
-    for residue in range(4):
-        both = dot_left(inv_h[residue], inv_l[residue], high_s[residue], low_s[residue])
-        field_s[residue] = both[:quarter] - quarter_turn(both[quarter:], sign_all)
-    h0, h1, h2, h3 = (field_s[k] for k in range(4))
-    even, odd = h0 + h2, h1 + h3
-    diff, turned = h0 - h2, quarter_turn(h1 - h3, sign_all)
-    swap = jnp.logical_and(special, lane >= slots)
-    for a, value in enumerate((even + odd, diff - turned, even - odd, diff + turned)):
-        extra = value[:, fields * lanes :]
-        for f in range(fields):
-            moved = extra if f == 0 else pltpu.roll(extra, lanes - f, 1)
-            final = jnp.where(swap, moved, value[:, f * lanes : (f + 1) * lanes])
-            out[a * per : (a + 1) * per, f] = final.reshape(per, rows, lanes)
-
-
-def z_inverse_kernel(one_h, one_l, two_h, two_l, data, *rest):
+    lane = lax.broadcasted_iota(jnp.int32, (1, lanes), 1)
+    slot_of = lane % slots
+    order = mine * slots + slot_of
+    zeros_at, twos_at = z_cells // 4, z_cells // 4 + z_cells // 8
+    kz = jnp.where(
+        order < zeros_at,
+        4 * order + 1,
+        jnp.where(order < twos_at, 4 * (order - zeros_at), 4 * (order - twos_at) + 2),
+    )
+    kz = jnp.where(kz < z_cells // 2, kz, kz - z_cells).astype(F32)
+    special = order == zeros_at
+    size = 32
+    for start in range(0, quarter, size):
+        rows = pl.ds(start, size)
+        row = lax.broadcasted_iota(jnp.int32, (size, lanes), 0) + start
+        full_kz = jnp.broadcast_to(kz, (size, lanes))
+        edge = [None] * FIELDS
+        for residue in range(4):
+            s = [load(f, residue, rows) for f in range(FIELDS)]
+            for f in range(FIELDS):
+                moved = s[f] if residue == 0 else pltpu.roll(s[f], residue, 1)
+                edge[f] = moved if residue == 0 else jnp.where(slot_of == residue, moved, edge[f])
+            count = 4 * row + residue
+            kx = jnp.where(count < x_cells // 2, count, count - x_cells).astype(F32)
+            odd_kx = jnp.where(count == x_cells // 2, 0.0, kx) if residue == 0 else kx
+            fresh = list(green(kx, full_kz, odd_kx, s))
+            if residue == 0 and start == 0:
+                anchor = jnp.logical_and(row == 0, special)
+                for f in range(FIELDS):
+                    fresh[f] = jnp.where(anchor, jnp.where(lane < slots, means[f], 0.0), fresh[f])
+            for chunk in chunks:
+                for block, f in enumerate(chunk):
+                    store(chunk, residue, rows, block, fresh[f])
+        count = 4 * row + slot_of
+        kx = jnp.where(count < x_cells // 2, count, count - x_cells).astype(F32)
+        odd_kx = jnp.where(count == x_cells // 2, kx, 0.0)
+        fresh = green(kx, jnp.full((size, lanes), -0.5 * z_cells, F32), odd_kx, edge)
+        for residue in range(4):
+            for chunk in chunks:
+                extra = None
+                for block, f in enumerate(chunk):
+                    shift = (block - residue) % lanes
+                    moved = fresh[f] if shift == 0 else pltpu.roll(fresh[f], shift, 1)
+                    extra = moved if block == 0 else jnp.where(slot_of == block, moved, extra)
+                store(chunk, residue, rows, len(chunk), extra)
+    copy = pltpu.make_async_copy(rest_out, rest_h, sem)
+    copy.start()
+    x_inverse(lambda residue: new[residue], table, twiddles, holds_edge(slots, z_cells), out)
+    copy.wait()
+
+
+def z_inverse_kernel(table, data, *rest):
     outs, held = rest[:-1], rest[-1]
     parts = len(GROUPS)
     place = lax.axis_index("gz")
@@ -314,9 +422,9 @@
     def columns(begin, end):
         return jnp.concatenate([data[k].reshape(fields * rows, lanes) for k in range(begin, end)], 1)
 
-    first = dot_right(columns(0, half), one_h[...], one_l[...])
-    zero = dot_right(columns(half, half + fourth), two_h[0], two_l[0])
-    two = dot_right(columns(half + fourth, sources), two_h[1], two_l[1])
+    first = dot_right(columns(0, half), table, 0)
+    zero = dot_right(columns(half, half + fourth), table, 1)
+    two = dot_right(columns(half + fourth, sources), table, 2)
     width = zero.shape[1]
     real, imag = first[:, :width], first[:, width:]
     plus, minus = zero + two, zero - two
@@ -324,21 +432,21 @@
         held[k] = value.reshape(fields, rows, width)
     for step in range(parts):
         target = lax.rem(place + step, parts)
-        outs[step][...] = held[target, 0:2]
-        outs[parts + step][...] = held[target, 2:3]
+        for slot in range(fields):
+            outs[slot * parts + step][...] = held[target, slot]
 
 
 def stress_kernel(moduli, mean, labels, normals, *rest):
     parts = len(GROUPS)
-    pairs, thirds = rest[:parts], rest[parts : 2 * parts]
-    strain_out, stress_out, held = rest[2 * parts :]
+    arrived, (strain_to, stress_to, held, strain_out, stress_out, sems) = rest[:-6], rest[-6:]
     place = lax.axis_index("gz")
     sections, cells_x, cells_z = labels.shape
     size = cells_x // normals.shape[1]
     for step in range(parts):
         source = lax.rem(place + parts - step, parts)
-        held[source, 0:2] = pairs[step][...]
-        held[source, 2:3] = thirds[step][...]
+        for slot in range(FIELDS):
+            held[source, slot] = arrived[slot * parts + step][...]
+    copies = []
     for section in range(sections):
         squares = tilt(normals, section, cells_z)
         for block in range(cells_x // size):
@@ -359,20 +467,32 @@
             for component in range(6):
                 strain_out[component, section, rows, :] = local[component]
                 stress_out[component, section, rows, :] = value[component]
-
-
-def call(kernel, outs, scratch, smem, args, limit, flops=0):
-    vmem = pl.BlockSpec(memory_space=pltpu.VMEM)
-    scalar = pl.BlockSpec(memory_space=pltpu.SMEM)
+        for k, (here, there) in enumerate(((strain_out, strain_to), (stress_out, stress_to))):
+            copy = pltpu.make_async_copy(here.at[:, section], there.at[:, section], sems.at[2 * section + k])
+            copy.start()
+            copies.append(copy)
+    for copy in copies:
+        copy.wait()
+
+
+def call(kernel, outs, scratch, args, limit, hbm=(), smem=0, hbm_out=()):
+    def space(k):
+        return pltpu.HBM if k in hbm else pltpu.SMEM if k < smem else pltpu.VMEM
+
+    args = [pltpu.with_memory_space_constraint(a, pltpu.HBM) if k in hbm else a for k, a in enumerate(args)]
     moved = sum(a.size * a.dtype.itemsize for a in args) + sum(math.prod(o) * 4 for o in outs)
     return pl.pallas_call(
         kernel,
-        out_shape=[jax.ShapeDtypeStruct(o, F32) for o in outs],
-        in_specs=[scalar] * smem + [vmem] * (len(args) - smem),
-        out_specs=[vmem] * len(outs),
+        out_shape=[
+            pltpu.HBM(o, F32) if k in hbm_out else jax.ShapeDtypeStruct(o, F32) for k, o in enumerate(outs)
+        ],
+        in_specs=[pl.BlockSpec(memory_space=space(k)) for k in range(len(args))],
+        out_specs=[
+            pl.BlockSpec(memory_space=pltpu.HBM if k in hbm_out else pltpu.VMEM) for k in range(len(outs))
+        ],
         scratch_shapes=scratch,
         compiler_params=pltpu.CompilerParams(vmem_limit_bytes=limit * MIB),
-        cost_estimate=pl.CostEstimate(flops=flops, bytes_accessed=moved, transcendentals=0),
+        cost_estimate=pl.CostEstimate(flops=0, bytes_accessed=moved, transcendentals=0),
     )(*args)
 
 
@@ -385,52 +505,97 @@
     lanes = 2 * slots
     z_fwd, z_inv = z_tables(z_total, slots, 1.0 / (x_total * z_total))
     x_tab = x_tables(x_total)
-    pair, third = (2, cells_x, cells_z), (1, cells_x, cells_z)
-
-    def travel(outs, sources, targets):
-        pairs, thirds = list(outs[:parts]), list(outs[parts:])
+    block = (cells_x, cells_z)
+    everyone = range(parts)
+
+    def travel(field, blocks, gather):
+        ends = INPLANE if field == 2 else everyone
+        moved = [blocks[0]]
         for step in range(1, parts):
             way = [(k, (k + step) % parts) for k in range(parts)]
-            some = [(a, b) for a, b in way if a in sources and b in targets]
-            pairs[step] = lax.ppermute(pairs[step], "gz", way)
-            thirds[step] = lax.ppermute(thirds[step], "gz", some)
-        return pairs + thirds
-
-    everyone = range(parts)
-    held = pltpu.VMEM((parts, 3, cells_x, cells_z), F32)
-    sent = call(
-        polarize_kernel, [pair] * parts + [third] * parts, [held], 1, (moduli, strain, labels, normals), 16
-    )
-    arrived = travel(sent, everyone, INPLANE)
-    grid = (x_devices, 3, cells_x, lanes)
-    (rows,) = call(z_forward_kernel, [grid], [held], 0, (*z_fwd, *arrived), 24)
-    rows = lax.all_to_all(rows, "gx", 0, 0, tiled=True)
-    index = lax.axis_index("gz")
-    inplane = functools.reduce(jnp.logical_or, [index == k for k in INPLANE])
-    mean = jnp.where(
-        inplane,
-        jnp.stack([mean_strain[XX], mean_strain[ZZ], mean_strain[XZ]]),
-        jnp.stack([mean_strain[XY], mean_strain[YZ], mean_strain[XZ]]),
-    )
+            way = [(a, b) for a, b in way if (b if gather else a) in ends]
+            moved.append(lax.ppermute(blocks[step], "gz", way))
+        return moved
+
+    def held(fields):
+        return pltpu.VMEM((parts, fields, cells_x, cells_z), F32)
+
+    blocks = call(
+        polarize_kernel,
+        [block] * (FIELDS * parts),
+        [
+            held(FIELDS),
+            pltpu.VMEM(strain.shape, F32),
+            pltpu.VMEM(labels.shape, jnp.int32),
+            pltpu.VMEM(normals.shape, jnp.int32),
+            pltpu.SMEM(moduli.shape, F32),
+            pltpu.SemaphoreType.DMA((2 + 2 * sections,)),
+        ],
+        (moduli, strain, labels, normals),
+        16,
+        range(4),
+    )
+    blocks = {f: list(blocks[f * parts : (f + 1) * parts]) for f in range(FIELDS)}
+    rows, spectrum = [], None
     quarter = x_total // 4
-    (rows,) = call(
-        functools.partial(green_kernel, x_total, z_total),
-        [grid],
+    for chunk in CHUNKS:
+        args = [a for f in chunk for a in travel(f, blocks.pop(f), True)]
+        args, blocks, rows = lax.optimization_barrier((args, blocks, rows))
+        grid = (x_devices, len(chunk), cells_x, lanes)
+        scratch, hbm = [held(len(chunk))], ()
+        if rows:
+            scratch.append(pltpu.SemaphoreType.DMA((len(args),)))
+            hbm = range(1, 1 + len(args))
+        (piece,) = call(z_forward_kernel, [grid], scratch, (z_fwd, *args), 24, hbm)
+        rows.append(lax.all_to_all(piece, "gx", 0, 0, tiled=True))
+    size = len(CHUNKS[0])
+    copied = [pltpu.VMEM(rows[0].shape, F32), pltpu.SemaphoreType.DMA]
+    (spectrum,) = call(x_forward_kernel, [(4, size, quarter, lanes)], copied, (*x_tab, rows[0]), 24, (2,))
+    last, rest = call(
+        functools.partial(green_kernel, x_total, z_total, CHUNKS),
+        [rows[1].shape, (4, quarter, (size + 1) * lanes)],
         [
-            pltpu.VMEM((4, quarter, 4 * lanes), BF16),
-            pltpu.VMEM((4, quarter, 4 * lanes), BF16),
-            pltpu.VMEM((4, quarter, 4 * lanes), F32),
+            pltpu.VMEM((4, len(CHUNKS[1]), quarter, lanes), F32),
+            pltpu.VMEM((4, quarter, (len(CHUNKS[1]) + 1) * lanes), F32),
+            pltpu.VMEM((4, quarter, (size + 1) * lanes), F32),
+            pltpu.SemaphoreType.DMA,
         ],
-        2,
-        (moduli, mean, *x_tab, rows),
+        (moduli, mean_strain, *x_tab, spectrum, rows[1]),
         32,
-    )
-    rows = lax.all_to_all(rows, "gx", 0, 0, tiled=True)
-    sent = call(z_inverse_kernel, [pair] * parts + [third] * parts, [held], 0, (*z_inv, rows), 24)
-    arrived = travel(sent, INPLANE, everyone)
+        smem=2,
+        hbm_out=(1,),
+    )
+
+    def to_z(chunk, piece):
+        size = len(chunk)
+        blocks = call(z_inverse_kernel, [block] * (size * parts), [held(size)], (z_inv, piece), 24)
+        return list(blocks)
+
+    def from_groups(chunk, blocks):
+        for slot, f in enumerate(chunk):
+            arrived[f] = travel(f, blocks[slot * parts : (slot + 1) * parts], False)
+
+    arrived = {}
+    last = lax.all_to_all(last, "gx", 0, 0, tiled=True)
+    copied = [pltpu.VMEM(rest.shape, F32), pltpu.SemaphoreType.DMA]
+    (rest,) = call(functools.partial(x_inverse_kernel, z_total), [rows[0].shape], copied, (*x_tab, rest), 24, (2,))
+    blocks = to_z(CHUNKS[1], last)
+    rest, blocks = lax.optimization_barrier((rest, blocks))
+    rest = lax.all_to_all(rest, "gx", 0, 0, tiled=True)
+    from_groups(CHUNKS[1], blocks)
+    from_groups(CHUNKS[0], to_z(CHUNKS[0], rest))
     full = (6, sections, cells_x, cells_z)
+    args = [a for f in range(FIELDS) for a in arrived[f]]
     return tuple(
-        call(stress_kernel, [full, full], [held], 2, (moduli, mean_strain, labels, normals, *arrived), 16)
+        call(
+            stress_kernel,
+            [full, full],
+            [held(FIELDS), pltpu.VMEM(full, F32), pltpu.VMEM(full, F32), pltpu.SemaphoreType.DMA((2 * sections,))],
+            (moduli, mean_strain, labels, normals, *args),
+            24,
+            smem=2,
+            hbm_out=(0, 1),
+        )
     )
 
 
@@ -500,7 +665,7 @@
     return -jnp.stack(result)
 
 
-def twiddle(left_ids, right_ids, length):
+def phases(left_ids, right_ids, length):
     product = left_ids[:, None] * right_ids[None, :] % length
     phase_angle = 2.0 * math.pi / length * product.astype(jnp.float32)
     return (jnp.cos(phase_angle), jnp.sin(phase_angle))
@@ -542,7 +707,7 @@
     empty_sum = jnp.zeros((6, cells_z, line_count), jnp.float32)
     pieces = lax.all_gather(flattened, "gz", axis=2, tiled=True)
     z_ids = jnp.arange(pieces.shape[2], dtype=jnp.int32)
-    cos_table, sin_table = twiddle(z_ids, own_block, z_total)
+    cos_table, sin_table = phases(z_ids, own_block, z_total)
     real_part = contract("cmz,zk->ckm", pieces, cos_table)
     imag_part = (empty_sum, empty_sum)[1] - contract("cmz,zk->ckm", pieces, sin_table)
     real_rows, imag_rows = (
@@ -553,7 +718,7 @@
     real_rows = real_rows.reshape(grid_shape)
     imag_rows = imag_rows.reshape(grid_shape)
     every_x = jnp.arange(x_total, dtype=jnp.int32)
-    cos_x, sin_x = twiddle(every_x, every_x, x_total)
+    cos_x, sin_x = phases(every_x, every_x, x_total)
     cos_x = cos_x.reshape(x_devices, cells_x, x_total)
     sin_x = sin_x.reshape(x_devices, cells_x, x_total)
     spec_real = contract("ckgsx,gxq->cksq", real_rows, cos_x) + contract(
@@ -587,7 +752,7 @@
         lax.all_to_all(back_imag, "gx", split_axis=2, concat_axis=1, tiled=True),
     )
     z_ids = jnp.arange(lax.axis_size("gz") * cells_z, dtype=jnp.int32)
-    cos_table, sin_table = twiddle(own_block, z_ids, z_total)
+    cos_table, sin_table = phases(own_block, z_ids, z_total)
     summed = lax.psum_scatter(
         contract("ckm,kz->zcm", real_part, cos_table)
         - contract("ckm,kz->zcm", imag_part, sin_table),

time: 135 us -> 127 us (0.941)
  blocking collectives: 23.4 us -> 0 us
  starting transfers between devices: 21.6 us -> 43 us
  Pallas kernels: 13.4 us -> 24.7 us
  local copies, waits for them, and re-layouts: 8.17 us -> 0.7 us
  waiting for transfers between devices: 64.4 us -> 57.7 us
  other arithmetic: 2.64 us -> 0 us
    all_to_all x1 -> x0, blocking collectives: 23.4 us -> none  [shards(): rows = lax.all_to_all(rows, 'gx', 0, 0, tiled=True)]
    all_to_all x1 -> x4, starting transfers between devices: 4.52 us -> 19.9 us  [the longest x2 9.95 us: shards(): rows.append(lax.all_to_all(piece, 'gx', 0, 0, tiled=True))]
    ppermute x12 -> x18, waiting for transfers between devices: 48.3 us -> 36.6 us  [travel(): moved.append(lax.ppermute(blocks[step], 'gz', way))]
    pallas_call x5 -> x9, Pallas kernels: 13.4 us -> 24.7 us  [call(): pl.pallas_call(kernel, out_shape=[pltpu.HBM(o, F32) if k in hbm_out else...]
    unnamed x40 -> x24, local copies, waits for them, and re-layouts: 7.44 us -> 0.7 us
    ppermute x12 -> x18, starting transfers between devices: 17.1 us -> 23 us  [travel(): moved.append(lax.ppermute(blocks[step], 'gz', way))]
    all_to_all x1 -> x4, waiting for transfers between devices: 16.1 us -> 21.1 us  [the longest x1 11.6 us: shards(): rest = lax.all_to_all(rest, 'gx', 0, 0, tiled=True)]
    select_n x1 -> x0, other arithmetic: 2.64 us -> none  [shards(): jnp.where(inplane, jnp.stack([mean_strain[XX], mean_strain[ZZ], mean_stra...]
  transfers between devices with their start and end apart: 13 -> 22, of which waited for: 5 -> 15; matrix products, arithmetic and copies ran while one was open for 2% -> 0% of each run, Pallas kernels for 0% -> 7%
where the time goes in v2:
time: 127 us
  waiting for transfers between devices  57.7 us (45%)
  starting transfers between devices  43 us (34%)
  Pallas kernels  24.7 us (19%)
    ppermute x18, waiting for transfers between devices, travel(): moved.append(lax.ppermute(blocks[step], 'gz', way))  36.6 us
    pallas_call x9, Pallas kernels, call(): pl.pallas_call(kernel, out_shape=[pltpu.HBM(o, F32) if k in hbm_out else...  24.7 us
    ppermute x18, starting transfers between devices, travel(): moved.append(lax.ppermute(blocks[step], 'gz', way))  23 us
    all_to_all x1, waiting for transfers between devices, shards(): rest = lax.all_to_all(rest, 'gx', 0, 0, tiled=True)  11.6 us
    all_to_all x2, starting transfers between devices, shards(): rows.append(lax.all_to_all(piece, 'gx', 0, 0, tiled=True))  9.95 us
    all_to_all x2, waiting for transfers between devices, shards(): rows.append(lax.all_to_all(piece, 'gx', 0, 0, tiled=True))  6.13 us
    all_to_all x1, starting transfers between devices, shards(): rest = lax.all_to_all(rest, 'gx', 0, 0, tiled=True)  5.02 us
    all_to_all x1, starting transfers between devices, shards(): last = lax.all_to_all(last, 'gx', 0, 0, tiled=True)  4.97 us
  transfers between devices with their start and end apart: 22, of which 15 were waited for; matrix products, arithmetic and copies ran while one was open for 0% of the time, Pallas kernels for 7%

profile of v2, /device:TPU:11, one launch (start us, length us, event | category | flops | bytes accessed | tf_op | source)
XLA Modules:
  0.0 126.9 jit_solution(2316812107206932865)
XLA Ops:
  0.6 2.0 %shard_map.104 = (f32[128,256]{1,0:T(8,128)S(1)}, f32[128,256]{1,0:T(8,128)S(1)}, f32[128,256]{1,0:T(8,128)S(1)}, f32[128,256]{1,0:T(8,128)S(1)}, f32[128,256]{1...) custom-call(f32[5]{0:T(128)} %moduli.3, ...), custom_call_target="tpu_custom_call" | custom-call | bytes 3408916 | tf_op jit(solution)/shard_map/pallas_call | solution.py:484
  3.3 3.2 %collective-permute-start = (f32[128,256]{1,0:T(8,128)S(1)}, f32[128,256]{1,0:T(8,128)S(1)}, u32[]{:S(2)}, u32[]{:S(2)}) collective-permute-start(f32[128,256]{1,0:T(8,128)S(1)} %get-tuple-element.51), channel_id=1, source_target_pairs={{0,8},{8,16},{1,9},{9,17},{2,10},{10,18},{3,11},{11,19},{4,12},{12... | collective-permute-start | bytes 393224 | tf_op jit(solution)/shard_map/ppermute | solution.py:517
  9.1 2.1 %collective-permute-start.3 = (f32[128,256]{1,0:T(8,128)S(1)}, f32[128,256]{1,0:T(8,128)S(1)}, u32[]{:S(2)}, u32[]{:S(2)}) collective-permute-start(f32[128,256]{1,0:T(8,128)S(1)} %get-tuple-element.55), channel_id=1, source_target_pairs={{0,8},{8,16},{16,24},{24,0},{1,9},{9,17},{17,25},{25,1},{2,10},{10... | collective-permute-start | bytes 393224 | tf_op jit(solution)/shard_map/ppermute | solution.py:517
  12.3 1.4 %collective-permute-start.5 = (f32[128,256]{1,0:T(8,128)S(1)}, f32[128,256]{1,0:T(8,128)S(1)}, u32[]{:S(2)}, u32[]{:S(2)}) collective-permute-start(f32[128,256]{1,0:T(8,128)S(1)} %get-tuple-element.57), channel_id=1, source_target_pairs={{0,24},{8,0},{16,8},{24,16},{1,25},{9,1},{17,9},{25,17},{2,26},{10... | collective-permute-start | bytes 393224 | tf_op jit(solution)/shard_map/ppermute | solution.py:517
  13.7 5.0 %collective-permute-done.2.rest_3_ = f32[128,256]{1,0:T(8,128)S(1)} collective-permute-done((f32[128,256]{1,0:T(8,128)S(1)}, f32[128,256]{1,0:T(8,128)S(1)}, u32[]{:S(2)}, u32[]{:S(2)}) %collective-permute-start.2) | collective-permute-done | bytes 131104 | tf_op jit(solution)/shard_map/ppermute | solution.py:517
  18.6 4.3 %collective-permute-done.4.rest_6_ = f32[128,256]{1,0:T(8,128)S(1)} collective-permute-done((f32[128,256]{1,0:T(8,128)S(1)}, f32[128,256]{1,0:T(8,128)S(1)}, u32[]{:S(2)}, u32[]{:S(2)}) %collective-permute-start.4) | collective-permute-done | bytes 131104 | tf_op jit(solution)/shard_map/ppermute | solution.py:517
  23.0 5.7 %collective-permute-done.5.rest_7_ = f32[128,256]{1,0:T(8,128)S(1)} collective-permute-done((f32[128,256]{1,0:T(8,128)S(1)}, f32[128,256]{1,0:T(8,128)S(1)}, u32[]{:S(2)}, u32[]{:S(2)}) %collective-permute-start.5) | collective-permute-done | bytes 131104 | tf_op jit(solution)/shard_map/ppermute | solution.py:517
  28.7 1.9 %shard_map.105 = f32[8,2,128,128]{3,2,1,0:T(8,128)} custom-call(bf16[2,768,512]{2,1,0:T(8,128)(2,1)S(1)} %copy-done.1, f32[128,256]{1,0:T(8,128)S(1)} %get-tuple-element.66.rest_0_, f32[128,256]{1,0:T(8,128)S(1)} %collective-permute-done.rest_1_, f32[128,256]{1,0:T(8,128)S(1)} %collective-permute-done.1.rest_2_, ...), custom_call_target="tpu_custom_call" | custom-call | bytes 3670016 | tf_op jit(solution)/shard_map/pallas_call | solution.py:484
  30.5 4.9 %all-to-all-start = ((f32[8,2,128,128]{3,2,1,0:T(8,128)}), f32[8,2,128,128]{3,2,1,0:T(8,128)}, u32[]{:S(2)}, u32[]{:S(2)}) async-start(f32[8,2,128,128]{3,2,1,0:T(8,128)} %shard_map.105), calls=%async_computation | async-start | bytes 2097152 | tf_op jit(solution)/shard_map/all_to_all | solution.py:550
  36.9 3.4 %collective-permute-done.6.rest_1_ = f32[128,256]{1,0:T(8,128)S(1)} collective-permute-done((f32[128,256]{1,0:T(8,128)S(1)}, f32[128,256]{1,0:T(8,128)S(1)}, u32[]{:S(2)}, u32[]{:S(2)}) %collective-permute-start.6) | collective-permute-done | bytes 131104 | tf_op jit(solution)/shard_map/ppermute | solution.py:517
  40.3 6.4 %collective-permute-done.7.rest_2_ = f32[128,256]{1,0:T(8,128)S(1)} collective-permute-done((f32[128,256]{1,0:T(8,128)S(1)}, f32[128,256]{1,0:T(8,128)S(1)}, u32[]{:S(2)}, u32[]{:S(2)}) %collective-permute-start.7) | collective-permute-done | bytes 131104 | tf_op jit(solution)/shard_map/ppermute | solution.py:517
  46.7 1.9 %collective-permute-done.8.rest_3_ = f32[128,256]{1,0:T(8,128)S(1)} collective-permute-done((f32[128,256]{1,0:T(8,128)S(1)}, f32[128,256]{1,0:T(8,128)S(1)}, u32[]{:S(2)}, u32[]{:S(2)}) %collective-permute-start.8) | collective-permute-done | bytes 131104 | tf_op jit(solution)/shard_map/ppermute | solution.py:517
  49.4 2.4 %shard_map.107 = f32[8,1,128,128]{3,2,1,0:T(8,128)} custom-call(bf16[2,768,512]{2,1,0:T(8,128)(2,1)S(1)} %copy-done.1, f32[128,256]{1,0:T(8,128)} %copy-done.5, f32[128,256]{1,0:T(8,128)} %copy-done.9, f32[128,256]{1,0:T(8,128)} %copy-done.10, f32[128,256]{1,0:T(8,128)} %copy-done.11), custom_call_target="tpu_custom_call" | custom-call | bytes 2621440 | tf_op jit(solution)/shard_map/pallas_call | solution.py:484
  51.8 5.0 %all-to-all-start.1 = ((f32[8,1,128,128]{3,2,1,0:T(8,128)}), f32[8,1,128,128]{3,2,1,0:T(8,128)S(1)}, u32[]{:S(2)}, u32[]{:S(2)}) async-start(f32[8,1,128,128]{3,2,1,0:T(8,128)} %shard_map.107), calls=%async_computation.1 | async-start | bytes 1048576 | tf_op jit(solution)/shard_map/all_to_all | solution.py:550
  56.9 2.8 %shard_map.106.done = f32[4,2,256,128]{3,2,1,0:T(8,128)S(1)} custom-call(bf16[2,512,256]{2,1,0:T(8,128)(2,1)S(1)} %copy-done.2, f32[256,8]{1,0:T(8,128)S(1)} %copy-done.3, f32[8,2,128,128]{3,2,1,0:T(8,128)} %all-to-all-done.data_h), custom_call_target="tpu_custom_call" | custom-call | bytes 2629632 | tf_op jit(solution)/shard_map/pallas_call | solution.py:484
  59.7 5.4 %all-to-all-done.1.data = f32[8,1,128,128]{3,2,1,0:T(8,128)S(1)} async-done(((f32[8,1,128,128]{3,2,1,0:T(8,128)}), f32[8,1,128,128]{3,2,1,0:T(8,128)S(1)}, u32[]{:S(2)}, u32[]{:S(2)}) %all-to-all-start.1) | async-done | bytes 524320 | tf_op jit(solution)/shard_map/all_to_all | solution.py:550
  65.1 6.0 %shard_map.108 = (f32[8,1,128,128]{3,2,1,0:T(8,128)}, f32[4,256,384]{2,1,0:T(8,128)}) custom-call(f32[5]{0:T(128)S(1)} %copy-done.7, f32[6]{0:T(128)S(1)} %copy-done.8, bf16[2,512,256]{2,1,0:T(8,128)(2,1)S(1)} %copy-done.2, f32[256,8]{1,0:T(8,128)S(1)} %copy-done.3, f32[4,2,256,128]{3,2,1,0:T(8,128)S(1)} %shard_map.106.done, ...), custom_call_target="tpu_custom_call" | custom-call | bytes 4202540 | tf_op jit(solution)/shard_map/pallas_call | solution.py:484
  71.1 5.0 %all-to-all-start.2 = ((f32[8,1,128,128]{3,2,1,0:T(8,128)}), f32[8,1,128,128]{3,2,1,0:T(8,128)S(1)}, u32[]{:S(2)}, u32[]{:S(2)}) async-start(f32[8,1,128,128]{3,2,1,0:T(8,128)} %get-tuple-element.80), calls=%async_computation.2 | async-start | bytes 1048576 | tf_op jit(solution)/shard_map/all_to_all | solution.py:579
  76.1 4.8 %shard_map.109 = f32[8,2,128,128]{3,2,1,0:T(8,128)} custom-call(bf16[2,512,256]{2,1,0:T(8,128)(2,1)S(1)} %copy-done.2, f32[256,8]{1,0:T(8,128)S(1)} %copy-done.3, f32[4,256,384]{2,1,0:T(8,128)} %get-tuple-element.79.data_h), custom_call_target="tpu_custom_call" | custom-call | bytes 3153920 | tf_op jit(solution)/shard_map/pallas_call | solution.py:484
  80.9 3.4 %all-to-all-done.2.data = f32[8,1,128,128]{3,2,1,0:T(8,128)S(1)} async-done(((f32[8,1,128,128]{3,2,1,0:T(8,128)}), f32[8,1,128,128]{3,2,1,0:T(8,128)S(1)}, u32[]{:S(2)}, u32[]{:S(2)}) %all-to-all-start.2) | async-done | bytes 524320 | tf_op jit(solution)/shard_map/all_to_all | solution.py:579
  85.6 5.0 %all-to-all-start.3 = ((f32[8,2,128,128]{3,2,1,0:T(8,128)}), f32[8,2,128,128]{3,2,1,0:T(8,128)S(1)}, u32[]{:S(2)}, u32[]{:S(2)}) async-start(f32[8,2,128,128]{3,2,1,0:T(8,128)} %shard_map.109), calls=%async_computation.3 | async-start | bytes 2097152 | tf_op jit(solution)/shard_map/all_to_all | solution.py:584
  91.5 1.4 %collective-permute-start.14 = (f32[128,256]{1,0:T(8,128)S(1)}, f32[128,256]{1,0:T(8,128)S(1)}, u32[]{:S(2)}, u32[]{:S(2)}) collective-permute-start(f32[128,256]{1,0:T(8,128)S(1)} %get-tuple-element.93), channel_id=1, source_target_pairs={{0,24},{8,0},{16,8},{24,16},{1,25},{9,1},{17,9},{25,17},{2,26},{10... | collective-permute-start | bytes 393224 | tf_op jit(solution)/shard_map/ppermute | solution.py:517
  92.9 11.6 %all-to-all-done.3.data = f32[8,2,128,128]{3,2,1,0:T(8,128)S(1)} async-done(((f32[8,2,128,128]{3,2,1,0:T(8,128)}), f32[8,2,128,128]{3,2,1,0:T(8,128)S(1)}, u32[]{:S(2)}, u32[]{:S(2)}) %all-to-all-start.3) | async-done | bytes 1048608 | tf_op jit(solution)/shard_map/all_to_all | solution.py:584
  106.3 1.4 %collective-permute-start.11 = (f32[128,256]{1,0:T(8,128)S(1)}, f32[128,256]{1,0:T(8,128)S(1)}, u32[]{:S(2)}, u32[]{:S(2)}) collective-permute-start(f32[128,256]{1,0:T(8,128)S(1)} %get-tuple-element.89), channel_id=1, source_target_pairs={{0,24},{8,0},{16,8},{24,16},{1,25},{9,1},{17,9},{25,17},{2,26},{10... | collective-permute-start | bytes 393224 | tf_op jit(solution)/shard_map/ppermute | solution.py:517
  107.7 2.3 %collective-permute-start.15 = (f32[128,256]{1,0:T(8,128)S(1)}, f32[128,256]{1,0:T(8,128)S(1)}, u32[]{:S(2)}, u32[]{:S(2)}) collective-permute-start(f32[128,256]{1,0:T(8,128)S(1)} %get-tuple-element.95), channel_id=1, source_target_pairs={{8,16},{16,24},{9,17},{17,25},{10,18},{18,26},{11,19},{19,27},{12,... | collective-permute-start | bytes 393224 | tf_op jit(solution)/shard_map/ppermute | solution.py:517
  110.0 2.5 %collective-permute-start.16 = (f32[128,256]{1,0:T(8,128)S(1)}, f32[128,256]{1,0:T(8,128)S(1)}, u32[]{:S(2)}, u32[]{:S(2)}) collective-permute-start(f32[128,256]{1,0:T(8,128)S(1)} %get-tuple-element.96), channel_id=1, source_target_pairs={{8,24},{16,0},{9,25},{17,1},{10,26},{18,2},{11,27},{19,3},{12,28},... | collective-permute-start | bytes 393224 | tf_op jit(solution)/shard_map/ppermute | solution.py:517
  112.5 1.9 %collective-permute-start.17 = (f32[128,256]{1,0:T(8,128)S(1)}, f32[128,256]{1,0:T(8,128)S(1)}, u32[]{:S(2)}, u32[]{:S(2)}) collective-permute-start(f32[128,256]{1,0:T(8,128)S(1)} %get-tuple-element.97), channel_id=1, source_target_pairs={{8,0},{16,8},{9,1},{17,9},{10,2},{18,10},{11,3},{19,11},{12,4},{20... | collective-permute-start | bytes 393224 | tf_op jit(solution)/shard_map/ppermute | solution.py:517
  114.4 2.2 %collective-permute-done.10.rest_2_ = f32[128,256]{1,0:T(8,128)S(1)} collective-permute-done((f32[128,256]{1,0:T(8,128)S(1)}, f32[128,256]{1,0:T(8,128)S(1)}, u32[]{:S(2)}, u32[]{:S(2)}) %collective-permute-start.10) | collective-permute-done | bytes 131104 | tf_op jit(solution)/shard_map/ppermute | solution.py:517
  116.6 2.0 %collective-permute-done.11.rest_3_ = f32[128,256]{1,0:T(8,128)S(1)} collective-permute-done((f32[128,256]{1,0:T(8,128)S(1)}, f32[128,256]{1,0:T(8,128)S(1)}, u32[]{:S(2)}, u32[]{:S(2)}) %collective-permute-start.11) | collective-permute-done | bytes 131104 | tf_op jit(solution)/shard_map/ppermute | solution.py:517
  119.4 2.8 %collective-permute-done.16.rest_10_ = f32[128,256]{1,0:T(8,128)S(1)} collective-permute-done((f32[128,256]{1,0:T(8,128)S(1)}, f32[128,256]{1,0:T(8,128)S(1)}, u32[]{:S(2)}, u32[]{:S(2)}) %collective-permute-start.16) | collective-permute-done | bytes 131104 | tf_op jit(solution)/shard_map/ppermute | solution.py:517
  122.3 2.0 %collective-permute-done.17.rest_11_ = f32[128,256]{1,0:T(8,128)S(1)} collective-permute-done((f32[128,256]{1,0:T(8,128)S(1)}, f32[128,256]{1,0:T(8,128)S(1)}, u32[]{:S(2)}, u32[]{:S(2)}) %collective-permute-start.17) | collective-permute-done | bytes 131104 | tf_op jit(solution)/shard_map/ppermute | solution.py:517
  124.3 2.6 %shard_map.112 = (f32[6,2,128,256]{3,2,1,0:T(8,128)}, f32[6,2,128,256]{3,2,1,0:T(8,128)}) custom-call(f32[5]{0:T(128)S(1)} %copy-done.7, f32[6]{0:T(128)S(1)} %copy-done.8, s32[2,128,256]{2,1,0:T(8,128)S(1)} %copy-done.4, s32[2,8,16]{2,1,0:T(8,128)S(1)} %copy-done.6, f32[128,256]{1,0:T(8,128)S(1)} %get-tuple-element.86.rest_0_, ...), custom_call_target="tpu_custom_call" | custom-call | bytes 4981804 | tf_op jit(solution)/shard_map/pallas_call | solution.py:484
  (45 shorter events, 11.4 us)
Async XLA Ops:
  0.6 28.0 %copy-start.1 = (bf16[2,768,512]{2,1,0:T(8,128)(2,1)S(1)}, bf16[2,768,512]{2,1,0:T(8,128)(2,1)}, u32[]{:S(2)}) copy-start(bf16[2,768,512]{2,1,0:T(8,128)(2,1)} %constant.8.clone.table) | copy-start | bytes 4718596
  3.3 8.9 %collective-permute-start = (f32[128,256]{1,0:T(8,128)S(1)}, f32[128,256]{1,0:T(8,128)S(1)}, u32[]{:S(2)}, u32[]{:S(2)}) collective-permute-start(f32[128,256]{1,0:T(8,128)S(1)} %get-tuple-element.51), channel_id=1, source_target_pairs={{0,8},{8,16},{1,9},{9,17},{2,10},{10,18},{3,11},{11,19},{4,12},{12... | collective-permute-start | bytes 393224 | tf_op jit(solution)/shard_map/ppermute | solution.py:517
  6.5 7.1 %collective-permute-start.1 = (f32[128,256]{1,0:T(8,128)S(1)}, f32[128,256]{1,0:T(8,128)S(1)}, u32[]{:S(2)}, u32[]{:S(2)}) collective-permute-start(f32[128,256]{1,0:T(8,128)S(1)} %get-tuple-element.52), channel_id=1, source_target_pairs={{0,16},{24,8},{1,17},{25,9},{2,18},{26,10},{3,19},{27,11},{4,20},{... | collective-permute-start | bytes 393224 | tf_op jit(solution)/shard_map/ppermute | solution.py:517
  7.8 10.8 %collective-permute-start.2 = (f32[128,256]{1,0:T(8,128)S(1)}, f32[128,256]{1,0:T(8,128)S(1)}, u32[]{:S(2)}, u32[]{:S(2)}) collective-permute-start(f32[128,256]{1,0:T(8,128)S(1)} %get-tuple-element.53), channel_id=1, source_target_pairs={{16,8},{24,16},{17,9},{25,17},{18,10},{26,18},{19,11},{27,19},{20,... | collective-permute-start | bytes 393224 | tf_op jit(solution)/shard_map/ppermute | solution.py:517
  9.1 9.5 %collective-permute-start.3 = (f32[128,256]{1,0:T(8,128)S(1)}, f32[128,256]{1,0:T(8,128)S(1)}, u32[]{:S(2)}, u32[]{:S(2)}) collective-permute-start(f32[128,256]{1,0:T(8,128)S(1)} %get-tuple-element.55), channel_id=1, source_target_pairs={{0,8},{8,16},{16,24},{24,0},{1,9},{9,17},{17,25},{25,1},{2,10},{10... | collective-permute-start | bytes 393224 | tf_op jit(solution)/shard_map/ppermute | solution.py:517
  11.3 11.7 %collective-permute-start.4 = (f32[128,256]{1,0:T(8,128)S(1)}, f32[128,256]{1,0:T(8,128)S(1)}, u32[]{:S(2)}, u32[]{:S(2)}) collective-permute-start(f32[128,256]{1,0:T(8,128)S(1)} %get-tuple-element.56), channel_id=1, source_target_pairs={{0,16},{8,24},{16,0},{24,8},{1,17},{9,25},{17,1},{25,9},{2,18},{10... | collective-permute-start | bytes 393224 | tf_op jit(solution)/shard_map/ppermute | solution.py:517
  12.3 16.4 %collective-permute-start.5 = (f32[128,256]{1,0:T(8,128)S(1)}, f32[128,256]{1,0:T(8,128)S(1)}, u32[]{:S(2)}, u32[]{:S(2)}) collective-permute-start(f32[128,256]{1,0:T(8,128)S(1)} %get-tuple-element.57), channel_id=1, source_target_pairs={{0,24},{8,0},{16,8},{24,16},{1,25},{9,1},{17,9},{25,17},{2,26},{10... | collective-permute-start | bytes 393224 | tf_op jit(solution)/shard_map/ppermute | solution.py:517
  30.5 18.9 %all-to-all-start = ((f32[8,2,128,128]{3,2,1,0:T(8,128)}), f32[8,2,128,128]{3,2,1,0:T(8,128)}, u32[]{:S(2)}, u32[]{:S(2)}) async-start(f32[8,2,128,128]{3,2,1,0:T(8,128)} %shard_map.105), calls=%async_computation | async-start | bytes 2097152 | tf_op jit(solution)/shard_map/all_to_all | solution.py:550
  35.5 21.4 %copy-start.2 = (bf16[2,512,256]{2,1,0:T(8,128)(2,1)S(1)}, bf16[2,512,256]{2,1,0:T(8,128)(2,1)}, u32[]{:S(2)}) copy-start(bf16[2,512,256]{2,1,0:T(8,128)(2,1)} %constant.11.clone.table) | copy-start | bytes 1572868
  35.5 21.4 %copy-start.3 = (f32[256,8]{1,0:T(8,128)S(1)}, f32[256,8]{1,0:T(8,128)}, u32[]{:S(2)}) copy-start(f32[256,8]{1,0:T(8,128)} %constant.10.clone.twiddles) | copy-start | bytes 24580
  35.5 4.8 %collective-permute-start.6 = (f32[128,256]{1,0:T(8,128)S(1)}, f32[128,256]{1,0:T(8,128)S(1)}, u32[]{:S(2)}, u32[]{:S(2)}) collective-permute-start(f32[128,256]{1,0:T(8,128)S(1)} %get-tuple-element.63), channel_id=1, source_target_pairs={{0,8},{8,16},{16,24},{24,0},{1,9},{9,17},{17,25},{25,1},{2,10},{10... | collective-permute-start | bytes 393224 | tf_op jit(solution)/shard_map/ppermute | solution.py:517
  35.5 11.3 %collective-permute-start.7 = (f32[128,256]{1,0:T(8,128)S(1)}, f32[128,256]{1,0:T(8,128)S(1)}, u32[]{:S(2)}, u32[]{:S(2)}) collective-permute-start(f32[128,256]{1,0:T(8,128)S(1)} %get-tuple-element.64), channel_id=1, source_target_pairs={{0,16},{8,24},{16,0},{24,8},{1,17},{9,25},{17,1},{25,9},{2,18},{10... | collective-permute-start | bytes 393224 | tf_op jit(solution)/shard_map/ppermute | solution.py:517
  36.2 12.5 %collective-permute-start.8 = (f32[128,256]{1,0:T(8,128)S(1)}, f32[128,256]{1,0:T(8,128)S(1)}, u32[]{:S(2)}, u32[]{:S(2)}) collective-permute-start(f32[128,256]{1,0:T(8,128)S(1)} %get-tuple-element.65), channel_id=1, source_target_pairs={{0,24},{8,0},{16,8},{24,16},{1,25},{9,1},{17,9},{25,17},{2,26},{10... | collective-permute-start | bytes 393224 | tf_op jit(solution)/shard_map/ppermute | solution.py:517
  40.3 9.1 %copy-start.9 = (f32[128,256]{1,0:T(8,128)}, f32[128,256]{1,0:T(8,128)S(1)}, u32[]{:S(2)}) copy-start(f32[128,256]{1,0:T(8,128)S(1)} %collective-permute-done.6.rest_1_) | copy-start | bytes 393220
  46.7 2.7 %copy-start.10 = (f32[128,256]{1,0:T(8,128)}, f32[128,256]{1,0:T(8,128)S(1)}, u32[]{:S(2)}) copy-start(f32[128,256]{1,0:T(8,128)S(1)} %collective-permute-done.7.rest_2_) | copy-start | bytes 393220
  51.8 13.2 %all-to-all-start.1 = ((f32[8,1,128,128]{3,2,1,0:T(8,128)}), f32[8,1,128,128]{3,2,1,0:T(8,128)S(1)}, u32[]{:S(2)}, u32[]{:S(2)}) async-start(f32[8,1,128,128]{3,2,1,0:T(8,128)} %shard_map.107), calls=%async_computation.1 | async-start | bytes 1048576 | tf_op jit(solution)/shard_map/all_to_all | solution.py:550
  56.9 8.2 %copy-start.7 = (f32[5]{0:T(128)S(1)}, f32[5]{0:T(128)}, u32[]{:S(2)}) copy-start(f32[5]{0:T(128)} %moduli.3) | copy-start | bytes 64
  56.9 8.2 %copy-start.8 = (f32[6]{0:T(128)S(1)}, f32[6]{0:T(128)}, u32[]{:S(2)}) copy-start(f32[6]{0:T(128)} %mean.3) | copy-start | bytes 76
  71.1 13.2 %all-to-all-start.2 = ((f32[8,1,128,128]{3,2,1,0:T(8,128)}), f32[8,1,128,128]{3,2,1,0:T(8,128)S(1)}, u32[]{:S(2)}, u32[]{:S(2)}) async-start(f32[8,1,128,128]{3,2,1,0:T(8,128)} %get-tuple-element.80), calls=%async_computation.2 | async-start | bytes 1048576 | tf_op jit(solution)/shard_map/all_to_all | solution.py:579
  76.1 8.2 %copy-start = (bf16[2,768,512]{2,1,0:T(8,128)(2,1)S(1)}, bf16[2,768,512]{2,1,0:T(8,128)(2,1)}, u32[]{:S(2)}) copy-start(bf16[2,768,512]{2,1,0:T(8,128)(2,1)} %constant.9.clone.table) | copy-start | bytes 4718596
  85.6 18.9 %all-to-all-start.3 = ((f32[8,2,128,128]{3,2,1,0:T(8,128)}), f32[8,2,128,128]{3,2,1,0:T(8,128)S(1)}, u32[]{:S(2)}, u32[]{:S(2)}) async-start(f32[8,2,128,128]{3,2,1,0:T(8,128)} %shard_map.109), calls=%async_computation.3 | async-start | bytes 2097152 | tf_op jit(solution)/shard_map/all_to_all | solution.py:584
  90.6 33.7 %copy-start.4 = (s32[2,128,256]{2,1,0:T(8,128)S(1)}, s32[2,128,256]{2,1,0:T(8,128)}, u32[]{:S(2)}) copy-start(s32[2,128,256]{2,1,0:T(8,128)} %labels.1) | copy-start | bytes 786436
  90.6 33.7 %copy-start.6 = (s32[2,8,16]{2,1,0:T(8,128)S(1)}, s32[2,8,16]{2,1,0:T(8,128)}, u32[]{:S(2)}) copy-start(s32[2,8,16]{2,1,0:T(8,128)} %normals.1) | copy-start | bytes 3076
  90.6 15.7 %collective-permute-start.12 = (f32[128,256]{1,0:T(8,128)}, f32[128,256]{1,0:T(8,128)S(1)}, u32[]{:S(2)}, u32[]{:S(2)}) collective-permute-start(f32[128,256]{1,0:T(8,128)} %get-tuple-element.91), channel_id=1, source_target_pairs={{0,8},{8,16},{16,24},{24,0},{1,9},{9,17},{17,25},{25,1},{2,10},{10... | collective-permute-start | bytes 393224 | tf_op jit(solution)/shard_map/ppermute | solution.py:517
  90.6 17.1 %collective-permute-start.13 = (f32[128,256]{1,0:T(8,128)}, f32[128,256]{1,0:T(8,128)S(1)}, u32[]{:S(2)}, u32[]{:S(2)}) collective-permute-start(f32[128,256]{1,0:T(8,128)} %get-tuple-element.92), channel_id=1, source_target_pairs={{0,16},{8,24},{16,0},{24,8},{1,17},{9,25},{17,1},{25,9},{2,18},{10... | collective-permute-start | bytes 393224 | tf_op jit(solution)/shard_map/ppermute | solution.py:517
  91.5 18.5 %collective-permute-start.14 = (f32[128,256]{1,0:T(8,128)S(1)}, f32[128,256]{1,0:T(8,128)S(1)}, u32[]{:S(2)}, u32[]{:S(2)}) collective-permute-start(f32[128,256]{1,0:T(8,128)S(1)} %get-tuple-element.93), channel_id=1, source_target_pairs={{0,24},{8,0},{16,8},{24,16},{1,25},{9,1},{17,9},{25,17},{2,26},{10... | collective-permute-start | bytes 393224 | tf_op jit(solution)/shard_map/ppermute | solution.py:517
  105.4 7.1 %collective-permute-start.9 = (f32[128,256]{1,0:T(8,128)S(1)}, f32[128,256]{1,0:T(8,128)S(1)}, u32[]{:S(2)}, u32[]{:S(2)}) collective-permute-start(f32[128,256]{1,0:T(8,128)S(1)} %get-tuple-element.87), channel_id=1, source_target_pairs={{0,8},{8,16},{16,24},{24,0},{1,9},{9,17},{17,25},{25,1},{2,10},{10... | collective-permute-start | bytes 393224 | tf_op jit(solution)/shard_map/ppermute | solution.py:517
  105.4 11.2 %collective-permute-start.10 = (f32[128,256]{1,0:T(8,128)S(1)}, f32[128,256]{1,0:T(8,128)S(1)}, u32[]{:S(2)}, u32[]{:S(2)}) collective-permute-start(f32[128,256]{1,0:T(8,128)S(1)} %get-tuple-element.88), channel_id=1, source_target_pairs={{0,16},{8,24},{16,0},{24,8},{1,17},{9,25},{17,1},{25,9},{2,18},{10... | collective-permute-start | bytes 393224 | tf_op jit(solution)/shard_map/ppermute | solution.py:517
  106.3 12.3 %collective-permute-start.11 = (f32[128,256]{1,0:T(8,128)S(1)}, f32[128,256]{1,0:T(8,128)S(1)}, u32[]{:S(2)}, u32[]{:S(2)}) collective-permute-start(f32[128,256]{1,0:T(8,128)S(1)} %get-tuple-element.89), channel_id=1, source_target_pairs={{0,24},{8,0},{16,8},{24,16},{1,25},{9,1},{17,9},{25,17},{2,26},{10... | collective-permute-start | bytes 393224 | tf_op jit(solution)/shard_map/ppermute | solution.py:517
  107.7 11.7 %collective-permute-start.15 = (f32[128,256]{1,0:T(8,128)S(1)}, f32[128,256]{1,0:T(8,128)S(1)}, u32[]{:S(2)}, u32[]{:S(2)}) collective-permute-start(f32[128,256]{1,0:T(8,128)S(1)} %get-tuple-element.95), channel_id=1, source_target_pairs={{8,16},{16,24},{9,17},{17,25},{10,18},{18,26},{11,19},{19,27},{12,... | collective-permute-start | bytes 393224 | tf_op jit(solution)/shard_map/ppermute | solution.py:517
  110.0 12.2 %collective-permute-start.16 = (f32[128,256]{1,0:T(8,128)S(1)}, f32[128,256]{1,0:T(8,128)S(1)}, u32[]{:S(2)}, u32[]{:S(2)}) collective-permute-start(f32[128,256]{1,0:T(8,128)S(1)} %get-tuple-element.96), channel_id=1, source_target_pairs={{8,24},{16,0},{9,25},{17,1},{10,26},{18,2},{11,27},{19,3},{12,28},... | collective-permute-start | bytes 393224 | tf_op jit(solution)/shard_map/ppermute | solution.py:517
  112.5 11.8 %collective-permute-start.17 = (f32[128,256]{1,0:T(8,128)S(1)}, f32[128,256]{1,0:T(8,128)S(1)}, u32[]{:S(2)}, u32[]{:S(2)}) collective-permute-start(f32[128,256]{1,0:T(8,128)S(1)} %get-tuple-element.97), channel_id=1, source_target_pairs={{8,0},{16,8},{9,1},{17,9},{10,2},{18,10},{11,3},{19,11},{12,4},{20... | collective-permute-start | bytes 393224 | tf_op jit(solution)/shard_map/ppermute | solution.py:517
  (2 other events, 1.4 us)

commit v3 on v2

--- a/solution.py
+++ b/solution.py
@@ -19,7 +19,7 @@
 )
 INPLANE = (1, 2)
 FIELDS = 3
-CHUNKS = ((2, 0), (1,))
+CHUNKS = ((0, 2), (1,))
 F32, BF16 = jnp.float32, jnp.bfloat16
 MIB = 1 << 20
 
@@ -189,22 +189,12 @@
 
 def z_forward_kernel(table, *rest):
     parts = len(GROUPS)
-    size = (len(rest) - 1) // parts
-    arrived, out, held, sems = rest[: size * parts], *rest[size * parts :][:2], rest[size * parts + 2 :]
+    arrived, (out, held) = rest[:-2], rest[-2:]
     place = lax.axis_index("gz")
-    copies = []
     for step in range(parts):
         source = lax.rem(place + parts - step, parts)
-        for slot in range(size):
-            block = arrived[slot * parts + step]
-            if sems:
-                copies.append(pltpu.make_async_copy(block, held.at[source, slot], sems[0].at[len(copies)]))
-            else:
-                held[source, slot] = block[...]
-    for copy in copies:
-        copy.start()
-    for copy in copies:
-        copy.wait()
+        for slot in range(held.shape[1]):
+            held[source, slot] = arrived[slot * parts + step][...]
     fields, rows, width = held.shape[1:]
     lanes = out.shape[3]
     z0, z1, z2, z3 = (held[k].reshape(fields * rows, width) for k in range(parts))
@@ -542,11 +532,7 @@
         args = [a for f in chunk for a in travel(f, blocks.pop(f), True)]
         args, blocks, rows = lax.optimization_barrier((args, blocks, rows))
         grid = (x_devices, len(chunk), cells_x, lanes)
-        scratch, hbm = [held(len(chunk))], ()
-        if rows:
-            scratch.append(pltpu.SemaphoreType.DMA((len(args),)))
-            hbm = range(1, 1 + len(args))
-        (piece,) = call(z_forward_kernel, [grid], scratch, (z_fwd, *args), 24, hbm)
+        (piece,) = call(z_forward_kernel, [grid], [held(len(chunk))], (z_fwd, *args), 16)
         rows.append(lax.all_to_all(piece, "gx", 0, 0, tiled=True))
     size = len(CHUNKS[0])
     copied = [pltpu.VMEM(rows[0].shape, F32), pltpu.SemaphoreType.DMA]

time: 127 us -> 120 us (0.945)
  waiting for transfers between devices: 57.7 us -> 54.4 us
  starting transfers between devices: 43 us -> 41 us
    ppermute x18, waiting for transfers between devices: 36.6 us -> 32 us  [travel(): moved.append(lax.ppermute(blocks[step], 'gz', way))]
    ppermute x18, starting transfers between devices: 23 us -> 21.2 us  [travel(): moved.append(lax.ppermute(blocks[step], 'gz', way))]
where the time goes in v3:
time: 120 us
  waiting for transfers between devices  54.4 us (45%)
  starting transfers between devices  41 us (34%)
  Pallas kernels  23.6 us (20%)
    ppermute x18, waiting for transfers between devices, travel(): moved.append(lax.ppermute(blocks[step], 'gz', way))  32 us
    pallas_call x9, Pallas kernels, call(): pl.pallas_call(kernel, out_shape=[pltpu.HBM(o, F32) if k in hbm_out else...  23.6 us
    ppermute x18, starting transfers between devices, travel(): moved.append(lax.ppermute(blocks[step], 'gz', way))  21.2 us
    all_to_all x1, waiting for transfers between devices, shards(): rest = lax.all_to_all(rest, 'gx', 0, 0, tiled=True)  11.8 us
    all_to_all x2, starting transfers between devices, shards(): rows.append(lax.all_to_all(piece, 'gx', 0, 0, tiled=True))  9.8 us
    all_to_all x2, waiting for transfers between devices, shards(): rows.append(lax.all_to_all(piece, 'gx', 0, 0, tiled=True))  7.15 us
    all_to_all x1, starting transfers between devices, shards(): rest = lax.all_to_all(rest, 'gx', 0, 0, tiled=True)  5.02 us
    all_to_all x1, starting transfers between devices, shards(): last = lax.all_to_all(last, 'gx', 0, 0, tiled=True)  4.97 us
  transfers between devices with their start and end apart: 22, of which 15 were waited for; matrix products, arithmetic and copies ran while one was open for 0% of the time, Pallas kernels for 7%

profile of v3, /device:TPU:11, one launch (start us, length us, event | category | flops | bytes accessed | tf_op | source)
XLA Modules:
  0.0 119.8 jit_solution(15655419311231922184)
XLA Ops:
  0.6 2.0 %shard_map.104 = (f32[128,256]{1,0:T(8,128)S(1)}, f32[128,256]{1,0:T(8,128)S(1)}, f32[128,256]{1,0:T(8,128)S(1)}, f32[128,256]{1,0:T(8,128)S(1)}, f32[128,256]{1...) custom-call(f32[5]{0:T(128)} %moduli.3, ...), custom_call_target="tpu_custom_call" | custom-call | bytes 3408916 | tf_op jit(solution)/shard_map/pallas_call | solution.py:474
  2.7 1.4 %collective-permute-start = (f32[128,256]{1,0:T(8,128)S(1)}, f32[128,256]{1,0:T(8,128)S(1)}, u32[]{:S(2)}, u32[]{:S(2)}) collective-permute-start(f32[128,256]{1,0:T(8,128)S(1)} %get-tuple-element.51), channel_id=1, source_target_pairs={{0,8},{8,16},{16,24},{24,0},{1,9},{9,17},{17,25},{25,1},{2,10},{10... | collective-permute-start | bytes 393224 | tf_op jit(solution)/shard_map/ppermute | solution.py:507
  5.1 1.4 %collective-permute-start.2 = (f32[128,256]{1,0:T(8,128)S(1)}, f32[128,256]{1,0:T(8,128)S(1)}, u32[]{:S(2)}, u32[]{:S(2)}) collective-permute-start(f32[128,256]{1,0:T(8,128)S(1)} %get-tuple-element.53), channel_id=1, source_target_pairs={{0,24},{8,0},{16,8},{24,16},{1,25},{9,1},{17,9},{25,17},{2,26},{10... | collective-permute-start | bytes 393224 | tf_op jit(solution)/shard_map/ppermute | solution.py:507
  6.5 2.0 %collective-permute-start.3 = (f32[128,256]{1,0:T(8,128)S(1)}, f32[128,256]{1,0:T(8,128)S(1)}, u32[]{:S(2)}, u32[]{:S(2)}) collective-permute-start(f32[128,256]{1,0:T(8,128)S(1)} %get-tuple-element.55), channel_id=1, source_target_pairs={{0,8},{8,16},{1,9},{9,17},{2,10},{10,18},{3,11},{11,19},{4,12},{12... | collective-permute-start | bytes 393224 | tf_op jit(solution)/shard_map/ppermute | solution.py:507
  11.1 3.4 %collective-permute-done.1.rest_2_ = f32[128,256]{1,0:T(8,128)S(1)} collective-permute-done((f32[128,256]{1,0:T(8,128)S(1)}, f32[128,256]{1,0:T(8,128)S(1)}, u32[]{:S(2)}, u32[]{:S(2)}) %collective-permute-start.1) | collective-permute-done | bytes 131104 | tf_op jit(solution)/shard_map/ppermute | solution.py:507
  14.5 5.8 %collective-permute-done.2.rest_3_ = f32[128,256]{1,0:T(8,128)S(1)} collective-permute-done((f32[128,256]{1,0:T(8,128)S(1)}, f32[128,256]{1,0:T(8,128)S(1)}, u32[]{:S(2)}, u32[]{:S(2)}) %collective-permute-start.2) | collective-permute-done | bytes 131104 | tf_op jit(solution)/shard_map/ppermute | solution.py:507
  20.2 2.8 %collective-permute-done.5.rest_7_ = f32[128,256]{1,0:T(8,128)S(1)} collective-permute-done((f32[128,256]{1,0:T(8,128)S(1)}, f32[128,256]{1,0:T(8,128)S(1)}, u32[]{:S(2)}, u32[]{:S(2)}) %collective-permute-start.5) | collective-permute-done | bytes 131104 | tf_op jit(solution)/shard_map/ppermute | solution.py:507
  23.0 1.9 %shard_map.105 = f32[8,2,128,128]{3,2,1,0:T(8,128)} custom-call(bf16[2,768,512]{2,1,0:T(8,128)(2,1)S(1)} %copy-done.1, f32[128,256]{1,0:T(8,128)S(1)} %get-tuple-element.66.rest_0_, f32[128,256]{1,0:T(8,128)S(1)} %collective-permute-done.rest_1_, f32[128,256]{1,0:T(8,128)S(1)} %collective-permute-done.1.rest_2_, ...), custom_call_target="tpu_custom_call" | custom-call | bytes 3670016 | tf_op jit(solution)/shard_map/pallas_call | solution.py:474
  24.9 4.8 %all-to-all-start = ((f32[8,2,128,128]{3,2,1,0:T(8,128)}), f32[8,2,128,128]{3,2,1,0:T(8,128)}, u32[]{:S(2)}, u32[]{:S(2)}) async-start(f32[8,2,128,128]{3,2,1,0:T(8,128)} %shard_map.105), calls=%async_computation | async-start | bytes 2097152 | tf_op jit(solution)/shard_map/all_to_all | solution.py:536
  31.4 3.1 %collective-permute-done.6.rest_1_ = f32[128,256]{1,0:T(8,128)S(1)} collective-permute-done((f32[128,256]{1,0:T(8,128)S(1)}, f32[128,256]{1,0:T(8,128)S(1)}, u32[]{:S(2)}, u32[]{:S(2)}) %collective-permute-start.6) | collective-permute-done | bytes 131104 | tf_op jit(solution)/shard_map/ppermute | solution.py:507
  34.5 6.6 %collective-permute-done.7.rest_2_ = f32[128,256]{1,0:T(8,128)S(1)} collective-permute-done((f32[128,256]{1,0:T(8,128)S(1)}, f32[128,256]{1,0:T(8,128)S(1)}, u32[]{:S(2)}, u32[]{:S(2)}) %collective-permute-start.7) | collective-permute-done | bytes 131104 | tf_op jit(solution)/shard_map/ppermute | solution.py:507
  41.9 1.8 %all-to-all-done.data_h = f32[8,2,128,128]{3,2,1,0:T(8,128)} async-done(((f32[8,2,128,128]{3,2,1,0:T(8,128)}), f32[8,2,128,128]{3,2,1,0:T(8,128)}, u32[]{:S(2)}, u32[]{:S(2)}) %all-to-all-start) | async-done | bytes 1048608 | tf_op jit(solution)/shard_map/all_to_all | solution.py:536
  43.7 1.3 %shard_map.107 = f32[8,1,128,128]{3,2,1,0:T(8,128)} custom-call(bf16[2,768,512]{2,1,0:T(8,128)(2,1)S(1)} %copy-done.1, f32[128,256]{1,0:T(8,128)S(1)} %get-tuple-element.75.rest_0_, f32[128,256]{1,0:T(8,128)S(1)} %collective-permute-done.6.rest_1_, f32[128,256]{1,0:T(8,128)S(1)} %collective-permute-done.7.rest_2_, f32[128,256]{1,0:T(8,128)S(1)} %collective-permute-done.8.rest_3_), custom_call_target="tpu_custom_call" | custom-call | bytes 2621440 | tf_op jit(solution)/shard_map/pallas_call | solution.py:474
  45.0 5.0 %all-to-all-start.1 = ((f32[8,1,128,128]{3,2,1,0:T(8,128)}), f32[8,1,128,128]{3,2,1,0:T(8,128)S(1)}, u32[]{:S(2)}, u32[]{:S(2)}) async-start(f32[8,1,128,128]{3,2,1,0:T(8,128)} %shard_map.107), calls=%async_computation.1 | async-start | bytes 1048576 | tf_op jit(solution)/shard_map/all_to_all | solution.py:536
  50.0 2.8 %shard_map.106.done = f32[4,2,256,128]{3,2,1,0:T(8,128)S(1)} custom-call(bf16[2,512,256]{2,1,0:T(8,128)(2,1)S(1)} %copy-done.2, f32[256,8]{1,0:T(8,128)S(1)} %copy-done.3, f32[8,2,128,128]{3,2,1,0:T(8,128)} %all-to-all-done.data_h), custom_call_target="tpu_custom_call" | custom-call | bytes 2629632 | tf_op jit(solution)/shard_map/pallas_call | solution.py:474
  52.8 5.4 %all-to-all-done.1.data = f32[8,1,128,128]{3,2,1,0:T(8,128)S(1)} async-done(((f32[8,1,128,128]{3,2,1,0:T(8,128)}), f32[8,1,128,128]{3,2,1,0:T(8,128)S(1)}, u32[]{:S(2)}, u32[]{:S(2)}) %all-to-all-start.1) | async-done | bytes 524320 | tf_op jit(solution)/shard_map/all_to_all | solution.py:536
  58.2 6.0 %shard_map.108 = (f32[8,1,128,128]{3,2,1,0:T(8,128)}, f32[4,256,384]{2,1,0:T(8,128)}) custom-call(f32[5]{0:T(128)S(1)} %copy-done.6, f32[6]{0:T(128)S(1)} %copy-done.7, bf16[2,512,256]{2,1,0:T(8,128)(2,1)S(1)} %copy-done.2, f32[256,8]{1,0:T(8,128)S(1)} %copy-done.3, f32[4,2,256,128]{3,2,1,0:T(8,128)S(1)} %shard_map.106.done, ...), custom_call_target="tpu_custom_call" | custom-call | bytes 4202540 | tf_op jit(solution)/shard_map/pallas_call | solution.py:474
  64.2 5.0 %all-to-all-start.2 = ((f32[8,1,128,128]{3,2,1,0:T(8,128)}), f32[8,1,128,128]{3,2,1,0:T(8,128)S(1)}, u32[]{:S(2)}, u32[]{:S(2)}) async-start(f32[8,1,128,128]{3,2,1,0:T(8,128)} %get-tuple-element.80), calls=%async_computation.2 | async-start | bytes 1048576 | tf_op jit(solution)/shard_map/all_to_all | solution.py:565
  69.2 4.8 %shard_map.109 = f32[8,2,128,128]{3,2,1,0:T(8,128)} custom-call(bf16[2,512,256]{2,1,0:T(8,128)(2,1)S(1)} %copy-done.2, f32[256,8]{1,0:T(8,128)S(1)} %copy-done.3, f32[4,256,384]{2,1,0:T(8,128)} %get-tuple-element.79.data_h), custom_call_target="tpu_custom_call" | custom-call | bytes 3153920 | tf_op jit(solution)/shard_map/pallas_call | solution.py:474
  74.0 3.4 %all-to-all-done.2.data = f32[8,1,128,128]{3,2,1,0:T(8,128)S(1)} async-done(((f32[8,1,128,128]{3,2,1,0:T(8,128)}), f32[8,1,128,128]{3,2,1,0:T(8,128)S(1)}, u32[]{:S(2)}, u32[]{:S(2)}) %all-to-all-start.2) | async-done | bytes 524320 | tf_op jit(solution)/shard_map/all_to_all | solution.py:565
  78.7 5.0 %all-to-all-start.3 = ((f32[8,2,128,128]{3,2,1,0:T(8,128)}), f32[8,2,128,128]{3,2,1,0:T(8,128)S(1)}, u32[]{:S(2)}, u32[]{:S(2)}) async-start(f32[8,2,128,128]{3,2,1,0:T(8,128)} %shard_map.109), calls=%async_computation.3 | async-start | bytes 2097152 | tf_op jit(solution)/shard_map/all_to_all | solution.py:570
  84.4 1.4 %collective-permute-start.14 = (f32[128,256]{1,0:T(8,128)S(1)}, f32[128,256]{1,0:T(8,128)S(1)}, u32[]{:S(2)}, u32[]{:S(2)}) collective-permute-start(f32[128,256]{1,0:T(8,128)S(1)} %get-tuple-element.93), channel_id=1, source_target_pairs={{0,24},{8,0},{16,8},{24,16},{1,25},{9,1},{17,9},{25,17},{2,26},{10... | collective-permute-start | bytes 393224 | tf_op jit(solution)/shard_map/ppermute | solution.py:507
  85.8 11.8 %all-to-all-done.3.data = f32[8,2,128,128]{3,2,1,0:T(8,128)S(1)} async-done(((f32[8,2,128,128]{3,2,1,0:T(8,128)}), f32[8,2,128,128]{3,2,1,0:T(8,128)S(1)}, u32[]{:S(2)}, u32[]{:S(2)}) %all-to-all-start.3) | async-done | bytes 1048608 | tf_op jit(solution)/shard_map/all_to_all | solution.py:570
  99.2 1.4 %collective-permute-start.11 = (f32[128,256]{1,0:T(8,128)S(1)}, f32[128,256]{1,0:T(8,128)S(1)}, u32[]{:S(2)}, u32[]{:S(2)}) collective-permute-start(f32[128,256]{1,0:T(8,128)S(1)} %get-tuple-element.89), channel_id=1, source_target_pairs={{0,24},{8,0},{16,8},{24,16},{1,25},{9,1},{17,9},{25,17},{2,26},{10... | collective-permute-start | bytes 393224 | tf_op jit(solution)/shard_map/ppermute | solution.py:507
  100.6 2.5 %collective-permute-start.15 = (f32[128,256]{1,0:T(8,128)S(1)}, f32[128,256]{1,0:T(8,128)S(1)}, u32[]{:S(2)}, u32[]{:S(2)}) collective-permute-start(f32[128,256]{1,0:T(8,128)S(1)} %get-tuple-element.95), channel_id=1, source_target_pairs={{8,16},{16,24},{9,17},{17,25},{10,18},{18,26},{11,19},{19,27},{12,... | collective-permute-start | bytes 393224 | tf_op jit(solution)/shard_map/ppermute | solution.py:507
  103.1 2.5 %collective-permute-start.16 = (f32[128,256]{1,0:T(8,128)S(1)}, f32[128,256]{1,0:T(8,128)S(1)}, u32[]{:S(2)}, u32[]{:S(2)}) collective-permute-start(f32[128,256]{1,0:T(8,128)S(1)} %get-tuple-element.96), channel_id=1, source_target_pairs={{8,24},{16,0},{9,25},{17,1},{10,26},{18,2},{11,27},{19,3},{12,28},... | collective-permute-start | bytes 393224 | tf_op jit(solution)/shard_map/ppermute | solution.py:507
  105.6 1.9 %collective-permute-start.17 = (f32[128,256]{1,0:T(8,128)S(1)}, f32[128,256]{1,0:T(8,128)S(1)}, u32[]{:S(2)}, u32[]{:S(2)}) collective-permute-start(f32[128,256]{1,0:T(8,128)S(1)} %get-tuple-element.97), channel_id=1, source_target_pairs={{8,0},{16,8},{9,1},{17,9},{10,2},{18,10},{11,3},{19,11},{12,4},{20... | collective-permute-start | bytes 393224 | tf_op jit(solution)/shard_map/ppermute | solution.py:507
  107.6 2.4 %collective-permute-done.10.rest_2_ = f32[128,256]{1,0:T(8,128)S(1)} collective-permute-done((f32[128,256]{1,0:T(8,128)S(1)}, f32[128,256]{1,0:T(8,128)S(1)}, u32[]{:S(2)}, u32[]{:S(2)}) %collective-permute-start.10) | collective-permute-done | bytes 131104 | tf_op jit(solution)/shard_map/ppermute | solution.py:507
  109.9 1.6 %collective-permute-done.11.rest_3_ = f32[128,256]{1,0:T(8,128)S(1)} collective-permute-done((f32[128,256]{1,0:T(8,128)S(1)}, f32[128,256]{1,0:T(8,128)S(1)}, u32[]{:S(2)}, u32[]{:S(2)}) %collective-permute-start.11) | collective-permute-done | bytes 131104 | tf_op jit(solution)/shard_map/ppermute | solution.py:507
  112.7 2.8 %collective-permute-done.16.rest_10_ = f32[128,256]{1,0:T(8,128)S(1)} collective-permute-done((f32[128,256]{1,0:T(8,128)S(1)}, f32[128,256]{1,0:T(8,128)S(1)}, u32[]{:S(2)}, u32[]{:S(2)}) %collective-permute-start.16) | collective-permute-done | bytes 131104 | tf_op jit(solution)/shard_map/ppermute | solution.py:507
  115.5 1.7 %collective-permute-done.17.rest_11_ = f32[128,256]{1,0:T(8,128)S(1)} collective-permute-done((f32[128,256]{1,0:T(8,128)S(1)}, f32[128,256]{1,0:T(8,128)S(1)}, u32[]{:S(2)}, u32[]{:S(2)}) %collective-permute-start.17) | collective-permute-done | bytes 131104 | tf_op jit(solution)/shard_map/ppermute | solution.py:507
  117.2 2.6 %shard_map.112 = (f32[6,2,128,256]{3,2,1,0:T(8,128)}, f32[6,2,128,256]{3,2,1,0:T(8,128)}) custom-call(f32[5]{0:T(128)S(1)} %copy-done.6, f32[6]{0:T(128)S(1)} %copy-done.7, s32[2,128,256]{2,1,0:T(8,128)S(1)} %copy-done.4, s32[2,8,16]{2,1,0:T(8,128)S(1)} %copy-done.5, f32[128,256]{1,0:T(8,128)S(1)} %get-tuple-element.86.rest_0_, ...), custom_call_target="tpu_custom_call" | custom-call | bytes 4981804 | tf_op jit(solution)/shard_map/pallas_call | solution.py:474
  (37 shorter events, 11.0 us)
Async XLA Ops:
  0.6 22.4 %copy-start.1 = (bf16[2,768,512]{2,1,0:T(8,128)(2,1)S(1)}, bf16[2,768,512]{2,1,0:T(8,128)(2,1)}, u32[]{:S(2)}) copy-start(bf16[2,768,512]{2,1,0:T(8,128)(2,1)} %constant.8.clone.table) | copy-start | bytes 4718596
  2.7 7.1 %collective-permute-start = (f32[128,256]{1,0:T(8,128)S(1)}, f32[128,256]{1,0:T(8,128)S(1)}, u32[]{:S(2)}, u32[]{:S(2)}) collective-permute-start(f32[128,256]{1,0:T(8,128)S(1)} %get-tuple-element.51), channel_id=1, source_target_pairs={{0,8},{8,16},{16,24},{24,0},{1,9},{9,17},{17,25},{25,1},{2,10},{10... | collective-permute-start | bytes 393224 | tf_op jit(solution)/shard_map/ppermute | solution.py:507
  4.0 10.4 %collective-permute-start.1 = (f32[128,256]{1,0:T(8,128)S(1)}, f32[128,256]{1,0:T(8,128)S(1)}, u32[]{:S(2)}, u32[]{:S(2)}) collective-permute-start(f32[128,256]{1,0:T(8,128)S(1)} %get-tuple-element.52), channel_id=1, source_target_pairs={{0,16},{8,24},{16,0},{24,8},{1,17},{9,25},{17,1},{25,9},{2,18},{10... | collective-permute-start | bytes 393224 | tf_op jit(solution)/shard_map/ppermute | solution.py:507
  5.1 15.1 %collective-permute-start.2 = (f32[128,256]{1,0:T(8,128)S(1)}, f32[128,256]{1,0:T(8,128)S(1)}, u32[]{:S(2)}, u32[]{:S(2)}) collective-permute-start(f32[128,256]{1,0:T(8,128)S(1)} %get-tuple-element.53), channel_id=1, source_target_pairs={{0,24},{8,0},{16,8},{24,16},{1,25},{9,1},{17,9},{25,17},{2,26},{10... | collective-permute-start | bytes 393224 | tf_op jit(solution)/shard_map/ppermute | solution.py:507
  6.5 13.7 %collective-permute-start.3 = (f32[128,256]{1,0:T(8,128)S(1)}, f32[128,256]{1,0:T(8,128)S(1)}, u32[]{:S(2)}, u32[]{:S(2)}) collective-permute-start(f32[128,256]{1,0:T(8,128)S(1)} %get-tuple-element.55), channel_id=1, source_target_pairs={{0,8},{8,16},{1,9},{9,17},{2,10},{10,18},{3,11},{11,19},{4,12},{12... | collective-permute-start | bytes 393224 | tf_op jit(solution)/shard_map/ppermute | solution.py:507
  8.5 11.8 %collective-permute-start.4 = (f32[128,256]{1,0:T(8,128)S(1)}, f32[128,256]{1,0:T(8,128)S(1)}, u32[]{:S(2)}, u32[]{:S(2)}) collective-permute-start(f32[128,256]{1,0:T(8,128)S(1)} %get-tuple-element.56), channel_id=1, source_target_pairs={{0,16},{24,8},{1,17},{25,9},{2,18},{26,10},{3,19},{27,11},{4,20},{... | collective-permute-start | bytes 393224 | tf_op jit(solution)/shard_map/ppermute | solution.py:507
  9.8 13.2 %collective-permute-start.5 = (f32[128,256]{1,0:T(8,128)S(1)}, f32[128,256]{1,0:T(8,128)S(1)}, u32[]{:S(2)}, u32[]{:S(2)}) collective-permute-start(f32[128,256]{1,0:T(8,128)S(1)} %get-tuple-element.57), channel_id=1, source_target_pairs={{16,8},{24,16},{17,9},{25,17},{18,10},{26,18},{19,11},{27,19},{20,... | collective-permute-start | bytes 393224 | tf_op jit(solution)/shard_map/ppermute | solution.py:507
  24.9 18.7 %all-to-all-start = ((f32[8,2,128,128]{3,2,1,0:T(8,128)}), f32[8,2,128,128]{3,2,1,0:T(8,128)}, u32[]{:S(2)}, u32[]{:S(2)}) async-start(f32[8,2,128,128]{3,2,1,0:T(8,128)} %shard_map.105), calls=%async_computation | async-start | bytes 2097152 | tf_op jit(solution)/shard_map/all_to_all | solution.py:536
  29.7 20.3 %copy-start.2 = (bf16[2,512,256]{2,1,0:T(8,128)(2,1)S(1)}, bf16[2,512,256]{2,1,0:T(8,128)(2,1)}, u32[]{:S(2)}) copy-start(bf16[2,512,256]{2,1,0:T(8,128)(2,1)} %constant.11.clone.table) | copy-start | bytes 1572868
  29.7 20.3 %copy-start.3 = (f32[256,8]{1,0:T(8,128)S(1)}, f32[256,8]{1,0:T(8,128)}, u32[]{:S(2)}) copy-start(f32[256,8]{1,0:T(8,128)} %constant.10.clone.twiddles) | copy-start | bytes 24580
  29.7 4.8 %collective-permute-start.6 = (f32[128,256]{1,0:T(8,128)S(1)}, f32[128,256]{1,0:T(8,128)S(1)}, u32[]{:S(2)}, u32[]{:S(2)}) collective-permute-start(f32[128,256]{1,0:T(8,128)S(1)} %get-tuple-element.63), channel_id=1, source_target_pairs={{0,8},{8,16},{16,24},{24,0},{1,9},{9,17},{17,25},{25,1},{2,10},{10... | collective-permute-start | bytes 393224 | tf_op jit(solution)/shard_map/ppermute | solution.py:507
  30.2 10.9 %collective-permute-start.7 = (f32[128,256]{1,0:T(8,128)S(1)}, f32[128,256]{1,0:T(8,128)S(1)}, u32[]{:S(2)}, u32[]{:S(2)}) collective-permute-start(f32[128,256]{1,0:T(8,128)S(1)} %get-tuple-element.64), channel_id=1, source_target_pairs={{0,16},{8,24},{16,0},{24,8},{1,17},{9,25},{17,1},{25,9},{2,18},{10... | collective-permute-start | bytes 393224 | tf_op jit(solution)/shard_map/ppermute | solution.py:507
  30.2 11.7 %collective-permute-start.8 = (f32[128,256]{1,0:T(8,128)S(1)}, f32[128,256]{1,0:T(8,128)S(1)}, u32[]{:S(2)}, u32[]{:S(2)}) collective-permute-start(f32[128,256]{1,0:T(8,128)S(1)} %get-tuple-element.65), channel_id=1, source_target_pairs={{0,24},{8,0},{16,8},{24,16},{1,25},{9,1},{17,9},{25,17},{2,26},{10... | collective-permute-start | bytes 393224 | tf_op jit(solution)/shard_map/ppermute | solution.py:507
  45.0 13.2 %all-to-all-start.1 = ((f32[8,1,128,128]{3,2,1,0:T(8,128)}), f32[8,1,128,128]{3,2,1,0:T(8,128)S(1)}, u32[]{:S(2)}, u32[]{:S(2)}) async-start(f32[8,1,128,128]{3,2,1,0:T(8,128)} %shard_map.107), calls=%async_computation.1 | async-start | bytes 1048576 | tf_op jit(solution)/shard_map/all_to_all | solution.py:536
  50.0 8.2 %copy-start.6 = (f32[5]{0:T(128)S(1)}, f32[5]{0:T(128)}, u32[]{:S(2)}) copy-start(f32[5]{0:T(128)} %moduli.3) | copy-start | bytes 64
  50.0 8.2 %copy-start.7 = (f32[6]{0:T(128)S(1)}, f32[6]{0:T(128)}, u32[]{:S(2)}) copy-start(f32[6]{0:T(128)} %mean.3) | copy-start | bytes 76
  64.2 13.2 %all-to-all-start.2 = ((f32[8,1,128,128]{3,2,1,0:T(8,128)}), f32[8,1,128,128]{3,2,1,0:T(8,128)S(1)}, u32[]{:S(2)}, u32[]{:S(2)}) async-start(f32[8,1,128,128]{3,2,1,0:T(8,128)} %get-tuple-element.80), calls=%async_computation.2 | async-start | bytes 1048576 | tf_op jit(solution)/shard_map/all_to_all | solution.py:565
  69.2 8.2 %copy-start = (bf16[2,768,512]{2,1,0:T(8,128)(2,1)S(1)}, bf16[2,768,512]{2,1,0:T(8,128)(2,1)}, u32[]{:S(2)}) copy-start(bf16[2,768,512]{2,1,0:T(8,128)(2,1)} %constant.9.clone.table) | copy-start | bytes 4718596
  78.7 18.9 %all-to-all-start.3 = ((f32[8,2,128,128]{3,2,1,0:T(8,128)}), f32[8,2,128,128]{3,2,1,0:T(8,128)S(1)}, u32[]{:S(2)}, u32[]{:S(2)}) async-start(f32[8,2,128,128]{3,2,1,0:T(8,128)} %shard_map.109), calls=%async_computation.3 | async-start | bytes 2097152 | tf_op jit(solution)/shard_map/all_to_all | solution.py:570
  83.7 33.5 %copy-start.4 = (s32[2,128,256]{2,1,0:T(8,128)S(1)}, s32[2,128,256]{2,1,0:T(8,128)}, u32[]{:S(2)}) copy-start(s32[2,128,256]{2,1,0:T(8,128)} %labels.1) | copy-start | bytes 786436
  83.7 33.5 %copy-start.5 = (s32[2,8,16]{2,1,0:T(8,128)S(1)}, s32[2,8,16]{2,1,0:T(8,128)}, u32[]{:S(2)}) copy-start(s32[2,8,16]{2,1,0:T(8,128)} %normals.1) | copy-start | bytes 3076
  83.7 15.5 %collective-permute-start.12 = (f32[128,256]{1,0:T(8,128)}, f32[128,256]{1,0:T(8,128)S(1)}, u32[]{:S(2)}, u32[]{:S(2)}) collective-permute-start(f32[128,256]{1,0:T(8,128)} %get-tuple-element.91), channel_id=1, source_target_pairs={{0,8},{8,16},{16,24},{24,0},{1,9},{9,17},{17,25},{25,1},{2,10},{10... | collective-permute-start | bytes 393224 | tf_op jit(solution)/shard_map/ppermute | solution.py:507
  84.2 16.5 %collective-permute-start.13 = (f32[128,256]{1,0:T(8,128)}, f32[128,256]{1,0:T(8,128)S(1)}, u32[]{:S(2)}, u32[]{:S(2)}) collective-permute-start(f32[128,256]{1,0:T(8,128)} %get-tuple-element.92), channel_id=1, source_target_pairs={{0,16},{8,24},{16,0},{24,8},{1,17},{9,25},{17,1},{25,9},{2,18},{10... | collective-permute-start | bytes 393224 | tf_op jit(solution)/shard_map/ppermute | solution.py:507
  84.4 18.7 %collective-permute-start.14 = (f32[128,256]{1,0:T(8,128)S(1)}, f32[128,256]{1,0:T(8,128)S(1)}, u32[]{:S(2)}, u32[]{:S(2)}) collective-permute-start(f32[128,256]{1,0:T(8,128)S(1)} %get-tuple-element.93), channel_id=1, source_target_pairs={{0,24},{8,0},{16,8},{24,16},{1,25},{9,1},{17,9},{25,17},{2,26},{10... | collective-permute-start | bytes 393224 | tf_op jit(solution)/shard_map/ppermute | solution.py:507
  98.5 7.1 %collective-permute-start.9 = (f32[128,256]{1,0:T(8,128)S(1)}, f32[128,256]{1,0:T(8,128)S(1)}, u32[]{:S(2)}, u32[]{:S(2)}) collective-permute-start(f32[128,256]{1,0:T(8,128)S(1)} %get-tuple-element.87), channel_id=1, source_target_pairs={{0,8},{8,16},{16,24},{24,0},{1,9},{9,17},{17,25},{25,1},{2,10},{10... | collective-permute-start | bytes 393224 | tf_op jit(solution)/shard_map/ppermute | solution.py:507
  99.0 10.9 %collective-permute-start.10 = (f32[128,256]{1,0:T(8,128)S(1)}, f32[128,256]{1,0:T(8,128)S(1)}, u32[]{:S(2)}, u32[]{:S(2)}) collective-permute-start(f32[128,256]{1,0:T(8,128)S(1)} %get-tuple-element.88), channel_id=1, source_target_pairs={{0,16},{8,24},{16,0},{24,8},{1,17},{9,25},{17,1},{25,9},{2,18},{10... | collective-permute-start | bytes 393224 | tf_op jit(solution)/shard_map/ppermute | solution.py:507
  99.2 12.3 %collective-permute-start.11 = (f32[128,256]{1,0:T(8,128)S(1)}, f32[128,256]{1,0:T(8,128)S(1)}, u32[]{:S(2)}, u32[]{:S(2)}) collective-permute-start(f32[128,256]{1,0:T(8,128)S(1)} %get-tuple-element.89), channel_id=1, source_target_pairs={{0,24},{8,0},{16,8},{24,16},{1,25},{9,1},{17,9},{25,17},{2,26},{10... | collective-permute-start | bytes 393224 | tf_op jit(solution)/shard_map/ppermute | solution.py:507
  100.6 12.1 %collective-permute-start.15 = (f32[128,256]{1,0:T(8,128)S(1)}, f32[128,256]{1,0:T(8,128)S(1)}, u32[]{:S(2)}, u32[]{:S(2)}) collective-permute-start(f32[128,256]{1,0:T(8,128)S(1)} %get-tuple-element.95), channel_id=1, source_target_pairs={{8,16},{16,24},{9,17},{17,25},{10,18},{18,26},{11,19},{19,27},{12,... | collective-permute-start | bytes 393224 | tf_op jit(solution)/shard_map/ppermute | solution.py:507
  103.1 12.4 %collective-permute-start.16 = (f32[128,256]{1,0:T(8,128)S(1)}, f32[128,256]{1,0:T(8,128)S(1)}, u32[]{:S(2)}, u32[]{:S(2)}) collective-permute-start(f32[128,256]{1,0:T(8,128)S(1)} %get-tuple-element.96), channel_id=1, source_target_pairs={{8,24},{16,0},{9,25},{17,1},{10,26},{18,2},{11,27},{19,3},{12,28},... | collective-permute-start | bytes 393224 | tf_op jit(solution)/shard_map/ppermute | solution.py:507
  105.6 11.6 %collective-permute-start.17 = (f32[128,256]{1,0:T(8,128)S(1)}, f32[128,256]{1,0:T(8,128)S(1)}, u32[]{:S(2)}, u32[]{:S(2)}) collective-permute-start(f32[128,256]{1,0:T(8,128)S(1)} %get-tuple-element.97), channel_id=1, source_target_pairs={{8,0},{16,8},{9,1},{17,9},{10,2},{18,10},{11,3},{19,11},{12,4},{20... | collective-permute-start | bytes 393224 | tf_op jit(solution)/shard_map/ppermute | solution.py:507

commit v4 on v3

--- a/solution.py
+++ b/solution.py
@@ -187,6 +187,43 @@
             outs[slot * parts + step][...] = held[target, slot]
 
 
+def deal(blocks, own, swapped):
+    mine = lax.axis_index("gx")
+    chip, core = mine // 2, lax.rem(mine, 2)
+    for step in range(own.shape[0]):
+        there = 2 * lax.bitwise_xor(chip, step)
+        own[step] = blocks[there + core, 0]
+        swapped[step] = blocks[there + 1 - core, 0]
+
+
+def collect(own, got, moved, blocks):
+    mine = lax.axis_index("gx")
+    chip, core = mine // 2, lax.rem(mine, 2)
+    for step in range(own.shape[0]):
+        there = 2 * lax.bitwise_xor(chip, step)
+        blocks[there + core, 0] = own[0] if step == 0 else moved[step - 1][0]
+        blocks[there + 1 - core, 0] = got[0] if step == 0 else moved[step - 1][1]
+
+
+def merge_kernel(own, got, *outs):
+    for k, out in enumerate(outs):
+        out[0] = own[k + 1]
+        out[1] = got[k + 1]
+
+
+def z_forward_deal_kernel(table, *rest):
+    arrived, (own, swapped, held, blocks) = rest[:-4], rest[-4:]
+    z_forward_kernel(table, *arrived, blocks, held)
+    deal(blocks, own, swapped)
+
+
+def z_inverse_collect_kernel(table, own, got, *rest):
+    chips = own.shape[0]
+    moved, outs, (held, blocks) = rest[: chips - 1], rest[chips - 1 : -2], rest[-2:]
+    collect(own, got, moved, blocks)
+    z_inverse_kernel(table, blocks, *outs, held)
+
+
 def z_forward_kernel(table, *rest):
     parts = len(GROUPS)
     arrived, (out, held) = rest[:-2], rest[-2:]
@@ -296,7 +333,11 @@
     x_inverse(lambda residue: data[residue], table, twiddles, special, out)
 
 
-def green_kernel(x_cells, z_cells, chunks, moduli, mean, table, twiddles, done, data, out, rest_h, own, new, rest_out, sem):
+def green_kernel(x_cells, z_cells, chunks, moduli, mean, table, twiddles, done, own_in, got, *rest):
+    chips = own_in.shape[0]
+    moved, rest = rest[: chips - 1], rest[chips - 1 :]
+    own_out, swapped, rest_h, data, out, own, new, rest_out, sem = rest
+    collect(own_in, got, moved, data)
     rest_chunk, own_chunk = chunks
     lanes = data.shape[3]
     slots = lanes // 2
@@ -398,6 +439,7 @@
     copy = pltpu.make_async_copy(rest_out, rest_h, sem)
     copy.start()
     x_inverse(lambda residue: new[residue], table, twiddles, holds_edge(slots, z_cells), out)
+    deal(out, own_out, swapped)
     copy.wait()
 
 
@@ -526,50 +568,60 @@
         range(4),
     )
     blocks = {f: list(blocks[f * parts : (f + 1) * parts]) for f in range(FIELDS)}
-    rows, spectrum = [], None
     quarter = x_total // 4
-    for chunk in CHUNKS:
-        args = [a for f in chunk for a in travel(f, blocks.pop(f), True)]
-        args, blocks, rows = lax.optimization_barrier((args, blocks, rows))
-        grid = (x_devices, len(chunk), cells_x, lanes)
-        (piece,) = call(z_forward_kernel, [grid], [held(len(chunk))], (z_fwd, *args), 16)
-        rows.append(lax.all_to_all(piece, "gx", 0, 0, tiled=True))
-    size = len(CHUNKS[0])
-    copied = [pltpu.VMEM(rows[0].shape, F32), pltpu.SemaphoreType.DMA]
-    (spectrum,) = call(x_forward_kernel, [(4, size, quarter, lanes)], copied, (*x_tab, rows[0]), 24, (2,))
-    last, rest = call(
+    chips = x_devices // 2
+    early, late = CHUNKS
+    size = len(early)
+    grid = (x_devices, size, cells_x, lanes)
+    tile = (chips, cells_x, lanes)
+    tiles = pltpu.VMEM((x_devices, 1, cells_x, lanes), F32)
+
+    def exchange(own, swapped, after):
+        got = lax.ppermute(swapped, "gx", [(k, k ^ 1) for k in range(x_devices)])
+        merged = call(merge_kernel, [(2, cells_x, lanes)] * (chips - 1), [], (own, got), 8)
+        merged, after = lax.optimization_barrier((merged, after))
+        moved = [
+            lax.ppermute(block, "gx", [(k, k ^ (2 * step)) for k in range(x_devices)])
+            for step, block in enumerate(merged, 1)
+        ]
+        return (own, got, *moved), after
+
+    args = [a for f in early for a in travel(f, blocks[f], True)]
+    args, blocks = lax.optimization_barrier((args, blocks))
+    (rows,) = call(z_forward_kernel, [grid], [held(size)], (z_fwd, *args), 16)
+    rows = lax.all_to_all(rows, "gx", 0, 0, tiled=True)
+    args = travel(late[0], blocks[late[0]], True)
+    args, rows = lax.optimization_barrier((args, rows))
+    own, swapped = call(z_forward_deal_kernel, [tile] * 2, [held(1), tiles], (z_fwd, *args), 16)
+    last, rows = exchange(own, swapped, rows)
+    copied = [pltpu.VMEM(grid, F32), pltpu.SemaphoreType.DMA]
+    (spectrum,) = call(x_forward_kernel, [(4, size, quarter, lanes)], copied, (*x_tab, rows), 24, (2,))
+    own, swapped, rest = call(
         functools.partial(green_kernel, x_total, z_total, CHUNKS),
-        [rows[1].shape, (4, quarter, (size + 1) * lanes)],
+        [tile, tile, (4, quarter, (size + 1) * lanes)],
         [
-            pltpu.VMEM((4, len(CHUNKS[1]), quarter, lanes), F32),
-            pltpu.VMEM((4, quarter, (len(CHUNKS[1]) + 1) * lanes), F32),
+            tiles,
+            tiles,
+            pltpu.VMEM((4, 1, quarter, lanes), F32),
+            pltpu.VMEM((4, quarter, 2 * lanes), F32),
             pltpu.VMEM((4, quarter, (size + 1) * lanes), F32),
             pltpu.SemaphoreType.DMA,
         ],
-        (moduli, mean_strain, *x_tab, spectrum, rows[1]),
+        (moduli, mean_strain, *x_tab, spectrum, *last),
         32,
         smem=2,
-        hbm_out=(1,),
-    )
-
-    def to_z(chunk, piece):
-        size = len(chunk)
-        blocks = call(z_inverse_kernel, [block] * (size * parts), [held(size)], (z_inv, piece), 24)
-        return list(blocks)
-
-    def from_groups(chunk, blocks):
-        for slot, f in enumerate(chunk):
-            arrived[f] = travel(f, blocks[slot * parts : (slot + 1) * parts], False)
-
-    arrived = {}
-    last = lax.all_to_all(last, "gx", 0, 0, tiled=True)
+        hbm_out=(2,),
+    )
+    last, rest = exchange(own, swapped, rest)
     copied = [pltpu.VMEM(rest.shape, F32), pltpu.SemaphoreType.DMA]
-    (rest,) = call(functools.partial(x_inverse_kernel, z_total), [rows[0].shape], copied, (*x_tab, rest), 24, (2,))
-    blocks = to_z(CHUNKS[1], last)
-    rest, blocks = lax.optimization_barrier((rest, blocks))
+    (rest,) = call(functools.partial(x_inverse_kernel, z_total), [grid], copied, (*x_tab, rest), 24, (2,))
+    blocks = call(z_inverse_collect_kernel, [block] * parts, [held(1), tiles], (z_inv, *last), 16)
+    rest, blocks = lax.optimization_barrier((rest, list(blocks)))
     rest = lax.all_to_all(rest, "gx", 0, 0, tiled=True)
-    from_groups(CHUNKS[1], blocks)
-    from_groups(CHUNKS[0], to_z(CHUNKS[0], rest))
+    arrived = {late[0]: travel(late[0], blocks, False)}
+    blocks = call(z_inverse_kernel, [block] * (size * parts), [held(size)], (z_inv, rest), 16)
+    for slot, f in enumerate(early):
+        arrived[f] = travel(f, blocks[slot * parts : (slot + 1) * parts], False)
     full = (6, sections, cells_x, cells_z)
     args = [a for f in range(FIELDS) for a in arrived[f]]
     return tuple(
@@ -762,7 +814,7 @@
         grouped = (
             sections == 2
             and parts == len(GROUPS)
-            and x_devices % 8 == 0
+            and x_devices == 8
             and z_total == 128 * x_devices
             and x_total % (128 * x_devices) == 0
         )

time: 120 us -> 115 us (0.958)
  waiting for transfers between devices: 54.4 us -> 50.2 us
  Pallas kernels: 23.6 us -> 22.3 us
    all_to_all x3 -> x1, starting transfers between devices: 14.8 us -> 4.8 us  [shards(): rows = lax.all_to_all(rows, 'gx', 0, 0, tiled=True)]
    all_to_all x3 -> x1, waiting for transfers between devices: 10.6 us -> 1.78 us  [shards(): rows = lax.all_to_all(rows, 'gx', 0, 0, tiled=True)]
    ppermute x0 -> x8, starting transfers between devices: none -> 8.47 us  [the longest x6 5.43 us: exchange(): lax.ppermute(block, 'gx', [(k, k ^ 2 * step) for k in range(x_devices)])]
    ppermute x0 -> x8, waiting for transfers between devices: none -> 4.63 us  [the longest x2 2.32 us: exchange(): got = lax.ppermute(swapped, 'gx', [(k, k ^ 1) for k in range(x_devices)])]
    pallas_call x9 -> x11, Pallas kernels: 23.6 us -> 22.3 us  [call(): pl.pallas_call(kernel, out_shape=[pltpu.HBM(o, F32) if k in hbm_out else...]
  transfers between devices with their start and end apart: 22 -> 28, of which waited for: 15 -> 18; matrix products, arithmetic and copies ran while one was open for 0% -> 0% of each run, Pallas kernels for 7% -> 7%
where the time goes in v4:
time: 115 us; the launch traced here: 114 us
  waiting for transfers between devices  50.2 us (44%)
  starting transfers between devices  40.8 us (35%)
  Pallas kernels  22.3 us (19%)
    ppermute x18, waiting for transfers between devices, travel(): moved.append(lax.ppermute(blocks[step], 'gz', way))  32.4 us
    pallas_call x11, Pallas kernels, call(): pl.pallas_call(kernel, out_shape=[pltpu.HBM(o, F32) if k in hbm_out else...  22.3 us
    ppermute x18, starting transfers between devices, travel(): moved.append(lax.ppermute(blocks[step], 'gz', way))  21.6 us
    all_to_all x1, waiting for transfers between devices, shards(): rest = lax.all_to_all(rest, 'gx', 0, 0, tiled=True)  11.4 us
    all_to_all x1, starting transfers between devices, shards(): rest = lax.all_to_all(rest, 'gx', 0, 0, tiled=True)  5.98 us
    ppermute x6, starting transfers between devices, exchange(): lax.ppermute(block, 'gx', [(k, k ^ 2 * step) for k in range(x_devices)])  5.43 us
    all_to_all x1, starting transfers between devices, shards(): rows = lax.all_to_all(rows, 'gx', 0, 0, tiled=True)  4.8 us
    ppermute x2, starting transfers between devices, exchange(): got = lax.ppermute(swapped, 'gx', [(k, k ^ 1) for k in range(x_devices)])  3.05 us
  transfers between devices with their start and end apart: 28, of which 18 were waited for; matrix products, arithmetic and copies ran while one was open for 0% of the time, Pallas kernels for 7%

profile of v4, /device:TPU:11, one launch (start us, length us, event | category | flops | bytes accessed | tf_op | source)
XLA Modules:
  0.0 114.1 jit_solution(9200052045494485306)
XLA Ops:
  0.6 2.0 %shard_map.104 = (f32[128,256]{1,0:T(8,128)S(1)}, f32[128,256]{1,0:T(8,128)S(1)}, f32[128,256]{1,0:T(8,128)S(1)}, f32[128,256]{1,0:T(8,128)S(1)}, f32[128,256]{1...) custom-call(f32[5]{0:T(128)} %moduli.3, ...), custom_call_target="tpu_custom_call" | custom-call | bytes 3408916 | tf_op jit(solution)/shard_map/pallas_call | solution.py:516
  2.7 1.4 %collective-permute-start = (f32[128,256]{1,0:T(8,128)S(1)}, f32[128,256]{1,0:T(8,128)S(1)}, u32[]{:S(2)}, u32[]{:S(2)}) collective-permute-start(f32[128,256]{1,0:T(8,128)S(1)} %get-tuple-element.68), channel_id=1, source_target_pairs={{0,8},{8,16},{16,24},{24,0},{1,9},{9,17},{17,25},{25,1},{2,10},{10... | collective-permute-start | bytes 393224 | tf_op jit(solution)/shard_map/ppermute | solution.py:549
  5.1 1.4 %collective-permute-start.2 = (f32[128,256]{1,0:T(8,128)S(1)}, f32[128,256]{1,0:T(8,128)S(1)}, u32[]{:S(2)}, u32[]{:S(2)}) collective-permute-start(f32[128,256]{1,0:T(8,128)S(1)} %get-tuple-element.70), channel_id=1, source_target_pairs={{0,24},{8,0},{16,8},{24,16},{1,25},{9,1},{17,9},{25,17},{2,26},{10... | collective-permute-start | bytes 393224 | tf_op jit(solution)/shard_map/ppermute | solution.py:549
  6.5 2.0 %collective-permute-start.3 = (f32[128,256]{1,0:T(8,128)S(1)}, f32[128,256]{1,0:T(8,128)S(1)}, u32[]{:S(2)}, u32[]{:S(2)}) collective-permute-start(f32[128,256]{1,0:T(8,128)S(1)} %get-tuple-element.72), channel_id=1, source_target_pairs={{0,8},{8,16},{1,9},{9,17},{2,10},{10,18},{3,11},{11,19},{4,12},{12... | collective-permute-start | bytes 393224 | tf_op jit(solution)/shard_map/ppermute | solution.py:549
  8.5 1.3 %collective-permute-start.4 = (f32[128,256]{1,0:T(8,128)S(1)}, f32[128,256]{1,0:T(8,128)S(1)}, u32[]{:S(2)}, u32[]{:S(2)}) collective-permute-start(f32[128,256]{1,0:T(8,128)S(1)} %get-tuple-element.73), channel_id=1, source_target_pairs={{0,16},{24,8},{1,17},{25,9},{2,18},{26,10},{3,19},{27,11},{4,20},{... | collective-permute-start | bytes 393224 | tf_op jit(solution)/shard_map/ppermute | solution.py:549
  11.1 3.4 %collective-permute-done.1.rest_2_ = f32[128,256]{1,0:T(8,128)S(1)} collective-permute-done((f32[128,256]{1,0:T(8,128)S(1)}, f32[128,256]{1,0:T(8,128)S(1)}, u32[]{:S(2)}, u32[]{:S(2)}) %collective-permute-start.1) | collective-permute-done | bytes 131104 | tf_op jit(solution)/shard_map/ppermute | solution.py:549
  14.5 5.8 %collective-permute-done.2.rest_3_ = f32[128,256]{1,0:T(8,128)S(1)} collective-permute-done((f32[128,256]{1,0:T(8,128)S(1)}, f32[128,256]{1,0:T(8,128)S(1)}, u32[]{:S(2)}, u32[]{:S(2)}) %collective-permute-start.2) | collective-permute-done | bytes 131104 | tf_op jit(solution)/shard_map/ppermute | solution.py:549
  20.2 2.8 %collective-permute-done.5.rest_7_ = f32[128,256]{1,0:T(8,128)S(1)} collective-permute-done((f32[128,256]{1,0:T(8,128)S(1)}, f32[128,256]{1,0:T(8,128)S(1)}, u32[]{:S(2)}, u32[]{:S(2)}) %collective-permute-start.5) | collective-permute-done | bytes 131104 | tf_op jit(solution)/shard_map/ppermute | solution.py:549
  23.0 1.9 %shard_map.105 = f32[8,2,128,128]{3,2,1,0:T(8,128)} custom-call(bf16[2,768,512]{2,1,0:T(8,128)(2,1)S(1)} %copy-done.1, f32[128,256]{1,0:T(8,128)S(1)} %get-tuple-element.83.rest_0_, f32[128,256]{1,0:T(8,128)S(1)} %collective-permute-done.rest_1_, f32[128,256]{1,0:T(8,128)S(1)} %collective-permute-done.1.rest_2_, ...), custom_call_target="tpu_custom_call" | custom-call | bytes 3670016 | tf_op jit(solution)/shard_map/pallas_call | solution.py:516
  24.9 4.8 %all-to-all-start = ((f32[8,2,128,128]{3,2,1,0:T(8,128)}), f32[8,2,128,128]{3,2,1,0:T(8,128)}, u32[]{:S(2)}, u32[]{:S(2)}) async-start(f32[8,2,128,128]{3,2,1,0:T(8,128)} %shard_map.105), calls=%async_computation | async-start | bytes 2097152 | tf_op jit(solution)/shard_map/all_to_all | solution.py:592
  31.4 3.1 %collective-permute-done.6.rest_1_ = f32[128,256]{1,0:T(8,128)S(1)} collective-permute-done((f32[128,256]{1,0:T(8,128)S(1)}, f32[128,256]{1,0:T(8,128)S(1)}, u32[]{:S(2)}, u32[]{:S(2)}) %collective-permute-start.6) | collective-permute-done | bytes 131104 | tf_op jit(solution)/shard_map/ppermute | solution.py:549
  34.6 6.6 %collective-permute-done.7.rest_2_ = f32[128,256]{1,0:T(8,128)S(1)} collective-permute-done((f32[128,256]{1,0:T(8,128)S(1)}, f32[128,256]{1,0:T(8,128)S(1)}, u32[]{:S(2)}, u32[]{:S(2)}) %collective-permute-start.7) | collective-permute-done | bytes 131104 | tf_op jit(solution)/shard_map/ppermute | solution.py:549
  41.9 1.8 %all-to-all-done.data_h = f32[8,2,128,128]{3,2,1,0:T(8,128)} async-done(((f32[8,2,128,128]{3,2,1,0:T(8,128)}), f32[8,2,128,128]{3,2,1,0:T(8,128)}, u32[]{:S(2)}, u32[]{:S(2)}) %all-to-all-start) | async-done | bytes 1048608 | tf_op jit(solution)/shard_map/all_to_all | solution.py:592
  46.0 1.3 %collective-permute-start.10 = (f32[2,128,128]{2,1,0:T(8,128)S(1)}, f32[2,128,128]{2,1,0:T(8,128)S(1)}, u32[]{:S(2)}, u32[]{:S(2)}) collective-permute-start(f32[2,128,128]{2,1,0:T(8,128)S(1)} %get-tuple-element.102), channel_id=1, source_target_pairs={{0,2},{1,3},{2,0},{3,1},{4,6},{5,7},{6,4},{7,5},{8,10},{9,11},{10,... | collective-permute-start | bytes 393224 | tf_op jit(solution)/shard_map/ppermute | solution.py:584
  48.7 2.8 %shard_map.108.done = f32[4,2,256,128]{3,2,1,0:T(8,128)S(1)} custom-call(bf16[2,512,256]{2,1,0:T(8,128)(2,1)S(1)} %copy-done.2, f32[256,8]{1,0:T(8,128)S(1)} %copy-done.3, f32[8,2,128,128]{3,2,1,0:T(8,128)} %all-to-all-done.data_h), custom_call_target="tpu_custom_call" | custom-call | bytes 2629632 | tf_op jit(solution)/shard_map/pallas_call | solution.py:516
  52.1 1.4 %collective-permute-done.12.rest_2_ = f32[2,128,128]{2,1,0:T(8,128)S(1)} collective-permute-done((f32[2,128,128]{2,1,0:T(8,128)S(1)}, f32[2,128,128]{2,1,0:T(8,128)S(1)}, u32[]{:S(2)}, u32[]{:S(2)}) %collective-permute-start.12) | collective-permute-done | bytes 131104 | tf_op jit(solution)/shard_map/ppermute | solution.py:584
  53.5 5.4 %shard_map.109 = (f32[4,128,128]{2,1,0:T(8,128)S(1)}, f32[4,128,128]{2,1,0:T(8,128)S(1)}, f32[4,256,384]{2,1,0:T(8,128)}) custom-call(f32[5]{0:T(128)S(1)} %copy-done.6, f32[6]{0:T(128)S(1)} %copy-done.7, bf16[2,512,256]{2,1,0:T(8,128)(2,1)S(1)} %copy-done.2, f32[256,8]{1,0:T(8,128)S(1)} %copy-done.3, f32[4,2,256,128]{3,2,1,0:T(8,128)S(1)} %shard_map.108.done, ...), custom_call_target="tpu_custom_call" | custom-call | bytes 4595756 | tf_op jit(solution)/shard_map/pallas_call | solution.py:516
  59.0 2.5 %collective-permute-start.13 = (f32[4,128,128]{2,1,0:T(8,128)S(1)}, f32[4,128,128]{2,1,0:T(8,128)S(1)}, u32[]{:S(2)}, u32[]{:S(2)}) collective-permute-start(f32[4,128,128]{2,1,0:T(8,128)S(1)} %get-tuple-element.106), channel_id=1, source_target_pairs={{0,1},{1,0},{2,3},{3,2},{4,5},{5,4},{6,7},{7,6},{8,9},{9,8},{10,11... | collective-permute-start | bytes 786440 | tf_op jit(solution)/shard_map/ppermute | solution.py:580
  63.9 1.5 %collective-permute-start.16 = (f32[2,128,128]{2,1,0:T(8,128)S(1)}, f32[2,128,128]{2,1,0:T(8,128)S(1)}, u32[]{:S(2)}, u32[]{:S(2)}) collective-permute-start(f32[2,128,128]{2,1,0:T(8,128)S(1)} %get-tuple-element.114), channel_id=1, source_target_pairs={{0,6},{1,7},{2,4},{3,5},{4,2},{5,3},{6,0},{7,1},{8,14},{9,15},{10,... | collective-permute-start | bytes 393224 | tf_op jit(solution)/shard_map/ppermute | solution.py:584
  65.4 4.7 %shard_map.111 = f32[8,2,128,128]{3,2,1,0:T(8,128)} custom-call(bf16[2,512,256]{2,1,0:T(8,128)(2,1)S(1)} %copy-done.2, f32[256,8]{1,0:T(8,128)S(1)} %copy-done.3, f32[4,256,384]{2,1,0:T(8,128)} %get-tuple-element.111.data_h), custom_call_target="tpu_custom_call" | custom-call | bytes 3153920 | tf_op jit(solution)/shard_map/pallas_call | solution.py:516
  71.7 6.0 %all-to-all-start.1 = ((f32[8,2,128,128]{3,2,1,0:T(8,128)}), f32[8,2,128,128]{3,2,1,0:T(8,128)S(1)}, u32[]{:S(2)}, u32[]{:S(2)}) async-start(f32[8,2,128,128]{3,2,1,0:T(8,128)} %shard_map.111), calls=%async_computation.1 | async-start | bytes 2097152 | tf_op jit(solution)/shard_map/all_to_all | solution.py:620
  78.7 1.4 %collective-permute-start.22 = (f32[128,256]{1,0:T(8,128)S(1)}, f32[128,256]{1,0:T(8,128)S(1)}, u32[]{:S(2)}, u32[]{:S(2)}) collective-permute-start(f32[128,256]{1,0:T(8,128)S(1)} %get-tuple-element.127), channel_id=1, source_target_pairs={{0,24},{8,0},{16,8},{24,16},{1,25},{9,1},{17,9},{25,17},{2,26},{10... | collective-permute-start | bytes 393224 | tf_op jit(solution)/shard_map/ppermute | solution.py:549
  80.1 11.4 %all-to-all-done.1.data = f32[8,2,128,128]{3,2,1,0:T(8,128)S(1)} async-done(((f32[8,2,128,128]{3,2,1,0:T(8,128)}), f32[8,2,128,128]{3,2,1,0:T(8,128)S(1)}, u32[]{:S(2)}, u32[]{:S(2)}) %all-to-all-start.1) | async-done | bytes 1048608 | tf_op jit(solution)/shard_map/all_to_all | solution.py:620
  93.6 1.4 %collective-permute-start.19 = (f32[128,256]{1,0:T(8,128)S(1)}, f32[128,256]{1,0:T(8,128)S(1)}, u32[]{:S(2)}, u32[]{:S(2)}) collective-permute-start(f32[128,256]{1,0:T(8,128)S(1)} %get-tuple-element.123), channel_id=1, source_target_pairs={{0,24},{8,0},{16,8},{24,16},{1,25},{9,1},{17,9},{25,17},{2,26},{10... | collective-permute-start | bytes 393224 | tf_op jit(solution)/shard_map/ppermute | solution.py:549
  95.0 2.1 %collective-permute-start.23 = (f32[128,256]{1,0:T(8,128)S(1)}, f32[128,256]{1,0:T(8,128)S(1)}, u32[]{:S(2)}, u32[]{:S(2)}) collective-permute-start(f32[128,256]{1,0:T(8,128)S(1)} %get-tuple-element.129), channel_id=1, source_target_pairs={{8,16},{16,24},{9,17},{17,25},{10,18},{18,26},{11,19},{19,27},{12,... | collective-permute-start | bytes 393224 | tf_op jit(solution)/shard_map/ppermute | solution.py:549
  97.1 2.5 %collective-permute-start.24 = (f32[128,256]{1,0:T(8,128)S(1)}, f32[128,256]{1,0:T(8,128)S(1)}, u32[]{:S(2)}, u32[]{:S(2)}) collective-permute-start(f32[128,256]{1,0:T(8,128)S(1)} %get-tuple-element.130), channel_id=1, source_target_pairs={{8,24},{16,0},{9,25},{17,1},{10,26},{18,2},{11,27},{19,3},{12,28},... | collective-permute-start | bytes 393224 | tf_op jit(solution)/shard_map/ppermute | solution.py:549
  99.6 1.9 %collective-permute-start.25 = (f32[128,256]{1,0:T(8,128)S(1)}, f32[128,256]{1,0:T(8,128)S(1)}, u32[]{:S(2)}, u32[]{:S(2)}) collective-permute-start(f32[128,256]{1,0:T(8,128)S(1)} %get-tuple-element.131), channel_id=1, source_target_pairs={{8,0},{16,8},{9,1},{17,9},{10,2},{18,10},{11,3},{19,11},{12,4},{20... | collective-permute-start | bytes 393224 | tf_op jit(solution)/shard_map/ppermute | solution.py:549
  101.5 2.3 %collective-permute-done.18.rest_2_ = f32[128,256]{1,0:T(8,128)S(1)} collective-permute-done((f32[128,256]{1,0:T(8,128)S(1)}, f32[128,256]{1,0:T(8,128)S(1)}, u32[]{:S(2)}, u32[]{:S(2)}) %collective-permute-start.18) | collective-permute-done | bytes 131104 | tf_op jit(solution)/shard_map/ppermute | solution.py:549
  103.8 2.0 %collective-permute-done.19.rest_3_ = f32[128,256]{1,0:T(8,128)S(1)} collective-permute-done((f32[128,256]{1,0:T(8,128)S(1)}, f32[128,256]{1,0:T(8,128)S(1)}, u32[]{:S(2)}, u32[]{:S(2)}) %collective-permute-start.19) | collective-permute-done | bytes 131104 | tf_op jit(solution)/shard_map/ppermute | solution.py:549
  106.6 2.8 %collective-permute-done.24.rest_10_ = f32[128,256]{1,0:T(8,128)S(1)} collective-permute-done((f32[128,256]{1,0:T(8,128)S(1)}, f32[128,256]{1,0:T(8,128)S(1)}, u32[]{:S(2)}, u32[]{:S(2)}) %collective-permute-start.24) | collective-permute-done | bytes 131104 | tf_op jit(solution)/shard_map/ppermute | solution.py:549
  109.4 2.1 %collective-permute-done.25.rest_11_ = f32[128,256]{1,0:T(8,128)S(1)} collective-permute-done((f32[128,256]{1,0:T(8,128)S(1)}, f32[128,256]{1,0:T(8,128)S(1)}, u32[]{:S(2)}, u32[]{:S(2)}) %collective-permute-start.25) | collective-permute-done | bytes 131104 | tf_op jit(solution)/shard_map/ppermute | solution.py:549
  111.5 2.6 %shard_map.114 = (f32[6,2,128,256]{3,2,1,0:T(8,128)}, f32[6,2,128,256]{3,2,1,0:T(8,128)}) custom-call(f32[5]{0:T(128)S(1)} %copy-done.6, f32[6]{0:T(128)S(1)} %copy-done.7, s32[2,128,256]{2,1,0:T(8,128)S(1)} %copy-done.4, s32[2,8,16]{2,1,0:T(8,128)S(1)} %copy-done.5, f32[128,256]{1,0:T(8,128)S(1)} %get-tuple-element.120.rest_0_, ...), custom_call_target="tpu_custom_call" | custom-call | bytes 4981804 | tf_op jit(solution)/shard_map/pallas_call | solution.py:516
  (51 shorter events, 17.1 us)
Async XLA Ops:
  0.6 22.4 %copy-start.1 = (bf16[2,768,512]{2,1,0:T(8,128)(2,1)S(1)}, bf16[2,768,512]{2,1,0:T(8,128)(2,1)}, u32[]{:S(2)}) copy-start(bf16[2,768,512]{2,1,0:T(8,128)(2,1)} %constant.8.clone.table) | copy-start | bytes 4718596
  2.7 7.1 %collective-permute-start = (f32[128,256]{1,0:T(8,128)S(1)}, f32[128,256]{1,0:T(8,128)S(1)}, u32[]{:S(2)}, u32[]{:S(2)}) collective-permute-start(f32[128,256]{1,0:T(8,128)S(1)} %get-tuple-element.68), channel_id=1, source_target_pairs={{0,8},{8,16},{16,24},{24,0},{1,9},{9,17},{17,25},{25,1},{2,10},{10... | collective-permute-start | bytes 393224 | tf_op jit(solution)/shard_map/ppermute | solution.py:549
  4.0 10.4 %collective-permute-start.1 = (f32[128,256]{1,0:T(8,128)S(1)}, f32[128,256]{1,0:T(8,128)S(1)}, u32[]{:S(2)}, u32[]{:S(2)}) collective-permute-start(f32[128,256]{1,0:T(8,128)S(1)} %get-tuple-element.69), channel_id=1, source_target_pairs={{0,16},{8,24},{16,0},{24,8},{1,17},{9,25},{17,1},{25,9},{2,18},{10... | collective-permute-start | bytes 393224 | tf_op jit(solution)/shard_map/ppermute | solution.py:549
  5.1 15.1 %collective-permute-start.2 = (f32[128,256]{1,0:T(8,128)S(1)}, f32[128,256]{1,0:T(8,128)S(1)}, u32[]{:S(2)}, u32[]{:S(2)}) collective-permute-start(f32[128,256]{1,0:T(8,128)S(1)} %get-tuple-element.70), channel_id=1, source_target_pairs={{0,24},{8,0},{16,8},{24,16},{1,25},{9,1},{17,9},{25,17},{2,26},{10... | collective-permute-start | bytes 393224 | tf_op jit(solution)/shard_map/ppermute | solution.py:549
  6.5 13.7 %collective-permute-start.3 = (f32[128,256]{1,0:T(8,128)S(1)}, f32[128,256]{1,0:T(8,128)S(1)}, u32[]{:S(2)}, u32[]{:S(2)}) collective-permute-start(f32[128,256]{1,0:T(8,128)S(1)} %get-tuple-element.72), channel_id=1, source_target_pairs={{0,8},{8,16},{1,9},{9,17},{2,10},{10,18},{3,11},{11,19},{4,12},{12... | collective-permute-start | bytes 393224 | tf_op jit(solution)/shard_map/ppermute | solution.py:549
  8.5 11.8 %collective-permute-start.4 = (f32[128,256]{1,0:T(8,128)S(1)}, f32[128,256]{1,0:T(8,128)S(1)}, u32[]{:S(2)}, u32[]{:S(2)}) collective-permute-start(f32[128,256]{1,0:T(8,128)S(1)} %get-tuple-element.73), channel_id=1, source_target_pairs={{0,16},{24,8},{1,17},{25,9},{2,18},{26,10},{3,19},{27,11},{4,20},{... | collective-permute-start | bytes 393224 | tf_op jit(solution)/shard_map/ppermute | solution.py:549
  9.8 13.2 %collective-permute-start.5 = (f32[128,256]{1,0:T(8,128)S(1)}, f32[128,256]{1,0:T(8,128)S(1)}, u32[]{:S(2)}, u32[]{:S(2)}) collective-permute-start(f32[128,256]{1,0:T(8,128)S(1)} %get-tuple-element.74), channel_id=1, source_target_pairs={{16,8},{24,16},{17,9},{25,17},{18,10},{26,18},{19,11},{27,19},{20,... | collective-permute-start | bytes 393224 | tf_op jit(solution)/shard_map/ppermute | solution.py:549
  24.9 18.7 %all-to-all-start = ((f32[8,2,128,128]{3,2,1,0:T(8,128)}), f32[8,2,128,128]{3,2,1,0:T(8,128)}, u32[]{:S(2)}, u32[]{:S(2)}) async-start(f32[8,2,128,128]{3,2,1,0:T(8,128)} %shard_map.105), calls=%async_computation | async-start | bytes 2097152 | tf_op jit(solution)/shard_map/all_to_all | solution.py:592
  29.7 18.9 %copy-start.3 = (f32[256,8]{1,0:T(8,128)S(1)}, f32[256,8]{1,0:T(8,128)}, u32[]{:S(2)}) copy-start(f32[256,8]{1,0:T(8,128)} %constant.10.clone.twiddles) | copy-start | bytes 24580
  29.7 4.8 %collective-permute-start.6 = (f32[128,256]{1,0:T(8,128)S(1)}, f32[128,256]{1,0:T(8,128)S(1)}, u32[]{:S(2)}, u32[]{:S(2)}) collective-permute-start(f32[128,256]{1,0:T(8,128)S(1)} %get-tuple-element.80), channel_id=1, source_target_pairs={{0,8},{8,16},{16,24},{24,0},{1,9},{9,17},{17,25},{25,1},{2,10},{10... | collective-permute-start | bytes 393224 | tf_op jit(solution)/shard_map/ppermute | solution.py:549
  30.2 10.9 %collective-permute-start.7 = (f32[128,256]{1,0:T(8,128)S(1)}, f32[128,256]{1,0:T(8,128)S(1)}, u32[]{:S(2)}, u32[]{:S(2)}) collective-permute-start(f32[128,256]{1,0:T(8,128)S(1)} %get-tuple-element.81), channel_id=1, source_target_pairs={{0,16},{8,24},{16,0},{24,8},{1,17},{9,25},{17,1},{25,9},{2,18},{10... | collective-permute-start | bytes 393224 | tf_op jit(solution)/shard_map/ppermute | solution.py:549
  30.2 11.7 %collective-permute-start.8 = (f32[128,256]{1,0:T(8,128)S(1)}, f32[128,256]{1,0:T(8,128)S(1)}, u32[]{:S(2)}, u32[]{:S(2)}) collective-permute-start(f32[128,256]{1,0:T(8,128)S(1)} %get-tuple-element.82), channel_id=1, source_target_pairs={{0,24},{8,0},{16,8},{24,16},{1,25},{9,1},{17,9},{25,17},{2,26},{10... | collective-permute-start | bytes 393224 | tf_op jit(solution)/shard_map/ppermute | solution.py:549
  44.2 1.7 %collective-permute-start.9 = (f32[4,128,128]{2,1,0:T(8,128)S(1)}, f32[4,128,128]{2,1,0:T(8,128)S(1)}, u32[]{:S(2)}, u32[]{:S(2)}) collective-permute-start(f32[4,128,128]{2,1,0:T(8,128)S(1)} %get-tuple-element.96), channel_id=1, source_target_pairs={{0,1},{1,0},{2,3},{3,2},{4,5},{5,4},{6,7},{7,6},{8,9},{9,8},{10,11... | collective-permute-start | bytes 786440 | tf_op jit(solution)/shard_map/ppermute | solution.py:580
  46.0 5.5 %collective-permute-start.10 = (f32[2,128,128]{2,1,0:T(8,128)S(1)}, f32[2,128,128]{2,1,0:T(8,128)S(1)}, u32[]{:S(2)}, u32[]{:S(2)}) collective-permute-start(f32[2,128,128]{2,1,0:T(8,128)S(1)} %get-tuple-element.102), channel_id=1, source_target_pairs={{0,2},{1,3},{2,0},{3,1},{4,6},{5,7},{6,4},{7,5},{8,10},{9,11},{10,... | collective-permute-start | bytes 393224 | tf_op jit(solution)/shard_map/ppermute | solution.py:584
  47.3 4.8 %collective-permute-start.11 = (f32[2,128,128]{2,1,0:T(8,128)S(1)}, f32[2,128,128]{2,1,0:T(8,128)S(1)}, u32[]{:S(2)}, u32[]{:S(2)}) collective-permute-start(f32[2,128,128]{2,1,0:T(8,128)S(1)} %get-tuple-element.103), channel_id=1, source_target_pairs={{0,4},{1,5},{2,6},{3,7},{4,0},{5,1},{6,2},{7,3},{8,12},{9,13},{10,... | collective-permute-start | bytes 393224 | tf_op jit(solution)/shard_map/ppermute | solution.py:584
  47.5 6.0 %collective-permute-start.12 = (f32[2,128,128]{2,1,0:T(8,128)S(1)}, f32[2,128,128]{2,1,0:T(8,128)S(1)}, u32[]{:S(2)}, u32[]{:S(2)}) collective-permute-start(f32[2,128,128]{2,1,0:T(8,128)S(1)} %get-tuple-element.104), channel_id=1, source_target_pairs={{0,6},{1,7},{2,4},{3,5},{4,2},{5,3},{6,0},{7,1},{8,14},{9,15},{10,... | collective-permute-start | bytes 393224 | tf_op jit(solution)/shard_map/ppermute | solution.py:584
  59.0 3.7 %collective-permute-start.13 = (f32[4,128,128]{2,1,0:T(8,128)S(1)}, f32[4,128,128]{2,1,0:T(8,128)S(1)}, u32[]{:S(2)}, u32[]{:S(2)}) collective-permute-start(f32[4,128,128]{2,1,0:T(8,128)S(1)} %get-tuple-element.106), channel_id=1, source_target_pairs={{0,1},{1,0},{2,3},{3,2},{4,5},{5,4},{6,7},{7,6},{8,9},{9,8},{10,11... | collective-permute-start | bytes 786440 | tf_op jit(solution)/shard_map/ppermute | solution.py:580
  62.7 7.4 %collective-permute-start.14 = (f32[2,128,128]{2,1,0:T(8,128)S(1)}, f32[2,128,128]{2,1,0:T(8,128)S(1)}, u32[]{:S(2)}, u32[]{:S(2)}) collective-permute-start(f32[2,128,128]{2,1,0:T(8,128)S(1)} %get-tuple-element.112), channel_id=1, source_target_pairs={{0,2},{1,3},{2,0},{3,1},{4,6},{5,7},{6,4},{7,5},{8,10},{9,11},{10,... | collective-permute-start | bytes 393224 | tf_op jit(solution)/shard_map/ppermute | solution.py:584
  63.0 7.1 %collective-permute-start.15 = (f32[2,128,128]{2,1,0:T(8,128)S(1)}, f32[2,128,128]{2,1,0:T(8,128)S(1)}, u32[]{:S(2)}, u32[]{:S(2)}) collective-permute-start(f32[2,128,128]{2,1,0:T(8,128)S(1)} %get-tuple-element.113), channel_id=1, source_target_pairs={{0,4},{1,5},{2,6},{3,7},{4,0},{5,1},{6,2},{7,3},{8,12},{9,13},{10,... | collective-permute-start | bytes 393224 | tf_op jit(solution)/shard_map/ppermute | solution.py:584
  63.9 6.4 %collective-permute-start.16 = (f32[2,128,128]{2,1,0:T(8,128)S(1)}, f32[2,128,128]{2,1,0:T(8,128)S(1)}, u32[]{:S(2)}, u32[]{:S(2)}) collective-permute-start(f32[2,128,128]{2,1,0:T(8,128)S(1)} %get-tuple-element.114), channel_id=1, source_target_pairs={{0,6},{1,7},{2,4},{3,5},{4,2},{5,3},{6,0},{7,1},{8,14},{9,15},{10,... | collective-permute-start | bytes 393224 | tf_op jit(solution)/shard_map/ppermute | solution.py:584
  71.7 19.8 %all-to-all-start.1 = ((f32[8,2,128,128]{3,2,1,0:T(8,128)}), f32[8,2,128,128]{3,2,1,0:T(8,128)S(1)}, u32[]{:S(2)}, u32[]{:S(2)}) async-start(f32[8,2,128,128]{3,2,1,0:T(8,128)} %shard_map.111), calls=%async_computation.1 | async-start | bytes 2097152 | tf_op jit(solution)/shard_map/all_to_all | solution.py:620
  77.6 33.9 %copy-start.4 = (s32[2,128,256]{2,1,0:T(8,128)S(1)}, s32[2,128,256]{2,1,0:T(8,128)}, u32[]{:S(2)}) copy-start(s32[2,128,256]{2,1,0:T(8,128)} %labels.1) | copy-start | bytes 786436
  77.7 33.9 %copy-start.5 = (s32[2,8,16]{2,1,0:T(8,128)S(1)}, s32[2,8,16]{2,1,0:T(8,128)}, u32[]{:S(2)}) copy-start(s32[2,8,16]{2,1,0:T(8,128)} %normals.1) | copy-start | bytes 3076
  77.7 15.9 %collective-permute-start.20 = (f32[128,256]{1,0:T(8,128)}, f32[128,256]{1,0:T(8,128)S(1)}, u32[]{:S(2)}, u32[]{:S(2)}) collective-permute-start(f32[128,256]{1,0:T(8,128)} %get-tuple-element.125), channel_id=1, source_target_pairs={{0,8},{8,16},{16,24},{24,0},{1,9},{9,17},{17,25},{25,1},{2,10},{10... | collective-permute-start | bytes 393224 | tf_op jit(solution)/shard_map/ppermute | solution.py:549
  78.1 16.9 %collective-permute-start.21 = (f32[128,256]{1,0:T(8,128)}, f32[128,256]{1,0:T(8,128)S(1)}, u32[]{:S(2)}, u32[]{:S(2)}) collective-permute-start(f32[128,256]{1,0:T(8,128)} %get-tuple-element.126), channel_id=1, source_target_pairs={{0,16},{8,24},{16,0},{24,8},{1,17},{9,25},{17,1},{25,9},{2,18},{10... | collective-permute-start | bytes 393224 | tf_op jit(solution)/shard_map/ppermute | solution.py:549
  78.7 18.3 %collective-permute-start.22 = (f32[128,256]{1,0:T(8,128)S(1)}, f32[128,256]{1,0:T(8,128)S(1)}, u32[]{:S(2)}, u32[]{:S(2)}) collective-permute-start(f32[128,256]{1,0:T(8,128)S(1)} %get-tuple-element.127), channel_id=1, source_target_pairs={{0,24},{8,0},{16,8},{24,16},{1,25},{9,1},{17,9},{25,17},{2,26},{10... | collective-permute-start | bytes 393224 | tf_op jit(solution)/shard_map/ppermute | solution.py:549
  92.4 7.1 %collective-permute-start.17 = (f32[128,256]{1,0:T(8,128)S(1)}, f32[128,256]{1,0:T(8,128)S(1)}, u32[]{:S(2)}, u32[]{:S(2)}) collective-permute-start(f32[128,256]{1,0:T(8,128)S(1)} %get-tuple-element.121), channel_id=1, source_target_pairs={{0,8},{8,16},{16,24},{24,0},{1,9},{9,17},{17,25},{25,1},{2,10},{10... | collective-permute-start | bytes 393224 | tf_op jit(solution)/shard_map/ppermute | solution.py:549
  92.9 10.9 %collective-permute-start.18 = (f32[128,256]{1,0:T(8,128)S(1)}, f32[128,256]{1,0:T(8,128)S(1)}, u32[]{:S(2)}, u32[]{:S(2)}) collective-permute-start(f32[128,256]{1,0:T(8,128)S(1)} %get-tuple-element.122), channel_id=1, source_target_pairs={{0,16},{8,24},{16,0},{24,8},{1,17},{9,25},{17,1},{25,9},{2,18},{10... | collective-permute-start | bytes 393224 | tf_op jit(solution)/shard_map/ppermute | solution.py:549
  93.6 12.3 %collective-permute-start.19 = (f32[128,256]{1,0:T(8,128)S(1)}, f32[128,256]{1,0:T(8,128)S(1)}, u32[]{:S(2)}, u32[]{:S(2)}) collective-permute-start(f32[128,256]{1,0:T(8,128)S(1)} %get-tuple-element.123), channel_id=1, source_target_pairs={{0,24},{8,0},{16,8},{24,16},{1,25},{9,1},{17,9},{25,17},{2,26},{10... | collective-permute-start | bytes 393224 | tf_op jit(solution)/shard_map/ppermute | solution.py:549
  95.0 11.7 %collective-permute-start.23 = (f32[128,256]{1,0:T(8,128)S(1)}, f32[128,256]{1,0:T(8,128)S(1)}, u32[]{:S(2)}, u32[]{:S(2)}) collective-permute-start(f32[128,256]{1,0:T(8,128)S(1)} %get-tuple-element.129), channel_id=1, source_target_pairs={{8,16},{16,24},{9,17},{17,25},{10,18},{18,26},{11,19},{19,27},{12,... | collective-permute-start | bytes 393224 | tf_op jit(solution)/shard_map/ppermute | solution.py:549
  97.1 12.4 %collective-permute-start.24 = (f32[128,256]{1,0:T(8,128)S(1)}, f32[128,256]{1,0:T(8,128)S(1)}, u32[]{:S(2)}, u32[]{:S(2)}) collective-permute-start(f32[128,256]{1,0:T(8,128)S(1)} %get-tuple-element.130), channel_id=1, source_target_pairs={{8,24},{16,0},{9,25},{17,1},{10,26},{18,2},{11,27},{19,3},{12,28},... | collective-permute-start | bytes 393224 | tf_op jit(solution)/shard_map/ppermute | solution.py:549
  99.6 12.0 %collective-permute-start.25 = (f32[128,256]{1,0:T(8,128)S(1)}, f32[128,256]{1,0:T(8,128)S(1)}, u32[]{:S(2)}, u32[]{:S(2)}) collective-permute-start(f32[128,256]{1,0:T(8,128)S(1)} %get-tuple-element.131), channel_id=1, source_target_pairs={{8,0},{16,8},{9,1},{17,9},{10,2},{18,10},{11,3},{19,11},{12,4},{20... | collective-permute-start | bytes 393224 | tf_op jit(solution)/shard_map/ppermute | solution.py:549
  (4 other events, 41.9 us)

commit v5 on v4

--- a/solution.py
+++ b/solution.py
@@ -277,38 +277,50 @@
     sources, fields, rows, lanes = data.shape
     quarter = sources * rows // 4
     per = sources // 4
-    sign = turn_sign(fields * lanes)
+    width = fields * lanes
+    sign = turn_sign(width)
     block = [
         jnp.concatenate([data[a * per : (a + 1) * per, f].reshape(quarter, lanes) for f in range(fields)], 1)
         for a in range(4)
     ]
     even, odd = block[0] + block[2], block[1] + block[3]
     diff, turned = block[0] - block[2], sign * swap(block[1] - block[3])
-    for residue, value in enumerate((even + odd, diff + turned, even - odd, diff - turned)):
-        both = dot_left(table, twiddle(twiddles, residue, value, sign))
-        yield both[:quarter] + sign * swap(both[quarter:])
+    values = (even + odd, diff + turned, even - odd, diff - turned)
+    values = [twiddle(twiddles, residue, value, sign) for residue, value in enumerate(values)]
+    both = dot_left(table, jnp.concatenate(values, 1))
+    for residue in range(4):
+        columns = slice(residue * width, (residue + 1) * width)
+        yield both[:quarter, columns] + sign * swap(both[quarter:, columns])
 
 
 def x_inverse(spectra, table, twiddles, is_special, out):
     sources, fields, rows, lanes = out.shape
     quarter = sources * rows // 4
     per = sources // 4
-    sign = turn_sign((fields + 1) * lanes)
-    parts = []
-    for residue in range(4):
-        both = dot_left(table, spectra(residue))
-        parts.append(twiddle(twiddles, residue, both[:quarter] - sign * swap(both[quarter:]), -sign))
-    h0, h1, h2, h3 = parts
-    even, odd = h0 + h2, h1 + h3
-    diff, turned = h0 - h2, sign * swap(h1 - h3)
-    lane = lax.broadcasted_iota(jnp.int32, (1, lanes), 1)
+    width = fields * lanes
+    sign = turn_sign(spectra.shape[1])
+    both = dot_left(table, spectra)
+    both = both[:quarter] - sign * swap(both[quarter:])
+    sign = sign[:, :width]
+
+    def join(values):
+        h0, h1, h2, h3 = [twiddle(twiddles, residue, value, -sign) for residue, value in enumerate(values)]
+        even, odd = h0 + h2, h1 + h3
+        diff, turned = h0 - h2, sign * swap(h1 - h3)
+        return even + odd, diff - turned, even - odd, diff + turned
+
+    packed = both[:, 4 * width :]
+    unpacked = [packed]
+    for residue in range(1, 4):
+        pieces = [pltpu.roll(packed[:, k : k + lanes], lanes - residue, 1) for k in range(0, width, lanes)]
+        unpacked.append(jnp.concatenate(pieces, 1))
+    lane = lax.broadcasted_iota(jnp.int32, (1, width), 1) % lanes
     edge = jnp.logical_and(is_special, lane == lanes // 2)
-    for a, value in enumerate((even + odd, diff - turned, even - odd, diff + turned)):
-        extra = value[:, fields * lanes :]
+    whole = join([both[:, residue * width : (residue + 1) * width] for residue in range(4)])
+    for a, (value, other) in enumerate(zip(whole, join(unpacked))):
+        final = jnp.where(edge, other, value)
         for f in range(fields):
-            moved = extra if f == 0 else pltpu.roll(extra, lanes - f, 1)
-            final = jnp.where(edge, moved, value[:, f * lanes : (f + 1) * lanes])
-            out[a * per : (a + 1) * per, f] = final.reshape(per, rows, lanes)
+            out[a * per : (a + 1) * per, f] = final[:, f * lanes : (f + 1) * lanes].reshape(per, rows, lanes)
 
 
 def holds_edge(slots, z_cells):
@@ -330,7 +342,7 @@
     copy.start()
     copy.wait()
     special = holds_edge(out.shape[3] // 2, z_cells)
-    x_inverse(lambda residue: data[residue], table, twiddles, special, out)
+    x_inverse(data[...], table, twiddles, special, out)
 
 
 def green_kernel(x_cells, z_cells, chunks, moduli, mean, table, twiddles, done, own_in, got, *rest):
@@ -368,16 +380,16 @@
             return own[residue, own_chunk.index(field), rows, :]
         return done[residue, rest_chunk.index(field), rows, :]
 
-    def store(chunk, residue, rows, block, value):
-        columns = slice(block * lanes, (block + 1) * lanes)
-        if chunk is own_chunk:
-            new[residue, rows, columns] = value
-        else:
-            rest_out[residue, rows, columns] = value
-
-    def green(kx, kz, odd_kx, s):
+    def store(field, residue, rows, value):
+        chunk, spectra = (own_chunk, new) if field in own_chunk else (rest_chunk, rest_out)
+        block = residue * len(chunk) + chunk.index(field)
+        spectra[rows, block * lanes : (block + 1) * lanes] = value
+
+    def green(kx, kz, odd_kx, s, anchored=False):
         radius = kx * kx + kz * kz
-        inverse = 1.0 / jnp.where(radius == 0.0, 1.0, radius)
+        if anchored:
+            radius = jnp.where(radius == 0.0, 1.0, radius)
+        inverse = 1.0 / radius
         a, b = kx * kx * inverse, kz * kz * inverse
         d = odd_kx * kz * inverse
         ab = c1 * (a * b)
@@ -407,38 +419,32 @@
         rows = pl.ds(start, size)
         row = lax.broadcasted_iota(jnp.int32, (size, lanes), 0) + start
         full_kz = jnp.broadcast_to(kz, (size, lanes))
+        first_kx = (4 * row - (x_cells if 2 * start >= quarter else 0)).astype(F32)
+        mirror = 2 * start == quarter
         edge = [None] * FIELDS
         for residue in range(4):
             s = [load(f, residue, rows) for f in range(FIELDS)]
             for f in range(FIELDS):
                 moved = s[f] if residue == 0 else pltpu.roll(s[f], residue, 1)
                 edge[f] = moved if residue == 0 else jnp.where(slot_of == residue, moved, edge[f])
-            count = 4 * row + residue
-            kx = jnp.where(count < x_cells // 2, count, count - x_cells).astype(F32)
-            odd_kx = jnp.where(count == x_cells // 2, 0.0, kx) if residue == 0 else kx
-            fresh = list(green(kx, full_kz, odd_kx, s))
-            if residue == 0 and start == 0:
+            kx = first_kx + float(residue)
+            odd_kx = jnp.where(row == start, 0.0, kx) if mirror and residue == 0 else kx
+            with_anchor = residue == 0 and start == 0
+            fresh = list(green(kx, full_kz, odd_kx, s, with_anchor))
+            if with_anchor:
                 anchor = jnp.logical_and(row == 0, special)
                 for f in range(FIELDS):
                     fresh[f] = jnp.where(anchor, jnp.where(lane < slots, means[f], 0.0), fresh[f])
-            for chunk in chunks:
-                for block, f in enumerate(chunk):
-                    store(chunk, residue, rows, block, fresh[f])
-        count = 4 * row + slot_of
-        kx = jnp.where(count < x_cells // 2, count, count - x_cells).astype(F32)
-        odd_kx = jnp.where(count == x_cells // 2, kx, 0.0)
+            for f in range(FIELDS):
+                store(f, residue, rows, fresh[f])
+        kx = first_kx + slot_of.astype(F32)
+        odd_kx = jnp.where(jnp.logical_and(row == start, slot_of == 0), kx, 0.0) if mirror else jnp.zeros_like(kx)
         fresh = green(kx, jnp.full((size, lanes), -0.5 * z_cells, F32), odd_kx, edge)
-        for residue in range(4):
-            for chunk in chunks:
-                extra = None
-                for block, f in enumerate(chunk):
-                    shift = (block - residue) % lanes
-                    moved = fresh[f] if shift == 0 else pltpu.roll(fresh[f], shift, 1)
-                    extra = moved if block == 0 else jnp.where(slot_of == block, moved, extra)
-                store(chunk, residue, rows, len(chunk), extra)
+        for f in range(FIELDS):
+            store(f, 4, rows, fresh[f])
     copy = pltpu.make_async_copy(rest_out, rest_h, sem)
     copy.start()
-    x_inverse(lambda residue: new[residue], table, twiddles, holds_edge(slots, z_cells), out)
+    x_inverse(new[...], table, twiddles, holds_edge(slots, z_cells), out)
     deal(out, own_out, swapped)
     copy.wait()
 
@@ -468,25 +474,27 @@
             outs[slot * parts + step][...] = held[target, slot]
 
 
-def stress_kernel(moduli, mean, labels, normals, *rest):
+def stress_kernel(slots, strain_parts, stress_parts, moduli, mean, labels, normals, *rest):
     parts = len(GROUPS)
-    arrived, (strain_to, stress_to, held, strain_out, stress_out, sems) = rest[:-6], rest[-6:]
+    arrived = rest[: len(slots) * parts]
+    strain_to, stress_to, held, strain_out, stress_out, sems = rest[-6:]
     place = lax.axis_index("gz")
     sections, cells_x, cells_z = labels.shape
     size = cells_x // normals.shape[1]
     for step in range(parts):
         source = lax.rem(place + parts - step, parts)
-        for slot in range(FIELDS):
-            held[source, slot] = arrived[slot * parts + step][...]
+        for k, slot in enumerate(slots):
+            held[source, slot] = arrived[k * parts + step][...]
     copies = []
     for section in range(sections):
         squares = tilt(normals, section, cells_z)
         for block in range(cells_x // size):
             rows = pl.ds(block * size, size)
-            local = {YY: jnp.full((size, cells_z), mean[YY], F32)}
+            local = {c: jnp.zeros((size, cells_z), F32) for c in range(6)}
+            local[YY] = jnp.full((size, cells_z), mean[YY], F32)
             for group, fields in enumerate(GROUPS):
                 for slot, (component, of) in enumerate(fields):
-                    if of == section:
+                    if of == section and slot in slots:
                         local[component] = held[group, slot, rows, :]
             value = law(
                 local,
@@ -496,18 +504,20 @@
                 (moduli[1], moduli[3]),
                 moduli[4],
             )
-            for component in range(6):
+            for component in strain_parts:
                 strain_out[component, section, rows, :] = local[component]
+            for component in stress_parts:
                 stress_out[component, section, rows, :] = value[component]
-        for k, (here, there) in enumerate(((strain_out, strain_to), (stress_out, stress_to))):
-            copy = pltpu.make_async_copy(here.at[:, section], there.at[:, section], sems.at[2 * section + k])
-            copy.start()
-            copies.append(copy)
+        for here, there, chosen in ((strain_out, strain_to, strain_parts), (stress_out, stress_to, stress_parts)):
+            for c in chosen:
+                copy = pltpu.make_async_copy(here.at[c, section], there.at[c, section], sems.at[len(copies)])
+                copy.start()
+                copies.append(copy)
     for copy in copies:
         copy.wait()
 
 
-def call(kernel, outs, scratch, args, limit, hbm=(), smem=0, hbm_out=()):
+def call(kernel, outs, scratch, args, limit, hbm=(), smem=0, hbm_out=(), aliases={}):
     def space(k):
         return pltpu.HBM if k in hbm else pltpu.SMEM if k < smem else pltpu.VMEM
 
@@ -523,6 +533,7 @@
             pl.BlockSpec(memory_space=pltpu.HBM if k in hbm_out else pltpu.VMEM) for k in range(len(outs))
         ],
         scratch_shapes=scratch,
+        input_output_aliases=aliases,
         compiler_params=pltpu.CompilerParams(vmem_limit_bytes=limit * MIB),
         cost_estimate=pl.CostEstimate(flops=0, bytes_accessed=moved, transcendentals=0),
     )(*args)
@@ -598,13 +609,13 @@
     (spectrum,) = call(x_forward_kernel, [(4, size, quarter, lanes)], copied, (*x_tab, rows), 24, (2,))
     own, swapped, rest = call(
         functools.partial(green_kernel, x_total, z_total, CHUNKS),
-        [tile, tile, (4, quarter, (size + 1) * lanes)],
+        [tile, tile, (quarter, 5 * size * lanes)],
         [
             tiles,
             tiles,
             pltpu.VMEM((4, 1, quarter, lanes), F32),
-            pltpu.VMEM((4, quarter, 2 * lanes), F32),
-            pltpu.VMEM((4, quarter, (size + 1) * lanes), F32),
+            pltpu.VMEM((quarter, 5 * lanes), F32),
+            pltpu.VMEM((quarter, 5 * size * lanes), F32),
             pltpu.SemaphoreType.DMA,
         ],
         (moduli, mean_strain, *x_tab, spectrum, *last),
@@ -623,18 +634,23 @@
     for slot, f in enumerate(early):
         arrived[f] = travel(f, blocks[slot * parts : (slot + 1) * parts], False)
     full = (6, sections, cells_x, cells_z)
-    args = [a for f in range(FIELDS) for a in arrived[f]]
-    return tuple(
-        call(
-            stress_kernel,
+    results = ()
+    for slots, strains, stresses in (((0, 1), (XX, YY, ZZ, YZ, XY), (YY, YZ, XY)), ((0, 1, 2), (XZ,), (XX, ZZ, XZ))):
+        args = (moduli, mean_strain, labels, normals, *[a for f in slots for a in arrived[f]], *results)
+        hbm = range(len(args) - len(results), len(args))
+        count = sections * (len(strains) + len(stresses))
+        results = call(
+            functools.partial(stress_kernel, slots, strains, stresses),
             [full, full],
-            [held(FIELDS), pltpu.VMEM(full, F32), pltpu.VMEM(full, F32), pltpu.SemaphoreType.DMA((2 * sections,))],
-            (moduli, mean_strain, labels, normals, *args),
-            24,
+            [held(FIELDS), pltpu.VMEM(full, F32), pltpu.VMEM(full, F32), pltpu.SemaphoreType.DMA((count,))],
+            args,
+            16,
+            hbm,
             smem=2,
             hbm_out=(0, 1),
+            aliases={k: out for out, k in enumerate(hbm)},
         )
-    )
+    return tuple(results)
 
 
 def orientation(normals, blk):

time: 115 us -> 113 us (0.983)
  waiting for transfers between devices: 50.2 us -> 48.1 us
    ppermute x18, waiting for transfers between devices: 32.4 us -> 30.3 us  [travel(): moved.append(lax.ppermute(blocks[step], 'gz', way))]
    pallas_call x11 -> x12, Pallas kernels: 22.3 us -> 23.1 us  [call(): pl.pallas_call(kernel, out_shape=[pltpu.HBM(o, F32) if k in hbm_out else...]
  transfers between devices with their start and end apart: 28 -> 28, of which waited for: 18 -> 17; matrix products, arithmetic and copies ran while one was open for 0% -> 0% of each run, Pallas kernels for 7% -> 9%
where the time goes in v5:
time: 113 us
  waiting for transfers between devices  48.1 us (43%)
  starting transfers between devices  40.8 us (36%)
  Pallas kernels  23.1 us (20%)
    ppermute x18, waiting for transfers between devices, travel(): moved.append(lax.ppermute(blocks[step], 'gz', way))  30.3 us
    pallas_call x12, Pallas kernels, call(): pl.pallas_call(kernel, out_shape=[pltpu.HBM(o, F32) if k in hbm_out else...  23.1 us
    ppermute x18, starting transfers between devices, travel(): moved.append(lax.ppermute(blocks[step], 'gz', way))  21.6 us
    all_to_all x1, waiting for transfers between devices, shards(): rest = lax.all_to_all(rest, 'gx', 0, 0, tiled=True)  11.4 us
    all_to_all x1, starting transfers between devices, shards(): rest = lax.all_to_all(rest, 'gx', 0, 0, tiled=True)  6 us
    ppermute x6, starting transfers between devices, exchange(): lax.ppermute(block, 'gx', [(k, k ^ 2 * step) for k in range(x_devices)])  5.43 us
    all_to_all x1, starting transfers between devices, shards(): rows = lax.all_to_all(rows, 'gx', 0, 0, tiled=True)  4.79 us
    ppermute x2, starting transfers between devices, exchange(): got = lax.ppermute(swapped, 'gx', [(k, k ^ 1) for k in range(x_devices)])  3.04 us
  transfers between devices with their start and end apart: 28, of which 17 were waited for; matrix products, arithmetic and copies ran while one was open for 0% of the time, Pallas kernels for 9%

profile of v5, /device:TPU:11, one launch (start us, length us, event | category | flops | bytes accessed | tf_op | source)
XLA Modules:
  0.0 112.9 jit_solution(8337685351999609049)
XLA Ops:
  0.6 2.0 %shard_map.104 = (f32[128,256]{1,0:T(8,128)S(1)}, f32[128,256]{1,0:T(8,128)S(1)}, f32[128,256]{1,0:T(8,128)S(1)}, f32[128,256]{1,0:T(8,128)S(1)}, f32[128,256]{1...) custom-call(f32[5]{0:T(128)} %moduli.5, ...), custom_call_target="tpu_custom_call" | custom-call | bytes 3408916 | tf_op jit(solution)/shard_map/pallas_call | solution.py:526
  2.7 1.4 %collective-permute-start = (f32[128,256]{1,0:T(8,128)S(1)}, f32[128,256]{1,0:T(8,128)S(1)}, u32[]{:S(2)}, u32[]{:S(2)}) collective-permute-start(f32[128,256]{1,0:T(8,128)S(1)} %get-tuple-element.70), channel_id=1, source_target_pairs={{0,8},{8,16},{16,24},{24,0},{1,9},{9,17},{17,25},{25,1},{2,10},{10... | collective-permute-start | bytes 393224 | tf_op jit(solution)/shard_map/ppermute | solution.py:560
  5.1 1.4 %collective-permute-start.2 = (f32[128,256]{1,0:T(8,128)S(1)}, f32[128,256]{1,0:T(8,128)S(1)}, u32[]{:S(2)}, u32[]{:S(2)}) collective-permute-start(f32[128,256]{1,0:T(8,128)S(1)} %get-tuple-element.72), channel_id=1, source_target_pairs={{0,24},{8,0},{16,8},{24,16},{1,25},{9,1},{17,9},{25,17},{2,26},{10... | collective-permute-start | bytes 393224 | tf_op jit(solution)/shard_map/ppermute | solution.py:560
  6.5 2.0 %collective-permute-start.3 = (f32[128,256]{1,0:T(8,128)S(1)}, f32[128,256]{1,0:T(8,128)S(1)}, u32[]{:S(2)}, u32[]{:S(2)}) collective-permute-start(f32[128,256]{1,0:T(8,128)S(1)} %get-tuple-element.74), channel_id=1, source_target_pairs={{0,8},{8,16},{1,9},{9,17},{2,10},{10,18},{3,11},{11,19},{4,12},{12... | collective-permute-start | bytes 393224 | tf_op jit(solution)/shard_map/ppermute | solution.py:560
  11.1 3.4 %collective-permute-done.1.rest_2_ = f32[128,256]{1,0:T(8,128)S(1)} collective-permute-done((f32[128,256]{1,0:T(8,128)S(1)}, f32[128,256]{1,0:T(8,128)S(1)}, u32[]{:S(2)}, u32[]{:S(2)}) %collective-permute-start.1) | collective-permute-done | bytes 131104 | tf_op jit(solution)/shard_map/ppermute | solution.py:560
  14.5 5.8 %collective-permute-done.2.rest_3_ = f32[128,256]{1,0:T(8,128)S(1)} collective-permute-done((f32[128,256]{1,0:T(8,128)S(1)}, f32[128,256]{1,0:T(8,128)S(1)}, u32[]{:S(2)}, u32[]{:S(2)}) %collective-permute-start.2) | collective-permute-done | bytes 131104 | tf_op jit(solution)/shard_map/ppermute | solution.py:560
  20.2 2.8 %collective-permute-done.5.rest_7_ = f32[128,256]{1,0:T(8,128)S(1)} collective-permute-done((f32[128,256]{1,0:T(8,128)S(1)}, f32[128,256]{1,0:T(8,128)S(1)}, u32[]{:S(2)}, u32[]{:S(2)}) %collective-permute-start.5) | collective-permute-done | bytes 131104 | tf_op jit(solution)/shard_map/ppermute | solution.py:560
  23.0 1.9 %shard_map.105 = f32[8,2,128,128]{3,2,1,0:T(8,128)} custom-call(bf16[2,768,512]{2,1,0:T(8,128)(2,1)S(1)} %copy-done.1, f32[128,256]{1,0:T(8,128)S(1)} %get-tuple-element.85.rest_0_, f32[128,256]{1,0:T(8,128)S(1)} %collective-permute-done.rest_1_, f32[128,256]{1,0:T(8,128)S(1)} %collective-permute-done.1.rest_2_, ...), custom_call_target="tpu_custom_call" | custom-call | bytes 3670016 | tf_op jit(solution)/shard_map/pallas_call | solution.py:526
  24.9 4.8 %all-to-all-start = ((f32[8,2,128,128]{3,2,1,0:T(8,128)}), f32[8,2,128,128]{3,2,1,0:T(8,128)}, u32[]{:S(2)}, u32[]{:S(2)}) async-start(f32[8,2,128,128]{3,2,1,0:T(8,128)} %shard_map.105), calls=%async_computation | async-start | bytes 2097152 | tf_op jit(solution)/shard_map/all_to_all | solution.py:603
  31.4 3.1 %collective-permute-done.6.rest_1_ = f32[128,256]{1,0:T(8,128)S(1)} collective-permute-done((f32[128,256]{1,0:T(8,128)S(1)}, f32[128,256]{1,0:T(8,128)S(1)}, u32[]{:S(2)}, u32[]{:S(2)}) %collective-permute-start.6) | collective-permute-done | bytes 131104 | tf_op jit(solution)/shard_map/ppermute | solution.py:560
  34.5 6.6 %collective-permute-done.7.rest_2_ = f32[128,256]{1,0:T(8,128)S(1)} collective-permute-done((f32[128,256]{1,0:T(8,128)S(1)}, f32[128,256]{1,0:T(8,128)S(1)}, u32[]{:S(2)}, u32[]{:S(2)}) %collective-permute-start.7) | collective-permute-done | bytes 131104 | tf_op jit(solution)/shard_map/ppermute | solution.py:560
  41.9 1.8 %all-to-all-done.data_h = f32[8,2,128,128]{3,2,1,0:T(8,128)} async-done(((f32[8,2,128,128]{3,2,1,0:T(8,128)}), f32[8,2,128,128]{3,2,1,0:T(8,128)}, u32[]{:S(2)}, u32[]{:S(2)}) %all-to-all-start) | async-done | bytes 1048608 | tf_op jit(solution)/shard_map/all_to_all | solution.py:603
  45.9 1.3 %collective-permute-start.10 = (f32[2,128,128]{2,1,0:T(8,128)S(1)}, f32[2,128,128]{2,1,0:T(8,128)S(1)}, u32[]{:S(2)}, u32[]{:S(2)}) collective-permute-start(f32[2,128,128]{2,1,0:T(8,128)S(1)} %get-tuple-element.104), channel_id=1, source_target_pairs={{0,2},{1,3},{2,0},{3,1},{4,6},{5,7},{6,4},{7,5},{8,10},{9,11},{10,... | collective-permute-start | bytes 393224 | tf_op jit(solution)/shard_map/ppermute | solution.py:595
  48.7 3.0 %shard_map.108.done = f32[4,2,256,128]{3,2,1,0:T(8,128)S(1)} custom-call(bf16[2,512,256]{2,1,0:T(8,128)(2,1)S(1)} %copy-done.2, f32[256,8]{1,0:T(8,128)S(1)} %copy-done.4, f32[8,2,128,128]{3,2,1,0:T(8,128)} %all-to-all-done.data_h), custom_call_target="tpu_custom_call" | custom-call | bytes 2629632 | tf_op jit(solution)/shard_map/pallas_call | solution.py:526
  52.1 1.4 %collective-permute-done.12.rest_2_ = f32[2,128,128]{2,1,0:T(8,128)S(1)} collective-permute-done((f32[2,128,128]{2,1,0:T(8,128)S(1)}, f32[2,128,128]{2,1,0:T(8,128)S(1)}, u32[]{:S(2)}, u32[]{:S(2)}) %collective-permute-start.12) | collective-permute-done | bytes 131104 | tf_op jit(solution)/shard_map/ppermute | solution.py:595
  53.5 4.9 %shard_map.109 = (f32[4,128,128]{2,1,0:T(8,128)S(1)}, f32[4,128,128]{2,1,0:T(8,128)S(1)}, f32[256,1280]{1,0:T(8,128)}) custom-call(f32[5]{0:T(128)S(1)} %copy-done.6, f32[6]{0:T(128)S(1)} %copy-done.7, bf16[2,512,256]{2,1,0:T(8,128)(2,1)S(1)} %copy-done.2, f32[256,8]{1,0:T(8,128)S(1)} %copy-done.4, f32[4,2,256,128]{3,2,1,0:T(8,128)S(1)} %shard_map.108.done, ...), custom_call_target="tpu_custom_call" | custom-call | bytes 4333612 | tf_op jit(solution)/shard_map/pallas_call | solution.py:526
  58.5 2.5 %collective-permute-start.13 = (f32[4,128,128]{2,1,0:T(8,128)S(1)}, f32[4,128,128]{2,1,0:T(8,128)S(1)}, u32[]{:S(2)}, u32[]{:S(2)}) collective-permute-start(f32[4,128,128]{2,1,0:T(8,128)S(1)} %get-tuple-element.108), channel_id=1, source_target_pairs={{0,1},{1,0},{2,3},{3,2},{4,5},{5,4},{6,7},{7,6},{8,9},{9,8},{10,11... | collective-permute-start | bytes 786440 | tf_op jit(solution)/shard_map/ppermute | solution.py:591
  63.5 1.5 %collective-permute-start.16 = (f32[2,128,128]{2,1,0:T(8,128)S(1)}, f32[2,128,128]{2,1,0:T(8,128)S(1)}, u32[]{:S(2)}, u32[]{:S(2)}) collective-permute-start(f32[2,128,128]{2,1,0:T(8,128)S(1)} %get-tuple-element.116), channel_id=1, source_target_pairs={{0,6},{1,7},{2,4},{3,5},{4,2},{5,3},{6,0},{7,1},{8,14},{9,15},{10,... | collective-permute-start | bytes 393224 | tf_op jit(solution)/shard_map/ppermute | solution.py:595
  64.9 4.4 %shard_map.111 = f32[8,2,128,128]{3,2,1,0:T(8,128)} custom-call(bf16[2,512,256]{2,1,0:T(8,128)(2,1)S(1)} %copy-done.2, f32[256,8]{1,0:T(8,128)S(1)} %copy-done.4, f32[256,1280]{1,0:T(8,128)} %get-tuple-element.113.data_h), custom_call_target="tpu_custom_call" | custom-call | bytes 2891776 | tf_op jit(solution)/shard_map/pallas_call | solution.py:526
  71.1 6.0 %all-to-all-start.1 = ((f32[8,2,128,128]{3,2,1,0:T(8,128)}), f32[8,2,128,128]{3,2,1,0:T(8,128)S(1)}, u32[]{:S(2)}, u32[]{:S(2)}) async-start(f32[8,2,128,128]{3,2,1,0:T(8,128)} %shard_map.111), calls=%async_computation.1 | async-start | bytes 2097152 | tf_op jit(solution)/shard_map/all_to_all | solution.py:631
  78.2 1.4 %collective-permute-start.22 = (f32[128,256]{1,0:T(8,128)S(1)}, f32[128,256]{1,0:T(8,128)S(1)}, u32[]{:S(2)}, u32[]{:S(2)}) collective-permute-start(f32[128,256]{1,0:T(8,128)S(1)} %get-tuple-element.129), channel_id=1, source_target_pairs={{0,24},{8,0},{16,8},{24,16},{1,25},{9,1},{17,9},{25,17},{2,26},{10... | collective-permute-start | bytes 393224 | tf_op jit(solution)/shard_map/ppermute | solution.py:560
  79.6 11.4 %all-to-all-done.1.data = f32[8,2,128,128]{3,2,1,0:T(8,128)S(1)} async-done(((f32[8,2,128,128]{3,2,1,0:T(8,128)}), f32[8,2,128,128]{3,2,1,0:T(8,128)S(1)}, u32[]{:S(2)}, u32[]{:S(2)}) %all-to-all-start.1) | async-done | bytes 1048608 | tf_op jit(solution)/shard_map/all_to_all | solution.py:631
  93.0 1.4 %collective-permute-start.19 = (f32[128,256]{1,0:T(8,128)S(1)}, f32[128,256]{1,0:T(8,128)S(1)}, u32[]{:S(2)}, u32[]{:S(2)}) collective-permute-start(f32[128,256]{1,0:T(8,128)S(1)} %get-tuple-element.125), channel_id=1, source_target_pairs={{0,24},{8,0},{16,8},{24,16},{1,25},{9,1},{17,9},{25,17},{2,26},{10... | collective-permute-start | bytes 393224 | tf_op jit(solution)/shard_map/ppermute | solution.py:560
  94.4 2.1 %collective-permute-start.23 = (f32[128,256]{1,0:T(8,128)S(1)}, f32[128,256]{1,0:T(8,128)S(1)}, u32[]{:S(2)}, u32[]{:S(2)}) collective-permute-start(f32[128,256]{1,0:T(8,128)S(1)} %get-tuple-element.131), channel_id=1, source_target_pairs={{8,16},{16,24},{9,17},{17,25},{10,18},{18,26},{11,19},{19,27},{12,... | collective-permute-start | bytes 393224 | tf_op jit(solution)/shard_map/ppermute | solution.py:560
  96.6 2.5 %collective-permute-start.24 = (f32[128,256]{1,0:T(8,128)S(1)}, f32[128,256]{1,0:T(8,128)S(1)}, u32[]{:S(2)}, u32[]{:S(2)}) collective-permute-start(f32[128,256]{1,0:T(8,128)S(1)} %get-tuple-element.132), channel_id=1, source_target_pairs={{8,24},{16,0},{9,25},{17,1},{10,26},{18,2},{11,27},{19,3},{12,28},... | collective-permute-start | bytes 393224 | tf_op jit(solution)/shard_map/ppermute | solution.py:560
  99.0 1.9 %collective-permute-start.25 = (f32[128,256]{1,0:T(8,128)S(1)}, f32[128,256]{1,0:T(8,128)S(1)}, u32[]{:S(2)}, u32[]{:S(2)}) collective-permute-start(f32[128,256]{1,0:T(8,128)S(1)} %get-tuple-element.133), channel_id=1, source_target_pairs={{8,0},{16,8},{9,1},{17,9},{10,2},{18,10},{11,3},{19,11},{12,4},{20... | collective-permute-start | bytes 393224 | tf_op jit(solution)/shard_map/ppermute | solution.py:560
  101.0 2.3 %collective-permute-done.18.rest_2_ = f32[128,256]{1,0:T(8,128)S(1)} collective-permute-done((f32[128,256]{1,0:T(8,128)S(1)}, f32[128,256]{1,0:T(8,128)S(1)}, u32[]{:S(2)}, u32[]{:S(2)}) %collective-permute-start.18) | collective-permute-done | bytes 131104 | tf_op jit(solution)/shard_map/ppermute | solution.py:560
  103.3 2.0 %collective-permute-done.19.rest_3_ = f32[128,256]{1,0:T(8,128)S(1)} collective-permute-done((f32[128,256]{1,0:T(8,128)S(1)}, f32[128,256]{1,0:T(8,128)S(1)}, u32[]{:S(2)}, u32[]{:S(2)}) %collective-permute-start.19) | collective-permute-done | bytes 131104 | tf_op jit(solution)/shard_map/ppermute | solution.py:560
  105.3 2.1 %shard_map.114 = (f32[6,2,128,256]{3,2,1,0:T(8,128)}, f32[6,2,128,256]{3,2,1,0:T(8,128)}) custom-call(f32[5]{0:T(128)S(1)} %copy-done.6, f32[6]{0:T(128)S(1)} %copy-done.7, s32[2,128,256]{2,1,0:T(8,128)S(1)} %copy-done.3, s32[2,8,16]{2,1,0:T(8,128)S(1)} %copy-done.5, f32[128,256]{1,0:T(8,128)S(1)} %get-tuple-element.122.rest_0_, ...), custom_call_target="tpu_custom_call" | custom-call | bytes 4457516 | tf_op jit(solution)/shard_map/pallas_call | solution.py:526
  107.5 1.4 %collective-permute-done.24.rest_10_ = f32[128,256]{1,0:T(8,128)S(1)} collective-permute-done((f32[128,256]{1,0:T(8,128)S(1)}, f32[128,256]{1,0:T(8,128)S(1)}, u32[]{:S(2)}, u32[]{:S(2)}) %collective-permute-start.24) | collective-permute-done | bytes 131104 | tf_op jit(solution)/shard_map/ppermute | solution.py:560
  108.9 2.1 %collective-permute-done.25.rest_11_ = f32[128,256]{1,0:T(8,128)S(1)} collective-permute-done((f32[128,256]{1,0:T(8,128)S(1)}, f32[128,256]{1,0:T(8,128)S(1)}, u32[]{:S(2)}, u32[]{:S(2)}) %collective-permute-start.25) | collective-permute-done | bytes 131104 | tf_op jit(solution)/shard_map/ppermute | solution.py:560
  111.0 1.9 %shard_map.115 = (f32[6,2,128,256]{3,2,1,0:T(8,128)}, f32[6,2,128,256]{3,2,1,0:T(8,128)}) custom-call(f32[5]{0:T(128)S(1)} %copy-done.6, f32[6]{0:T(128)S(1)} %copy-done.7, s32[2,128,256]{2,1,0:T(8,128)S(1)} %copy-done.3, s32[2,8,16]{2,1,0:T(8,128)S(1)} %copy-done.5, ...), custom_call_target="tpu_custom_call", output_to_operand_aliasing={{0}: (16, {}), {1}: (17, {})} | custom-call | bytes 8127532 | tf_op jit(solution)/shard_map/pallas_call | solution.py:526
  (52 shorter events, 17.6 us)
Async XLA Ops:
  0.6 22.4 %copy-start.1 = (bf16[2,768,512]{2,1,0:T(8,128)(2,1)S(1)}, bf16[2,768,512]{2,1,0:T(8,128)(2,1)}, u32[]{:S(2)}) copy-start(bf16[2,768,512]{2,1,0:T(8,128)(2,1)} %constant.8.clone.table) | copy-start | bytes 4718596
  2.7 7.1 %collective-permute-start = (f32[128,256]{1,0:T(8,128)S(1)}, f32[128,256]{1,0:T(8,128)S(1)}, u32[]{:S(2)}, u32[]{:S(2)}) collective-permute-start(f32[128,256]{1,0:T(8,128)S(1)} %get-tuple-element.70), channel_id=1, source_target_pairs={{0,8},{8,16},{16,24},{24,0},{1,9},{9,17},{17,25},{25,1},{2,10},{10... | collective-permute-start | bytes 393224 | tf_op jit(solution)/shard_map/ppermute | solution.py:560
  4.0 10.4 %collective-permute-start.1 = (f32[128,256]{1,0:T(8,128)S(1)}, f32[128,256]{1,0:T(8,128)S(1)}, u32[]{:S(2)}, u32[]{:S(2)}) collective-permute-start(f32[128,256]{1,0:T(8,128)S(1)} %get-tuple-element.71), channel_id=1, source_target_pairs={{0,16},{8,24},{16,0},{24,8},{1,17},{9,25},{17,1},{25,9},{2,18},{10... | collective-permute-start | bytes 393224 | tf_op jit(solution)/shard_map/ppermute | solution.py:560
  5.1 15.1 %collective-permute-start.2 = (f32[128,256]{1,0:T(8,128)S(1)}, f32[128,256]{1,0:T(8,128)S(1)}, u32[]{:S(2)}, u32[]{:S(2)}) collective-permute-start(f32[128,256]{1,0:T(8,128)S(1)} %get-tuple-element.72), channel_id=1, source_target_pairs={{0,24},{8,0},{16,8},{24,16},{1,25},{9,1},{17,9},{25,17},{2,26},{10... | collective-permute-start | bytes 393224 | tf_op jit(solution)/shard_map/ppermute | solution.py:560
  6.5 13.7 %collective-permute-start.3 = (f32[128,256]{1,0:T(8,128)S(1)}, f32[128,256]{1,0:T(8,128)S(1)}, u32[]{:S(2)}, u32[]{:S(2)}) collective-permute-start(f32[128,256]{1,0:T(8,128)S(1)} %get-tuple-element.74), channel_id=1, source_target_pairs={{0,8},{8,16},{1,9},{9,17},{2,10},{10,18},{3,11},{11,19},{4,12},{12... | collective-permute-start | bytes 393224 | tf_op jit(solution)/shard_map/ppermute | solution.py:560
  8.5 11.8 %collective-permute-start.4 = (f32[128,256]{1,0:T(8,128)S(1)}, f32[128,256]{1,0:T(8,128)S(1)}, u32[]{:S(2)}, u32[]{:S(2)}) collective-permute-start(f32[128,256]{1,0:T(8,128)S(1)} %get-tuple-element.75), channel_id=1, source_target_pairs={{0,16},{24,8},{1,17},{25,9},{2,18},{26,10},{3,19},{27,11},{4,20},{... | collective-permute-start | bytes 393224 | tf_op jit(solution)/shard_map/ppermute | solution.py:560
  9.8 13.2 %collective-permute-start.5 = (f32[128,256]{1,0:T(8,128)S(1)}, f32[128,256]{1,0:T(8,128)S(1)}, u32[]{:S(2)}, u32[]{:S(2)}) collective-permute-start(f32[128,256]{1,0:T(8,128)S(1)} %get-tuple-element.76), channel_id=1, source_target_pairs={{16,8},{24,16},{17,9},{25,17},{18,10},{26,18},{19,11},{27,19},{20,... | collective-permute-start | bytes 393224 | tf_op jit(solution)/shard_map/ppermute | solution.py:560
  24.9 18.7 %all-to-all-start = ((f32[8,2,128,128]{3,2,1,0:T(8,128)}), f32[8,2,128,128]{3,2,1,0:T(8,128)}, u32[]{:S(2)}, u32[]{:S(2)}) async-start(f32[8,2,128,128]{3,2,1,0:T(8,128)} %shard_map.105), calls=%async_computation | async-start | bytes 2097152 | tf_op jit(solution)/shard_map/all_to_all | solution.py:603
  29.7 18.9 %copy-start.4 = (f32[256,8]{1,0:T(8,128)S(1)}, f32[256,8]{1,0:T(8,128)}, u32[]{:S(2)}) copy-start(f32[256,8]{1,0:T(8,128)} %constant.10.clone.twiddles) | copy-start | bytes 24580
  29.7 4.8 %collective-permute-start.6 = (f32[128,256]{1,0:T(8,128)S(1)}, f32[128,256]{1,0:T(8,128)S(1)}, u32[]{:S(2)}, u32[]{:S(2)}) collective-permute-start(f32[128,256]{1,0:T(8,128)S(1)} %get-tuple-element.82), channel_id=1, source_target_pairs={{0,8},{8,16},{16,24},{24,0},{1,9},{9,17},{17,25},{25,1},{2,10},{10... | collective-permute-start | bytes 393224 | tf_op jit(solution)/shard_map/ppermute | solution.py:560
  30.2 10.9 %collective-permute-start.7 = (f32[128,256]{1,0:T(8,128)S(1)}, f32[128,256]{1,0:T(8,128)S(1)}, u32[]{:S(2)}, u32[]{:S(2)}) collective-permute-start(f32[128,256]{1,0:T(8,128)S(1)} %get-tuple-element.83), channel_id=1, source_target_pairs={{0,16},{8,24},{16,0},{24,8},{1,17},{9,25},{17,1},{25,9},{2,18},{10... | collective-permute-start | bytes 393224 | tf_op jit(solution)/shard_map/ppermute | solution.py:560
  30.2 11.7 %collective-permute-start.8 = (f32[128,256]{1,0:T(8,128)S(1)}, f32[128,256]{1,0:T(8,128)S(1)}, u32[]{:S(2)}, u32[]{:S(2)}) collective-permute-start(f32[128,256]{1,0:T(8,128)S(1)} %get-tuple-element.84), channel_id=1, source_target_pairs={{0,24},{8,0},{16,8},{24,16},{1,25},{9,1},{17,9},{25,17},{2,26},{10... | collective-permute-start | bytes 393224 | tf_op jit(solution)/shard_map/ppermute | solution.py:560
  44.2 1.7 %collective-permute-start.9 = (f32[4,128,128]{2,1,0:T(8,128)S(1)}, f32[4,128,128]{2,1,0:T(8,128)S(1)}, u32[]{:S(2)}, u32[]{:S(2)}) collective-permute-start(f32[4,128,128]{2,1,0:T(8,128)S(1)} %get-tuple-element.98), channel_id=1, source_target_pairs={{0,1},{1,0},{2,3},{3,2},{4,5},{5,4},{6,7},{7,6},{8,9},{9,8},{10,11... | collective-permute-start | bytes 786440 | tf_op jit(solution)/shard_map/ppermute | solution.py:591
  45.9 5.7 %collective-permute-start.10 = (f32[2,128,128]{2,1,0:T(8,128)S(1)}, f32[2,128,128]{2,1,0:T(8,128)S(1)}, u32[]{:S(2)}, u32[]{:S(2)}) collective-permute-start(f32[2,128,128]{2,1,0:T(8,128)S(1)} %get-tuple-element.104), channel_id=1, source_target_pairs={{0,2},{1,3},{2,0},{3,1},{4,6},{5,7},{6,4},{7,5},{8,10},{9,11},{10,... | collective-permute-start | bytes 393224 | tf_op jit(solution)/shard_map/ppermute | solution.py:595
  47.3 4.8 %collective-permute-start.11 = (f32[2,128,128]{2,1,0:T(8,128)S(1)}, f32[2,128,128]{2,1,0:T(8,128)S(1)}, u32[]{:S(2)}, u32[]{:S(2)}) collective-permute-start(f32[2,128,128]{2,1,0:T(8,128)S(1)} %get-tuple-element.105), channel_id=1, source_target_pairs={{0,4},{1,5},{2,6},{3,7},{4,0},{5,1},{6,2},{7,3},{8,12},{9,13},{10,... | collective-permute-start | bytes 393224 | tf_op jit(solution)/shard_map/ppermute | solution.py:595
  47.5 6.0 %collective-permute-start.12 = (f32[2,128,128]{2,1,0:T(8,128)S(1)}, f32[2,128,128]{2,1,0:T(8,128)S(1)}, u32[]{:S(2)}, u32[]{:S(2)}) collective-permute-start(f32[2,128,128]{2,1,0:T(8,128)S(1)} %get-tuple-element.106), channel_id=1, source_target_pairs={{0,6},{1,7},{2,4},{3,5},{4,2},{5,3},{6,0},{7,1},{8,14},{9,15},{10,... | collective-permute-start | bytes 393224 | tf_op jit(solution)/shard_map/ppermute | solution.py:595
  58.5 3.7 %collective-permute-start.13 = (f32[4,128,128]{2,1,0:T(8,128)S(1)}, f32[4,128,128]{2,1,0:T(8,128)S(1)}, u32[]{:S(2)}, u32[]{:S(2)}) collective-permute-start(f32[4,128,128]{2,1,0:T(8,128)S(1)} %get-tuple-element.108), channel_id=1, source_target_pairs={{0,1},{1,0},{2,3},{3,2},{4,5},{5,4},{6,7},{7,6},{8,9},{9,8},{10,11... | collective-permute-start | bytes 786440 | tf_op jit(solution)/shard_map/ppermute | solution.py:591
  62.2 7.1 %collective-permute-start.14 = (f32[2,128,128]{2,1,0:T(8,128)S(1)}, f32[2,128,128]{2,1,0:T(8,128)S(1)}, u32[]{:S(2)}, u32[]{:S(2)}) collective-permute-start(f32[2,128,128]{2,1,0:T(8,128)S(1)} %get-tuple-element.114), channel_id=1, source_target_pairs={{0,2},{1,3},{2,0},{3,1},{4,6},{5,7},{6,4},{7,5},{8,10},{9,11},{10,... | collective-permute-start | bytes 393224 | tf_op jit(solution)/shard_map/ppermute | solution.py:595
  62.5 6.8 %collective-permute-start.15 = (f32[2,128,128]{2,1,0:T(8,128)S(1)}, f32[2,128,128]{2,1,0:T(8,128)S(1)}, u32[]{:S(2)}, u32[]{:S(2)}) collective-permute-start(f32[2,128,128]{2,1,0:T(8,128)S(1)} %get-tuple-element.115), channel_id=1, source_target_pairs={{0,4},{1,5},{2,6},{3,7},{4,0},{5,1},{6,2},{7,3},{8,12},{9,13},{10,... | collective-permute-start | bytes 393224 | tf_op jit(solution)/shard_map/ppermute | solution.py:595
  63.5 6.4 %collective-permute-start.16 = (f32[2,128,128]{2,1,0:T(8,128)S(1)}, f32[2,128,128]{2,1,0:T(8,128)S(1)}, u32[]{:S(2)}, u32[]{:S(2)}) collective-permute-start(f32[2,128,128]{2,1,0:T(8,128)S(1)} %get-tuple-element.116), channel_id=1, source_target_pairs={{0,6},{1,7},{2,4},{3,5},{4,2},{5,3},{6,0},{7,1},{8,14},{9,15},{10,... | collective-permute-start | bytes 393224 | tf_op jit(solution)/shard_map/ppermute | solution.py:595
  71.1 19.8 %all-to-all-start.1 = ((f32[8,2,128,128]{3,2,1,0:T(8,128)}), f32[8,2,128,128]{3,2,1,0:T(8,128)S(1)}, u32[]{:S(2)}, u32[]{:S(2)}) async-start(f32[8,2,128,128]{3,2,1,0:T(8,128)} %shard_map.111), calls=%async_computation.1 | async-start | bytes 2097152 | tf_op jit(solution)/shard_map/all_to_all | solution.py:631
  77.1 28.2 %copy-start.3 = (s32[2,128,256]{2,1,0:T(8,128)S(1)}, s32[2,128,256]{2,1,0:T(8,128)}, u32[]{:S(2)}) copy-start(s32[2,128,256]{2,1,0:T(8,128)} %labels.3) | copy-start | bytes 786436
  77.1 28.2 %copy-start.5 = (s32[2,8,16]{2,1,0:T(8,128)S(1)}, s32[2,8,16]{2,1,0:T(8,128)}, u32[]{:S(2)}) copy-start(s32[2,8,16]{2,1,0:T(8,128)} %normals.3) | copy-start | bytes 3076
  77.1 15.9 %collective-permute-start.20 = (f32[128,256]{1,0:T(8,128)}, f32[128,256]{1,0:T(8,128)S(1)}, u32[]{:S(2)}, u32[]{:S(2)}) collective-permute-start(f32[128,256]{1,0:T(8,128)} %get-tuple-element.127), channel_id=1, source_target_pairs={{0,8},{8,16},{16,24},{24,0},{1,9},{9,17},{17,25},{25,1},{2,10},{10... | collective-permute-start | bytes 393224 | tf_op jit(solution)/shard_map/ppermute | solution.py:560
  77.6 16.9 %collective-permute-start.21 = (f32[128,256]{1,0:T(8,128)}, f32[128,256]{1,0:T(8,128)S(1)}, u32[]{:S(2)}, u32[]{:S(2)}) collective-permute-start(f32[128,256]{1,0:T(8,128)} %get-tuple-element.128), channel_id=1, source_target_pairs={{0,16},{8,24},{16,0},{24,8},{1,17},{9,25},{17,1},{25,9},{2,18},{10... | collective-permute-start | bytes 393224 | tf_op jit(solution)/shard_map/ppermute | solution.py:560
  78.2 18.3 %collective-permute-start.22 = (f32[128,256]{1,0:T(8,128)S(1)}, f32[128,256]{1,0:T(8,128)S(1)}, u32[]{:S(2)}, u32[]{:S(2)}) collective-permute-start(f32[128,256]{1,0:T(8,128)S(1)} %get-tuple-element.129), channel_id=1, source_target_pairs={{0,24},{8,0},{16,8},{24,16},{1,25},{9,1},{17,9},{25,17},{2,26},{10... | collective-permute-start | bytes 393224 | tf_op jit(solution)/shard_map/ppermute | solution.py:560
  91.9 7.1 %collective-permute-start.17 = (f32[128,256]{1,0:T(8,128)S(1)}, f32[128,256]{1,0:T(8,128)S(1)}, u32[]{:S(2)}, u32[]{:S(2)}) collective-permute-start(f32[128,256]{1,0:T(8,128)S(1)} %get-tuple-element.123), channel_id=1, source_target_pairs={{0,8},{8,16},{16,24},{24,0},{1,9},{9,17},{17,25},{25,1},{2,10},{10... | collective-permute-start | bytes 393224 | tf_op jit(solution)/shard_map/ppermute | solution.py:560
  92.4 10.9 %collective-permute-start.18 = (f32[128,256]{1,0:T(8,128)S(1)}, f32[128,256]{1,0:T(8,128)S(1)}, u32[]{:S(2)}, u32[]{:S(2)}) collective-permute-start(f32[128,256]{1,0:T(8,128)S(1)} %get-tuple-element.124), channel_id=1, source_target_pairs={{0,16},{8,24},{16,0},{24,8},{1,17},{9,25},{17,1},{25,9},{2,18},{10... | collective-permute-start | bytes 393224 | tf_op jit(solution)/shard_map/ppermute | solution.py:560
  93.0 12.3 %collective-permute-start.19 = (f32[128,256]{1,0:T(8,128)S(1)}, f32[128,256]{1,0:T(8,128)S(1)}, u32[]{:S(2)}, u32[]{:S(2)}) collective-permute-start(f32[128,256]{1,0:T(8,128)S(1)} %get-tuple-element.125), channel_id=1, source_target_pairs={{0,24},{8,0},{16,8},{24,16},{1,25},{9,1},{17,9},{25,17},{2,26},{10... | collective-permute-start | bytes 393224 | tf_op jit(solution)/shard_map/ppermute | solution.py:560
  94.4 13.1 %collective-permute-start.23 = (f32[128,256]{1,0:T(8,128)S(1)}, f32[128,256]{1,0:T(8,128)S(1)}, u32[]{:S(2)}, u32[]{:S(2)}) collective-permute-start(f32[128,256]{1,0:T(8,128)S(1)} %get-tuple-element.131), channel_id=1, source_target_pairs={{8,16},{16,24},{9,17},{17,25},{10,18},{18,26},{11,19},{19,27},{12,... | collective-permute-start | bytes 393224 | tf_op jit(solution)/shard_map/ppermute | solution.py:560
  96.6 12.4 %collective-permute-start.24 = (f32[128,256]{1,0:T(8,128)S(1)}, f32[128,256]{1,0:T(8,128)S(1)}, u32[]{:S(2)}, u32[]{:S(2)}) collective-permute-start(f32[128,256]{1,0:T(8,128)S(1)} %get-tuple-element.132), channel_id=1, source_target_pairs={{8,24},{16,0},{9,25},{17,1},{10,26},{18,2},{11,27},{19,3},{12,28},... | collective-permute-start | bytes 393224 | tf_op jit(solution)/shard_map/ppermute | solution.py:560
  99.0 12.0 %collective-permute-start.25 = (f32[128,256]{1,0:T(8,128)S(1)}, f32[128,256]{1,0:T(8,128)S(1)}, u32[]{:S(2)}, u32[]{:S(2)}) collective-permute-start(f32[128,256]{1,0:T(8,128)S(1)} %get-tuple-element.133), channel_id=1, source_target_pairs={{8,0},{16,8},{9,1},{17,9},{10,2},{18,10},{11,3},{19,11},{12,4},{20... | collective-permute-start | bytes 393224 | tf_op jit(solution)/shard_map/ppermute | solution.py:560
  (4 other events, 41.9 us)

commit v6 on v5

--- a/solution.py
+++ b/solution.py
@@ -337,23 +337,9 @@
             out[residue, f] = spectrum[:, f * lanes : (f + 1) * lanes]
 
 
-def x_inverse_kernel(z_cells, table, twiddles, data_h, out, data, sem):
-    copy = pltpu.make_async_copy(data_h, data, sem)
-    copy.start()
-    copy.wait()
-    special = holds_edge(out.shape[3] // 2, z_cells)
-    x_inverse(data[...], table, twiddles, special, out)
-
-
-def green_kernel(x_cells, z_cells, chunks, moduli, mean, table, twiddles, done, own_in, got, *rest):
-    chips = own_in.shape[0]
-    moved, rest = rest[: chips - 1], rest[chips - 1 :]
-    own_out, swapped, rest_h, data, out, own, new, rest_out, sem = rest
-    collect(own_in, got, moved, data)
-    rest_chunk, own_chunk = chunks
-    lanes = data.shape[3]
+def green_rows(x_cells, z_cells, chunk, moduli, mean, load, new):
+    quarter, lanes = new.shape[0], new.shape[1] // (5 * len(chunk))
     slots = lanes // 2
-    quarter = x_cells // 4
     place, mine = lax.axis_index("gz"), lax.axis_index("gx")
     inplane = functools.reduce(jnp.logical_or, [place == k for k in INPLANE])
     lame_ref = 0.5 * (moduli[0] + moduli[2])
@@ -371,19 +357,9 @@
         total * mean[XZ],
     )
 
-    for residue, spectrum in enumerate(x_forward(data, table, twiddles)):
-        for slot in range(len(own_chunk)):
-            own[residue, slot] = spectrum[:, slot * lanes : (slot + 1) * lanes]
-
-    def load(field, residue, rows):
-        if field in own_chunk:
-            return own[residue, own_chunk.index(field), rows, :]
-        return done[residue, rest_chunk.index(field), rows, :]
-
     def store(field, residue, rows, value):
-        chunk, spectra = (own_chunk, new) if field in own_chunk else (rest_chunk, rest_out)
         block = residue * len(chunk) + chunk.index(field)
-        spectra[rows, block * lanes : (block + 1) * lanes] = value
+        new[rows, block * lanes : (block + 1) * lanes] = value
 
     def green(kx, kz, odd_kx, s, anchored=False):
         radius = kx * kx + kz * kz
@@ -397,11 +373,12 @@
         h02, h12 = d * (ca - k2), d * (cb - k2)
         m01 = ab - ka * d
         twice = 2.0 * s[2]
-        return (
-            a * (ca - k1) * s[0] + m01 * s[1] + h02 * twice,
-            m01 * s[0] + b * (cb - k1) * s[1] + h12 * twice,
-            h02 * s[0] + h12 * s[1] + (2.0 * ab - k2) * s[2],
+        rows = (
+            lambda: a * (ca - k1) * s[0] + m01 * s[1] + h02 * twice,
+            lambda: m01 * s[0] + b * (cb - k1) * s[1] + h12 * twice,
+            lambda: h02 * s[0] + h12 * s[1] + (2.0 * ab - k2) * s[2],
         )
+        return {f: rows[f]() for f in chunk}
 
     lane = lax.broadcasted_iota(jnp.int32, (1, lanes), 1)
     slot_of = lane % slots
@@ -430,23 +407,45 @@
             kx = first_kx + float(residue)
             odd_kx = jnp.where(row == start, 0.0, kx) if mirror and residue == 0 else kx
             with_anchor = residue == 0 and start == 0
-            fresh = list(green(kx, full_kz, odd_kx, s, with_anchor))
+            fresh = green(kx, full_kz, odd_kx, s, with_anchor)
             if with_anchor:
                 anchor = jnp.logical_and(row == 0, special)
-                for f in range(FIELDS):
+                for f in chunk:
                     fresh[f] = jnp.where(anchor, jnp.where(lane < slots, means[f], 0.0), fresh[f])
-            for f in range(FIELDS):
+            for f in chunk:
                 store(f, residue, rows, fresh[f])
         kx = first_kx + slot_of.astype(F32)
         odd_kx = jnp.where(jnp.logical_and(row == start, slot_of == 0), kx, 0.0) if mirror else jnp.zeros_like(kx)
         fresh = green(kx, jnp.full((size, lanes), -0.5 * z_cells, F32), odd_kx, edge)
-        for f in range(FIELDS):
+        for f in chunk:
             store(f, 4, rows, fresh[f])
-    copy = pltpu.make_async_copy(rest_out, rest_h, sem)
-    copy.start()
-    x_inverse(new[...], table, twiddles, holds_edge(slots, z_cells), out)
+
+
+def loader(chunks, early, late):
+    def load(field, residue, rows):
+        spectra, chunk = (early, chunks[0]) if field in chunks[0] else (late, chunks[1])
+        return spectra[residue, chunk.index(field), rows, :]
+
+    return load
+
+
+def early_inverse_kernel(x_cells, z_cells, chunks, moduli, mean, table, twiddles, early, late, out, new):
+    green_rows(x_cells, z_cells, chunks[0], moduli, mean, loader(chunks, early, late), new)
+    x_inverse(new[...], table, twiddles, holds_edge(out.shape[3] // 2, z_cells), out)
+
+
+def late_kernel(x_cells, z_cells, chunks, moduli, mean, table, twiddles, early, own_in, got, *rest):
+    chips = own_in.shape[0]
+    moved, rest = rest[: chips - 1], rest[chips - 1 :]
+    own_out, swapped, late, data, out, new = rest
+    collect(own_in, got, moved, data)
+    lanes = data.shape[3]
+    for residue, spectrum in enumerate(x_forward(data, table, twiddles)):
+        for slot in range(data.shape[1]):
+            late[residue, slot] = spectrum[:, slot * lanes : (slot + 1) * lanes]
+    green_rows(x_cells, z_cells, chunks[1], moduli, mean, loader(chunks, early, late), new)
+    x_inverse(new[...], table, twiddles, holds_edge(lanes // 2, z_cells), out)
     deal(out, own_out, swapped)
-    copy.wait()
 
 
 def z_inverse_kernel(table, data, *rest):
@@ -607,25 +606,23 @@
     last, rows = exchange(own, swapped, rows)
     copied = [pltpu.VMEM(grid, F32), pltpu.SemaphoreType.DMA]
     (spectrum,) = call(x_forward_kernel, [(4, size, quarter, lanes)], copied, (*x_tab, rows), 24, (2,))
-    own, swapped, rest = call(
-        functools.partial(green_kernel, x_total, z_total, CHUNKS),
-        [tile, tile, (quarter, 5 * size * lanes)],
-        [
-            tiles,
-            tiles,
-            pltpu.VMEM((4, 1, quarter, lanes), F32),
-            pltpu.VMEM((quarter, 5 * lanes), F32),
-            pltpu.VMEM((quarter, 5 * size * lanes), F32),
-            pltpu.SemaphoreType.DMA,
-        ],
+    own, swapped, late_spectrum = call(
+        functools.partial(late_kernel, x_total, z_total, CHUNKS),
+        [tile, tile, (4, 1, quarter, lanes)],
+        [tiles, tiles, pltpu.VMEM((quarter, 5 * lanes), F32)],
         (moduli, mean_strain, *x_tab, spectrum, *last),
-        32,
+        24,
         smem=2,
-        hbm_out=(2,),
-    )
-    last, rest = exchange(own, swapped, rest)
-    copied = [pltpu.VMEM(rest.shape, F32), pltpu.SemaphoreType.DMA]
-    (rest,) = call(functools.partial(x_inverse_kernel, z_total), [grid], copied, (*x_tab, rest), 24, (2,))
+    )
+    last, late_spectrum = exchange(own, swapped, late_spectrum)
+    (rest,) = call(
+        functools.partial(early_inverse_kernel, x_total, z_total, CHUNKS),
+        [grid],
+        [pltpu.VMEM((quarter, 5 * size * lanes), F32)],
+        (moduli, mean_strain, *x_tab, spectrum, late_spectrum),
+        24,
+        smem=2,
+    )
     blocks = call(z_inverse_collect_kernel, [block] * parts, [held(1), tiles], (z_inv, *last), 16)
     rest, blocks = lax.optimization_barrier((rest, list(blocks)))
     rest = lax.all_to_all(rest, "gx", 0, 0, tiled=True)

time: 113 us -> 112 us (level)
  Pallas kernels: 23.1 us -> 21.8 us
    pallas_call x12, Pallas kernels: 23.1 us -> 21.8 us  [call(): pl.pallas_call(kernel, out_shape=[pltpu.HBM(o, F32) if k in hbm_out else...]
  transfers between devices with their start and end apart: 28 -> 28, of which waited for: 17 -> 17; matrix products, arithmetic and copies ran while one was open for 0% -> 0% of each run, Pallas kernels for 9% -> 10%
where the time goes in v6:
time: 112 us; the launch traced here: 111 us
  waiting for transfers between devices  48 us (43%)
  starting transfers between devices  40.8 us (36%)
  Pallas kernels  21.8 us (19%)
    ppermute x18, waiting for transfers between devices, travel(): moved.append(lax.ppermute(blocks[step], 'gz', way))  30.3 us
    pallas_call x12, Pallas kernels, call(): pl.pallas_call(kernel, out_shape=[pltpu.HBM(o, F32) if k in hbm_out else...  21.8 us
    ppermute x18, starting transfers between devices, travel(): moved.append(lax.ppermute(blocks[step], 'gz', way))  21.5 us
    all_to_all x1, waiting for transfers between devices, shards(): rest = lax.all_to_all(rest, 'gx', 0, 0, tiled=True)  11.4 us
    all_to_all x1, starting transfers between devices, shards(): rest = lax.all_to_all(rest, 'gx', 0, 0, tiled=True)  6.01 us
    ppermute x6, starting transfers between devices, exchange(): lax.ppermute(block, 'gx', [(k, k ^ 2 * step) for k in range(x_devices)])  5.43 us
    all_to_all x1, starting transfers between devices, shards(): rows = lax.all_to_all(rows, 'gx', 0, 0, tiled=True)  4.79 us
    ppermute x2, starting transfers between devices, exchange(): got = lax.ppermute(swapped, 'gx', [(k, k ^ 1) for k in range(x_devices)])  3.04 us
  transfers between devices with their start and end apart: 28, of which 17 were waited for; matrix products, arithmetic and copies ran while one was open for 0% of the time, Pallas kernels for 10%

profile of v6, /device:TPU:11, one launch (start us, length us, event | category | flops | bytes accessed | tf_op | source)
XLA Modules:
  0.0 111.4 jit_solution(16334972043250834208)
XLA Ops:
  0.6 2.0 %shard_map.104 = (f32[128,256]{1,0:T(8,128)S(1)}, f32[128,256]{1,0:T(8,128)S(1)}, f32[128,256]{1,0:T(8,128)S(1)}, f32[128,256]{1,0:T(8,128)S(1)}, f32[128,256]{1...) custom-call(f32[5]{0:T(128)} %moduli.7, ...), custom_call_target="tpu_custom_call" | custom-call | bytes 3408916 | tf_op jit(solution)/shard_map/pallas_call | solution.py:525
  2.7 1.4 %collective-permute-start = (f32[128,256]{1,0:T(8,128)S(1)}, f32[128,256]{1,0:T(8,128)S(1)}, u32[]{:S(2)}, u32[]{:S(2)}) collective-permute-start(f32[128,256]{1,0:T(8,128)S(1)} %get-tuple-element.70), channel_id=1, source_target_pairs={{0,8},{8,16},{16,24},{24,0},{1,9},{9,17},{17,25},{25,1},{2,10},{10... | collective-permute-start | bytes 393224 | tf_op jit(solution)/shard_map/ppermute | solution.py:559
  5.1 1.4 %collective-permute-start.2 = (f32[128,256]{1,0:T(8,128)S(1)}, f32[128,256]{1,0:T(8,128)S(1)}, u32[]{:S(2)}, u32[]{:S(2)}) collective-permute-start(f32[128,256]{1,0:T(8,128)S(1)} %get-tuple-element.72), channel_id=1, source_target_pairs={{0,24},{8,0},{16,8},{24,16},{1,25},{9,1},{17,9},{25,17},{2,26},{10... | collective-permute-start | bytes 393224 | tf_op jit(solution)/shard_map/ppermute | solution.py:559
  6.5 2.0 %collective-permute-start.3 = (f32[128,256]{1,0:T(8,128)S(1)}, f32[128,256]{1,0:T(8,128)S(1)}, u32[]{:S(2)}, u32[]{:S(2)}) collective-permute-start(f32[128,256]{1,0:T(8,128)S(1)} %get-tuple-element.74), channel_id=1, source_target_pairs={{0,8},{8,16},{1,9},{9,17},{2,10},{10,18},{3,11},{11,19},{4,12},{12... | collective-permute-start | bytes 393224 | tf_op jit(solution)/shard_map/ppermute | solution.py:559
  11.1 3.4 %collective-permute-done.1.rest_2_ = f32[128,256]{1,0:T(8,128)S(1)} collective-permute-done((f32[128,256]{1,0:T(8,128)S(1)}, f32[128,256]{1,0:T(8,128)S(1)}, u32[]{:S(2)}, u32[]{:S(2)}) %collective-permute-start.1) | collective-permute-done | bytes 131104 | tf_op jit(solution)/shard_map/ppermute | solution.py:559
  14.5 5.8 %collective-permute-done.2.rest_3_ = f32[128,256]{1,0:T(8,128)S(1)} collective-permute-done((f32[128,256]{1,0:T(8,128)S(1)}, f32[128,256]{1,0:T(8,128)S(1)}, u32[]{:S(2)}, u32[]{:S(2)}) %collective-permute-start.2) | collective-permute-done | bytes 131104 | tf_op jit(solution)/shard_map/ppermute | solution.py:559
  20.2 2.8 %collective-permute-done.5.rest_7_ = f32[128,256]{1,0:T(8,128)S(1)} collective-permute-done((f32[128,256]{1,0:T(8,128)S(1)}, f32[128,256]{1,0:T(8,128)S(1)}, u32[]{:S(2)}, u32[]{:S(2)}) %collective-permute-start.5) | collective-permute-done | bytes 131104 | tf_op jit(solution)/shard_map/ppermute | solution.py:559
  23.0 1.9 %shard_map.105 = f32[8,2,128,128]{3,2,1,0:T(8,128)} custom-call(bf16[2,768,512]{2,1,0:T(8,128)(2,1)S(1)} %copy-done.1, f32[128,256]{1,0:T(8,128)S(1)} %get-tuple-element.85.rest_0_, f32[128,256]{1,0:T(8,128)S(1)} %collective-permute-done.rest_1_, f32[128,256]{1,0:T(8,128)S(1)} %collective-permute-done.1.rest_2_, ...), custom_call_target="tpu_custom_call" | custom-call | bytes 3670016 | tf_op jit(solution)/shard_map/pallas_call | solution.py:525
  24.9 4.8 %all-to-all-start = ((f32[8,2,128,128]{3,2,1,0:T(8,128)}), f32[8,2,128,128]{3,2,1,0:T(8,128)}, u32[]{:S(2)}, u32[]{:S(2)}) async-start(f32[8,2,128,128]{3,2,1,0:T(8,128)} %shard_map.105), calls=%async_computation | async-start | bytes 2097152 | tf_op jit(solution)/shard_map/all_to_all | solution.py:602
  31.4 3.1 %collective-permute-done.6.rest_1_ = f32[128,256]{1,0:T(8,128)S(1)} collective-permute-done((f32[128,256]{1,0:T(8,128)S(1)}, f32[128,256]{1,0:T(8,128)S(1)}, u32[]{:S(2)}, u32[]{:S(2)}) %collective-permute-start.6) | collective-permute-done | bytes 131104 | tf_op jit(solution)/shard_map/ppermute | solution.py:559
  34.5 6.6 %collective-permute-done.7.rest_2_ = f32[128,256]{1,0:T(8,128)S(1)} collective-permute-done((f32[128,256]{1,0:T(8,128)S(1)}, f32[128,256]{1,0:T(8,128)S(1)}, u32[]{:S(2)}, u32[]{:S(2)}) %collective-permute-start.7) | collective-permute-done | bytes 131104 | tf_op jit(solution)/shard_map/ppermute | solution.py:559
  41.9 1.8 %all-to-all-done.data_h = f32[8,2,128,128]{3,2,1,0:T(8,128)} async-done(((f32[8,2,128,128]{3,2,1,0:T(8,128)}), f32[8,2,128,128]{3,2,1,0:T(8,128)}, u32[]{:S(2)}, u32[]{:S(2)}) %all-to-all-start) | async-done | bytes 1048608 | tf_op jit(solution)/shard_map/all_to_all | solution.py:602
  45.9 1.3 %collective-permute-start.10 = (f32[2,128,128]{2,1,0:T(8,128)S(1)}, f32[2,128,128]{2,1,0:T(8,128)S(1)}, u32[]{:S(2)}, u32[]{:S(2)}) collective-permute-start(f32[2,128,128]{2,1,0:T(8,128)S(1)} %get-tuple-element.104), channel_id=1, source_target_pairs={{0,2},{1,3},{2,0},{3,1},{4,6},{5,7},{6,4},{7,5},{8,10},{9,11},{10,... | collective-permute-start | bytes 393224 | tf_op jit(solution)/shard_map/ppermute | solution.py:594
  48.7 3.0 %shard_map.108.early = f32[4,2,256,128]{3,2,1,0:T(8,128)S(1)} custom-call(bf16[2,512,256]{2,1,0:T(8,128)(2,1)S(1)} %copy-done.2, f32[256,8]{1,0:T(8,128)S(1)} %copy-done.4, f32[8,2,128,128]{3,2,1,0:T(8,128)} %all-to-all-done.data_h), custom_call_target="tpu_custom_call" | custom-call | bytes 2629632 | tf_op jit(solution)/shard_map/pallas_call | solution.py:525
  52.1 1.4 %collective-permute-done.12.rest_2_ = f32[2,128,128]{2,1,0:T(8,128)S(1)} collective-permute-done((f32[2,128,128]{2,1,0:T(8,128)S(1)}, f32[2,128,128]{2,1,0:T(8,128)S(1)}, u32[]{:S(2)}, u32[]{:S(2)}) %collective-permute-start.12) | collective-permute-done | bytes 131104 | tf_op jit(solution)/shard_map/ppermute | solution.py:594
  53.5 3.4 %shard_map.109 = (f32[4,128,128]{2,1,0:T(8,128)S(1)}, f32[4,128,128]{2,1,0:T(8,128)S(1)}, f32[4,1,256,128]{3,2,1,0:T(8,128)S(1)}) custom-call(f32[5]{0:T(128)S(1)} %copy-done.6, f32[6]{0:T(128)S(1)} %copy-done.7, bf16[2,512,256]{2,1,0:T(8,128)(2,1)S(1)} %copy-done.2, f32[256,8]{1,0:T(8,128)S(1)} %copy-done.4, f32[4,2,256,128]{3,2,1,0:T(8,128)S(1)} %shard_map.108.early, ...), custom_call_target="tpu_custom_call" | custom-call | bytes 3547180 | tf_op jit(solution)/shard_map/pallas_call | solution.py:525
  57.0 2.5 %collective-permute-start.13 = (f32[4,128,128]{2,1,0:T(8,128)S(1)}, f32[4,128,128]{2,1,0:T(8,128)S(1)}, u32[]{:S(2)}, u32[]{:S(2)}) collective-permute-start(f32[4,128,128]{2,1,0:T(8,128)S(1)} %get-tuple-element.108), channel_id=1, source_target_pairs={{0,1},{1,0},{2,3},{3,2},{4,5},{5,4},{6,7},{7,6},{8,9},{9,8},{10,11... | collective-permute-start | bytes 786440 | tf_op jit(solution)/shard_map/ppermute | solution.py:590
  61.9 1.5 %collective-permute-start.16 = (f32[2,128,128]{2,1,0:T(8,128)S(1)}, f32[2,128,128]{2,1,0:T(8,128)S(1)}, u32[]{:S(2)}, u32[]{:S(2)}) collective-permute-start(f32[2,128,128]{2,1,0:T(8,128)S(1)} %get-tuple-element.116), channel_id=1, source_target_pairs={{0,6},{1,7},{2,4},{3,5},{4,2},{5,3},{6,0},{7,1},{8,14},{9,15},{10,... | collective-permute-start | bytes 393224 | tf_op jit(solution)/shard_map/ppermute | solution.py:594
  63.4 4.6 %shard_map.111 = f32[8,2,128,128]{3,2,1,0:T(8,128)} custom-call(f32[5]{0:T(128)S(1)} %copy-done.6, f32[6]{0:T(128)S(1)} %copy-done.7, bf16[2,512,256]{2,1,0:T(8,128)(2,1)S(1)} %copy-done.2, f32[256,8]{1,0:T(8,128)S(1)} %copy-done.4, f32[4,2,256,128]{3,2,1,0:T(8,128)S(1)} %shard_map.108.early, f32[4,1,256,128]{3,2,1,0:T(8,128)S(1)} %get-tuple-element.113.late), custom_call_target="tpu_custom_call" | custom-call | bytes 3153964 | tf_op jit(solution)/shard_map/pallas_call | solution.py:525
  69.6 6.0 %all-to-all-start.1 = ((f32[8,2,128,128]{3,2,1,0:T(8,128)}), f32[8,2,128,128]{3,2,1,0:T(8,128)S(1)}, u32[]{:S(2)}, u32[]{:S(2)}) async-start(f32[8,2,128,128]{3,2,1,0:T(8,128)} %shard_map.111), calls=%async_computation.1 | async-start | bytes 2097152 | tf_op jit(solution)/shard_map/all_to_all | solution.py:628
  76.7 1.4 %collective-permute-start.22 = (f32[128,256]{1,0:T(8,128)S(1)}, f32[128,256]{1,0:T(8,128)S(1)}, u32[]{:S(2)}, u32[]{:S(2)}) collective-permute-start(f32[128,256]{1,0:T(8,128)S(1)} %get-tuple-element.129), channel_id=1, source_target_pairs={{0,24},{8,0},{16,8},{24,16},{1,25},{9,1},{17,9},{25,17},{2,26},{10... | collective-permute-start | bytes 393224 | tf_op jit(solution)/shard_map/ppermute | solution.py:559
  78.1 11.4 %all-to-all-done.1.data = f32[8,2,128,128]{3,2,1,0:T(8,128)S(1)} async-done(((f32[8,2,128,128]{3,2,1,0:T(8,128)}), f32[8,2,128,128]{3,2,1,0:T(8,128)S(1)}, u32[]{:S(2)}, u32[]{:S(2)}) %all-to-all-start.1) | async-done | bytes 1048608 | tf_op jit(solution)/shard_map/all_to_all | solution.py:628
  91.5 1.4 %collective-permute-start.19 = (f32[128,256]{1,0:T(8,128)S(1)}, f32[128,256]{1,0:T(8,128)S(1)}, u32[]{:S(2)}, u32[]{:S(2)}) collective-permute-start(f32[128,256]{1,0:T(8,128)S(1)} %get-tuple-element.125), channel_id=1, source_target_pairs={{0,24},{8,0},{16,8},{24,16},{1,25},{9,1},{17,9},{25,17},{2,26},{10... | collective-permute-start | bytes 393224 | tf_op jit(solution)/shard_map/ppermute | solution.py:559
  92.9 2.1 %collective-permute-start.23 = (f32[128,256]{1,0:T(8,128)S(1)}, f32[128,256]{1,0:T(8,128)S(1)}, u32[]{:S(2)}, u32[]{:S(2)}) collective-permute-start(f32[128,256]{1,0:T(8,128)S(1)} %get-tuple-element.131), channel_id=1, source_target_pairs={{8,16},{16,24},{9,17},{17,25},{10,18},{18,26},{11,19},{19,27},{12,... | collective-permute-start | bytes 393224 | tf_op jit(solution)/shard_map/ppermute | solution.py:559
  95.1 2.5 %collective-permute-start.24 = (f32[128,256]{1,0:T(8,128)S(1)}, f32[128,256]{1,0:T(8,128)S(1)}, u32[]{:S(2)}, u32[]{:S(2)}) collective-permute-start(f32[128,256]{1,0:T(8,128)S(1)} %get-tuple-element.132), channel_id=1, source_target_pairs={{8,24},{16,0},{9,25},{17,1},{10,26},{18,2},{11,27},{19,3},{12,28},... | collective-permute-start | bytes 393224 | tf_op jit(solution)/shard_map/ppermute | solution.py:559
  97.5 1.9 %collective-permute-start.25 = (f32[128,256]{1,0:T(8,128)S(1)}, f32[128,256]{1,0:T(8,128)S(1)}, u32[]{:S(2)}, u32[]{:S(2)}) collective-permute-start(f32[128,256]{1,0:T(8,128)S(1)} %get-tuple-element.133), channel_id=1, source_target_pairs={{8,0},{16,8},{9,1},{17,9},{10,2},{18,10},{11,3},{19,11},{12,4},{20... | collective-permute-start | bytes 393224 | tf_op jit(solution)/shard_map/ppermute | solution.py:559
  99.5 2.3 %collective-permute-done.18.rest_2_ = f32[128,256]{1,0:T(8,128)S(1)} collective-permute-done((f32[128,256]{1,0:T(8,128)S(1)}, f32[128,256]{1,0:T(8,128)S(1)}, u32[]{:S(2)}, u32[]{:S(2)}) %collective-permute-start.18) | collective-permute-done | bytes 131104 | tf_op jit(solution)/shard_map/ppermute | solution.py:559
  101.8 2.0 %collective-permute-done.19.rest_3_ = f32[128,256]{1,0:T(8,128)S(1)} collective-permute-done((f32[128,256]{1,0:T(8,128)S(1)}, f32[128,256]{1,0:T(8,128)S(1)}, u32[]{:S(2)}, u32[]{:S(2)}) %collective-permute-start.19) | collective-permute-done | bytes 131104 | tf_op jit(solution)/shard_map/ppermute | solution.py:559
  103.8 2.1 %shard_map.114 = (f32[6,2,128,256]{3,2,1,0:T(8,128)}, f32[6,2,128,256]{3,2,1,0:T(8,128)}) custom-call(f32[5]{0:T(128)S(1)} %copy-done.6, f32[6]{0:T(128)S(1)} %copy-done.7, s32[2,128,256]{2,1,0:T(8,128)S(1)} %copy-done.3, s32[2,8,16]{2,1,0:T(8,128)S(1)} %copy-done.5, f32[128,256]{1,0:T(8,128)S(1)} %get-tuple-element.122.rest_0_, ...), custom_call_target="tpu_custom_call" | custom-call | bytes 4457516 | tf_op jit(solution)/shard_map/pallas_call | solution.py:525
  106.0 1.4 %collective-permute-done.24.rest_10_ = f32[128,256]{1,0:T(8,128)S(1)} collective-permute-done((f32[128,256]{1,0:T(8,128)S(1)}, f32[128,256]{1,0:T(8,128)S(1)}, u32[]{:S(2)}, u32[]{:S(2)}) %collective-permute-start.24) | collective-permute-done | bytes 131104 | tf_op jit(solution)/shard_map/ppermute | solution.py:559
  107.4 2.1 %collective-permute-done.25.rest_11_ = f32[128,256]{1,0:T(8,128)S(1)} collective-permute-done((f32[128,256]{1,0:T(8,128)S(1)}, f32[128,256]{1,0:T(8,128)S(1)}, u32[]{:S(2)}, u32[]{:S(2)}) %collective-permute-start.25) | collective-permute-done | bytes 131104 | tf_op jit(solution)/shard_map/ppermute | solution.py:559
  109.5 1.9 %shard_map.115 = (f32[6,2,128,256]{3,2,1,0:T(8,128)}, f32[6,2,128,256]{3,2,1,0:T(8,128)}) custom-call(f32[5]{0:T(128)S(1)} %copy-done.6, f32[6]{0:T(128)S(1)} %copy-done.7, s32[2,128,256]{2,1,0:T(8,128)S(1)} %copy-done.3, s32[2,8,16]{2,1,0:T(8,128)S(1)} %copy-done.5, ...), custom_call_target="tpu_custom_call", output_to_operand_aliasing={{0}: (16, {}), {1}: (17, {})} | custom-call | bytes 8127532 | tf_op jit(solution)/shard_map/pallas_call | solution.py:525
  (52 shorter events, 17.5 us)
Async XLA Ops:
  0.6 22.4 %copy-start.1 = (bf16[2,768,512]{2,1,0:T(8,128)(2,1)S(1)}, bf16[2,768,512]{2,1,0:T(8,128)(2,1)}, u32[]{:S(2)}) copy-start(bf16[2,768,512]{2,1,0:T(8,128)(2,1)} %constant.8.clone.table) | copy-start | bytes 4718596
  2.7 7.1 %collective-permute-start = (f32[128,256]{1,0:T(8,128)S(1)}, f32[128,256]{1,0:T(8,128)S(1)}, u32[]{:S(2)}, u32[]{:S(2)}) collective-permute-start(f32[128,256]{1,0:T(8,128)S(1)} %get-tuple-element.70), channel_id=1, source_target_pairs={{0,8},{8,16},{16,24},{24,0},{1,9},{9,17},{17,25},{25,1},{2,10},{10... | collective-permute-start | bytes 393224 | tf_op jit(solution)/shard_map/ppermute | solution.py:559
  4.0 10.4 %collective-permute-start.1 = (f32[128,256]{1,0:T(8,128)S(1)}, f32[128,256]{1,0:T(8,128)S(1)}, u32[]{:S(2)}, u32[]{:S(2)}) collective-permute-start(f32[128,256]{1,0:T(8,128)S(1)} %get-tuple-element.71), channel_id=1, source_target_pairs={{0,16},{8,24},{16,0},{24,8},{1,17},{9,25},{17,1},{25,9},{2,18},{10... | collective-permute-start | bytes 393224 | tf_op jit(solution)/shard_map/ppermute | solution.py:559
  5.1 15.1 %collective-permute-start.2 = (f32[128,256]{1,0:T(8,128)S(1)}, f32[128,256]{1,0:T(8,128)S(1)}, u32[]{:S(2)}, u32[]{:S(2)}) collective-permute-start(f32[128,256]{1,0:T(8,128)S(1)} %get-tuple-element.72), channel_id=1, source_target_pairs={{0,24},{8,0},{16,8},{24,16},{1,25},{9,1},{17,9},{25,17},{2,26},{10... | collective-permute-start | bytes 393224 | tf_op jit(solution)/shard_map/ppermute | solution.py:559
  6.5 13.7 %collective-permute-start.3 = (f32[128,256]{1,0:T(8,128)S(1)}, f32[128,256]{1,0:T(8,128)S(1)}, u32[]{:S(2)}, u32[]{:S(2)}) collective-permute-start(f32[128,256]{1,0:T(8,128)S(1)} %get-tuple-element.74), channel_id=1, source_target_pairs={{0,8},{8,16},{1,9},{9,17},{2,10},{10,18},{3,11},{11,19},{4,12},{12... | collective-permute-start | bytes 393224 | tf_op jit(solution)/shard_map/ppermute | solution.py:559
  8.5 11.8 %collective-permute-start.4 = (f32[128,256]{1,0:T(8,128)S(1)}, f32[128,256]{1,0:T(8,128)S(1)}, u32[]{:S(2)}, u32[]{:S(2)}) collective-permute-start(f32[128,256]{1,0:T(8,128)S(1)} %get-tuple-element.75), channel_id=1, source_target_pairs={{0,16},{24,8},{1,17},{25,9},{2,18},{26,10},{3,19},{27,11},{4,20},{... | collective-permute-start | bytes 393224 | tf_op jit(solution)/shard_map/ppermute | solution.py:559
  9.8 13.2 %collective-permute-start.5 = (f32[128,256]{1,0:T(8,128)S(1)}, f32[128,256]{1,0:T(8,128)S(1)}, u32[]{:S(2)}, u32[]{:S(2)}) collective-permute-start(f32[128,256]{1,0:T(8,128)S(1)} %get-tuple-element.76), channel_id=1, source_target_pairs={{16,8},{24,16},{17,9},{25,17},{18,10},{26,18},{19,11},{27,19},{20,... | collective-permute-start | bytes 393224 | tf_op jit(solution)/shard_map/ppermute | solution.py:559
  24.9 18.7 %all-to-all-start = ((f32[8,2,128,128]{3,2,1,0:T(8,128)}), f32[8,2,128,128]{3,2,1,0:T(8,128)}, u32[]{:S(2)}, u32[]{:S(2)}) async-start(f32[8,2,128,128]{3,2,1,0:T(8,128)} %shard_map.105), calls=%async_computation | async-start | bytes 2097152 | tf_op jit(solution)/shard_map/all_to_all | solution.py:602
  29.7 19.0 %copy-start.4 = (f32[256,8]{1,0:T(8,128)S(1)}, f32[256,8]{1,0:T(8,128)}, u32[]{:S(2)}) copy-start(f32[256,8]{1,0:T(8,128)} %constant.10.clone.twiddles) | copy-start | bytes 24580
  29.7 4.8 %collective-permute-start.6 = (f32[128,256]{1,0:T(8,128)S(1)}, f32[128,256]{1,0:T(8,128)S(1)}, u32[]{:S(2)}, u32[]{:S(2)}) collective-permute-start(f32[128,256]{1,0:T(8,128)S(1)} %get-tuple-element.82), channel_id=1, source_target_pairs={{0,8},{8,16},{16,24},{24,0},{1,9},{9,17},{17,25},{25,1},{2,10},{10... | collective-permute-start | bytes 393224 | tf_op jit(solution)/shard_map/ppermute | solution.py:559
  30.2 10.9 %collective-permute-start.7 = (f32[128,256]{1,0:T(8,128)S(1)}, f32[128,256]{1,0:T(8,128)S(1)}, u32[]{:S(2)}, u32[]{:S(2)}) collective-permute-start(f32[128,256]{1,0:T(8,128)S(1)} %get-tuple-element.83), channel_id=1, source_target_pairs={{0,16},{8,24},{16,0},{24,8},{1,17},{9,25},{17,1},{25,9},{2,18},{10... | collective-permute-start | bytes 393224 | tf_op jit(solution)/shard_map/ppermute | solution.py:559
  30.2 11.7 %collective-permute-start.8 = (f32[128,256]{1,0:T(8,128)S(1)}, f32[128,256]{1,0:T(8,128)S(1)}, u32[]{:S(2)}, u32[]{:S(2)}) collective-permute-start(f32[128,256]{1,0:T(8,128)S(1)} %get-tuple-element.84), channel_id=1, source_target_pairs={{0,24},{8,0},{16,8},{24,16},{1,25},{9,1},{17,9},{25,17},{2,26},{10... | collective-permute-start | bytes 393224 | tf_op jit(solution)/shard_map/ppermute | solution.py:559
  44.2 1.7 %collective-permute-start.9 = (f32[4,128,128]{2,1,0:T(8,128)S(1)}, f32[4,128,128]{2,1,0:T(8,128)S(1)}, u32[]{:S(2)}, u32[]{:S(2)}) collective-permute-start(f32[4,128,128]{2,1,0:T(8,128)S(1)} %get-tuple-element.98), channel_id=1, source_target_pairs={{0,1},{1,0},{2,3},{3,2},{4,5},{5,4},{6,7},{7,6},{8,9},{9,8},{10,11... | collective-permute-start | bytes 786440 | tf_op jit(solution)/shard_map/ppermute | solution.py:590
  45.9 5.7 %collective-permute-start.10 = (f32[2,128,128]{2,1,0:T(8,128)S(1)}, f32[2,128,128]{2,1,0:T(8,128)S(1)}, u32[]{:S(2)}, u32[]{:S(2)}) collective-permute-start(f32[2,128,128]{2,1,0:T(8,128)S(1)} %get-tuple-element.104), channel_id=1, source_target_pairs={{0,2},{1,3},{2,0},{3,1},{4,6},{5,7},{6,4},{7,5},{8,10},{9,11},{10,... | collective-permute-start | bytes 393224 | tf_op jit(solution)/shard_map/ppermute | solution.py:594
  47.3 4.8 %collective-permute-start.11 = (f32[2,128,128]{2,1,0:T(8,128)S(1)}, f32[2,128,128]{2,1,0:T(8,128)S(1)}, u32[]{:S(2)}, u32[]{:S(2)}) collective-permute-start(f32[2,128,128]{2,1,0:T(8,128)S(1)} %get-tuple-element.105), channel_id=1, source_target_pairs={{0,4},{1,5},{2,6},{3,7},{4,0},{5,1},{6,2},{7,3},{8,12},{9,13},{10,... | collective-permute-start | bytes 393224 | tf_op jit(solution)/shard_map/ppermute | solution.py:594
  47.5 6.0 %collective-permute-start.12 = (f32[2,128,128]{2,1,0:T(8,128)S(1)}, f32[2,128,128]{2,1,0:T(8,128)S(1)}, u32[]{:S(2)}, u32[]{:S(2)}) collective-permute-start(f32[2,128,128]{2,1,0:T(8,128)S(1)} %get-tuple-element.106), channel_id=1, source_target_pairs={{0,6},{1,7},{2,4},{3,5},{4,2},{5,3},{6,0},{7,1},{8,14},{9,15},{10,... | collective-permute-start | bytes 393224 | tf_op jit(solution)/shard_map/ppermute | solution.py:594
  57.0 3.7 %collective-permute-start.13 = (f32[4,128,128]{2,1,0:T(8,128)S(1)}, f32[4,128,128]{2,1,0:T(8,128)S(1)}, u32[]{:S(2)}, u32[]{:S(2)}) collective-permute-start(f32[4,128,128]{2,1,0:T(8,128)S(1)} %get-tuple-element.108), channel_id=1, source_target_pairs={{0,1},{1,0},{2,3},{3,2},{4,5},{5,4},{6,7},{7,6},{8,9},{9,8},{10,11... | collective-permute-start | bytes 786440 | tf_op jit(solution)/shard_map/ppermute | solution.py:590
  60.7 7.3 %collective-permute-start.14 = (f32[2,128,128]{2,1,0:T(8,128)S(1)}, f32[2,128,128]{2,1,0:T(8,128)S(1)}, u32[]{:S(2)}, u32[]{:S(2)}) collective-permute-start(f32[2,128,128]{2,1,0:T(8,128)S(1)} %get-tuple-element.114), channel_id=1, source_target_pairs={{0,2},{1,3},{2,0},{3,1},{4,6},{5,7},{6,4},{7,5},{8,10},{9,11},{10,... | collective-permute-start | bytes 393224 | tf_op jit(solution)/shard_map/ppermute | solution.py:594
  61.0 7.0 %collective-permute-start.15 = (f32[2,128,128]{2,1,0:T(8,128)S(1)}, f32[2,128,128]{2,1,0:T(8,128)S(1)}, u32[]{:S(2)}, u32[]{:S(2)}) collective-permute-start(f32[2,128,128]{2,1,0:T(8,128)S(1)} %get-tuple-element.115), channel_id=1, source_target_pairs={{0,4},{1,5},{2,6},{3,7},{4,0},{5,1},{6,2},{7,3},{8,12},{9,13},{10,... | collective-permute-start | bytes 393224 | tf_op jit(solution)/shard_map/ppermute | solution.py:594
  61.9 6.4 %collective-permute-start.16 = (f32[2,128,128]{2,1,0:T(8,128)S(1)}, f32[2,128,128]{2,1,0:T(8,128)S(1)}, u32[]{:S(2)}, u32[]{:S(2)}) collective-permute-start(f32[2,128,128]{2,1,0:T(8,128)S(1)} %get-tuple-element.116), channel_id=1, source_target_pairs={{0,6},{1,7},{2,4},{3,5},{4,2},{5,3},{6,0},{7,1},{8,14},{9,15},{10,... | collective-permute-start | bytes 393224 | tf_op jit(solution)/shard_map/ppermute | solution.py:594
  69.6 19.8 %all-to-all-start.1 = ((f32[8,2,128,128]{3,2,1,0:T(8,128)}), f32[8,2,128,128]{3,2,1,0:T(8,128)S(1)}, u32[]{:S(2)}, u32[]{:S(2)}) async-start(f32[8,2,128,128]{3,2,1,0:T(8,128)} %shard_map.111), calls=%async_computation.1 | async-start | bytes 2097152 | tf_op jit(solution)/shard_map/all_to_all | solution.py:628
  75.6 28.2 %copy-start.3 = (s32[2,128,256]{2,1,0:T(8,128)S(1)}, s32[2,128,256]{2,1,0:T(8,128)}, u32[]{:S(2)}) copy-start(s32[2,128,256]{2,1,0:T(8,128)} %labels.3) | copy-start | bytes 786436
  75.6 28.2 %copy-start.5 = (s32[2,8,16]{2,1,0:T(8,128)S(1)}, s32[2,8,16]{2,1,0:T(8,128)}, u32[]{:S(2)}) copy-start(s32[2,8,16]{2,1,0:T(8,128)} %normals.3) | copy-start | bytes 3076
  75.6 15.9 %collective-permute-start.20 = (f32[128,256]{1,0:T(8,128)}, f32[128,256]{1,0:T(8,128)S(1)}, u32[]{:S(2)}, u32[]{:S(2)}) collective-permute-start(f32[128,256]{1,0:T(8,128)} %get-tuple-element.127), channel_id=1, source_target_pairs={{0,8},{8,16},{16,24},{24,0},{1,9},{9,17},{17,25},{25,1},{2,10},{10... | collective-permute-start | bytes 393224 | tf_op jit(solution)/shard_map/ppermute | solution.py:559
  76.1 16.9 %collective-permute-start.21 = (f32[128,256]{1,0:T(8,128)}, f32[128,256]{1,0:T(8,128)S(1)}, u32[]{:S(2)}, u32[]{:S(2)}) collective-permute-start(f32[128,256]{1,0:T(8,128)} %get-tuple-element.128), channel_id=1, source_target_pairs={{0,16},{8,24},{16,0},{24,8},{1,17},{9,25},{17,1},{25,9},{2,18},{10... | collective-permute-start | bytes 393224 | tf_op jit(solution)/shard_map/ppermute | solution.py:559
  76.7 18.3 %collective-permute-start.22 = (f32[128,256]{1,0:T(8,128)S(1)}, f32[128,256]{1,0:T(8,128)S(1)}, u32[]{:S(2)}, u32[]{:S(2)}) collective-permute-start(f32[128,256]{1,0:T(8,128)S(1)} %get-tuple-element.129), channel_id=1, source_target_pairs={{0,24},{8,0},{16,8},{24,16},{1,25},{9,1},{17,9},{25,17},{2,26},{10... | collective-permute-start | bytes 393224 | tf_op jit(solution)/shard_map/ppermute | solution.py:559
  90.4 7.1 %collective-permute-start.17 = (f32[128,256]{1,0:T(8,128)S(1)}, f32[128,256]{1,0:T(8,128)S(1)}, u32[]{:S(2)}, u32[]{:S(2)}) collective-permute-start(f32[128,256]{1,0:T(8,128)S(1)} %get-tuple-element.123), channel_id=1, source_target_pairs={{0,8},{8,16},{16,24},{24,0},{1,9},{9,17},{17,25},{25,1},{2,10},{10... | collective-permute-start | bytes 393224 | tf_op jit(solution)/shard_map/ppermute | solution.py:559
  90.9 10.9 %collective-permute-start.18 = (f32[128,256]{1,0:T(8,128)S(1)}, f32[128,256]{1,0:T(8,128)S(1)}, u32[]{:S(2)}, u32[]{:S(2)}) collective-permute-start(f32[128,256]{1,0:T(8,128)S(1)} %get-tuple-element.124), channel_id=1, source_target_pairs={{0,16},{8,24},{16,0},{24,8},{1,17},{9,25},{17,1},{25,9},{2,18},{10... | collective-permute-start | bytes 393224 | tf_op jit(solution)/shard_map/ppermute | solution.py:559
  91.5 12.3 %collective-permute-start.19 = (f32[128,256]{1,0:T(8,128)S(1)}, f32[128,256]{1,0:T(8,128)S(1)}, u32[]{:S(2)}, u32[]{:S(2)}) collective-permute-start(f32[128,256]{1,0:T(8,128)S(1)} %get-tuple-element.125), channel_id=1, source_target_pairs={{0,24},{8,0},{16,8},{24,16},{1,25},{9,1},{17,9},{25,17},{2,26},{10... | collective-permute-start | bytes 393224 | tf_op jit(solution)/shard_map/ppermute | solution.py:559
  92.9 13.1 %collective-permute-start.23 = (f32[128,256]{1,0:T(8,128)S(1)}, f32[128,256]{1,0:T(8,128)S(1)}, u32[]{:S(2)}, u32[]{:S(2)}) collective-permute-start(f32[128,256]{1,0:T(8,128)S(1)} %get-tuple-element.131), channel_id=1, source_target_pairs={{8,16},{16,24},{9,17},{17,25},{10,18},{18,26},{11,19},{19,27},{12,... | collective-permute-start | bytes 393224 | tf_op jit(solution)/shard_map/ppermute | solution.py:559
  95.1 12.4 %collective-permute-start.24 = (f32[128,256]{1,0:T(8,128)S(1)}, f32[128,256]{1,0:T(8,128)S(1)}, u32[]{:S(2)}, u32[]{:S(2)}) collective-permute-start(f32[128,256]{1,0:T(8,128)S(1)} %get-tuple-element.132), channel_id=1, source_target_pairs={{8,24},{16,0},{9,25},{17,1},{10,26},{18,2},{11,27},{19,3},{12,28},... | collective-permute-start | bytes 393224 | tf_op jit(solution)/shard_map/ppermute | solution.py:559
  97.5 12.0 %collective-permute-start.25 = (f32[128,256]{1,0:T(8,128)S(1)}, f32[128,256]{1,0:T(8,128)S(1)}, u32[]{:S(2)}, u32[]{:S(2)}) collective-permute-start(f32[128,256]{1,0:T(8,128)S(1)} %get-tuple-element.133), channel_id=1, source_target_pairs={{8,0},{16,8},{9,1},{17,9},{10,2},{18,10},{11,3},{19,11},{12,4},{20... | collective-permute-start | bytes 393224 | tf_op jit(solution)/shard_map/ppermute | solution.py:559
  (4 other events, 41.9 us)

commit v7 on v6

--- a/solution.py
+++ b/solution.py
@@ -192,8 +192,8 @@
     chip, core = mine // 2, lax.rem(mine, 2)
     for step in range(own.shape[0]):
         there = 2 * lax.bitwise_xor(chip, step)
-        own[step] = blocks[there + core, 0]
-        swapped[step] = blocks[there + 1 - core, 0]
+        own[step] = blocks[there + core]
+        swapped[step] = blocks[there + 1 - core]
 
 
 def collect(own, got, moved, blocks):
@@ -201,8 +201,8 @@
     chip, core = mine // 2, lax.rem(mine, 2)
     for step in range(own.shape[0]):
         there = 2 * lax.bitwise_xor(chip, step)
-        blocks[there + core, 0] = own[0] if step == 0 else moved[step - 1][0]
-        blocks[there + 1 - core, 0] = got[0] if step == 0 else moved[step - 1][1]
+        blocks[there + core] = own[0] if step == 0 else moved[step - 1][0]
+        blocks[there + 1 - core] = got[0] if step == 0 else moved[step - 1][1]
 
 
 def merge_kernel(own, got, *outs):
@@ -429,9 +429,10 @@
     return load
 
 
-def early_inverse_kernel(x_cells, z_cells, chunks, moduli, mean, table, twiddles, early, late, out, new):
+def early_inverse_kernel(x_cells, z_cells, chunks, moduli, mean, table, twiddles, early, late, own, swapped, out, new):
     green_rows(x_cells, z_cells, chunks[0], moduli, mean, loader(chunks, early, late), new)
     x_inverse(new[...], table, twiddles, holds_edge(out.shape[3] // 2, z_cells), out)
+    deal(out, own, swapped)
 
 
 def late_kernel(x_cells, z_cells, chunks, moduli, mean, table, twiddles, early, own_in, got, *rest):
@@ -583,12 +584,13 @@
     early, late = CHUNKS
     size = len(early)
     grid = (x_devices, size, cells_x, lanes)
-    tile = (chips, cells_x, lanes)
+    tile = (chips, 1, cells_x, lanes)
+    tile_early = (chips, size, cells_x, lanes)
     tiles = pltpu.VMEM((x_devices, 1, cells_x, lanes), F32)
 
     def exchange(own, swapped, after):
         got = lax.ppermute(swapped, "gx", [(k, k ^ 1) for k in range(x_devices)])
-        merged = call(merge_kernel, [(2, cells_x, lanes)] * (chips - 1), [], (own, got), 8)
+        merged = call(merge_kernel, [(2, *own.shape[1:])] * (chips - 1), [], (own, got), 8)
         merged, after = lax.optimization_barrier((merged, after))
         moved = [
             lax.ppermute(block, "gx", [(k, k ^ (2 * step)) for k in range(x_devices)])
@@ -615,19 +617,20 @@
         smem=2,
     )
     last, late_spectrum = exchange(own, swapped, late_spectrum)
-    (rest,) = call(
+    rest = call(
         functools.partial(early_inverse_kernel, x_total, z_total, CHUNKS),
-        [grid],
-        [pltpu.VMEM((quarter, 5 * size * lanes), F32)],
+        [tile_early] * 2,
+        [pltpu.VMEM(grid, F32), pltpu.VMEM((quarter, 5 * size * lanes), F32)],
         (moduli, mean_strain, *x_tab, spectrum, late_spectrum),
         24,
         smem=2,
     )
+    rest, last = lax.optimization_barrier((rest, last))
     blocks = call(z_inverse_collect_kernel, [block] * parts, [held(1), tiles], (z_inv, *last), 16)
-    rest, blocks = lax.optimization_barrier((rest, list(blocks)))
-    rest = lax.all_to_all(rest, "gx", 0, 0, tiled=True)
+    rest, blocks = exchange(*rest, list(blocks))
     arrived = {late[0]: travel(late[0], blocks, False)}
-    blocks = call(z_inverse_kernel, [block] * (size * parts), [held(size)], (z_inv, rest), 16)
+    scratch = [held(size), pltpu.VMEM(grid, F32)]
+    blocks = call(z_inverse_collect_kernel, [block] * (size * parts), scratch, (z_inv, *rest), 16)
     for slot, f in enumerate(early):
         arrived[f] = travel(f, blocks[slot * parts : (slot + 1) * parts], False)
     full = (6, sections, cells_x, cells_z)

time: 112 us -> 109 us (0.973)
  starting transfers between devices: 40.8 us -> 37.8 us
  Pallas kernels: 21.8 us -> 20.3 us
    all_to_all x1 -> x0, waiting for transfers between devices: 11.4 us -> none  [shards(): rest = lax.all_to_all(rest, 'gx', 0, 0, tiled=True)]
    ppermute x6 -> x9, waiting for transfers between devices: 2.19 us -> 12.9 us  [exchange(): lax.ppermute(block, 'gx', [(k, k ^ 2 * step) for k in range(x_devices)])]
    all_to_all x1 -> x0, starting transfers between devices: 6.01 us -> none  [shards(): rest = lax.all_to_all(rest, 'gx', 0, 0, tiled=True)]
    ppermute x6 -> x9, starting transfers between devices: 5.43 us -> 8.14 us  [exchange(): lax.ppermute(block, 'gx', [(k, k ^ 2 * step) for k in range(x_devices)])]
    pallas_call x12 -> x13, Pallas kernels: 21.8 us -> 20.3 us  [call(): pl.pallas_call(kernel, out_shape=[pltpu.HBM(o, F32) if k in hbm_out else...]
    ppermute x2 -> x3, starting transfers between devices: 3.04 us -> 4.43 us  [exchange(): got = lax.ppermute(swapped, 'gx', [(k, k ^ 1) for k in range(x_devices)])]
    ppermute x18, starting transfers between devices: 21.5 us -> 20.4 us  [travel(): moved.append(lax.ppermute(blocks[step], 'gz', way))]
    ppermute x2 -> x3, waiting for transfers between devices: 2.32 us -> 3.27 us  [exchange(): got = lax.ppermute(swapped, 'gx', [(k, k ^ 1) for k in range(x_devices)])]
  transfers between devices with their start and end apart: 28 -> 31, of which waited for: 17 -> 18; matrix products, arithmetic and copies ran while one was open for 0% -> 0% of each run, Pallas kernels for 10% -> 10%
where the time goes in v7:
time: 109 us; the launch traced here: 108 us
  waiting for transfers between devices  48.5 us (44%)
  starting transfers between devices  37.8 us (35%)
  Pallas kernels  20.3 us (19%)
    ppermute x18, waiting for transfers between devices, travel(): moved.append(lax.ppermute(blocks[step], 'gz', way))  30.5 us
    ppermute x18, starting transfers between devices, travel(): moved.append(lax.ppermute(blocks[step], 'gz', way))  20.4 us
    pallas_call x13, Pallas kernels, call(): pl.pallas_call(kernel, out_shape=[pltpu.HBM(o, F32) if k in hbm_out else...  20.3 us
    ppermute x9, waiting for transfers between devices, exchange(): lax.ppermute(block, 'gx', [(k, k ^ 2 * step) for k in range(x_devices)])  12.9 us
    ppermute x9, starting transfers between devices, exchange(): lax.ppermute(block, 'gx', [(k, k ^ 2 * step) for k in range(x_devices)])  8.14 us
    all_to_all x1, starting transfers between devices, shards(): rows = lax.all_to_all(rows, 'gx', 0, 0, tiled=True)  4.8 us
    ppermute x3, starting transfers between devices, exchange(): got = lax.ppermute(swapped, 'gx', [(k, k ^ 1) for k in range(x_devices)])  4.43 us
    ppermute x3, waiting for transfers between devices, exchange(): got = lax.ppermute(swapped, 'gx', [(k, k ^ 1) for k in range(x_devices)])  3.27 us
  transfers between devices with their start and end apart: 31, of which 18 were waited for; matrix products, arithmetic and copies ran while one was open for 0% of the time, Pallas kernels for 10%

profile of v7, /device:TPU:11, one launch (start us, length us, event | category | flops | bytes accessed | tf_op | source)
XLA Modules:
  0.0 107.5 jit_solution(495428115917171980)
XLA Ops:
  0.6 2.0 %shard_map.104 = (f32[128,256]{1,0:T(8,128)S(1)}, f32[128,256]{1,0:T(8,128)S(1)}, f32[128,256]{1,0:T(8,128)S(1)}, f32[128,256]{1,0:T(8,128)S(1)}, f32[128,256]{1...) custom-call(f32[5]{0:T(128)} %moduli.7, ...), custom_call_target="tpu_custom_call" | custom-call | bytes 3408916 | tf_op jit(solution)/shard_map/pallas_call | solution.py:526
  2.7 1.4 %collective-permute-start = (f32[128,256]{1,0:T(8,128)S(1)}, f32[128,256]{1,0:T(8,128)S(1)}, u32[]{:S(2)}, u32[]{:S(2)}) collective-permute-start(f32[128,256]{1,0:T(8,128)S(1)} %get-tuple-element.84), channel_id=1, source_target_pairs={{0,8},{8,16},{16,24},{24,0},{1,9},{9,17},{17,25},{25,1},{2,10},{10... | collective-permute-start | bytes 393224 | tf_op jit(solution)/shard_map/ppermute | solution.py:560
  5.1 1.4 %collective-permute-start.2 = (f32[128,256]{1,0:T(8,128)S(1)}, f32[128,256]{1,0:T(8,128)S(1)}, u32[]{:S(2)}, u32[]{:S(2)}) collective-permute-start(f32[128,256]{1,0:T(8,128)S(1)} %get-tuple-element.86), channel_id=1, source_target_pairs={{0,24},{8,0},{16,8},{24,16},{1,25},{9,1},{17,9},{25,17},{2,26},{10... | collective-permute-start | bytes 393224 | tf_op jit(solution)/shard_map/ppermute | solution.py:560
  6.5 2.0 %collective-permute-start.3 = (f32[128,256]{1,0:T(8,128)S(1)}, f32[128,256]{1,0:T(8,128)S(1)}, u32[]{:S(2)}, u32[]{:S(2)}) collective-permute-start(f32[128,256]{1,0:T(8,128)S(1)} %get-tuple-element.88), channel_id=1, source_target_pairs={{0,8},{8,16},{1,9},{9,17},{2,10},{10,18},{3,11},{11,19},{4,12},{12... | collective-permute-start | bytes 393224 | tf_op jit(solution)/shard_map/ppermute | solution.py:560
  8.5 1.3 %collective-permute-start.4 = (f32[128,256]{1,0:T(8,128)S(1)}, f32[128,256]{1,0:T(8,128)S(1)}, u32[]{:S(2)}, u32[]{:S(2)}) collective-permute-start(f32[128,256]{1,0:T(8,128)S(1)} %get-tuple-element.89), channel_id=1, source_target_pairs={{0,16},{24,8},{1,17},{25,9},{2,18},{26,10},{3,19},{27,11},{4,20},{... | collective-permute-start | bytes 393224 | tf_op jit(solution)/shard_map/ppermute | solution.py:560
  11.1 3.4 %collective-permute-done.1.rest_2_ = f32[128,256]{1,0:T(8,128)S(1)} collective-permute-done((f32[128,256]{1,0:T(8,128)S(1)}, f32[128,256]{1,0:T(8,128)S(1)}, u32[]{:S(2)}, u32[]{:S(2)}) %collective-permute-start.1) | collective-permute-done | bytes 131104 | tf_op jit(solution)/shard_map/ppermute | solution.py:560
  14.5 5.8 %collective-permute-done.2.rest_3_ = f32[128,256]{1,0:T(8,128)S(1)} collective-permute-done((f32[128,256]{1,0:T(8,128)S(1)}, f32[128,256]{1,0:T(8,128)S(1)}, u32[]{:S(2)}, u32[]{:S(2)}) %collective-permute-start.2) | collective-permute-done | bytes 131104 | tf_op jit(solution)/shard_map/ppermute | solution.py:560
  20.2 2.8 %collective-permute-done.5.rest_7_ = f32[128,256]{1,0:T(8,128)S(1)} collective-permute-done((f32[128,256]{1,0:T(8,128)S(1)}, f32[128,256]{1,0:T(8,128)S(1)}, u32[]{:S(2)}, u32[]{:S(2)}) %collective-permute-start.5) | collective-permute-done | bytes 131104 | tf_op jit(solution)/shard_map/ppermute | solution.py:560
  23.0 1.9 %shard_map.105 = f32[8,2,128,128]{3,2,1,0:T(8,128)} custom-call(bf16[2,768,512]{2,1,0:T(8,128)(2,1)S(1)} %copy-done, f32[128,256]{1,0:T(8,128)S(1)} %get-tuple-element.99.rest_0_, f32[128,256]{1,0:T(8,128)S(1)} %collective-permute-done.rest_1_, f32[128,256]{1,0:T(8,128)S(1)} %collective-permute-done.1.rest_2_, ...), custom_call_target="tpu_custom_call" | custom-call | bytes 3670016 | tf_op jit(solution)/shard_map/pallas_call | solution.py:526
  24.9 4.8 %all-to-all-start = ((f32[8,2,128,128]{3,2,1,0:T(8,128)}), f32[8,2,128,128]{3,2,1,0:T(8,128)}, u32[]{:S(2)}, u32[]{:S(2)}) async-start(f32[8,2,128,128]{3,2,1,0:T(8,128)} %shard_map.105), calls=%async_computation | async-start | bytes 2097152 | tf_op jit(solution)/shard_map/all_to_all | solution.py:604
  31.4 3.1 %collective-permute-done.6.rest_1_ = f32[128,256]{1,0:T(8,128)S(1)} collective-permute-done((f32[128,256]{1,0:T(8,128)S(1)}, f32[128,256]{1,0:T(8,128)S(1)}, u32[]{:S(2)}, u32[]{:S(2)}) %collective-permute-start.6) | collective-permute-done | bytes 131104 | tf_op jit(solution)/shard_map/ppermute | solution.py:560
  34.5 6.6 %collective-permute-done.7.rest_2_ = f32[128,256]{1,0:T(8,128)S(1)} collective-permute-done((f32[128,256]{1,0:T(8,128)S(1)}, f32[128,256]{1,0:T(8,128)S(1)}, u32[]{:S(2)}, u32[]{:S(2)}) %collective-permute-start.7) | collective-permute-done | bytes 131104 | tf_op jit(solution)/shard_map/ppermute | solution.py:560
  41.9 1.8 %all-to-all-done.data_h = f32[8,2,128,128]{3,2,1,0:T(8,128)} async-done(((f32[8,2,128,128]{3,2,1,0:T(8,128)}), f32[8,2,128,128]{3,2,1,0:T(8,128)}, u32[]{:S(2)}, u32[]{:S(2)}) %all-to-all-start) | async-done | bytes 1048608 | tf_op jit(solution)/shard_map/all_to_all | solution.py:604
  46.0 1.3 %collective-permute-start.10 = (f32[2,1,128,128]{3,2,1,0:T(8,128)S(1)}, f32[2,1,128,128]{3,2,1,0:T(8,128)S(1)}, u32[]{:S(2)}, u32[]{:S(2)}) collective-permute-start(f32[2,1,128,128]{3,2,1,0:T(8,128)S(1)} %get-tuple-element.118), channel_id=1, source_target_pairs={{0,2},{1,3},{2,0},{3,1},{4,6},{5,7},{6,4},{7,5},{8,10},{9,11},{10,... | collective-permute-start | bytes 393224 | tf_op jit(solution)/shard_map/ppermute | solution.py:596
  48.7 3.0 %shard_map.108.early = f32[4,2,256,128]{3,2,1,0:T(8,128)S(1)} custom-call(bf16[2,512,256]{2,1,0:T(8,128)(2,1)S(1)} %copy-done.2, f32[256,8]{1,0:T(8,128)S(1)} %copy-done.4, f32[8,2,128,128]{3,2,1,0:T(8,128)} %all-to-all-done.data_h), custom_call_target="tpu_custom_call" | custom-call | bytes 2629632 | tf_op jit(solution)/shard_map/pallas_call | solution.py:526
  52.1 1.4 %collective-permute-done.12.rest_2_ = f32[2,1,128,128]{3,2,1,0:T(8,128)S(1)} collective-permute-done((f32[2,1,128,128]{3,2,1,0:T(8,128)S(1)}, f32[2,1,128,128]{3,2,1,0:T(8,128)S(1)}, u32[]{:S(2)}, u32[]{:S(2)}) %collective-permute-start.12) | collective-permute-done | bytes 131104 | tf_op jit(solution)/shard_map/ppermute | solution.py:596
  53.5 3.4 %shard_map.109 = (f32[4,1,128,128]{3,2,1,0:T(8,128)S(1)}, f32[4,1,128,128]{3,2,1,0:T(8,128)S(1)}, f32[4,1,256,128]{3,2,1,0:T(8,128)S(1)}) custom-call(f32[5]{0:T(128)S(1)} %copy-done.6, f32[6]{0:T(128)S(1)} %copy-done.7, bf16[2,512,256]{2,1,0:T(8,128)(2,1)S(1)} %copy-done.2, f32[256,8]{1,0:T(8,128)S(1)} %copy-done.4, ...), custom_call_target="tpu_custom_call" | custom-call | bytes 3547180 | tf_op jit(solution)/shard_map/pallas_call | solution.py:526
  57.0 2.5 %collective-permute-start.13 = (f32[4,1,128,128]{3,2,1,0:T(8,128)S(1)}, f32[4,1,128,128]{3,2,1,0:T(8,128)S(1)}, u32[]{:S(2)}, u32[]{:S(2)}) collective-permute-start(f32[4,1,128,128]{3,2,1,0:T(8,128)S(1)} %get-tuple-element.122), channel_id=1, source_target_pairs={{0,1},{1,0},{2,3},{3,2},{4,5},{5,4},{6,7},{7,6},{8,9},{9,8},{10,11... | collective-permute-start | bytes 786440 | tf_op jit(solution)/shard_map/ppermute | solution.py:592
  61.9 1.5 %collective-permute-start.16 = (f32[2,1,128,128]{3,2,1,0:T(8,128)S(1)}, f32[2,1,128,128]{3,2,1,0:T(8,128)S(1)}, u32[]{:S(2)}, u32[]{:S(2)}) collective-permute-start(f32[2,1,128,128]{3,2,1,0:T(8,128)S(1)} %get-tuple-element.132), channel_id=1, source_target_pairs={{0,6},{1,7},{2,4},{3,5},{4,2},{5,3},{6,0},{7,1},{8,14},{9,15},{10,... | collective-permute-start | bytes 393224 | tf_op jit(solution)/shard_map/ppermute | solution.py:596
  63.4 3.7 %shard_map.111 = (f32[4,2,128,128]{3,2,1,0:T(8,128)S(1)}, f32[4,2,128,128]{3,2,1,0:T(8,128)S(1)}) custom-call(f32[5]{0:T(128)S(1)} %copy-done.6, f32[6]{0:T(128)S(1)} %copy-done.7, bf16[2,512,256]{2,1,0:T(8,128)(2,1)S(1)} %copy-done.2, f32[256,8]{1,0:T(8,128)S(1)} %copy-done.4, f32[4,2,256,128]{3,2,1,0:T(8,128)S(1)} %shard_map.108.early, ...), custom_call_target="tpu_custom_call" | custom-call | bytes 3153964 | tf_op jit(solution)/shard_map/pallas_call | solution.py:526
  68.4 1.4 %collective-permute-start.17 = (f32[4,2,128,128]{3,2,1,0:T(8,128)S(1)}, f32[4,2,128,128]{3,2,1,0:T(8,128)S(1)}, u32[]{:S(2)}, u32[]{:S(2)}) collective-permute-start(f32[4,2,128,128]{3,2,1,0:T(8,128)S(1)} %get-tuple-element.134), channel_id=1, source_target_pairs={{0,1},{1,0},{2,3},{3,2},{4,5},{5,4},{6,7},{7,6},{8,9},{9,8},{10,11... | collective-permute-start | bytes 1572872 | tf_op jit(solution)/shard_map/ppermute | solution.py:592
  71.4 1.3 %collective-permute-start.18 = (f32[2,2,128,128]{3,2,1,0:T(8,128)S(1)}, f32[2,2,128,128]{3,2,1,0:T(8,128)S(1)}, u32[]{:S(2)}, u32[]{:S(2)}) collective-permute-start(f32[2,2,128,128]{3,2,1,0:T(8,128)S(1)} %get-tuple-element.147), channel_id=1, source_target_pairs={{0,2},{1,3},{2,0},{3,1},{4,6},{5,7},{6,4},{7,5},{8,10},{9,11},{10,... | collective-permute-start | bytes 786440 | tf_op jit(solution)/shard_map/ppermute | solution.py:596
  75.4 3.6 %collective-permute-done.18.rest_0_ = f32[2,2,128,128]{3,2,1,0:T(8,128)S(1)} collective-permute-done((f32[2,2,128,128]{3,2,1,0:T(8,128)S(1)}, f32[2,2,128,128]{3,2,1,0:T(8,128)S(1)}, u32[]{:S(2)}, u32[]{:S(2)}) %collective-permute-start.18) | collective-permute-done | bytes 262176 | tf_op jit(solution)/shard_map/ppermute | solution.py:596
  80.1 5.2 %collective-permute-done.20.rest_2_ = f32[2,2,128,128]{3,2,1,0:T(8,128)S(1)} collective-permute-done((f32[2,2,128,128]{3,2,1,0:T(8,128)S(1)}, f32[2,2,128,128]{3,2,1,0:T(8,128)S(1)}, u32[]{:S(2)}, u32[]{:S(2)}) %collective-permute-start.20) | collective-permute-done | bytes 262176 | tf_op jit(solution)/shard_map/ppermute | solution.py:596
  87.9 1.4 %collective-permute-start.23 = (f32[128,256]{1,0:T(8,128)S(1)}, f32[128,256]{1,0:T(8,128)S(1)}, u32[]{:S(2)}, u32[]{:S(2)}) collective-permute-start(f32[128,256]{1,0:T(8,128)S(1)} %get-tuple-element.153), channel_id=1, source_target_pairs={{0,24},{8,0},{16,8},{24,16},{1,25},{9,1},{17,9},{25,17},{2,26},{10... | collective-permute-start | bytes 393224 | tf_op jit(solution)/shard_map/ppermute | solution.py:560
  89.3 2.0 %collective-permute-start.27 = (f32[128,256]{1,0:T(8,128)S(1)}, f32[128,256]{1,0:T(8,128)S(1)}, u32[]{:S(2)}, u32[]{:S(2)}) collective-permute-start(f32[128,256]{1,0:T(8,128)S(1)} %get-tuple-element.159), channel_id=1, source_target_pairs={{8,16},{16,24},{9,17},{17,25},{10,18},{18,26},{11,19},{19,27},{12,... | collective-permute-start | bytes 393224 | tf_op jit(solution)/shard_map/ppermute | solution.py:560
  91.3 2.0 %collective-permute-start.28 = (f32[128,256]{1,0:T(8,128)S(1)}, f32[128,256]{1,0:T(8,128)S(1)}, u32[]{:S(2)}, u32[]{:S(2)}) collective-permute-start(f32[128,256]{1,0:T(8,128)S(1)} %get-tuple-element.160), channel_id=1, source_target_pairs={{8,24},{16,0},{9,25},{17,1},{10,26},{18,2},{11,27},{19,3},{12,28},... | collective-permute-start | bytes 393224 | tf_op jit(solution)/shard_map/ppermute | solution.py:560
  93.4 1.9 %collective-permute-start.29 = (f32[128,256]{1,0:T(8,128)S(1)}, f32[128,256]{1,0:T(8,128)S(1)}, u32[]{:S(2)}, u32[]{:S(2)}) collective-permute-start(f32[128,256]{1,0:T(8,128)S(1)} %get-tuple-element.161), channel_id=1, source_target_pairs={{8,0},{16,8},{9,1},{17,9},{10,2},{18,10},{11,3},{19,11},{12,4},{20... | collective-permute-start | bytes 393224 | tf_op jit(solution)/shard_map/ppermute | solution.py:560
  95.3 4.9 %collective-permute-done.23.rest_3_ = f32[128,256]{1,0:T(8,128)S(1)} collective-permute-done((f32[128,256]{1,0:T(8,128)S(1)}, f32[128,256]{1,0:T(8,128)S(1)}, u32[]{:S(2)}, u32[]{:S(2)}) %collective-permute-start.23) | collective-permute-done | bytes 131104 | tf_op jit(solution)/shard_map/ppermute | solution.py:560
  100.2 2.1 %shard_map.115 = (f32[6,2,128,256]{3,2,1,0:T(8,128)}, f32[6,2,128,256]{3,2,1,0:T(8,128)}) custom-call(f32[5]{0:T(128)S(1)} %copy-done.6, f32[6]{0:T(128)S(1)} %copy-done.7, s32[2,128,256]{2,1,0:T(8,128)S(1)} %copy-done.3, s32[2,8,16]{2,1,0:T(8,128)S(1)} %copy-done.5, f32[128,256]{1,0:T(8,128)S(1)} %get-tuple-element.150.rest_0_, ...), custom_call_target="tpu_custom_call" | custom-call | bytes 4457516 | tf_op jit(solution)/shard_map/pallas_call | solution.py:526
  102.4 3.2 %collective-permute-done.29.rest_11_ = f32[128,256]{1,0:T(8,128)S(1)} collective-permute-done((f32[128,256]{1,0:T(8,128)S(1)}, f32[128,256]{1,0:T(8,128)S(1)}, u32[]{:S(2)}, u32[]{:S(2)}) %collective-permute-start.29) | collective-permute-done | bytes 131104 | tf_op jit(solution)/shard_map/ppermute | solution.py:560
  105.6 1.9 %shard_map.116 = (f32[6,2,128,256]{3,2,1,0:T(8,128)}, f32[6,2,128,256]{3,2,1,0:T(8,128)}) custom-call(f32[5]{0:T(128)S(1)} %copy-done.6, f32[6]{0:T(128)S(1)} %copy-done.7, s32[2,128,256]{2,1,0:T(8,128)S(1)} %copy-done.3, s32[2,8,16]{2,1,0:T(8,128)S(1)} %copy-done.5, ...), custom_call_target="tpu_custom_call", output_to_operand_aliasing={{0}: (16, {}), {1}: (17, {})} | custom-call | bytes 8127532 | tf_op jit(solution)/shard_map/pallas_call | solution.py:526
  (59 shorter events, 20.8 us)
Async XLA Ops:
  2.7 7.1 %collective-permute-start = (f32[128,256]{1,0:T(8,128)S(1)}, f32[128,256]{1,0:T(8,128)S(1)}, u32[]{:S(2)}, u32[]{:S(2)}) collective-permute-start(f32[128,256]{1,0:T(8,128)S(1)} %get-tuple-element.84), channel_id=1, source_target_pairs={{0,8},{8,16},{16,24},{24,0},{1,9},{9,17},{17,25},{25,1},{2,10},{10... | collective-permute-start | bytes 393224 | tf_op jit(solution)/shard_map/ppermute | solution.py:560
  4.0 10.4 %collective-permute-start.1 = (f32[128,256]{1,0:T(8,128)S(1)}, f32[128,256]{1,0:T(8,128)S(1)}, u32[]{:S(2)}, u32[]{:S(2)}) collective-permute-start(f32[128,256]{1,0:T(8,128)S(1)} %get-tuple-element.85), channel_id=1, source_target_pairs={{0,16},{8,24},{16,0},{24,8},{1,17},{9,25},{17,1},{25,9},{2,18},{10... | collective-permute-start | bytes 393224 | tf_op jit(solution)/shard_map/ppermute | solution.py:560
  5.1 15.1 %collective-permute-start.2 = (f32[128,256]{1,0:T(8,128)S(1)}, f32[128,256]{1,0:T(8,128)S(1)}, u32[]{:S(2)}, u32[]{:S(2)}) collective-permute-start(f32[128,256]{1,0:T(8,128)S(1)} %get-tuple-element.86), channel_id=1, source_target_pairs={{0,24},{8,0},{16,8},{24,16},{1,25},{9,1},{17,9},{25,17},{2,26},{10... | collective-permute-start | bytes 393224 | tf_op jit(solution)/shard_map/ppermute | solution.py:560
  6.5 13.7 %collective-permute-start.3 = (f32[128,256]{1,0:T(8,128)S(1)}, f32[128,256]{1,0:T(8,128)S(1)}, u32[]{:S(2)}, u32[]{:S(2)}) collective-permute-start(f32[128,256]{1,0:T(8,128)S(1)} %get-tuple-element.88), channel_id=1, source_target_pairs={{0,8},{8,16},{1,9},{9,17},{2,10},{10,18},{3,11},{11,19},{4,12},{12... | collective-permute-start | bytes 393224 | tf_op jit(solution)/shard_map/ppermute | solution.py:560
  8.5 11.8 %collective-permute-start.4 = (f32[128,256]{1,0:T(8,128)S(1)}, f32[128,256]{1,0:T(8,128)S(1)}, u32[]{:S(2)}, u32[]{:S(2)}) collective-permute-start(f32[128,256]{1,0:T(8,128)S(1)} %get-tuple-element.89), channel_id=1, source_target_pairs={{0,16},{24,8},{1,17},{25,9},{2,18},{26,10},{3,19},{27,11},{4,20},{... | collective-permute-start | bytes 393224 | tf_op jit(solution)/shard_map/ppermute | solution.py:560
  9.8 13.2 %collective-permute-start.5 = (f32[128,256]{1,0:T(8,128)S(1)}, f32[128,256]{1,0:T(8,128)S(1)}, u32[]{:S(2)}, u32[]{:S(2)}) collective-permute-start(f32[128,256]{1,0:T(8,128)S(1)} %get-tuple-element.90), channel_id=1, source_target_pairs={{16,8},{24,16},{17,9},{25,17},{18,10},{26,18},{19,11},{27,19},{20,... | collective-permute-start | bytes 393224 | tf_op jit(solution)/shard_map/ppermute | solution.py:560
  24.9 18.7 %all-to-all-start = ((f32[8,2,128,128]{3,2,1,0:T(8,128)}), f32[8,2,128,128]{3,2,1,0:T(8,128)}, u32[]{:S(2)}, u32[]{:S(2)}) async-start(f32[8,2,128,128]{3,2,1,0:T(8,128)} %shard_map.105), calls=%async_computation | async-start | bytes 2097152 | tf_op jit(solution)/shard_map/all_to_all | solution.py:604
  29.7 4.8 %collective-permute-start.6 = (f32[128,256]{1,0:T(8,128)S(1)}, f32[128,256]{1,0:T(8,128)S(1)}, u32[]{:S(2)}, u32[]{:S(2)}) collective-permute-start(f32[128,256]{1,0:T(8,128)S(1)} %get-tuple-element.96), channel_id=1, source_target_pairs={{0,8},{8,16},{16,24},{24,0},{1,9},{9,17},{17,25},{25,1},{2,10},{10... | collective-permute-start | bytes 393224 | tf_op jit(solution)/shard_map/ppermute | solution.py:560
  30.2 10.9 %collective-permute-start.7 = (f32[128,256]{1,0:T(8,128)S(1)}, f32[128,256]{1,0:T(8,128)S(1)}, u32[]{:S(2)}, u32[]{:S(2)}) collective-permute-start(f32[128,256]{1,0:T(8,128)S(1)} %get-tuple-element.97), channel_id=1, source_target_pairs={{0,16},{8,24},{16,0},{24,8},{1,17},{9,25},{17,1},{25,9},{2,18},{10... | collective-permute-start | bytes 393224 | tf_op jit(solution)/shard_map/ppermute | solution.py:560
  30.2 11.7 %collective-permute-start.8 = (f32[128,256]{1,0:T(8,128)S(1)}, f32[128,256]{1,0:T(8,128)S(1)}, u32[]{:S(2)}, u32[]{:S(2)}) collective-permute-start(f32[128,256]{1,0:T(8,128)S(1)} %get-tuple-element.98), channel_id=1, source_target_pairs={{0,24},{8,0},{16,8},{24,16},{1,25},{9,1},{17,9},{25,17},{2,26},{10... | collective-permute-start | bytes 393224 | tf_op jit(solution)/shard_map/ppermute | solution.py:560
  44.2 1.7 %collective-permute-start.9 = (f32[4,1,128,128]{3,2,1,0:T(8,128)S(1)}, f32[4,1,128,128]{3,2,1,0:T(8,128)S(1)}, u32[]{:S(2)}, u32[]{:S(2)}) collective-permute-start(f32[4,1,128,128]{3,2,1,0:T(8,128)S(1)} %get-tuple-element.112), channel_id=1, source_target_pairs={{0,1},{1,0},{2,3},{3,2},{4,5},{5,4},{6,7},{7,6},{8,9},{9,8},{10,11... | collective-permute-start | bytes 786440 | tf_op jit(solution)/shard_map/ppermute | solution.py:592
  46.0 5.7 %collective-permute-start.10 = (f32[2,1,128,128]{3,2,1,0:T(8,128)S(1)}, f32[2,1,128,128]{3,2,1,0:T(8,128)S(1)}, u32[]{:S(2)}, u32[]{:S(2)}) collective-permute-start(f32[2,1,128,128]{3,2,1,0:T(8,128)S(1)} %get-tuple-element.118), channel_id=1, source_target_pairs={{0,2},{1,3},{2,0},{3,1},{4,6},{5,7},{6,4},{7,5},{8,10},{9,11},{10,... | collective-permute-start | bytes 393224 | tf_op jit(solution)/shard_map/ppermute | solution.py:596
  47.3 4.8 %collective-permute-start.11 = (f32[2,1,128,128]{3,2,1,0:T(8,128)S(1)}, f32[2,1,128,128]{3,2,1,0:T(8,128)S(1)}, u32[]{:S(2)}, u32[]{:S(2)}) collective-permute-start(f32[2,1,128,128]{3,2,1,0:T(8,128)S(1)} %get-tuple-element.119), channel_id=1, source_target_pairs={{0,4},{1,5},{2,6},{3,7},{4,0},{5,1},{6,2},{7,3},{8,12},{9,13},{10,... | collective-permute-start | bytes 393224 | tf_op jit(solution)/shard_map/ppermute | solution.py:596
  47.5 6.0 %collective-permute-start.12 = (f32[2,1,128,128]{3,2,1,0:T(8,128)S(1)}, f32[2,1,128,128]{3,2,1,0:T(8,128)S(1)}, u32[]{:S(2)}, u32[]{:S(2)}) collective-permute-start(f32[2,1,128,128]{3,2,1,0:T(8,128)S(1)} %get-tuple-element.120), channel_id=1, source_target_pairs={{0,6},{1,7},{2,4},{3,5},{4,2},{5,3},{6,0},{7,1},{8,14},{9,15},{10,... | collective-permute-start | bytes 393224 | tf_op jit(solution)/shard_map/ppermute | solution.py:596
  57.0 3.7 %collective-permute-start.13 = (f32[4,1,128,128]{3,2,1,0:T(8,128)S(1)}, f32[4,1,128,128]{3,2,1,0:T(8,128)S(1)}, u32[]{:S(2)}, u32[]{:S(2)}) collective-permute-start(f32[4,1,128,128]{3,2,1,0:T(8,128)S(1)} %get-tuple-element.122), channel_id=1, source_target_pairs={{0,1},{1,0},{2,3},{3,2},{4,5},{5,4},{6,7},{7,6},{8,9},{9,8},{10,11... | collective-permute-start | bytes 786440 | tf_op jit(solution)/shard_map/ppermute | solution.py:592
  60.7 6.4 %collective-permute-start.14 = (f32[2,1,128,128]{3,2,1,0:T(8,128)S(1)}, f32[2,1,128,128]{3,2,1,0:T(8,128)S(1)}, u32[]{:S(2)}, u32[]{:S(2)}) collective-permute-start(f32[2,1,128,128]{3,2,1,0:T(8,128)S(1)} %get-tuple-element.130), channel_id=1, source_target_pairs={{0,2},{1,3},{2,0},{3,1},{4,6},{5,7},{6,4},{7,5},{8,10},{9,11},{10,... | collective-permute-start | bytes 393224 | tf_op jit(solution)/shard_map/ppermute | solution.py:596
  61.0 6.1 %collective-permute-start.15 = (f32[2,1,128,128]{3,2,1,0:T(8,128)S(1)}, f32[2,1,128,128]{3,2,1,0:T(8,128)S(1)}, u32[]{:S(2)}, u32[]{:S(2)}) collective-permute-start(f32[2,1,128,128]{3,2,1,0:T(8,128)S(1)} %get-tuple-element.131), channel_id=1, source_target_pairs={{0,4},{1,5},{2,6},{3,7},{4,0},{5,1},{6,2},{7,3},{8,12},{9,13},{10,... | collective-permute-start | bytes 393224 | tf_op jit(solution)/shard_map/ppermute | solution.py:596
  61.9 6.4 %collective-permute-start.16 = (f32[2,1,128,128]{3,2,1,0:T(8,128)S(1)}, f32[2,1,128,128]{3,2,1,0:T(8,128)S(1)}, u32[]{:S(2)}, u32[]{:S(2)}) collective-permute-start(f32[2,1,128,128]{3,2,1,0:T(8,128)S(1)} %get-tuple-element.132), channel_id=1, source_target_pairs={{0,6},{1,7},{2,4},{3,5},{4,2},{5,3},{6,0},{7,1},{8,14},{9,15},{10,... | collective-permute-start | bytes 393224 | tf_op jit(solution)/shard_map/ppermute | solution.py:596
  68.4 2.9 %collective-permute-start.17 = (f32[4,2,128,128]{3,2,1,0:T(8,128)S(1)}, f32[4,2,128,128]{3,2,1,0:T(8,128)S(1)}, u32[]{:S(2)}, u32[]{:S(2)}) collective-permute-start(f32[4,2,128,128]{3,2,1,0:T(8,128)S(1)} %get-tuple-element.134), channel_id=1, source_target_pairs={{0,1},{1,0},{2,3},{3,2},{4,5},{5,4},{6,7},{7,6},{8,9},{9,8},{10,11... | collective-permute-start | bytes 1572872 | tf_op jit(solution)/shard_map/ppermute | solution.py:592
  71.3 28.9 %copy-start.3 = (s32[2,128,256]{2,1,0:T(8,128)S(1)}, s32[2,128,256]{2,1,0:T(8,128)}, u32[]{:S(2)}) copy-start(s32[2,128,256]{2,1,0:T(8,128)} %labels.3) | copy-start | bytes 786436
  71.4 7.6 %collective-permute-start.18 = (f32[2,2,128,128]{3,2,1,0:T(8,128)S(1)}, f32[2,2,128,128]{3,2,1,0:T(8,128)S(1)}, u32[]{:S(2)}, u32[]{:S(2)}) collective-permute-start(f32[2,2,128,128]{3,2,1,0:T(8,128)S(1)} %get-tuple-element.147), channel_id=1, source_target_pairs={{0,2},{1,3},{2,0},{3,1},{4,6},{5,7},{6,4},{7,5},{8,10},{9,11},{10,... | collective-permute-start | bytes 786440 | tf_op jit(solution)/shard_map/ppermute | solution.py:596
  72.6 7.4 %collective-permute-start.19 = (f32[2,2,128,128]{3,2,1,0:T(8,128)S(1)}, f32[2,2,128,128]{3,2,1,0:T(8,128)S(1)}, u32[]{:S(2)}, u32[]{:S(2)}) collective-permute-start(f32[2,2,128,128]{3,2,1,0:T(8,128)S(1)} %get-tuple-element.148), channel_id=1, source_target_pairs={{0,4},{1,5},{2,6},{3,7},{4,0},{5,1},{6,2},{7,3},{8,12},{9,13},{10,... | collective-permute-start | bytes 786440 | tf_op jit(solution)/shard_map/ppermute | solution.py:596
  72.9 12.4 %collective-permute-start.20 = (f32[2,2,128,128]{3,2,1,0:T(8,128)S(1)}, f32[2,2,128,128]{3,2,1,0:T(8,128)S(1)}, u32[]{:S(2)}, u32[]{:S(2)}) collective-permute-start(f32[2,2,128,128]{3,2,1,0:T(8,128)S(1)} %get-tuple-element.149), channel_id=1, source_target_pairs={{0,6},{1,7},{2,4},{3,5},{4,2},{5,3},{6,0},{7,1},{8,14},{9,15},{10,... | collective-permute-start | bytes 786440 | tf_op jit(solution)/shard_map/ppermute | solution.py:596
  74.1 13.9 %collective-permute-start.24 = (f32[128,256]{1,0:T(8,128)S(1)}, f32[128,256]{1,0:T(8,128)S(1)}, u32[]{:S(2)}, u32[]{:S(2)}) collective-permute-start(f32[128,256]{1,0:T(8,128)S(1)} %get-tuple-element.155), channel_id=1, source_target_pairs={{0,8},{8,16},{16,24},{24,0},{1,9},{9,17},{17,25},{25,1},{2,10},{10... | collective-permute-start | bytes 393224 | tf_op jit(solution)/shard_map/ppermute | solution.py:560
  74.5 14.8 %collective-permute-start.25 = (f32[128,256]{1,0:T(8,128)S(1)}, f32[128,256]{1,0:T(8,128)S(1)}, u32[]{:S(2)}, u32[]{:S(2)}) collective-permute-start(f32[128,256]{1,0:T(8,128)S(1)} %get-tuple-element.156), channel_id=1, source_target_pairs={{0,16},{8,24},{16,0},{24,8},{1,17},{9,25},{17,1},{25,9},{2,18},{10... | collective-permute-start | bytes 393224 | tf_op jit(solution)/shard_map/ppermute | solution.py:560
  78.9 12.4 %collective-permute-start.26 = (f32[128,256]{1,0:T(8,128)S(1)}, f32[128,256]{1,0:T(8,128)S(1)}, u32[]{:S(2)}, u32[]{:S(2)}) collective-permute-start(f32[128,256]{1,0:T(8,128)S(1)} %get-tuple-element.157), channel_id=1, source_target_pairs={{0,24},{8,0},{16,8},{24,16},{1,25},{9,1},{17,9},{25,17},{2,26},{10... | collective-permute-start | bytes 393224 | tf_op jit(solution)/shard_map/ppermute | solution.py:560
  86.3 7.1 %collective-permute-start.21 = (f32[128,256]{1,0:T(8,128)S(1)}, f32[128,256]{1,0:T(8,128)S(1)}, u32[]{:S(2)}, u32[]{:S(2)}) collective-permute-start(f32[128,256]{1,0:T(8,128)S(1)} %get-tuple-element.151), channel_id=1, source_target_pairs={{0,8},{8,16},{16,24},{24,0},{1,9},{9,17},{17,25},{25,1},{2,10},{10... | collective-permute-start | bytes 393224 | tf_op jit(solution)/shard_map/ppermute | solution.py:560
  86.8 8.6 %collective-permute-start.22 = (f32[128,256]{1,0:T(8,128)S(1)}, f32[128,256]{1,0:T(8,128)S(1)}, u32[]{:S(2)}, u32[]{:S(2)}) collective-permute-start(f32[128,256]{1,0:T(8,128)S(1)} %get-tuple-element.152), channel_id=1, source_target_pairs={{0,16},{8,24},{16,0},{24,8},{1,17},{9,25},{17,1},{25,9},{2,18},{10... | collective-permute-start | bytes 393224 | tf_op jit(solution)/shard_map/ppermute | solution.py:560
  87.9 12.3 %collective-permute-start.23 = (f32[128,256]{1,0:T(8,128)S(1)}, f32[128,256]{1,0:T(8,128)S(1)}, u32[]{:S(2)}, u32[]{:S(2)}) collective-permute-start(f32[128,256]{1,0:T(8,128)S(1)} %get-tuple-element.153), channel_id=1, source_target_pairs={{0,24},{8,0},{16,8},{24,16},{1,25},{9,1},{17,9},{25,17},{2,26},{10... | collective-permute-start | bytes 393224 | tf_op jit(solution)/shard_map/ppermute | solution.py:560
  89.3 13.1 %collective-permute-start.27 = (f32[128,256]{1,0:T(8,128)S(1)}, f32[128,256]{1,0:T(8,128)S(1)}, u32[]{:S(2)}, u32[]{:S(2)}) collective-permute-start(f32[128,256]{1,0:T(8,128)S(1)} %get-tuple-element.159), channel_id=1, source_target_pairs={{8,16},{16,24},{9,17},{17,25},{10,18},{18,26},{11,19},{19,27},{12,... | collective-permute-start | bytes 393224 | tf_op jit(solution)/shard_map/ppermute | solution.py:560
  91.3 11.1 %collective-permute-start.28 = (f32[128,256]{1,0:T(8,128)S(1)}, f32[128,256]{1,0:T(8,128)S(1)}, u32[]{:S(2)}, u32[]{:S(2)}) collective-permute-start(f32[128,256]{1,0:T(8,128)S(1)} %get-tuple-element.160), channel_id=1, source_target_pairs={{8,24},{16,0},{9,25},{17,1},{10,26},{18,2},{11,27},{19,3},{12,28},... | collective-permute-start | bytes 393224 | tf_op jit(solution)/shard_map/ppermute | solution.py:560
  93.4 12.2 %collective-permute-start.29 = (f32[128,256]{1,0:T(8,128)S(1)}, f32[128,256]{1,0:T(8,128)S(1)}, u32[]{:S(2)}, u32[]{:S(2)}) collective-permute-start(f32[128,256]{1,0:T(8,128)S(1)} %get-tuple-element.161), channel_id=1, source_target_pairs={{8,0},{16,8},{9,1},{17,9},{10,2},{18,10},{11,3},{19,11},{12,4},{20... | collective-permute-start | bytes 393224 | tf_op jit(solution)/shard_map/ppermute | solution.py:560
  (7 other events, 117.2 us)

commit v8 on v7

--- a/solution.py
+++ b/solution.py
@@ -327,10 +327,9 @@
     return lax.axis_index("gx") * slots == z_cells // 4
 
 
-def x_forward_kernel(table, twiddles, data_h, out, data, sem):
-    copy = pltpu.make_async_copy(data_h, data, sem)
-    copy.start()
-    copy.wait()
+def x_forward_kernel(table, twiddles, own, got, *rest):
+    moved, (out, data) = rest[:-2], rest[-2:]
+    collect(own, got, moved, data)
     fields, lanes = data.shape[1], data.shape[3]
     for residue, spectrum in enumerate(x_forward(data, table, twiddles)):
         for f in range(fields):
@@ -600,14 +599,16 @@
 
     args = [a for f in early for a in travel(f, blocks[f], True)]
     args, blocks = lax.optimization_barrier((args, blocks))
-    (rows,) = call(z_forward_kernel, [grid], [held(size)], (z_fwd, *args), 16)
-    rows = lax.all_to_all(rows, "gx", 0, 0, tiled=True)
+    scratch = [held(size), pltpu.VMEM(grid, F32)]
+    dealt = call(z_forward_deal_kernel, [tile_early] * 2, scratch, (z_fwd, *args), 16)
+    rows, blocks = exchange(*dealt, blocks)
     args = travel(late[0], blocks[late[0]], True)
     args, rows = lax.optimization_barrier((args, rows))
     own, swapped = call(z_forward_deal_kernel, [tile] * 2, [held(1), tiles], (z_fwd, *args), 16)
     last, rows = exchange(own, swapped, rows)
-    copied = [pltpu.VMEM(grid, F32), pltpu.SemaphoreType.DMA]
-    (spectrum,) = call(x_forward_kernel, [(4, size, quarter, lanes)], copied, (*x_tab, rows), 24, (2,))
+    (spectrum,) = call(
+        x_forward_kernel, [(4, size, quarter, lanes)], [pltpu.VMEM(grid, F32)], (*x_tab, *rows), 24
+    )
     own, swapped, late_spectrum = call(
         functools.partial(late_kernel, x_total, z_total, CHUNKS),
         [tile, tile, (4, 1, quarter, lanes)],

time: 109 us -> 108 us (level)
  Pallas kernels: 20.3 us -> 18.3 us
  waiting for transfers between devices: 48.5 us -> 49.7 us
    all_to_all x1 -> x0, starting transfers between devices: 4.8 us -> none  [shards(): rows = lax.all_to_all(rows, 'gx', 0, 0, tiled=True)]
    ppermute x9 -> x12, starting transfers between devices: 8.14 us -> 10.8 us  [exchange(): lax.ppermute(block, 'gx', [(k, k ^ 2 * step) for k in range(x_devices)])]
    ppermute x18, starting transfers between devices: 20.4 us -> 22.4 us  [travel(): moved.append(lax.ppermute(blocks[step], 'gz', way))]
    pallas_call x13 -> x14, Pallas kernels: 20.3 us -> 18.3 us  [call(): pl.pallas_call(kernel, out_shape=[pltpu.HBM(o, F32) if k in hbm_out else...]
    all_to_all x1 -> x0, waiting for transfers between devices: 1.78 us -> none  [shards(): rows = lax.all_to_all(rows, 'gx', 0, 0, tiled=True)]
    ppermute x18, waiting for transfers between devices: 30.5 us -> 32.1 us  [travel(): moved.append(lax.ppermute(blocks[step], 'gz', way))]
    ppermute x3 -> x4, waiting for transfers between devices: 3.27 us -> 4.8 us  [exchange(): got = lax.ppermute(swapped, 'gx', [(k, k ^ 1) for k in range(x_devices)])]
    ppermute x9 -> x12, waiting for transfers between devices: 12.9 us -> 12.7 us  [exchange(): lax.ppermute(block, 'gx', [(k, k ^ 2 * step) for k in range(x_devices)])]
  transfers between devices with their start and end apart: 31 -> 34, of which waited for: 18 -> 19; matrix products, arithmetic and copies ran while one was open for 0% -> 0% of each run, Pallas kernels for 10% -> 9%
where the time goes in v8:
time: 108 us; the launch traced here: 107 us
  waiting for transfers between devices  49.7 us (46%)
  starting transfers between devices  37.6 us (35%)
  Pallas kernels  18.3 us (17%)
    ppermute x18, waiting for transfers between devices, travel(): moved.append(lax.ppermute(blocks[step], 'gz', way))  32.1 us
    ppermute x18, starting transfers between devices, travel(): moved.append(lax.ppermute(blocks[step], 'gz', way))  22.4 us
    pallas_call x14, Pallas kernels, call(): pl.pallas_call(kernel, out_shape=[pltpu.HBM(o, F32) if k in hbm_out else...  18.3 us
    ppermute x12, waiting for transfers between devices, exchange(): lax.ppermute(block, 'gx', [(k, k ^ 2 * step) for k in range(x_devices)])  12.7 us
    ppermute x12, starting transfers between devices, exchange(): lax.ppermute(block, 'gx', [(k, k ^ 2 * step) for k in range(x_devices)])  10.8 us
    ppermute x4, waiting for transfers between devices, exchange(): got = lax.ppermute(swapped, 'gx', [(k, k ^ 1) for k in range(x_devices)])  4.8 us
    ppermute x4, starting transfers between devices, exchange(): got = lax.ppermute(swapped, 'gx', [(k, k ^ 1) for k in range(x_devices)])  4.39 us
  transfers between devices with their start and end apart: 34, of which 19 were waited for; matrix products, arithmetic and copies ran while one was open for 0% of the time, Pallas kernels for 9%

profile of v8, /device:TPU:11, one launch (start us, length us, event | category | flops | bytes accessed | tf_op | source)
XLA Modules:
  0.0 106.7 jit_solution(3275267516631435248)
XLA Ops:
  0.6 2.0 %shard_map.104 = (f32[128,256]{1,0:T(8,128)S(1)}, f32[128,256]{1,0:T(8,128)S(1)}, f32[128,256]{1,0:T(8,128)S(1)}, f32[128,256]{1,0:T(8,128)S(1)}, f32[128,256]{1...) custom-call(f32[5]{0:T(128)} %moduli.7, ...), custom_call_target="tpu_custom_call" | custom-call | bytes 3408916 | tf_op jit(solution)/shard_map/pallas_call | solution.py:525
  2.7 1.4 %collective-permute-start = (f32[128,256]{1,0:T(8,128)S(1)}, f32[128,256]{1,0:T(8,128)S(1)}, u32[]{:S(2)}, u32[]{:S(2)}) collective-permute-start(f32[128,256]{1,0:T(8,128)S(1)} %get-tuple-element.104), channel_id=1, source_target_pairs={{0,8},{8,16},{16,24},{24,0},{1,9},{9,17},{17,25},{25,1},{2,10},{10... | collective-permute-start | bytes 393224 | tf_op jit(solution)/shard_map/ppermute | solution.py:559
  5.1 1.4 %collective-permute-start.2 = (f32[128,256]{1,0:T(8,128)S(1)}, f32[128,256]{1,0:T(8,128)S(1)}, u32[]{:S(2)}, u32[]{:S(2)}) collective-permute-start(f32[128,256]{1,0:T(8,128)S(1)} %get-tuple-element.106), channel_id=1, source_target_pairs={{0,24},{8,0},{16,8},{24,16},{1,25},{9,1},{17,9},{25,17},{2,26},{10... | collective-permute-start | bytes 393224 | tf_op jit(solution)/shard_map/ppermute | solution.py:559
  6.5 2.0 %collective-permute-start.3 = (f32[128,256]{1,0:T(8,128)S(1)}, f32[128,256]{1,0:T(8,128)S(1)}, u32[]{:S(2)}, u32[]{:S(2)}) collective-permute-start(f32[128,256]{1,0:T(8,128)S(1)} %get-tuple-element.108), channel_id=1, source_target_pairs={{0,8},{8,16},{1,9},{9,17},{2,10},{10,18},{3,11},{11,19},{4,12},{12... | collective-permute-start | bytes 393224 | tf_op jit(solution)/shard_map/ppermute | solution.py:559
  8.5 1.3 %collective-permute-start.4 = (f32[128,256]{1,0:T(8,128)S(1)}, f32[128,256]{1,0:T(8,128)S(1)}, u32[]{:S(2)}, u32[]{:S(2)}) collective-permute-start(f32[128,256]{1,0:T(8,128)S(1)} %get-tuple-element.109), channel_id=1, source_target_pairs={{0,16},{24,8},{1,17},{25,9},{2,18},{26,10},{3,19},{27,11},{4,20},{... | collective-permute-start | bytes 393224 | tf_op jit(solution)/shard_map/ppermute | solution.py:559
  9.8 1.3 %collective-permute-start.5 = (f32[128,256]{1,0:T(8,128)S(1)}, f32[128,256]{1,0:T(8,128)S(1)}, u32[]{:S(2)}, u32[]{:S(2)}) collective-permute-start(f32[128,256]{1,0:T(8,128)S(1)} %get-tuple-element.110), channel_id=1, source_target_pairs={{16,8},{24,16},{17,9},{25,17},{18,10},{26,18},{19,11},{27,19},{20,... | collective-permute-start | bytes 393224 | tf_op jit(solution)/shard_map/ppermute | solution.py:559
  11.1 3.4 %collective-permute-done.1.rest_2_ = f32[128,256]{1,0:T(8,128)S(1)} collective-permute-done((f32[128,256]{1,0:T(8,128)S(1)}, f32[128,256]{1,0:T(8,128)S(1)}, u32[]{:S(2)}, u32[]{:S(2)}) %collective-permute-start.1) | collective-permute-done | bytes 131104 | tf_op jit(solution)/shard_map/ppermute | solution.py:559
  14.5 5.8 %collective-permute-done.2.rest_3_ = f32[128,256]{1,0:T(8,128)S(1)} collective-permute-done((f32[128,256]{1,0:T(8,128)S(1)}, f32[128,256]{1,0:T(8,128)S(1)}, u32[]{:S(2)}, u32[]{:S(2)}) %collective-permute-start.2) | collective-permute-done | bytes 131104 | tf_op jit(solution)/shard_map/ppermute | solution.py:559
  20.2 2.8 %collective-permute-done.5.rest_7_ = f32[128,256]{1,0:T(8,128)S(1)} collective-permute-done((f32[128,256]{1,0:T(8,128)S(1)}, f32[128,256]{1,0:T(8,128)S(1)}, u32[]{:S(2)}, u32[]{:S(2)}) %collective-permute-start.5) | collective-permute-done | bytes 131104 | tf_op jit(solution)/shard_map/ppermute | solution.py:559
  24.6 1.5 %collective-permute-done.6.got = f32[4,2,128,128]{3,2,1,0:T(8,128)S(1)} collective-permute-done((f32[4,2,128,128]{3,2,1,0:T(8,128)S(1)}, f32[4,2,128,128]{3,2,1,0:T(8,128)S(1)}, u32[]{:S(2)}, u32[]{:S(2)}) %collective-permute-start.6) | collective-permute-done | bytes 524320 | tf_op jit(solution)/shard_map/ppermute | solution.py:591
  27.0 1.2 %collective-permute-start.11 = (f32[2,2,128,128]{3,2,1,0:T(8,128)S(1)}, f32[2,2,128,128]{3,2,1,0:T(8,128)S(1)}, u32[]{:S(2)}, u32[]{:S(2)}) collective-permute-start(f32[2,2,128,128]{3,2,1,0:T(8,128)S(1)} %get-tuple-element.137), channel_id=1, source_target_pairs={{0,4},{1,5},{2,6},{3,7},{4,0},{5,1},{6,2},{7,3},{8,12},{9,13},{10,... | collective-permute-start | bytes 786440 | tf_op jit(solution)/shard_map/ppermute | solution.py:595
  29.4 1.6 %collective-permute-done.7.rest_1_ = f32[128,256]{1,0:T(8,128)S(1)} collective-permute-done((f32[128,256]{1,0:T(8,128)S(1)}, f32[128,256]{1,0:T(8,128)S(1)}, u32[]{:S(2)}, u32[]{:S(2)}) %collective-permute-start.7) | collective-permute-done | bytes 131104 | tf_op jit(solution)/shard_map/ppermute | solution.py:559
  31.0 6.4 %collective-permute-done.8.rest_2_ = f32[128,256]{1,0:T(8,128)S(1)} collective-permute-done((f32[128,256]{1,0:T(8,128)S(1)}, f32[128,256]{1,0:T(8,128)S(1)}, u32[]{:S(2)}, u32[]{:S(2)}) %collective-permute-start.8) | collective-permute-done | bytes 131104 | tf_op jit(solution)/shard_map/ppermute | solution.py:559
  37.3 3.3 %collective-permute-done.9.rest_3_ = f32[128,256]{1,0:T(8,128)S(1)} collective-permute-done((f32[128,256]{1,0:T(8,128)S(1)}, f32[128,256]{1,0:T(8,128)S(1)}, u32[]{:S(2)}, u32[]{:S(2)}) %collective-permute-start.9) | collective-permute-done | bytes 131104 | tf_op jit(solution)/shard_map/ppermute | solution.py:559
  41.2 1.5 %collective-permute-start.13 = (f32[4,1,128,128]{3,2,1,0:T(8,128)S(1)}, f32[4,1,128,128]{3,2,1,0:T(8,128)S(1)}, u32[]{:S(2)}, u32[]{:S(2)}) collective-permute-start(f32[4,1,128,128]{3,2,1,0:T(8,128)S(1)} %get-tuple-element.144), channel_id=1, source_target_pairs={{0,1},{1,0},{2,3},{3,2},{4,5},{5,4},{6,7},{7,6},{8,9},{9,8},{10,11... | collective-permute-start | bytes 786440 | tf_op jit(solution)/shard_map/ppermute | solution.py:591
  46.6 1.9 %shard_map.109.early = f32[4,2,256,128]{3,2,1,0:T(8,128)S(1)} custom-call(bf16[2,512,256]{2,1,0:T(8,128)(2,1)S(1)} %copy-done.2, f32[256,8]{1,0:T(8,128)S(1)} %copy-done.4, f32[4,2,128,128]{3,2,1,0:T(8,128)S(1)} %get-tuple-element.153.own, f32[4,2,128,128]{3,2,1,0:T(8,128)S(1)} %collective-permute-done.6.got, ...), custom_call_target="tpu_custom_call" | custom-call | bytes 3416064 | tf_op jit(solution)/shard_map/pallas_call | solution.py:525
  48.9 3.3 %collective-permute-done.16.rest_2_ = f32[2,1,128,128]{3,2,1,0:T(8,128)S(1)} collective-permute-done((f32[2,1,128,128]{3,2,1,0:T(8,128)S(1)}, f32[2,1,128,128]{3,2,1,0:T(8,128)S(1)}, u32[]{:S(2)}, u32[]{:S(2)}) %collective-permute-start.16) | collective-permute-done | bytes 131104 | tf_op jit(solution)/shard_map/ppermute | solution.py:595
  52.2 3.4 %shard_map.110 = (f32[4,1,128,128]{3,2,1,0:T(8,128)S(1)}, f32[4,1,128,128]{3,2,1,0:T(8,128)S(1)}, f32[4,1,256,128]{3,2,1,0:T(8,128)S(1)}) custom-call(f32[5]{0:T(128)S(1)} %copy-done.6, f32[6]{0:T(128)S(1)} %copy-done.7, bf16[2,512,256]{2,1,0:T(8,128)(2,1)S(1)} %copy-done.2, f32[256,8]{1,0:T(8,128)S(1)} %copy-done.4, ...), custom_call_target="tpu_custom_call" | custom-call | bytes 3547180 | tf_op jit(solution)/shard_map/pallas_call | solution.py:525
  60.7 3.7 %shard_map.112 = (f32[4,2,128,128]{3,2,1,0:T(8,128)S(1)}, f32[4,2,128,128]{3,2,1,0:T(8,128)S(1)}) custom-call(f32[5]{0:T(128)S(1)} %copy-done.6, f32[6]{0:T(128)S(1)} %copy-done.7, bf16[2,512,256]{2,1,0:T(8,128)(2,1)S(1)} %copy-done.2, f32[256,8]{1,0:T(8,128)S(1)} %copy-done.4, f32[4,2,256,128]{3,2,1,0:T(8,128)S(1)} %shard_map.109.early, ...), custom_call_target="tpu_custom_call" | custom-call | bytes 3153964 | tf_op jit(solution)/shard_map/pallas_call | solution.py:525
  64.4 2.1 %collective-permute-done.20.rest_2_ = f32[2,1,128,128]{3,2,1,0:T(8,128)S(1)} collective-permute-done((f32[2,1,128,128]{3,2,1,0:T(8,128)S(1)}, f32[2,1,128,128]{3,2,1,0:T(8,128)S(1)}, u32[]{:S(2)}, u32[]{:S(2)}) %collective-permute-start.20) | collective-permute-done | bytes 131104 | tf_op jit(solution)/shard_map/ppermute | solution.py:595
  72.1 3.0 %collective-permute-start.29 = (f32[128,256]{1,0:T(8,128)S(1)}, f32[128,256]{1,0:T(8,128)S(1)}, u32[]{:S(2)}, u32[]{:S(2)}) collective-permute-start(f32[128,256]{1,0:T(8,128)S(1)} %get-tuple-element.196), channel_id=1, source_target_pairs={{0,16},{8,24},{16,0},{24,8},{1,17},{9,25},{17,1},{25,9},{2,18},{10... | collective-permute-start | bytes 393224 | tf_op jit(solution)/shard_map/ppermute | solution.py:559
  75.1 1.8 %collective-permute-done.22.rest_0_ = f32[2,2,128,128]{3,2,1,0:T(8,128)S(1)} collective-permute-done((f32[2,2,128,128]{3,2,1,0:T(8,128)S(1)}, f32[2,2,128,128]{3,2,1,0:T(8,128)S(1)}, u32[]{:S(2)}, u32[]{:S(2)}) %collective-permute-start.22) | collective-permute-done | bytes 262176 | tf_op jit(solution)/shard_map/ppermute | solution.py:595
  77.9 5.2 %collective-permute-done.24.rest_2_ = f32[2,2,128,128]{3,2,1,0:T(8,128)S(1)} collective-permute-done((f32[2,2,128,128]{3,2,1,0:T(8,128)S(1)}, f32[2,2,128,128]{3,2,1,0:T(8,128)S(1)}, u32[]{:S(2)}, u32[]{:S(2)}) %collective-permute-start.24) | collective-permute-done | bytes 262176 | tf_op jit(solution)/shard_map/ppermute | solution.py:595
  84.1 2.8 %collective-permute-start.26 = (f32[128,256]{1,0:T(8,128)S(1)}, f32[128,256]{1,0:T(8,128)S(1)}, u32[]{:S(2)}, u32[]{:S(2)}) collective-permute-start(f32[128,256]{1,0:T(8,128)S(1)} %get-tuple-element.192), channel_id=1, source_target_pairs={{0,16},{8,24},{16,0},{24,8},{1,17},{9,25},{17,1},{25,9},{2,18},{10... | collective-permute-start | bytes 393224 | tf_op jit(solution)/shard_map/ppermute | solution.py:559
  86.9 3.4 %collective-permute-start.31 = (f32[128,256]{1,0:T(8,128)S(1)}, f32[128,256]{1,0:T(8,128)S(1)}, u32[]{:S(2)}, u32[]{:S(2)}) collective-permute-start(f32[128,256]{1,0:T(8,128)S(1)} %get-tuple-element.199), channel_id=1, source_target_pairs={{8,16},{16,24},{9,17},{17,25},{10,18},{18,26},{11,19},{19,27},{12,... | collective-permute-start | bytes 393224 | tf_op jit(solution)/shard_map/ppermute | solution.py:559
  90.3 1.3 %collective-permute-start.32 = (f32[128,256]{1,0:T(8,128)S(1)}, f32[128,256]{1,0:T(8,128)S(1)}, u32[]{:S(2)}, u32[]{:S(2)}) collective-permute-start(f32[128,256]{1,0:T(8,128)S(1)} %get-tuple-element.200), channel_id=1, source_target_pairs={{8,24},{16,0},{9,25},{17,1},{10,26},{18,2},{11,27},{19,3},{12,28},... | collective-permute-start | bytes 393224 | tf_op jit(solution)/shard_map/ppermute | solution.py:559
  91.6 1.9 %collective-permute-start.33 = (f32[128,256]{1,0:T(8,128)S(1)}, f32[128,256]{1,0:T(8,128)S(1)}, u32[]{:S(2)}, u32[]{:S(2)}) collective-permute-start(f32[128,256]{1,0:T(8,128)S(1)} %get-tuple-element.201), channel_id=1, source_target_pairs={{8,0},{16,8},{9,1},{17,9},{10,2},{18,10},{11,3},{19,11},{12,4},{20... | collective-permute-start | bytes 393224 | tf_op jit(solution)/shard_map/ppermute | solution.py:559
  93.6 2.0 %collective-permute-done.26.rest_2_ = f32[128,256]{1,0:T(8,128)S(1)} collective-permute-done((f32[128,256]{1,0:T(8,128)S(1)}, f32[128,256]{1,0:T(8,128)S(1)}, u32[]{:S(2)}, u32[]{:S(2)}) %collective-permute-start.26) | collective-permute-done | bytes 131104 | tf_op jit(solution)/shard_map/ppermute | solution.py:559
  95.5 3.5 %collective-permute-done.27.rest_3_ = f32[128,256]{1,0:T(8,128)S(1)} collective-permute-done((f32[128,256]{1,0:T(8,128)S(1)}, f32[128,256]{1,0:T(8,128)S(1)}, u32[]{:S(2)}, u32[]{:S(2)}) %collective-permute-start.27) | collective-permute-done | bytes 131104 | tf_op jit(solution)/shard_map/ppermute | solution.py:559
  99.0 2.1 %shard_map.116 = (f32[6,2,128,256]{3,2,1,0:T(8,128)}, f32[6,2,128,256]{3,2,1,0:T(8,128)}) custom-call(f32[5]{0:T(128)S(1)} %copy-done.6, f32[6]{0:T(128)S(1)} %copy-done.7, s32[2,128,256]{2,1,0:T(8,128)S(1)} %copy-done.3, s32[2,8,16]{2,1,0:T(8,128)S(1)} %copy-done.5, f32[128,256]{1,0:T(8,128)S(1)} %get-tuple-element.190.rest_0_, ...), custom_call_target="tpu_custom_call" | custom-call | bytes 4457516 | tf_op jit(solution)/shard_map/pallas_call | solution.py:525
  101.2 3.5 %collective-permute-done.33.rest_11_ = f32[128,256]{1,0:T(8,128)S(1)} collective-permute-done((f32[128,256]{1,0:T(8,128)S(1)}, f32[128,256]{1,0:T(8,128)S(1)}, u32[]{:S(2)}, u32[]{:S(2)}) %collective-permute-start.33) | collective-permute-done | bytes 131104 | tf_op jit(solution)/shard_map/ppermute | solution.py:559
  104.7 1.9 %shard_map.117 = (f32[6,2,128,256]{3,2,1,0:T(8,128)}, f32[6,2,128,256]{3,2,1,0:T(8,128)}) custom-call(f32[5]{0:T(128)S(1)} %copy-done.6, f32[6]{0:T(128)S(1)} %copy-done.7, s32[2,128,256]{2,1,0:T(8,128)S(1)} %copy-done.3, s32[2,8,16]{2,1,0:T(8,128)S(1)} %copy-done.5, ...), custom_call_target="tpu_custom_call", output_to_operand_aliasing={{0}: (16, {}), {1}: (17, {})} | custom-call | bytes 8127532 | tf_op jit(solution)/shard_map/pallas_call | solution.py:525
  (66 shorter events, 22.3 us)
Async XLA Ops:
  2.7 7.1 %collective-permute-start = (f32[128,256]{1,0:T(8,128)S(1)}, f32[128,256]{1,0:T(8,128)S(1)}, u32[]{:S(2)}, u32[]{:S(2)}) collective-permute-start(f32[128,256]{1,0:T(8,128)S(1)} %get-tuple-element.104), channel_id=1, source_target_pairs={{0,8},{8,16},{16,24},{24,0},{1,9},{9,17},{17,25},{25,1},{2,10},{10... | collective-permute-start | bytes 393224 | tf_op jit(solution)/shard_map/ppermute | solution.py:559
  4.0 10.4 %collective-permute-start.1 = (f32[128,256]{1,0:T(8,128)S(1)}, f32[128,256]{1,0:T(8,128)S(1)}, u32[]{:S(2)}, u32[]{:S(2)}) collective-permute-start(f32[128,256]{1,0:T(8,128)S(1)} %get-tuple-element.105), channel_id=1, source_target_pairs={{0,16},{8,24},{16,0},{24,8},{1,17},{9,25},{17,1},{25,9},{2,18},{10... | collective-permute-start | bytes 393224 | tf_op jit(solution)/shard_map/ppermute | solution.py:559
  5.1 15.1 %collective-permute-start.2 = (f32[128,256]{1,0:T(8,128)S(1)}, f32[128,256]{1,0:T(8,128)S(1)}, u32[]{:S(2)}, u32[]{:S(2)}) collective-permute-start(f32[128,256]{1,0:T(8,128)S(1)} %get-tuple-element.106), channel_id=1, source_target_pairs={{0,24},{8,0},{16,8},{24,16},{1,25},{9,1},{17,9},{25,17},{2,26},{10... | collective-permute-start | bytes 393224 | tf_op jit(solution)/shard_map/ppermute | solution.py:559
  6.5 13.7 %collective-permute-start.3 = (f32[128,256]{1,0:T(8,128)S(1)}, f32[128,256]{1,0:T(8,128)S(1)}, u32[]{:S(2)}, u32[]{:S(2)}) collective-permute-start(f32[128,256]{1,0:T(8,128)S(1)} %get-tuple-element.108), channel_id=1, source_target_pairs={{0,8},{8,16},{1,9},{9,17},{2,10},{10,18},{3,11},{11,19},{4,12},{12... | collective-permute-start | bytes 393224 | tf_op jit(solution)/shard_map/ppermute | solution.py:559
  8.5 11.8 %collective-permute-start.4 = (f32[128,256]{1,0:T(8,128)S(1)}, f32[128,256]{1,0:T(8,128)S(1)}, u32[]{:S(2)}, u32[]{:S(2)}) collective-permute-start(f32[128,256]{1,0:T(8,128)S(1)} %get-tuple-element.109), channel_id=1, source_target_pairs={{0,16},{24,8},{1,17},{25,9},{2,18},{26,10},{3,19},{27,11},{4,20},{... | collective-permute-start | bytes 393224 | tf_op jit(solution)/shard_map/ppermute | solution.py:559
  9.8 13.2 %collective-permute-start.5 = (f32[128,256]{1,0:T(8,128)S(1)}, f32[128,256]{1,0:T(8,128)S(1)}, u32[]{:S(2)}, u32[]{:S(2)}) collective-permute-start(f32[128,256]{1,0:T(8,128)S(1)} %get-tuple-element.110), channel_id=1, source_target_pairs={{16,8},{24,16},{17,9},{25,17},{18,10},{26,18},{19,11},{27,19},{20,... | collective-permute-start | bytes 393224 | tf_op jit(solution)/shard_map/ppermute | solution.py:559
  26.2 4.8 %collective-permute-start.7 = (f32[128,256]{1,0:T(8,128)S(1)}, f32[128,256]{1,0:T(8,128)S(1)}, u32[]{:S(2)}, u32[]{:S(2)}) collective-permute-start(f32[128,256]{1,0:T(8,128)S(1)} %get-tuple-element.133), channel_id=1, source_target_pairs={{0,8},{8,16},{16,24},{24,0},{1,9},{9,17},{17,25},{25,1},{2,10},{10... | collective-permute-start | bytes 393224 | tf_op jit(solution)/shard_map/ppermute | solution.py:559
  26.7 13.9 %collective-permute-start.10 = (f32[2,2,128,128]{3,2,1,0:T(8,128)S(1)}, f32[2,2,128,128]{3,2,1,0:T(8,128)S(1)}, u32[]{:S(2)}, u32[]{:S(2)}) collective-permute-start(f32[2,2,128,128]{3,2,1,0:T(8,128)S(1)} %get-tuple-element.136), channel_id=1, source_target_pairs={{0,2},{1,3},{2,0},{3,1},{4,6},{5,7},{6,4},{7,5},{8,10},{9,11},{10,... | collective-permute-start | bytes 786440 | tf_op jit(solution)/shard_map/ppermute | solution.py:595
  27.0 13.6 %collective-permute-start.11 = (f32[2,2,128,128]{3,2,1,0:T(8,128)S(1)}, f32[2,2,128,128]{3,2,1,0:T(8,128)S(1)}, u32[]{:S(2)}, u32[]{:S(2)}) collective-permute-start(f32[2,2,128,128]{3,2,1,0:T(8,128)S(1)} %get-tuple-element.137), channel_id=1, source_target_pairs={{0,4},{1,5},{2,6},{3,7},{4,0},{5,1},{6,2},{7,3},{8,12},{9,13},{10,... | collective-permute-start | bytes 786440 | tf_op jit(solution)/shard_map/ppermute | solution.py:595
  28.2 12.4 %collective-permute-start.12 = (f32[2,2,128,128]{3,2,1,0:T(8,128)S(1)}, f32[2,2,128,128]{3,2,1,0:T(8,128)S(1)}, u32[]{:S(2)}, u32[]{:S(2)}) collective-permute-start(f32[2,2,128,128]{3,2,1,0:T(8,128)S(1)} %get-tuple-element.138), channel_id=1, source_target_pairs={{0,6},{1,7},{2,4},{3,5},{4,2},{5,3},{6,0},{7,1},{8,14},{9,15},{10,... | collective-permute-start | bytes 786440 | tf_op jit(solution)/shard_map/ppermute | solution.py:595
  29.4 8.0 %collective-permute-start.8 = (f32[128,256]{1,0:T(8,128)S(1)}, f32[128,256]{1,0:T(8,128)S(1)}, u32[]{:S(2)}, u32[]{:S(2)}) collective-permute-start(f32[128,256]{1,0:T(8,128)S(1)} %get-tuple-element.134), channel_id=1, source_target_pairs={{0,16},{8,24},{16,0},{24,8},{1,17},{9,25},{17,1},{25,9},{2,18},{10... | collective-permute-start | bytes 393224 | tf_op jit(solution)/shard_map/ppermute | solution.py:559
  31.0 9.6 %collective-permute-start.9 = (f32[128,256]{1,0:T(8,128)S(1)}, f32[128,256]{1,0:T(8,128)S(1)}, u32[]{:S(2)}, u32[]{:S(2)}) collective-permute-start(f32[128,256]{1,0:T(8,128)S(1)} %get-tuple-element.135), channel_id=1, source_target_pairs={{0,24},{8,0},{16,8},{24,16},{1,25},{9,1},{17,9},{25,17},{2,26},{10... | collective-permute-start | bytes 393224 | tf_op jit(solution)/shard_map/ppermute | solution.py:559
  41.2 2.6 %collective-permute-start.13 = (f32[4,1,128,128]{3,2,1,0:T(8,128)S(1)}, f32[4,1,128,128]{3,2,1,0:T(8,128)S(1)}, u32[]{:S(2)}, u32[]{:S(2)}) collective-permute-start(f32[4,1,128,128]{3,2,1,0:T(8,128)S(1)} %get-tuple-element.144), channel_id=1, source_target_pairs={{0,1},{1,0},{2,3},{3,2},{4,5},{5,4},{6,7},{7,6},{8,9},{9,8},{10,11... | collective-permute-start | bytes 786440 | tf_op jit(solution)/shard_map/ppermute | solution.py:591
  43.9 4.8 %collective-permute-start.14 = (f32[2,1,128,128]{3,2,1,0:T(8,128)S(1)}, f32[2,1,128,128]{3,2,1,0:T(8,128)S(1)}, u32[]{:S(2)}, u32[]{:S(2)}) collective-permute-start(f32[2,1,128,128]{3,2,1,0:T(8,128)S(1)} %get-tuple-element.158), channel_id=1, source_target_pairs={{0,2},{1,3},{2,0},{3,1},{4,6},{5,7},{6,4},{7,5},{8,10},{9,11},{10,... | collective-permute-start | bytes 393224 | tf_op jit(solution)/shard_map/ppermute | solution.py:595
  44.5 4.4 %collective-permute-start.15 = (f32[2,1,128,128]{3,2,1,0:T(8,128)S(1)}, f32[2,1,128,128]{3,2,1,0:T(8,128)S(1)}, u32[]{:S(2)}, u32[]{:S(2)}) collective-permute-start(f32[2,1,128,128]{3,2,1,0:T(8,128)S(1)} %get-tuple-element.159), channel_id=1, source_target_pairs={{0,4},{1,5},{2,6},{3,7},{4,0},{5,1},{6,2},{7,3},{8,12},{9,13},{10,... | collective-permute-start | bytes 393224 | tf_op jit(solution)/shard_map/ppermute | solution.py:595
  45.7 6.4 %collective-permute-start.16 = (f32[2,1,128,128]{3,2,1,0:T(8,128)S(1)}, f32[2,1,128,128]{3,2,1,0:T(8,128)S(1)}, u32[]{:S(2)}, u32[]{:S(2)}) collective-permute-start(f32[2,1,128,128]{3,2,1,0:T(8,128)S(1)} %get-tuple-element.160), channel_id=1, source_target_pairs={{0,6},{1,7},{2,4},{3,5},{4,2},{5,3},{6,0},{7,1},{8,14},{9,15},{10,... | collective-permute-start | bytes 393224 | tf_op jit(solution)/shard_map/ppermute | solution.py:595
  58.0 6.4 %collective-permute-start.18 = (f32[2,1,128,128]{3,2,1,0:T(8,128)S(1)}, f32[2,1,128,128]{3,2,1,0:T(8,128)S(1)}, u32[]{:S(2)}, u32[]{:S(2)}) collective-permute-start(f32[2,1,128,128]{3,2,1,0:T(8,128)S(1)} %get-tuple-element.170), channel_id=1, source_target_pairs={{0,2},{1,3},{2,0},{3,1},{4,6},{5,7},{6,4},{7,5},{8,10},{9,11},{10,... | collective-permute-start | bytes 393224 | tf_op jit(solution)/shard_map/ppermute | solution.py:595
  58.9 5.5 %collective-permute-start.19 = (f32[2,1,128,128]{3,2,1,0:T(8,128)S(1)}, f32[2,1,128,128]{3,2,1,0:T(8,128)S(1)}, u32[]{:S(2)}, u32[]{:S(2)}) collective-permute-start(f32[2,1,128,128]{3,2,1,0:T(8,128)S(1)} %get-tuple-element.171), channel_id=1, source_target_pairs={{0,4},{1,5},{2,6},{3,7},{4,0},{5,1},{6,2},{7,3},{8,12},{9,13},{10,... | collective-permute-start | bytes 393224 | tf_op jit(solution)/shard_map/ppermute | solution.py:595
  59.8 6.7 %collective-permute-start.20 = (f32[2,1,128,128]{3,2,1,0:T(8,128)S(1)}, f32[2,1,128,128]{3,2,1,0:T(8,128)S(1)}, u32[]{:S(2)}, u32[]{:S(2)}) collective-permute-start(f32[2,1,128,128]{3,2,1,0:T(8,128)S(1)} %get-tuple-element.172), channel_id=1, source_target_pairs={{0,6},{1,7},{2,4},{3,5},{4,2},{5,3},{6,0},{7,1},{8,14},{9,15},{10,... | collective-permute-start | bytes 393224 | tf_op jit(solution)/shard_map/ppermute | solution.py:595
  66.5 2.7 %collective-permute-start.21 = (f32[4,2,128,128]{3,2,1,0:T(8,128)S(1)}, f32[4,2,128,128]{3,2,1,0:T(8,128)S(1)}, u32[]{:S(2)}, u32[]{:S(2)}) collective-permute-start(f32[4,2,128,128]{3,2,1,0:T(8,128)S(1)} %get-tuple-element.174), channel_id=1, source_target_pairs={{0,1},{1,0},{2,3},{3,2},{4,5},{5,4},{6,7},{7,6},{8,9},{9,8},{10,11... | collective-permute-start | bytes 1572872 | tf_op jit(solution)/shard_map/ppermute | solution.py:591
  69.3 7.6 %collective-permute-start.22 = (f32[2,2,128,128]{3,2,1,0:T(8,128)S(1)}, f32[2,2,128,128]{3,2,1,0:T(8,128)S(1)}, u32[]{:S(2)}, u32[]{:S(2)}) collective-permute-start(f32[2,2,128,128]{3,2,1,0:T(8,128)S(1)} %get-tuple-element.187), channel_id=1, source_target_pairs={{0,2},{1,3},{2,0},{3,1},{4,6},{5,7},{6,4},{7,5},{8,10},{9,11},{10,... | collective-permute-start | bytes 786440 | tf_op jit(solution)/shard_map/ppermute | solution.py:595
  69.9 8.0 %collective-permute-start.23 = (f32[2,2,128,128]{3,2,1,0:T(8,128)S(1)}, f32[2,2,128,128]{3,2,1,0:T(8,128)S(1)}, u32[]{:S(2)}, u32[]{:S(2)}) collective-permute-start(f32[2,2,128,128]{3,2,1,0:T(8,128)S(1)} %get-tuple-element.188), channel_id=1, source_target_pairs={{0,4},{1,5},{2,6},{3,7},{4,0},{5,1},{6,2},{7,3},{8,12},{9,13},{10,... | collective-permute-start | bytes 786440 | tf_op jit(solution)/shard_map/ppermute | solution.py:595
  71.1 12.0 %collective-permute-start.24 = (f32[2,2,128,128]{3,2,1,0:T(8,128)S(1)}, f32[2,2,128,128]{3,2,1,0:T(8,128)S(1)}, u32[]{:S(2)}, u32[]{:S(2)}) collective-permute-start(f32[2,2,128,128]{3,2,1,0:T(8,128)S(1)} %get-tuple-element.189), channel_id=1, source_target_pairs={{0,6},{1,7},{2,4},{3,5},{4,2},{5,3},{6,0},{7,1},{8,14},{9,15},{10,... | collective-permute-start | bytes 786440 | tf_op jit(solution)/shard_map/ppermute | solution.py:595
  72.0 14.9 %collective-permute-start.28 = (f32[128,256]{1,0:T(8,128)S(1)}, f32[128,256]{1,0:T(8,128)S(1)}, u32[]{:S(2)}, u32[]{:S(2)}) collective-permute-start(f32[128,256]{1,0:T(8,128)S(1)} %get-tuple-element.195), channel_id=1, source_target_pairs={{0,8},{8,16},{16,24},{24,0},{1,9},{9,17},{17,25},{25,1},{2,10},{10... | collective-permute-start | bytes 393224 | tf_op jit(solution)/shard_map/ppermute | solution.py:559
  72.1 14.9 %collective-permute-start.29 = (f32[128,256]{1,0:T(8,128)S(1)}, f32[128,256]{1,0:T(8,128)S(1)}, u32[]{:S(2)}, u32[]{:S(2)}) collective-permute-start(f32[128,256]{1,0:T(8,128)S(1)} %get-tuple-element.196), channel_id=1, source_target_pairs={{0,16},{8,24},{16,0},{24,8},{1,17},{9,25},{17,1},{25,9},{2,18},{10... | collective-permute-start | bytes 393224 | tf_op jit(solution)/shard_map/ppermute | solution.py:559
  76.9 13.4 %collective-permute-start.30 = (f32[128,256]{1,0:T(8,128)S(1)}, f32[128,256]{1,0:T(8,128)S(1)}, u32[]{:S(2)}, u32[]{:S(2)}) collective-permute-start(f32[128,256]{1,0:T(8,128)S(1)} %get-tuple-element.197), channel_id=1, source_target_pairs={{0,24},{8,0},{16,8},{24,16},{1,25},{9,1},{17,9},{25,17},{2,26},{10... | collective-permute-start | bytes 393224 | tf_op jit(solution)/shard_map/ppermute | solution.py:559
  84.1 7.6 %collective-permute-start.25 = (f32[128,256]{1,0:T(8,128)S(1)}, f32[128,256]{1,0:T(8,128)S(1)}, u32[]{:S(2)}, u32[]{:S(2)}) collective-permute-start(f32[128,256]{1,0:T(8,128)S(1)} %get-tuple-element.191), channel_id=1, source_target_pairs={{0,8},{8,16},{16,24},{24,0},{1,9},{9,17},{17,25},{25,1},{2,10},{10... | collective-permute-start | bytes 393224 | tf_op jit(solution)/shard_map/ppermute | solution.py:559
  84.1 11.4 %collective-permute-start.26 = (f32[128,256]{1,0:T(8,128)S(1)}, f32[128,256]{1,0:T(8,128)S(1)}, u32[]{:S(2)}, u32[]{:S(2)}) collective-permute-start(f32[128,256]{1,0:T(8,128)S(1)} %get-tuple-element.192), channel_id=1, source_target_pairs={{0,16},{8,24},{16,0},{24,8},{1,17},{9,25},{17,1},{25,9},{2,18},{10... | collective-permute-start | bytes 393224 | tf_op jit(solution)/shard_map/ppermute | solution.py:559
  86.9 12.1 %collective-permute-start.27 = (f32[128,256]{1,0:T(8,128)S(1)}, f32[128,256]{1,0:T(8,128)S(1)}, u32[]{:S(2)}, u32[]{:S(2)}) collective-permute-start(f32[128,256]{1,0:T(8,128)S(1)} %get-tuple-element.193), channel_id=1, source_target_pairs={{0,24},{8,0},{16,8},{24,16},{1,25},{9,1},{17,9},{25,17},{2,26},{10... | collective-permute-start | bytes 393224 | tf_op jit(solution)/shard_map/ppermute | solution.py:559
  86.9 14.2 %collective-permute-start.31 = (f32[128,256]{1,0:T(8,128)S(1)}, f32[128,256]{1,0:T(8,128)S(1)}, u32[]{:S(2)}, u32[]{:S(2)}) collective-permute-start(f32[128,256]{1,0:T(8,128)S(1)} %get-tuple-element.199), channel_id=1, source_target_pairs={{8,16},{16,24},{9,17},{17,25},{10,18},{18,26},{11,19},{19,27},{12,... | collective-permute-start | bytes 393224 | tf_op jit(solution)/shard_map/ppermute | solution.py:559
  90.3 10.8 %collective-permute-start.32 = (f32[128,256]{1,0:T(8,128)S(1)}, f32[128,256]{1,0:T(8,128)S(1)}, u32[]{:S(2)}, u32[]{:S(2)}) collective-permute-start(f32[128,256]{1,0:T(8,128)S(1)} %get-tuple-element.200), channel_id=1, source_target_pairs={{8,24},{16,0},{9,25},{17,1},{10,26},{18,2},{11,27},{19,3},{12,28},... | collective-permute-start | bytes 393224 | tf_op jit(solution)/shard_map/ppermute | solution.py:559
  91.6 13.0 %collective-permute-start.33 = (f32[128,256]{1,0:T(8,128)S(1)}, f32[128,256]{1,0:T(8,128)S(1)}, u32[]{:S(2)}, u32[]{:S(2)}) collective-permute-start(f32[128,256]{1,0:T(8,128)S(1)} %get-tuple-element.201), channel_id=1, source_target_pairs={{8,0},{16,8},{9,1},{17,9},{10,2},{18,10},{11,3},{19,11},{12,4},{20... | collective-permute-start | bytes 393224 | tf_op jit(solution)/shard_map/ppermute | solution.py:559
  (10 other events, 155.8 us)

commit v9 on v8

--- a/solution.py
+++ b/solution.py
@@ -482,8 +482,13 @@
     size = cells_x // normals.shape[1]
     for step in range(parts):
         source = lax.rem(place + parts - step, parts)
-        for k, slot in enumerate(slots):
-            held[source, slot] = arrived[k * parts + step][...]
+        needed = functools.reduce(jnp.logical_or, [source == g for g in INPLANE]) if XZ in strain_parts else True
+
+        @pl.when(needed)
+        def _(source=source, step=step):
+            for k, slot in enumerate(slots):
+                held[source, slot] = arrived[k * parts + step][...]
+
     copies = []
     for section in range(sections):
         squares = tilt(normals, section, cells_z)
@@ -493,7 +498,7 @@
             local[YY] = jnp.full((size, cells_z), mean[YY], F32)
             for group, fields in enumerate(GROUPS):
                 for slot, (component, of) in enumerate(fields):
-                    if of == section and slot in slots:
+                    if of == section and slot in slots and (group in INPLANE or XZ not in strain_parts):
                         local[component] = held[group, slot, rows, :]
             value = law(
                 local,

time: 108 us -> 108 us (level)
  no operation moved by 1% of the time
where the time goes in v9:
time: 108 us; the launch traced here: 107 us
  waiting for transfers between devices  49.7 us (46%)
  starting transfers between devices  37.6 us (35%)
  Pallas kernels  18.3 us (17%)
    ppermute x18, waiting for transfers between devices, travel(): moved.append(lax.ppermute(blocks[step], 'gz', way))  32.1 us
    ppermute x18, starting transfers between devices, travel(): moved.append(lax.ppermute(blocks[step], 'gz', way))  22.4 us
    pallas_call x14, Pallas kernels, call(): pl.pallas_call(kernel, out_shape=[pltpu.HBM(o, F32) if k in hbm_out else...  18.3 us
    ppermute x12, waiting for transfers between devices, exchange(): lax.ppermute(block, 'gx', [(k, k ^ 2 * step) for k in range(x_devices)])  12.7 us
    ppermute x12, starting transfers between devices, exchange(): lax.ppermute(block, 'gx', [(k, k ^ 2 * step) for k in range(x_devices)])  10.8 us
    ppermute x4, waiting for transfers between devices, exchange(): got = lax.ppermute(swapped, 'gx', [(k, k ^ 1) for k in range(x_devices)])  4.8 us
    ppermute x4, starting transfers between devices, exchange(): got = lax.ppermute(swapped, 'gx', [(k, k ^ 1) for k in range(x_devices)])  4.39 us
  transfers between devices with their start and end apart: 34, of which 19 were waited for; matrix products, arithmetic and copies ran while one was open for 0% of the time, Pallas kernels for 9%

profile of v9, /device:TPU:11, one launch (start us, length us, event | category | flops | bytes accessed | tf_op | source)
XLA Modules:
  0.0 106.7 jit_solution(2701945228215696298)
XLA Ops:
  0.6 2.0 %shard_map.104 = (f32[128,256]{1,0:T(8,128)S(1)}, f32[128,256]{1,0:T(8,128)S(1)}, f32[128,256]{1,0:T(8,128)S(1)}, f32[128,256]{1,0:T(8,128)S(1)}, f32[128,256]{1...) custom-call(f32[5]{0:T(128)} %moduli.7, ...), custom_call_target="tpu_custom_call" | custom-call | bytes 3408916 | tf_op jit(solution)/shard_map/pallas_call | solution.py:530
  2.7 1.4 %collective-permute-start = (f32[128,256]{1,0:T(8,128)S(1)}, f32[128,256]{1,0:T(8,128)S(1)}, u32[]{:S(2)}, u32[]{:S(2)}) collective-permute-start(f32[128,256]{1,0:T(8,128)S(1)} %get-tuple-element.104), channel_id=1, source_target_pairs={{0,8},{8,16},{16,24},{24,0},{1,9},{9,17},{17,25},{25,1},{2,10},{10... | collective-permute-start | bytes 393224 | tf_op jit(solution)/shard_map/ppermute | solution.py:564
  5.1 1.4 %collective-permute-start.2 = (f32[128,256]{1,0:T(8,128)S(1)}, f32[128,256]{1,0:T(8,128)S(1)}, u32[]{:S(2)}, u32[]{:S(2)}) collective-permute-start(f32[128,256]{1,0:T(8,128)S(1)} %get-tuple-element.106), channel_id=1, source_target_pairs={{0,24},{8,0},{16,8},{24,16},{1,25},{9,1},{17,9},{25,17},{2,26},{10... | collective-permute-start | bytes 393224 | tf_op jit(solution)/shard_map/ppermute | solution.py:564
  6.5 2.0 %collective-permute-start.3 = (f32[128,256]{1,0:T(8,128)S(1)}, f32[128,256]{1,0:T(8,128)S(1)}, u32[]{:S(2)}, u32[]{:S(2)}) collective-permute-start(f32[128,256]{1,0:T(8,128)S(1)} %get-tuple-element.108), channel_id=1, source_target_pairs={{0,8},{8,16},{1,9},{9,17},{2,10},{10,18},{3,11},{11,19},{4,12},{12... | collective-permute-start | bytes 393224 | tf_op jit(solution)/shard_map/ppermute | solution.py:564
  8.5 1.3 %collective-permute-start.4 = (f32[128,256]{1,0:T(8,128)S(1)}, f32[128,256]{1,0:T(8,128)S(1)}, u32[]{:S(2)}, u32[]{:S(2)}) collective-permute-start(f32[128,256]{1,0:T(8,128)S(1)} %get-tuple-element.109), channel_id=1, source_target_pairs={{0,16},{24,8},{1,17},{25,9},{2,18},{26,10},{3,19},{27,11},{4,20},{... | collective-permute-start | bytes 393224 | tf_op jit(solution)/shard_map/ppermute | solution.py:564
  9.8 1.3 %collective-permute-start.5 = (f32[128,256]{1,0:T(8,128)S(1)}, f32[128,256]{1,0:T(8,128)S(1)}, u32[]{:S(2)}, u32[]{:S(2)}) collective-permute-start(f32[128,256]{1,0:T(8,128)S(1)} %get-tuple-element.110), channel_id=1, source_target_pairs={{16,8},{24,16},{17,9},{25,17},{18,10},{26,18},{19,11},{27,19},{20,... | collective-permute-start | bytes 393224 | tf_op jit(solution)/shard_map/ppermute | solution.py:564
  11.1 3.4 %collective-permute-done.1.rest_2_ = f32[128,256]{1,0:T(8,128)S(1)} collective-permute-done((f32[128,256]{1,0:T(8,128)S(1)}, f32[128,256]{1,0:T(8,128)S(1)}, u32[]{:S(2)}, u32[]{:S(2)}) %collective-permute-start.1) | collective-permute-done | bytes 131104 | tf_op jit(solution)/shard_map/ppermute | solution.py:564
  14.5 5.8 %collective-permute-done.2.rest_3_ = f32[128,256]{1,0:T(8,128)S(1)} collective-permute-done((f32[128,256]{1,0:T(8,128)S(1)}, f32[128,256]{1,0:T(8,128)S(1)}, u32[]{:S(2)}, u32[]{:S(2)}) %collective-permute-start.2) | collective-permute-done | bytes 131104 | tf_op jit(solution)/shard_map/ppermute | solution.py:564
  20.2 2.8 %collective-permute-done.5.rest_7_ = f32[128,256]{1,0:T(8,128)S(1)} collective-permute-done((f32[128,256]{1,0:T(8,128)S(1)}, f32[128,256]{1,0:T(8,128)S(1)}, u32[]{:S(2)}, u32[]{:S(2)}) %collective-permute-start.5) | collective-permute-done | bytes 131104 | tf_op jit(solution)/shard_map/ppermute | solution.py:564
  24.6 1.5 %collective-permute-done.6.got = f32[4,2,128,128]{3,2,1,0:T(8,128)S(1)} collective-permute-done((f32[4,2,128,128]{3,2,1,0:T(8,128)S(1)}, f32[4,2,128,128]{3,2,1,0:T(8,128)S(1)}, u32[]{:S(2)}, u32[]{:S(2)}) %collective-permute-start.6) | collective-permute-done | bytes 524320 | tf_op jit(solution)/shard_map/ppermute | solution.py:596
  27.0 1.2 %collective-permute-start.11 = (f32[2,2,128,128]{3,2,1,0:T(8,128)S(1)}, f32[2,2,128,128]{3,2,1,0:T(8,128)S(1)}, u32[]{:S(2)}, u32[]{:S(2)}) collective-permute-start(f32[2,2,128,128]{3,2,1,0:T(8,128)S(1)} %get-tuple-element.137), channel_id=1, source_target_pairs={{0,4},{1,5},{2,6},{3,7},{4,0},{5,1},{6,2},{7,3},{8,12},{9,13},{10,... | collective-permute-start | bytes 786440 | tf_op jit(solution)/shard_map/ppermute | solution.py:600
  29.4 1.6 %collective-permute-done.7.rest_1_ = f32[128,256]{1,0:T(8,128)S(1)} collective-permute-done((f32[128,256]{1,0:T(8,128)S(1)}, f32[128,256]{1,0:T(8,128)S(1)}, u32[]{:S(2)}, u32[]{:S(2)}) %collective-permute-start.7) | collective-permute-done | bytes 131104 | tf_op jit(solution)/shard_map/ppermute | solution.py:564
  31.0 6.4 %collective-permute-done.8.rest_2_ = f32[128,256]{1,0:T(8,128)S(1)} collective-permute-done((f32[128,256]{1,0:T(8,128)S(1)}, f32[128,256]{1,0:T(8,128)S(1)}, u32[]{:S(2)}, u32[]{:S(2)}) %collective-permute-start.8) | collective-permute-done | bytes 131104 | tf_op jit(solution)/shard_map/ppermute | solution.py:564
  37.3 3.3 %collective-permute-done.9.rest_3_ = f32[128,256]{1,0:T(8,128)S(1)} collective-permute-done((f32[128,256]{1,0:T(8,128)S(1)}, f32[128,256]{1,0:T(8,128)S(1)}, u32[]{:S(2)}, u32[]{:S(2)}) %collective-permute-start.9) | collective-permute-done | bytes 131104 | tf_op jit(solution)/shard_map/ppermute | solution.py:564
  41.2 1.5 %collective-permute-start.13 = (f32[4,1,128,128]{3,2,1,0:T(8,128)S(1)}, f32[4,1,128,128]{3,2,1,0:T(8,128)S(1)}, u32[]{:S(2)}, u32[]{:S(2)}) collective-permute-start(f32[4,1,128,128]{3,2,1,0:T(8,128)S(1)} %get-tuple-element.144), channel_id=1, source_target_pairs={{0,1},{1,0},{2,3},{3,2},{4,5},{5,4},{6,7},{7,6},{8,9},{9,8},{10,11... | collective-permute-start | bytes 786440 | tf_op jit(solution)/shard_map/ppermute | solution.py:596
  46.6 1.9 %shard_map.109.early = f32[4,2,256,128]{3,2,1,0:T(8,128)S(1)} custom-call(bf16[2,512,256]{2,1,0:T(8,128)(2,1)S(1)} %copy-done.2, f32[256,8]{1,0:T(8,128)S(1)} %copy-done.4, f32[4,2,128,128]{3,2,1,0:T(8,128)S(1)} %get-tuple-element.153.own, f32[4,2,128,128]{3,2,1,0:T(8,128)S(1)} %collective-permute-done.6.got, ...), custom_call_target="tpu_custom_call" | custom-call | bytes 3416064 | tf_op jit(solution)/shard_map/pallas_call | solution.py:530
  48.9 3.3 %collective-permute-done.16.rest_2_ = f32[2,1,128,128]{3,2,1,0:T(8,128)S(1)} collective-permute-done((f32[2,1,128,128]{3,2,1,0:T(8,128)S(1)}, f32[2,1,128,128]{3,2,1,0:T(8,128)S(1)}, u32[]{:S(2)}, u32[]{:S(2)}) %collective-permute-start.16) | collective-permute-done | bytes 131104 | tf_op jit(solution)/shard_map/ppermute | solution.py:600
  52.2 3.4 %shard_map.110 = (f32[4,1,128,128]{3,2,1,0:T(8,128)S(1)}, f32[4,1,128,128]{3,2,1,0:T(8,128)S(1)}, f32[4,1,256,128]{3,2,1,0:T(8,128)S(1)}) custom-call(f32[5]{0:T(128)S(1)} %copy-done.6, f32[6]{0:T(128)S(1)} %copy-done.7, bf16[2,512,256]{2,1,0:T(8,128)(2,1)S(1)} %copy-done.2, f32[256,8]{1,0:T(8,128)S(1)} %copy-done.4, ...), custom_call_target="tpu_custom_call" | custom-call | bytes 3547180 | tf_op jit(solution)/shard_map/pallas_call | solution.py:530
  60.7 3.7 %shard_map.112 = (f32[4,2,128,128]{3,2,1,0:T(8,128)S(1)}, f32[4,2,128,128]{3,2,1,0:T(8,128)S(1)}) custom-call(f32[5]{0:T(128)S(1)} %copy-done.6, f32[6]{0:T(128)S(1)} %copy-done.7, bf16[2,512,256]{2,1,0:T(8,128)(2,1)S(1)} %copy-done.2, f32[256,8]{1,0:T(8,128)S(1)} %copy-done.4, f32[4,2,256,128]{3,2,1,0:T(8,128)S(1)} %shard_map.109.early, ...), custom_call_target="tpu_custom_call" | custom-call | bytes 3153964 | tf_op jit(solution)/shard_map/pallas_call | solution.py:530
  64.4 2.1 %collective-permute-done.20.rest_2_ = f32[2,1,128,128]{3,2,1,0:T(8,128)S(1)} collective-permute-done((f32[2,1,128,128]{3,2,1,0:T(8,128)S(1)}, f32[2,1,128,128]{3,2,1,0:T(8,128)S(1)}, u32[]{:S(2)}, u32[]{:S(2)}) %collective-permute-start.20) | collective-permute-done | bytes 131104 | tf_op jit(solution)/shard_map/ppermute | solution.py:600
  72.1 3.0 %collective-permute-start.29 = (f32[128,256]{1,0:T(8,128)S(1)}, f32[128,256]{1,0:T(8,128)S(1)}, u32[]{:S(2)}, u32[]{:S(2)}) collective-permute-start(f32[128,256]{1,0:T(8,128)S(1)} %get-tuple-element.196), channel_id=1, source_target_pairs={{0,16},{8,24},{16,0},{24,8},{1,17},{9,25},{17,1},{25,9},{2,18},{10... | collective-permute-start | bytes 393224 | tf_op jit(solution)/shard_map/ppermute | solution.py:564
  75.1 1.8 %collective-permute-done.22.rest_0_ = f32[2,2,128,128]{3,2,1,0:T(8,128)S(1)} collective-permute-done((f32[2,2,128,128]{3,2,1,0:T(8,128)S(1)}, f32[2,2,128,128]{3,2,1,0:T(8,128)S(1)}, u32[]{:S(2)}, u32[]{:S(2)}) %collective-permute-start.22) | collective-permute-done | bytes 262176 | tf_op jit(solution)/shard_map/ppermute | solution.py:600
  77.9 5.2 %collective-permute-done.24.rest_2_ = f32[2,2,128,128]{3,2,1,0:T(8,128)S(1)} collective-permute-done((f32[2,2,128,128]{3,2,1,0:T(8,128)S(1)}, f32[2,2,128,128]{3,2,1,0:T(8,128)S(1)}, u32[]{:S(2)}, u32[]{:S(2)}) %collective-permute-start.24) | collective-permute-done | bytes 262176 | tf_op jit(solution)/shard_map/ppermute | solution.py:600
  84.1 2.8 %collective-permute-start.26 = (f32[128,256]{1,0:T(8,128)S(1)}, f32[128,256]{1,0:T(8,128)S(1)}, u32[]{:S(2)}, u32[]{:S(2)}) collective-permute-start(f32[128,256]{1,0:T(8,128)S(1)} %get-tuple-element.192), channel_id=1, source_target_pairs={{0,16},{8,24},{16,0},{24,8},{1,17},{9,25},{17,1},{25,9},{2,18},{10... | collective-permute-start | bytes 393224 | tf_op jit(solution)/shard_map/ppermute | solution.py:564
  86.9 3.4 %collective-permute-start.31 = (f32[128,256]{1,0:T(8,128)S(1)}, f32[128,256]{1,0:T(8,128)S(1)}, u32[]{:S(2)}, u32[]{:S(2)}) collective-permute-start(f32[128,256]{1,0:T(8,128)S(1)} %get-tuple-element.199), channel_id=1, source_target_pairs={{8,16},{16,24},{9,17},{17,25},{10,18},{18,26},{11,19},{19,27},{12,... | collective-permute-start | bytes 393224 | tf_op jit(solution)/shard_map/ppermute | solution.py:564
  90.3 1.3 %collective-permute-start.32 = (f32[128,256]{1,0:T(8,128)S(1)}, f32[128,256]{1,0:T(8,128)S(1)}, u32[]{:S(2)}, u32[]{:S(2)}) collective-permute-start(f32[128,256]{1,0:T(8,128)S(1)} %get-tuple-element.200), channel_id=1, source_target_pairs={{8,24},{16,0},{9,25},{17,1},{10,26},{18,2},{11,27},{19,3},{12,28},... | collective-permute-start | bytes 393224 | tf_op jit(solution)/shard_map/ppermute | solution.py:564
  91.6 1.9 %collective-permute-start.33 = (f32[128,256]{1,0:T(8,128)S(1)}, f32[128,256]{1,0:T(8,128)S(1)}, u32[]{:S(2)}, u32[]{:S(2)}) collective-permute-start(f32[128,256]{1,0:T(8,128)S(1)} %get-tuple-element.201), channel_id=1, source_target_pairs={{8,0},{16,8},{9,1},{17,9},{10,2},{18,10},{11,3},{19,11},{12,4},{20... | collective-permute-start | bytes 393224 | tf_op jit(solution)/shard_map/ppermute | solution.py:564
  93.6 2.0 %collective-permute-done.26.rest_2_ = f32[128,256]{1,0:T(8,128)S(1)} collective-permute-done((f32[128,256]{1,0:T(8,128)S(1)}, f32[128,256]{1,0:T(8,128)S(1)}, u32[]{:S(2)}, u32[]{:S(2)}) %collective-permute-start.26) | collective-permute-done | bytes 131104 | tf_op jit(solution)/shard_map/ppermute | solution.py:564
  95.5 3.5 %collective-permute-done.27.rest_3_ = f32[128,256]{1,0:T(8,128)S(1)} collective-permute-done((f32[128,256]{1,0:T(8,128)S(1)}, f32[128,256]{1,0:T(8,128)S(1)}, u32[]{:S(2)}, u32[]{:S(2)}) %collective-permute-start.27) | collective-permute-done | bytes 131104 | tf_op jit(solution)/shard_map/ppermute | solution.py:564
  99.0 2.1 %shard_map.116 = (f32[6,2,128,256]{3,2,1,0:T(8,128)}, f32[6,2,128,256]{3,2,1,0:T(8,128)}) custom-call(f32[5]{0:T(128)S(1)} %copy-done.6, f32[6]{0:T(128)S(1)} %copy-done.7, s32[2,128,256]{2,1,0:T(8,128)S(1)} %copy-done.3, s32[2,8,16]{2,1,0:T(8,128)S(1)} %copy-done.5, f32[128,256]{1,0:T(8,128)S(1)} %get-tuple-element.190.rest_0_, ...), custom_call_target="tpu_custom_call" | custom-call | bytes 4457516 | tf_op jit(solution)/shard_map/pallas_call | solution.py:530
  101.2 3.5 %collective-permute-done.33.rest_11_ = f32[128,256]{1,0:T(8,128)S(1)} collective-permute-done((f32[128,256]{1,0:T(8,128)S(1)}, f32[128,256]{1,0:T(8,128)S(1)}, u32[]{:S(2)}, u32[]{:S(2)}) %collective-permute-start.33) | collective-permute-done | bytes 131104 | tf_op jit(solution)/shard_map/ppermute | solution.py:564
  104.7 1.9 %shard_map.117 = (f32[6,2,128,256]{3,2,1,0:T(8,128)}, f32[6,2,128,256]{3,2,1,0:T(8,128)}) custom-call(f32[5]{0:T(128)S(1)} %copy-done.6, f32[6]{0:T(128)S(1)} %copy-done.7, s32[2,128,256]{2,1,0:T(8,128)S(1)} %copy-done.3, s32[2,8,16]{2,1,0:T(8,128)S(1)} %copy-done.5, ...), custom_call_target="tpu_custom_call", output_to_operand_aliasing={{0}: (16, {}), {1}: (17, {})} | custom-call | bytes 8127532 | tf_op jit(solution)/shard_map/pallas_call | solution.py:530
  (66 shorter events, 22.3 us)
Async XLA Ops:
  2.7 7.1 %collective-permute-start = (f32[128,256]{1,0:T(8,128)S(1)}, f32[128,256]{1,0:T(8,128)S(1)}, u32[]{:S(2)}, u32[]{:S(2)}) collective-permute-start(f32[128,256]{1,0:T(8,128)S(1)} %get-tuple-element.104), channel_id=1, source_target_pairs={{0,8},{8,16},{16,24},{24,0},{1,9},{9,17},{17,25},{25,1},{2,10},{10... | collective-permute-start | bytes 393224 | tf_op jit(solution)/shard_map/ppermute | solution.py:564
  4.0 10.4 %collective-permute-start.1 = (f32[128,256]{1,0:T(8,128)S(1)}, f32[128,256]{1,0:T(8,128)S(1)}, u32[]{:S(2)}, u32[]{:S(2)}) collective-permute-start(f32[128,256]{1,0:T(8,128)S(1)} %get-tuple-element.105), channel_id=1, source_target_pairs={{0,16},{8,24},{16,0},{24,8},{1,17},{9,25},{17,1},{25,9},{2,18},{10... | collective-permute-start | bytes 393224 | tf_op jit(solution)/shard_map/ppermute | solution.py:564
  5.1 15.1 %collective-permute-start.2 = (f32[128,256]{1,0:T(8,128)S(1)}, f32[128,256]{1,0:T(8,128)S(1)}, u32[]{:S(2)}, u32[]{:S(2)}) collective-permute-start(f32[128,256]{1,0:T(8,128)S(1)} %get-tuple-element.106), channel_id=1, source_target_pairs={{0,24},{8,0},{16,8},{24,16},{1,25},{9,1},{17,9},{25,17},{2,26},{10... | collective-permute-start | bytes 393224 | tf_op jit(solution)/shard_map/ppermute | solution.py:564
  6.5 13.7 %collective-permute-start.3 = (f32[128,256]{1,0:T(8,128)S(1)}, f32[128,256]{1,0:T(8,128)S(1)}, u32[]{:S(2)}, u32[]{:S(2)}) collective-permute-start(f32[128,256]{1,0:T(8,128)S(1)} %get-tuple-element.108), channel_id=1, source_target_pairs={{0,8},{8,16},{1,9},{9,17},{2,10},{10,18},{3,11},{11,19},{4,12},{12... | collective-permute-start | bytes 393224 | tf_op jit(solution)/shard_map/ppermute | solution.py:564
  8.5 11.8 %collective-permute-start.4 = (f32[128,256]{1,0:T(8,128)S(1)}, f32[128,256]{1,0:T(8,128)S(1)}, u32[]{:S(2)}, u32[]{:S(2)}) collective-permute-start(f32[128,256]{1,0:T(8,128)S(1)} %get-tuple-element.109), channel_id=1, source_target_pairs={{0,16},{24,8},{1,17},{25,9},{2,18},{26,10},{3,19},{27,11},{4,20},{... | collective-permute-start | bytes 393224 | tf_op jit(solution)/shard_map/ppermute | solution.py:564
  9.8 13.2 %collective-permute-start.5 = (f32[128,256]{1,0:T(8,128)S(1)}, f32[128,256]{1,0:T(8,128)S(1)}, u32[]{:S(2)}, u32[]{:S(2)}) collective-permute-start(f32[128,256]{1,0:T(8,128)S(1)} %get-tuple-element.110), channel_id=1, source_target_pairs={{16,8},{24,16},{17,9},{25,17},{18,10},{26,18},{19,11},{27,19},{20,... | collective-permute-start | bytes 393224 | tf_op jit(solution)/shard_map/ppermute | solution.py:564
  26.2 4.8 %collective-permute-start.7 = (f32[128,256]{1,0:T(8,128)S(1)}, f32[128,256]{1,0:T(8,128)S(1)}, u32[]{:S(2)}, u32[]{:S(2)}) collective-permute-start(f32[128,256]{1,0:T(8,128)S(1)} %get-tuple-element.133), channel_id=1, source_target_pairs={{0,8},{8,16},{16,24},{24,0},{1,9},{9,17},{17,25},{25,1},{2,10},{10... | collective-permute-start | bytes 393224 | tf_op jit(solution)/shard_map/ppermute | solution.py:564
  26.7 13.9 %collective-permute-start.10 = (f32[2,2,128,128]{3,2,1,0:T(8,128)S(1)}, f32[2,2,128,128]{3,2,1,0:T(8,128)S(1)}, u32[]{:S(2)}, u32[]{:S(2)}) collective-permute-start(f32[2,2,128,128]{3,2,1,0:T(8,128)S(1)} %get-tuple-element.136), channel_id=1, source_target_pairs={{0,2},{1,3},{2,0},{3,1},{4,6},{5,7},{6,4},{7,5},{8,10},{9,11},{10,... | collective-permute-start | bytes 786440 | tf_op jit(solution)/shard_map/ppermute | solution.py:600
  27.0 13.6 %collective-permute-start.11 = (f32[2,2,128,128]{3,2,1,0:T(8,128)S(1)}, f32[2,2,128,128]{3,2,1,0:T(8,128)S(1)}, u32[]{:S(2)}, u32[]{:S(2)}) collective-permute-start(f32[2,2,128,128]{3,2,1,0:T(8,128)S(1)} %get-tuple-element.137), channel_id=1, source_target_pairs={{0,4},{1,5},{2,6},{3,7},{4,0},{5,1},{6,2},{7,3},{8,12},{9,13},{10,... | collective-permute-start | bytes 786440 | tf_op jit(solution)/shard_map/ppermute | solution.py:600
  28.2 12.4 %collective-permute-start.12 = (f32[2,2,128,128]{3,2,1,0:T(8,128)S(1)}, f32[2,2,128,128]{3,2,1,0:T(8,128)S(1)}, u32[]{:S(2)}, u32[]{:S(2)}) collective-permute-start(f32[2,2,128,128]{3,2,1,0:T(8,128)S(1)} %get-tuple-element.138), channel_id=1, source_target_pairs={{0,6},{1,7},{2,4},{3,5},{4,2},{5,3},{6,0},{7,1},{8,14},{9,15},{10,... | collective-permute-start | bytes 786440 | tf_op jit(solution)/shard_map/ppermute | solution.py:600
  29.4 8.0 %collective-permute-start.8 = (f32[128,256]{1,0:T(8,128)S(1)}, f32[128,256]{1,0:T(8,128)S(1)}, u32[]{:S(2)}, u32[]{:S(2)}) collective-permute-start(f32[128,256]{1,0:T(8,128)S(1)} %get-tuple-element.134), channel_id=1, source_target_pairs={{0,16},{8,24},{16,0},{24,8},{1,17},{9,25},{17,1},{25,9},{2,18},{10... | collective-permute-start | bytes 393224 | tf_op jit(solution)/shard_map/ppermute | solution.py:564
  31.0 9.6 %collective-permute-start.9 = (f32[128,256]{1,0:T(8,128)S(1)}, f32[128,256]{1,0:T(8,128)S(1)}, u32[]{:S(2)}, u32[]{:S(2)}) collective-permute-start(f32[128,256]{1,0:T(8,128)S(1)} %get-tuple-element.135), channel_id=1, source_target_pairs={{0,24},{8,0},{16,8},{24,16},{1,25},{9,1},{17,9},{25,17},{2,26},{10... | collective-permute-start | bytes 393224 | tf_op jit(solution)/shard_map/ppermute | solution.py:564
  41.2 2.6 %collective-permute-start.13 = (f32[4,1,128,128]{3,2,1,0:T(8,128)S(1)}, f32[4,1,128,128]{3,2,1,0:T(8,128)S(1)}, u32[]{:S(2)}, u32[]{:S(2)}) collective-permute-start(f32[4,1,128,128]{3,2,1,0:T(8,128)S(1)} %get-tuple-element.144), channel_id=1, source_target_pairs={{0,1},{1,0},{2,3},{3,2},{4,5},{5,4},{6,7},{7,6},{8,9},{9,8},{10,11... | collective-permute-start | bytes 786440 | tf_op jit(solution)/shard_map/ppermute | solution.py:596
  43.9 4.8 %collective-permute-start.14 = (f32[2,1,128,128]{3,2,1,0:T(8,128)S(1)}, f32[2,1,128,128]{3,2,1,0:T(8,128)S(1)}, u32[]{:S(2)}, u32[]{:S(2)}) collective-permute-start(f32[2,1,128,128]{3,2,1,0:T(8,128)S(1)} %get-tuple-element.158), channel_id=1, source_target_pairs={{0,2},{1,3},{2,0},{3,1},{4,6},{5,7},{6,4},{7,5},{8,10},{9,11},{10,... | collective-permute-start | bytes 393224 | tf_op jit(solution)/shard_map/ppermute | solution.py:600
  44.5 4.4 %collective-permute-start.15 = (f32[2,1,128,128]{3,2,1,0:T(8,128)S(1)}, f32[2,1,128,128]{3,2,1,0:T(8,128)S(1)}, u32[]{:S(2)}, u32[]{:S(2)}) collective-permute-start(f32[2,1,128,128]{3,2,1,0:T(8,128)S(1)} %get-tuple-element.159), channel_id=1, source_target_pairs={{0,4},{1,5},{2,6},{3,7},{4,0},{5,1},{6,2},{7,3},{8,12},{9,13},{10,... | collective-permute-start | bytes 393224 | tf_op jit(solution)/shard_map/ppermute | solution.py:600
  45.7 6.4 %collective-permute-start.16 = (f32[2,1,128,128]{3,2,1,0:T(8,128)S(1)}, f32[2,1,128,128]{3,2,1,0:T(8,128)S(1)}, u32[]{:S(2)}, u32[]{:S(2)}) collective-permute-start(f32[2,1,128,128]{3,2,1,0:T(8,128)S(1)} %get-tuple-element.160), channel_id=1, source_target_pairs={{0,6},{1,7},{2,4},{3,5},{4,2},{5,3},{6,0},{7,1},{8,14},{9,15},{10,... | collective-permute-start | bytes 393224 | tf_op jit(solution)/shard_map/ppermute | solution.py:600
  58.0 6.4 %collective-permute-start.18 = (f32[2,1,128,128]{3,2,1,0:T(8,128)S(1)}, f32[2,1,128,128]{3,2,1,0:T(8,128)S(1)}, u32[]{:S(2)}, u32[]{:S(2)}) collective-permute-start(f32[2,1,128,128]{3,2,1,0:T(8,128)S(1)} %get-tuple-element.170), channel_id=1, source_target_pairs={{0,2},{1,3},{2,0},{3,1},{4,6},{5,7},{6,4},{7,5},{8,10},{9,11},{10,... | collective-permute-start | bytes 393224 | tf_op jit(solution)/shard_map/ppermute | solution.py:600
  58.9 5.5 %collective-permute-start.19 = (f32[2,1,128,128]{3,2,1,0:T(8,128)S(1)}, f32[2,1,128,128]{3,2,1,0:T(8,128)S(1)}, u32[]{:S(2)}, u32[]{:S(2)}) collective-permute-start(f32[2,1,128,128]{3,2,1,0:T(8,128)S(1)} %get-tuple-element.171), channel_id=1, source_target_pairs={{0,4},{1,5},{2,6},{3,7},{4,0},{5,1},{6,2},{7,3},{8,12},{9,13},{10,... | collective-permute-start | bytes 393224 | tf_op jit(solution)/shard_map/ppermute | solution.py:600
  59.8 6.7 %collective-permute-start.20 = (f32[2,1,128,128]{3,2,1,0:T(8,128)S(1)}, f32[2,1,128,128]{3,2,1,0:T(8,128)S(1)}, u32[]{:S(2)}, u32[]{:S(2)}) collective-permute-start(f32[2,1,128,128]{3,2,1,0:T(8,128)S(1)} %get-tuple-element.172), channel_id=1, source_target_pairs={{0,6},{1,7},{2,4},{3,5},{4,2},{5,3},{6,0},{7,1},{8,14},{9,15},{10,... | collective-permute-start | bytes 393224 | tf_op jit(solution)/shard_map/ppermute | solution.py:600
  66.5 2.7 %collective-permute-start.21 = (f32[4,2,128,128]{3,2,1,0:T(8,128)S(1)}, f32[4,2,128,128]{3,2,1,0:T(8,128)S(1)}, u32[]{:S(2)}, u32[]{:S(2)}) collective-permute-start(f32[4,2,128,128]{3,2,1,0:T(8,128)S(1)} %get-tuple-element.174), channel_id=1, source_target_pairs={{0,1},{1,0},{2,3},{3,2},{4,5},{5,4},{6,7},{7,6},{8,9},{9,8},{10,11... | collective-permute-start | bytes 1572872 | tf_op jit(solution)/shard_map/ppermute | solution.py:596
  69.3 7.6 %collective-permute-start.22 = (f32[2,2,128,128]{3,2,1,0:T(8,128)S(1)}, f32[2,2,128,128]{3,2,1,0:T(8,128)S(1)}, u32[]{:S(2)}, u32[]{:S(2)}) collective-permute-start(f32[2,2,128,128]{3,2,1,0:T(8,128)S(1)} %get-tuple-element.187), channel_id=1, source_target_pairs={{0,2},{1,3},{2,0},{3,1},{4,6},{5,7},{6,4},{7,5},{8,10},{9,11},{10,... | collective-permute-start | bytes 786440 | tf_op jit(solution)/shard_map/ppermute | solution.py:600
  69.9 8.0 %collective-permute-start.23 = (f32[2,2,128,128]{3,2,1,0:T(8,128)S(1)}, f32[2,2,128,128]{3,2,1,0:T(8,128)S(1)}, u32[]{:S(2)}, u32[]{:S(2)}) collective-permute-start(f32[2,2,128,128]{3,2,1,0:T(8,128)S(1)} %get-tuple-element.188), channel_id=1, source_target_pairs={{0,4},{1,5},{2,6},{3,7},{4,0},{5,1},{6,2},{7,3},{8,12},{9,13},{10,... | collective-permute-start | bytes 786440 | tf_op jit(solution)/shard_map/ppermute | solution.py:600
  71.1 12.0 %collective-permute-start.24 = (f32[2,2,128,128]{3,2,1,0:T(8,128)S(1)}, f32[2,2,128,128]{3,2,1,0:T(8,128)S(1)}, u32[]{:S(2)}, u32[]{:S(2)}) collective-permute-start(f32[2,2,128,128]{3,2,1,0:T(8,128)S(1)} %get-tuple-element.189), channel_id=1, source_target_pairs={{0,6},{1,7},{2,4},{3,5},{4,2},{5,3},{6,0},{7,1},{8,14},{9,15},{10,... | collective-permute-start | bytes 786440 | tf_op jit(solution)/shard_map/ppermute | solution.py:600
  72.0 14.9 %collective-permute-start.28 = (f32[128,256]{1,0:T(8,128)S(1)}, f32[128,256]{1,0:T(8,128)S(1)}, u32[]{:S(2)}, u32[]{:S(2)}) collective-permute-start(f32[128,256]{1,0:T(8,128)S(1)} %get-tuple-element.195), channel_id=1, source_target_pairs={{0,8},{8,16},{16,24},{24,0},{1,9},{9,17},{17,25},{25,1},{2,10},{10... | collective-permute-start | bytes 393224 | tf_op jit(solution)/shard_map/ppermute | solution.py:564
  72.1 14.9 %collective-permute-start.29 = (f32[128,256]{1,0:T(8,128)S(1)}, f32[128,256]{1,0:T(8,128)S(1)}, u32[]{:S(2)}, u32[]{:S(2)}) collective-permute-start(f32[128,256]{1,0:T(8,128)S(1)} %get-tuple-element.196), channel_id=1, source_target_pairs={{0,16},{8,24},{16,0},{24,8},{1,17},{9,25},{17,1},{25,9},{2,18},{10... | collective-permute-start | bytes 393224 | tf_op jit(solution)/shard_map/ppermute | solution.py:564
  76.9 13.4 %collective-permute-start.30 = (f32[128,256]{1,0:T(8,128)S(1)}, f32[128,256]{1,0:T(8,128)S(1)}, u32[]{:S(2)}, u32[]{:S(2)}) collective-permute-start(f32[128,256]{1,0:T(8,128)S(1)} %get-tuple-element.197), channel_id=1, source_target_pairs={{0,24},{8,0},{16,8},{24,16},{1,25},{9,1},{17,9},{25,17},{2,26},{10... | collective-permute-start | bytes 393224 | tf_op jit(solution)/shard_map/ppermute | solution.py:564
  84.1 7.6 %collective-permute-start.25 = (f32[128,256]{1,0:T(8,128)S(1)}, f32[128,256]{1,0:T(8,128)S(1)}, u32[]{:S(2)}, u32[]{:S(2)}) collective-permute-start(f32[128,256]{1,0:T(8,128)S(1)} %get-tuple-element.191), channel_id=1, source_target_pairs={{0,8},{8,16},{16,24},{24,0},{1,9},{9,17},{17,25},{25,1},{2,10},{10... | collective-permute-start | bytes 393224 | tf_op jit(solution)/shard_map/ppermute | solution.py:564
  84.1 11.4 %collective-permute-start.26 = (f32[128,256]{1,0:T(8,128)S(1)}, f32[128,256]{1,0:T(8,128)S(1)}, u32[]{:S(2)}, u32[]{:S(2)}) collective-permute-start(f32[128,256]{1,0:T(8,128)S(1)} %get-tuple-element.192), channel_id=1, source_target_pairs={{0,16},{8,24},{16,0},{24,8},{1,17},{9,25},{17,1},{25,9},{2,18},{10... | collective-permute-start | bytes 393224 | tf_op jit(solution)/shard_map/ppermute | solution.py:564
  86.9 12.1 %collective-permute-start.27 = (f32[128,256]{1,0:T(8,128)S(1)}, f32[128,256]{1,0:T(8,128)S(1)}, u32[]{:S(2)}, u32[]{:S(2)}) collective-permute-start(f32[128,256]{1,0:T(8,128)S(1)} %get-tuple-element.193), channel_id=1, source_target_pairs={{0,24},{8,0},{16,8},{24,16},{1,25},{9,1},{17,9},{25,17},{2,26},{10... | collective-permute-start | bytes 393224 | tf_op jit(solution)/shard_map/ppermute | solution.py:564
  86.9 14.2 %collective-permute-start.31 = (f32[128,256]{1,0:T(8,128)S(1)}, f32[128,256]{1,0:T(8,128)S(1)}, u32[]{:S(2)}, u32[]{:S(2)}) collective-permute-start(f32[128,256]{1,0:T(8,128)S(1)} %get-tuple-element.199), channel_id=1, source_target_pairs={{8,16},{16,24},{9,17},{17,25},{10,18},{18,26},{11,19},{19,27},{12,... | collective-permute-start | bytes 393224 | tf_op jit(solution)/shard_map/ppermute | solution.py:564
  90.3 10.8 %collective-permute-start.32 = (f32[128,256]{1,0:T(8,128)S(1)}, f32[128,256]{1,0:T(8,128)S(1)}, u32[]{:S(2)}, u32[]{:S(2)}) collective-permute-start(f32[128,256]{1,0:T(8,128)S(1)} %get-tuple-element.200), channel_id=1, source_target_pairs={{8,24},{16,0},{9,25},{17,1},{10,26},{18,2},{11,27},{19,3},{12,28},... | collective-permute-start | bytes 393224 | tf_op jit(solution)/shard_map/ppermute | solution.py:564
  91.6 13.0 %collective-permute-start.33 = (f32[128,256]{1,0:T(8,128)S(1)}, f32[128,256]{1,0:T(8,128)S(1)}, u32[]{:S(2)}, u32[]{:S(2)}) collective-permute-start(f32[128,256]{1,0:T(8,128)S(1)} %get-tuple-element.201), channel_id=1, source_target_pairs={{8,0},{16,8},{9,1},{17,9},{10,2},{18,10},{11,3},{19,11},{12,4},{20... | collective-permute-start | bytes 393224 | tf_op jit(solution)/shard_map/ppermute | solution.py:564
  (10 other events, 155.8 us)
